TPU v7x, 32 devices: a whole 2x2x4 slice. The times are simulated.
32 devices in a mesh: fib: 4 (over z), wav: 4 (over y, x), exp: 2 (over core).
Axes of the slice: x: 2, y: 2, z: 4, core: 2. Of those that a mesh axis runs over, the one named last changes fastest.
Arguments:
- pixels: float32 [8, 1920, 1024], P('exp', 'wav', 'fib'), may hold values from -6 to 6
- pixel_ivar: float32 [8, 1920, 1024], P('exp', 'wav', 'fib'), may hold values from 0.25 to 4
- clip_bits: int32 [8, 128, 1024], P('exp', 'wav', 'fib'), may hold values from 0 to 32767
- coupling: float32 [1024], P('fib'), may hold values from 0.5 to 200
- counts: int32 [1024], P('fib'), may hold values from 1 to 8
- good_flags: int32 [8, 1024], P('exp', 'fib'), may hold values 0 or 1
- owner_slot: int32 [1024], replicated, may hold values from 0 to 1023, as said below
Outputs:
- coadd_flux: float32 [1920, 1024], P(('wav', 'exp'), 'fib')
- coadd_ivar: float32 [1920, 1024], P(('wav', 'exp'), 'fib')
- coadd_res: float32 [3, 1920, 1024], P(None, ('wav', 'exp'), 'fib')
Inputs may be any that keep to these rules, and one draw needn't show every extreme that they name: A permutation of the fibres; fibre f belongs to coadd index owner_slot[f] // 256 of fib, and the 256 fibres of each index of fib go 64 to every coadd index.
All inputs are finite; a program needn't handle non-finite values. No bound on the sum of `good_flags` on one device may be relied on, other than what follows from the above.
Results may differ from a plain program's by a relative error of at most 0.0001.
Values sent between devices are 32-bit elements; how exact they have to be, the bound alone decides.
No kernel may reach another device: no remote copies, remote signals or barrier semaphores. Data moves between devices by JAX's collectives and lax.ppermute only.
A program may use at most 128 MiB of HBM per device.

v0:
```python
import functools

import jax
import jax.numpy as jnp
from jax import lax
from jax.experimental import pallas as pl
from jax.experimental.pallas import tpu as pltpu
from jax.sharding import PartitionSpec as P

HALO = 50
BITS = 15
LANES = 128
ROWS = 8
GROUP = 120
VMEM_BYTES = 48 * 1024 * 1024
F32 = jnp.float32
BF16 = jnp.bfloat16
NT = (((1,), (1,)), ((), ()))

in_vmem = pl.BlockSpec(memory_space=pltpu.VMEM)
in_smem = pl.BlockSpec(memory_space=pltpu.SMEM)
in_place = pl.BlockSpec(memory_space=pl.ANY)


def params():
    return pltpu.CompilerParams(vmem_limit_bytes=VMEM_BYTES)


def cost(flops, moved):
    return pl.CostEstimate(flops=int(flops), bytes_accessed=int(moved), transcendentals=0)


def shaped(shape, dtype=F32):
    return jax.ShapeDtypeStruct(shape, dtype)


def usable_rows(place_ref, counts_ref, good_ref):
    count = good_ref.shape[0]
    return [
        good_ref[e : e + 1, :].astype(F32)
        * jnp.where(place_ref[2] * count + e < counts_ref[...], 1.0, 0.0)
        for e in range(count)
    ]


def tile_bits(tile):
    first, last = (ROWS * tile) // BITS, (ROWS * tile + ROWS - 1) // BITS
    split = BITS * last - ROWS * tile
    row = lax.broadcasted_iota(jnp.int32, (ROWS, 1), 0)
    word = jnp.where(row >= split, last, first)
    return first, last, split, jnp.left_shift(1, ROWS * tile + row - BITS * word)


def tile_words(words, tile):
    first, last, split, mask = tile_bits(tile)
    picked = words[first : first + 1, :]
    if last != first:
        row = lax.broadcasted_iota(jnp.int32, (ROWS, 1), 0)
        picked = jnp.where(row >= split, words[last : last + 1, :], picked)
    return (picked & mask) != 0


def weights_kernel(total, place_ref, coupling_ref, counts_ref, good_ref, ivar_ref, bits_ref, theirs_ref, mine_ref):
    step = pl.program_id(0)
    steps = pl.num_programs(0)
    expos, group, _ = ivar_ref.shape
    at = (step + (1 - place_ref[2]) * (steps // 2)) % steps
    start = place_ref[1] * (steps * group) + at * group
    coupling = coupling_ref[...]
    usable = usable_rows(place_ref, counts_ref, good_ref)
    tiles = group // ROWS
    results = []
    for tile in range(tiles):
        links = 4.0 * coupling
        if tile in (0, tiles - 1):
            row = start + ROWS * tile + lax.broadcasted_iota(jnp.int32, (ROWS, 1), 0)
            links = jnp.where((row == 0) | (row == total - 1), 2.0, 4.0) * coupling
        weight_sum = band_sum = None
        for e in range(expos):
            ivar = ivar_ref[e, ROWS * tile : ROWS * (tile + 1), :]
            kept = tile_words(bits_ref[e], tile)
            weight = jnp.where(kept, ivar * usable[e], 0.0)
            band = weight / (ivar + links)
            weight_sum = weight if e == 0 else weight_sum + weight
            band_sum = band if e == 0 else band_sum + band
        results.append((weight_sum, band_sum * coupling))

    def store(ref):
        for tile, pair in enumerate(results):
            ref[0, ROWS * tile : ROWS * (tile + 1), :] = pair[0]
            ref[1, ROWS * tile : ROWS * (tile + 1), :] = pair[1]

    @pl.when(step < steps // 2)
    def _():
        store(theirs_ref)

    @pl.when(step >= steps // 2)
    def _():
        store(mine_ref)


def weight_sums(place, coupling, counts, good, ivar, bits, total):
    expos, width, fibres = ivar.shape
    steps = width // GROUP
    half = steps // 2

    def at(i, place):
        return (i + (1 - place[2]) * half) % steps

    row = pl.BlockSpec((1, fibres), lambda i, place: (0, 0))
    out = shaped((2, width // 2, fibres))
    return pl.pallas_call(
        functools.partial(weights_kernel, total),
        grid_spec=pltpu.PrefetchScalarGridSpec(
            num_scalar_prefetch=1,
            grid=(steps,),
            in_specs=[
                row,
                row,
                pl.BlockSpec((expos, fibres), lambda i, place: (0, 0)),
                pl.BlockSpec((expos, GROUP, fibres), lambda i, place: (0, at(i, place), 0)),
                pl.BlockSpec((expos, GROUP // BITS, fibres), lambda i, place: (0, at(i, place), 0)),
            ],
            out_specs=[
                pl.BlockSpec((2, GROUP, fibres), lambda i, place: (0, jnp.minimum(i, half - 1), 0)),
                pl.BlockSpec((2, GROUP, fibres), lambda i, place: (0, jnp.maximum(i - half, 0), 0)),
            ],
        ),
        out_shape=[out, out],
        compiler_params=params(),
        cost_estimate=cost(20 * ivar.size, 6 * ivar.size),
        name="weight_sums",
    )(place, coupling, counts, good, ivar, bits)


def stream_coupling(coupling_ref, expos):
    coupling = coupling_ref[...]
    blocks = coupling.shape[1] // LANES
    return jnp.concatenate(
        [jnp.broadcast_to(coupling[:, h * LANES : (h + 1) * LANES], (expos, LANES)) for h in range(blocks)], 0
    )


def fetch_streams(source_ref, first, count, scratch_ref, sems, sem_at):
    expos, _, fibres = source_ref.shape
    copies = []
    for h in range(fibres // LANES):
        for e in range(expos):
            stream = h * expos + e
            copy = pltpu.make_async_copy(
                source_ref.at[e, pl.ds(first, count), pl.ds(h * LANES, LANES)],
                scratch_ref.at[pl.ds(stream * count, count), :],
                sems.at[sem_at + stream],
            )
            copy.start()
            copies.append(copy)
    return copies


def advance(state, ivar, pixel, back_coupling):
    n, d, b = state
    d = d + n * back_coupling
    return (n + ivar * d, d, b + (ivar * pixel) * d)


def prep_kernel(
    fib_count, pack, per, rel, place_ref, coupling_ref, slots_ref, pixels_ref, ivar_ref,
    edges_ref, send_ref, recv_ref, ivar_s, pixel_s, sems,
):
    expos, width, fibres = pixels_ref.shape
    streams = expos * fibres // LANES
    count = ivar_s.shape[1] // streams
    waits = []
    for side, first in enumerate((width - count, 0)):
        waits += fetch_streams(ivar_ref, first, count, ivar_s.at[side], sems, (2 * side) * streams)
        waits += fetch_streams(pixels_ref, first, count, pixel_s.at[side], sems, (2 * side + 1) * streams)

    lanes = pack * per
    me = place_ref[0]
    slots = slots_ref[...].astype(F32)
    owner = jnp.floor((slots + 0.5) * (1.0 / fibres))
    slot_within = slots - owner * fibres
    sources = slots.shape[0]
    source = lax.broadcasted_iota(jnp.int32, (sources, fibres), 0)
    my_owner = jnp.sum(jnp.where(source == me, owner, 0.0), axis=0, keepdims=True).astype(jnp.int32)
    rows_i = lax.broadcasted_iota(jnp.int32, (fibres, fibres), 0)
    cols_i = lax.broadcasted_iota(jnp.int32, (fibres, fibres), 1)
    earlier = (rows_i < cols_i).astype(F32).astype(BF16)
    to_owner = (source == my_owner).astype(F32)
    counted = jnp.dot(to_owner.astype(BF16), earlier, preferred_element_type=F32)
    rank = jnp.sum(to_owner * counted, axis=0, keepdims=True).astype(jnp.int32)
    target = my_owner
    if rel:
        target = jnp.where(my_owner >= me, my_owner - me, my_owner - me + fib_count)
    base = target * lanes + rank
    place_of = jnp.concatenate([base + h * per for h in range(pack)], 1)
    total_lanes = fib_count * lanes
    wide = lax.broadcasted_iota(jnp.int32, (total_lanes, pack * fibres), 0)
    send_ref[...] = (wide == place_of).astype(F32).astype(BF16)

    mine = (owner == me.astype(F32)).astype(F32)
    rank_in = jnp.dot(mine.astype(BF16), earlier, preferred_element_type=F32).astype(jnp.int32)
    order = source
    if rel:
        order = jnp.where(me >= source, me - source, me - source + fib_count)
    arrival = jnp.where(mine > 0.0, order * lanes + rank_in, -total_lanes)
    tall = lax.broadcasted_iota(jnp.int32, (total_lanes, fibres), 0)
    landing = jnp.zeros((ROWS, total_lanes), F32)
    for s in range(fib_count):
        hit = tall == arrival[s : s + 1, :]
        for h in range(1, pack):
            hit = hit | (tall == arrival[s : s + 1, :] + h * per)
        values = jnp.broadcast_to(slot_within[s : s + 1, :], (ROWS, fibres)).astype(BF16)
        landing = landing + lax.dot_general(
            values, hit.astype(F32).astype(BF16), NT, preferred_element_type=F32
        )
    lane = lax.broadcasted_iota(jnp.int32, (1, total_lanes), 1)
    landing = landing[0:1, :].astype(jnp.int32)
    for h in range(1, pack):
        inside = (lane % lanes >= h * per) & (lane % lanes < (h + 1) * per)
        landing = jnp.where(inside, landing + h * fibres, landing)
    high = lax.broadcasted_iota(jnp.int32, (pack * fibres, total_lanes), 0)
    recv_ref[...] = (high == landing).astype(F32).astype(BF16)

    for wait in waits:
        wait.wait()
    back = 1.0 / stream_coupling(coupling_ref, expos)
    zero = jnp.zeros((streams, LANES), F32)
    states = [(zero, zero + 1.0, zero), (zero, zero + 1.0, zero)]
    for i in range(HALO):
        for side, row in enumerate((count - HALO + i, HALO - 1 - i)):
            at = pl.ds(row, streams, stride=count)
            states[side] = advance(states[side], ivar_s[side, at, :], pixel_s[side, at, :], back)
            if i % 10 == 9:
                scale = 1.0 / states[side][1]
                states[side] = tuple(part * scale for part in states[side])
    for side in range(2):
        n, d, b = states[side]
        scale = 1.0 / (d + n * back)
        edges_ref[side, 0] = n * scale
        edges_ref[side, 1] = b * scale


def prepare(place, coupling, slots, pixels, ivar, pack, per, rel):
    expos, width, fibres = pixels.shape
    fib_count = slots.shape[0]
    if fib_count % ROWS:
        slots = jnp.concatenate([slots, jnp.full((ROWS - fib_count % ROWS, fibres), -1, slots.dtype)], 0)
    streams = expos * fibres // LANES
    count = -(-HALO // ROWS) * ROWS
    total_lanes = fib_count * pack * per
    return pl.pallas_call(
        functools.partial(prep_kernel, fib_count, pack, per, rel),
        in_specs=[in_smem, in_vmem, in_vmem, in_place, in_place],
        out_specs=[in_vmem, in_vmem, in_vmem],
        out_shape=[
            shaped((2, 2, streams, LANES)),
            shaped((total_lanes, pack * fibres), BF16),
            shaped((pack * fibres, total_lanes), BF16),
        ],
        scratch_shapes=[
            pltpu.VMEM((2, streams * count, LANES), F32),
            pltpu.VMEM((2, streams * count, LANES), F32),
            pltpu.SemaphoreType.DMA((4 * streams,)),
        ],
        compiler_params=params(),
        cost_estimate=cost(1e8, 2e6),
        name="prepare",
    )(place, coupling, slots, pixels, ivar)


def solve_kernel(
    place_ref, coupling_ref, counts_ref, good_ref, left_ref, right_ref, pixels_ref, ivar_ref, bits_ref,
    theirs_ref, mine_ref, ivar_s, pixel_s, lead_s, rest_s, sems,
):
    expos, width, fibres = pixels_ref.shape
    streams = expos * fibres // LANES
    middle = width // 2
    waits = fetch_streams(ivar_ref, 0, width, ivar_s, sems, 0)
    waits += fetch_streams(pixels_ref, 0, width, pixel_s, sems, streams)
    coupling = stream_coupling(coupling_ref, expos)
    back = 1.0 / coupling
    for wait in waits:
        wait.wait()

    def row_at(i):
        return pl.ds(i, streams, stride=width)

    def begin(edge_ref):
        u = edge_ref[0]
        return (u, 1.0 - u * back, edge_ref[1])

    def keep(side, i, state):
        n, d, b = state
        inverse = 1.0 / (d + n * back)
        lead_s[side, i] = d * inverse
        rest_s[side, i] = (b * back) * inverse

    def eliminate(it, states):
        states = list(states)
        for k in range(ROWS):
            i = it * ROWS + k
            for side, row in enumerate((i, width - 1 - i)):
                keep(side, i, states[side])
                states[side] = advance(states[side], ivar_s[row_at(row), :], pixel_s[row_at(row), :], back)
        scaled = []
        for n, d, b in states:
            scale = 1.0 / d
            scaled.append((n * scale, d * scale, b * scale))
        return tuple(scaled)

    states = lax.fori_loop(0, middle // ROWS, eliminate, (begin(left_ref), begin(right_ref)))
    for side in range(2):
        keep(side, middle, states[side])
    lead, rest = lead_s[0, middle], rest_s[0, middle]
    lead_r, rest_r = lead_s[1, middle], rest_s[1, middle]
    left = (rest + lead * rest_r) / (1.0 - lead * lead_r)
    right = rest_r + lead_r * left

    def substitute(it, values):
        values = list(values)
        for k in range(ROWS):
            i = middle - 1 - (it * ROWS + k)
            for side, row in enumerate((i, width - 1 - i)):
                pixel_s[row_at(row), :] = values[side]
                values[side] = rest_s[side, i] + lead_s[side, i] * values[side]
        return tuple(values)

    lax.fori_loop(0, middle // ROWS, substitute, (left, right))

    usable = usable_rows(place_ref, counts_ref, good_ref)
    groups = width // GROUP
    blocks = fibres // LANES

    def coadd(out_ref, which):
        def body(g, carry):
            start = (which * (groups // 2) + g) * GROUP
            words_at = (which * (groups // 2) + g) * (GROUP // BITS)
            words = [bits_ref[e, pl.ds(pl.multiple_of(words_at, GROUP // BITS), GROUP // BITS), :] for e in range(expos)]
            for tile in range(GROUP // ROWS):
                kept = [tile_words(words[e], tile) for e in range(expos)]
                for h in range(blocks):
                    cut = slice(h * LANES, (h + 1) * LANES)
                    total = None
                    for e in range(expos):
                        at = pl.ds(pl.multiple_of((h * expos + e) * width + start + ROWS * tile, ROWS), ROWS)
                        weight = jnp.where(kept[e][:, cut], ivar_s[at, :] * usable[e][:, cut], 0.0)
                        term = weight * pixel_s[at, :]
                        total = term if e == 0 else total + term
                    out_ref[pl.ds(pl.multiple_of(g * GROUP + ROWS * tile, ROWS), ROWS), cut] = total
            return carry

        lax.fori_loop(0, groups // 2, body, 0)

    coadd(theirs_ref, 1 - place_ref[2])
    coadd(mine_ref, place_ref[2])


def flux_sums(place, coupling, counts, good, left, right, pixels, ivar, bits):
    expos, width, fibres = pixels.shape
    streams = expos * fibres // LANES
    out = shaped((width // 2, fibres))
    stream_scratch = pltpu.VMEM((streams * width, LANES), F32)
    factor_scratch = pltpu.VMEM((2, width // 2 + 1, streams, LANES), F32)
    return pl.pallas_call(
        solve_kernel,
        in_specs=[in_smem] + [in_vmem] * 5 + [in_place, in_place, in_vmem],
        out_specs=[in_vmem, in_vmem],
        out_shape=[out, out],
        scratch_shapes=[
            stream_scratch,
            stream_scratch,
            factor_scratch,
            factor_scratch,
            pltpu.SemaphoreType.DMA((2 * streams,)),
        ],
        compiler_params=params(),
        cost_estimate=cost(30 * pixels.size, 10 * pixels.size),
        name="flux_sums",
    )(place, coupling, counts, good, left, right, pixels, ivar, bits)


def split_dot(x, table, dims):
    top = x.astype(BF16)
    low = (x - top.astype(F32)).astype(BF16)
    both = lax.dot_general(jnp.concatenate([top, low], 0), table, dims, preferred_element_type=F32)
    return both[: x.shape[0]] + both[x.shape[0] :]


def sort_kernel(pack, theirs_ref, mine_ref, table_ref, *out_refs):
    values, rows, _ = mine_ref.shape
    part = rows // pack
    totals = [mine_ref[v] + theirs_ref[v] for v in range(values)]
    x = jnp.concatenate(
        [jnp.concatenate([t[h * part : (h + 1) * part] for h in range(pack)], 1) for t in totals], 0
    )
    moved = split_dot(x, table_ref[...], NT)
    lanes = moved.shape[1] // len(out_refs)
    for d, out_ref in enumerate(out_refs):
        for v in range(values):
            out_ref[v] = moved[v * part : (v + 1) * part, d * lanes : (d + 1) * lanes]


def sort_fibres(theirs, mine, table, pack, pieces):
    values, rows, _ = mine.shape
    lanes = table.shape[0] // pieces
    return pl.pallas_call(
        functools.partial(sort_kernel, pack),
        in_specs=[in_vmem] * 3,
        out_specs=[in_vmem] * pieces,
        out_shape=[shaped((values, rows // pack, lanes))] * pieces,
        compiler_params=params(),
        cost_estimate=cost(4 * values * rows * table.size // pack, 3 * mine.size * 4),
        name="sort_fibres",
    )(theirs, mine, table)


def exchange(pieces, fib_count):
    if len(pieces) == 1:
        return [lax.all_to_all(pieces[0], "fib", split_axis=2, concat_axis=2, tiled=True)]
    arrived = [pieces[0]]
    for d in range(1, fib_count):
        arrived.append(lax.ppermute(pieces[d], "fib", [(i, (i + d) % fib_count) for i in range(fib_count)]))
    return arrived


def landed(refs, table):
    values, part, _ = refs[0].shape
    x = jnp.concatenate(
        [jnp.concatenate([ref[v] for ref in refs], 1) if len(refs) > 1 else refs[0][v] for v in range(values)], 0
    )
    moved = split_dot(x, table, NT)
    return [moved[v * part : (v + 1) * part] for v in range(values)]


def weights_end_kernel(pack, total, place_ref, table_ref, *refs):
    *piece_refs, ivar_ref, res_ref = refs
    weight, band = landed(piece_refs, table_ref[...])
    rows, fibres = ivar_ref.shape
    part = rows // pack
    start = (place_ref[1] * 2 + place_ref[2]) * rows
    for h in range(pack):
        at = slice(h * part, (h + 1) * part)
        cut = slice(h * fibres, (h + 1) * fibres)
        row = start + h * part + lax.broadcasted_iota(jnp.int32, (part, 1), 0)
        w, b = weight[:, cut], band[:, cut]
        inverse = 1.0 / jnp.maximum(w, 1.0)
        before = jnp.where(row == 0, 0.0, b)
        after = jnp.where(row == total - 1, 0.0, b)
        ivar_ref[at, :] = w
        res_ref[0, at, :] = before * inverse
        res_ref[1, at, :] = (w - before - after) * inverse
        res_ref[2, at, :] = after * inverse


def end_weights(place, table, pieces, pack, fibres, total):
    rows = pieces[0].shape[1] * pack
    return pl.pallas_call(
        functools.partial(weights_end_kernel, pack, total),
        in_specs=[in_smem] + [in_vmem] * (1 + len(pieces)),
        out_specs=[in_vmem] * 2,
        out_shape=[shaped((rows, fibres)), shaped((3, rows, fibres))],
        compiler_params=params(),
        cost_estimate=cost(4 * rows * table.size, 6 * rows * fibres * 4),
        name="end_weights",
    )(place, table, *pieces)


def flux_end_kernel(pack, table_ref, ivar_ref, *refs):
    *piece_refs, flux_ref = refs
    (flux,) = landed(piece_refs, table_ref[...])
    rows, fibres = flux_ref.shape
    part = rows // pack
    for h in range(pack):
        at = slice(h * part, (h + 1) * part)
        flux_ref[at, :] = flux[:, h * fibres : (h + 1) * fibres] / jnp.maximum(ivar_ref[at, :], 1.0)


def end_flux(table, ivar, pieces, pack):
    rows, fibres = ivar.shape
    return pl.pallas_call(
        functools.partial(flux_end_kernel, pack),
        in_specs=[in_vmem] * (2 + len(pieces)),
        out_specs=in_vmem,
        out_shape=shaped((rows, fibres)),
        compiler_params=params(),
        cost_estimate=cost(2 * rows * table.size, 3 * rows * fibres * 4),
        name="end_flux",
    )(table, ivar, *pieces)


def per_device(pixels, pixel_ivar, clip_bits, coupling, counts, good_flags, owner_slot):
    expos, width, fibres = pixels.shape
    fib_count, wav_count = lax.axis_size("fib"), lax.axis_size("wav")
    total = width * wav_count
    per = fibres // fib_count
    rows = width // 2
    pack = max(1, LANES // per)
    while pack > 1 and rows % (pack * ROWS):
        pack //= 2
    rel = pack * per == LANES
    pieces = fib_count if rel else 1
    place = jnp.stack([lax.axis_index(axis) for axis in ("fib", "wav", "exp")]).astype(jnp.int32)
    coupling, counts = coupling[None], counts[None]
    swap = [(0, 1), (1, 0)]

    theirs, mine = weight_sums(place, coupling, counts, good_flags, pixel_ivar, clip_bits, total)
    theirs = lax.ppermute(theirs, "exp", swap)
    edges, send_table, recv_table = prepare(
        place, coupling, owner_slot.reshape(fib_count, fibres), pixels, pixel_ivar, pack, per, rel
    )
    up = [(i, i + 1) for i in range(wav_count - 1)]
    left = lax.ppermute(edges[0], "wav", up)
    right = lax.ppermute(edges[1], "wav", [(j, i) for i, j in up])
    weight_pieces = exchange(sort_fibres(theirs, mine, send_table, pack, pieces), fib_count)

    theirs, mine = flux_sums(
        place, coupling, counts, good_flags, left, right, pixels, pixel_ivar, clip_bits
    )
    theirs = lax.ppermute(theirs, "exp", swap)
    flux_pieces = exchange(sort_fibres(theirs[None], mine[None], send_table, pack, pieces), fib_count)

    ivar, res = end_weights(place, recv_table, weight_pieces, pack, fibres, total)
    flux = end_flux(recv_table, ivar, flux_pieces, pack)
    return (flux, ivar, res)


def solution(mesh):
    return jax.shard_map(
        per_device,
        mesh=mesh,
        in_specs=(
            P("exp", "wav", "fib"),
            P("exp", "wav", "fib"),
            P("exp", "wav", "fib"),
            P("fib"),
            P("fib"),
            P("exp", "fib"),
            P(),
        ),
        out_specs=(
            P(("wav", "exp"), "fib"),
            P(("wav", "exp"), "fib"),
            P(None, ("wav", "exp"), "fib"),
        ),
        check_vma=False,
    )
```

profile of v0, /device:TPU:13, one launch (start us, length us, event | category | flops | bytes accessed | tf_op | source)
XLA Modules:
  0.0 49.0 jit_solution(8861090188775170254)
XLA Ops:
  0.7 1.5 %copy-done = f32[4,480,256]{2,1,0:T(8,128)S(1)} copy-done((f32[4,480,256]{2,1,0:T(8,128)S(1)}, f32[4,480,256]{2,1,0:T(8,128)}, u32[]{:S(2)}) %copy-start) | copy-done | bytes 1966104
  2.3 0.9 %copy-done.3 = s32[4,32,256]{2,1,0:T(8,128)S(1)} copy-done((s32[4,32,256]{2,1,0:T(8,128)S(1)}, s32[4,32,256]{2,1,0:T(8,128)}, u32[]{:S(2)}) %copy-start.3) | copy-done | bytes 131096
  3.2 0.7 %copy-done.6 = s32[4,256]{1,0:T(4,128)S(1)} copy-done((s32[4,256]{1,0:T(4,128)S(1)}, s32[4,256]{1,0:T(4,128)}, u32[]{:S(2)}) %copy-start.6) | copy-done | bytes 4120
  3.9 0.7 %copy-done.8 = f32[256]{0:T(256)S(1)} copy-done((f32[256]{0:T(256)S(1)}, f32[256]{0:T(256)}, u32[]{:S(2)}) %copy-start.8) | copy-done | bytes 1048
  4.6 0.7 %copy-done.10 = s32[256]{0:T(256)S(1)} copy-done((s32[256]{0:T(256)S(1)}, s32[256]{0:T(256)}, u32[]{:S(2)}) %copy-start.10) | copy-done | bytes 1048
  5.2 1.8 %weight_sums.1 = (f32[2,240,256]{2,1,0:T(8,128)S(1)}, f32[2,240,256]{2,1,0:T(8,128)S(1)}) custom-call(s32[3]{0:T(128)S(1)} %pad_add_fusion.place_ref, f32[1,256]{1,0:T(1,128)S(1)} %bitcast.13, s32[1,256]{1,0:T(1,128)S(1)} %bitcast.16, s32[4,256]{1,0:T(4,128)S(1)} %copy-done.6, f32[4,480,256]{2,1,0:T(8,128)S(1)} %copy-done, s32[4,32,256]{2,1,0:T(8,128)S(1)} %copy-done.3), custom_call_target="tpu_custom_call" | custom-call | flops 9830400 | bytes 2949120 | tf_op jit(solution)/shard_map/weight_sums/pallas_call | solution.py:112
  7.0 0.7 %collective-permute-start = (f32[2,240,256]{2,1,0:T(8,128)S(1)}, f32[2,240,256]{2,1,0:T(8,128)S(1)}, u32[]{:S(2)}, u32[]{:S(2)}) collective-permute-start(f32[2,240,256]{2,1,0:T(8,128)S(1)} %get-tuple-element.21), channel_id=1, source_target_pairs={{0,1},{1,0},{2,3},{3,2},{4,5},{5,4},{6,7},{7,6},{8,9},{9,8},{10,11... | collective-permute-start | bytes 1474568 | tf_op jit(solution)/shard_map/ppermute | solution.py:508
  7.8 1.5 %copy-done.2 = f32[4,480,256]{2,1,0:T(8,128)S(1)} copy-done((f32[4,480,256]{2,1,0:T(8,128)S(1)}, f32[4,480,256]{2,1,0:T(8,128)}, u32[]{:S(2)}) %copy-start.2) | copy-done | bytes 1966104
  9.4 2.4 %prepare.1 = (f32[2,2,8,128]{3,2,1,0:T(8,128)S(1)}, bf16[512,512]{1,0:T(8,128)(2,1)S(1)}, bf16[512,512]{1,0:T(8,128)(2,1)S(1)}) custom-call(s32[3]{0:T(128)S(1)} %pad_add_fusion.place_ref, f32[1,256]{1,0:T(1,128)S(1)} %bitcast.14, s32[8,256]{1,0:T(8,128)S(1)} %concatenate.3.slots_ref, f32[4,480,256]{2,1,0:T(8,128)S(1)} %copy-done.2, f32[4,480,256]{2,1,0:T(8,128)S(1)} %copy-done.1), custom_call_target="tpu_custom_call" | custom-call | flops 100000000 | bytes 2000000 | tf_op jit(solution)/shard_map/prepare/pallas_call | solution.py:252
  11.8 3.1 %collective-permute-start.5 = (f32[2,8,128]{2,1,0:T(8,128)S(1)}, f32[2,8,128]{2,1,0:T(8,128)S(1)}, u32[]{:S(2)}, u32[]{:S(2)}) collective-permute-start(f32[2,8,128]{2,1,0:T(8,128)S(1)} %get-tuple-element.37), channel_id=1, source_target_pairs={{2,0},{4,2},{6,4},{3,1},{5,3},{7,5},{10,8},{12,10},{14,12},{11,9},... | collective-permute-start | bytes 24584 | tf_op jit(solution)/shard_map/ppermute | solution.py:514
  14.8 2.2 %collective-permute-start.4 = (f32[2,8,128]{2,1,0:T(8,128)S(1)}, f32[2,8,128]{2,1,0:T(8,128)S(1)}, u32[]{:S(2)}, u32[]{:S(2)}) collective-permute-start(f32[2,8,128]{2,1,0:T(8,128)S(1)} %get-tuple-element.38), channel_id=1, source_target_pairs={{0,2},{2,4},{4,6},{1,3},{3,5},{5,7},{8,10},{10,12},{12,14},{9,11},... | collective-permute-start | bytes 24584 | tf_op jit(solution)/shard_map/ppermute | solution.py:513
  17.1 3.1 %collective-permute-done.4.left_ref = f32[2,8,128]{2,1,0:T(8,128)S(1)} collective-permute-done((f32[2,8,128]{2,1,0:T(8,128)S(1)}, f32[2,8,128]{2,1,0:T(8,128)S(1)}, u32[]{:S(2)}, u32[]{:S(2)}) %collective-permute-start.4) | collective-permute-done | bytes 8224 | tf_op jit(solution)/shard_map/ppermute | solution.py:513
  20.2 5.5 %flux_sums.1 = (f32[240,256]{1,0:T(8,128)S(1)}, f32[240,256]{1,0:T(8,128)S(1)}) custom-call(s32[3]{0:T(128)S(1)} %pad_add_fusion.place_ref, f32[1,256]{1,0:T(1,128)S(1)} %bitcast.15, s32[1,256]{1,0:T(1,128)S(1)} %bitcast.17, s32[4,256]{1,0:T(4,128)S(1)} %copy-done.7, f32[2,8,128]{2,1,0:T(8,128)S(1)} %collective-permute-done.4.left_ref, ...), custom_call_target="tpu_custom_call" | custom-call | flops 14745600 | bytes 4915200 | tf_op jit(solution)/shard_map/flux_sums/pallas_call | solution.py:365
  25.7 1.5 %collective-permute-start.6 = (f32[240,256]{1,0:T(8,128)S(1)}, f32[240,256]{1,0:T(8,128)S(1)}, u32[]{:S(2)}, u32[]{:S(2)}) collective-permute-start(f32[240,256]{1,0:T(8,128)S(1)} %get-tuple-element.30), channel_id=1, source_target_pairs={{0,1},{1,0},{2,3},{3,2},{4,5},{5,4},{6,7},{7,6},{8,9},{9,8},{10,11... | collective-permute-start | bytes 737288 | tf_op jit(solution)/shard_map/ppermute | solution.py:520
  27.7 1.3 %collective-permute-start.1 = (f32[2,120,128]{2,1,0:T(8,128)S(1)}, f32[2,120,128]{2,1,0:T(8,128)S(1)}, u32[]{:S(2)}, u32[]{:S(2)}) collective-permute-start(f32[2,120,128]{2,1,0:T(8,128)S(1)} %get-tuple-element.25), channel_id=1, source_target_pairs={{0,8},{8,16},{16,24},{24,0},{1,9},{9,17},{17,25},{25,1},{2,10},{10... | collective-permute-start | bytes 368648 | tf_op jit(solution)/shard_map/ppermute | solution.py:423
  29.0 1.1 %collective-permute-start.2 = (f32[2,120,128]{2,1,0:T(8,128)S(1)}, f32[2,120,128]{2,1,0:T(8,128)S(1)}, u32[]{:S(2)}, u32[]{:S(2)}) collective-permute-start(f32[2,120,128]{2,1,0:T(8,128)S(1)} %get-tuple-element.26), channel_id=1, source_target_pairs={{0,16},{8,24},{16,0},{24,8},{1,17},{9,25},{17,1},{25,9},{2,18},{10... | collective-permute-start | bytes 368648 | tf_op jit(solution)/shard_map/ppermute | solution.py:423
  30.1 1.4 %collective-permute-start.3 = (f32[2,120,128]{2,1,0:T(8,128)S(1)}, f32[2,120,128]{2,1,0:T(8,128)S(1)}, u32[]{:S(2)}, u32[]{:S(2)}) collective-permute-start(f32[2,120,128]{2,1,0:T(8,128)S(1)} %get-tuple-element.27), channel_id=1, source_target_pairs={{0,24},{8,0},{16,8},{24,16},{1,25},{9,1},{17,9},{25,17},{2,26},{10... | collective-permute-start | bytes 368648 | tf_op jit(solution)/shard_map/ppermute | solution.py:423
  32.0 3.1 %collective-permute-start.8 = (f32[1,120,128]{2,1,0:T(8,128)S(1)}, f32[1,120,128]{2,1,0:T(8,128)S(1)}, u32[]{:S(2)}, u32[]{:S(2)}) collective-permute-start(f32[1,120,128]{2,1,0:T(8,128)S(1)} %get-tuple-element.34), channel_id=1, source_target_pairs={{0,16},{8,24},{16,0},{24,8},{1,17},{9,25},{17,1},{25,9},{2,18},{10... | collective-permute-start | bytes 184328 | tf_op jit(solution)/shard_map/ppermute | solution.py:423
  35.1 7.2 %collective-permute-done.2.refs_2_ = f32[2,120,128]{2,1,0:T(8,128)S(1)} collective-permute-done((f32[2,120,128]{2,1,0:T(8,128)S(1)}, f32[2,120,128]{2,1,0:T(8,128)S(1)}, u32[]{:S(2)}, u32[]{:S(2)}) %collective-permute-start.2) | collective-permute-done | bytes 122912 | tf_op jit(solution)/shard_map/ppermute | solution.py:423
  42.3 2.1 %collective-permute-done.3.refs_3_ = f32[2,120,128]{2,1,0:T(8,128)S(1)} collective-permute-done((f32[2,120,128]{2,1,0:T(8,128)S(1)}, f32[2,120,128]{2,1,0:T(8,128)S(1)}, u32[]{:S(2)}, u32[]{:S(2)}) %collective-permute-start.3) | collective-permute-done | bytes 122912 | tf_op jit(solution)/shard_map/ppermute | solution.py:423
  44.4 1.9 %end_weights.1 = (f32[240,256]{1,0:T(8,128)}, f32[3,240,256]{2,1,0:T(8,128)}) custom-call(s32[3]{0:T(128)S(1)} %pad_add_fusion.place_ref, bf16[512,512]{1,0:T(8,128)(2,1)S(1)} %get-tuple-element.20.table_ref, f32[2,120,128]{2,1,0:T(8,128)S(1)} %get-tuple-element.24.refs_0_, f32[2,120,128]{2,1,0:T(8,128)S(1)} %collective-permute-done.1.refs_1_, ...), custom_call_target="tpu_custom_call" | custom-call | flops 251658240 | bytes 1474560 | tf_op jit(solution)/shard_map/end_weights/pallas_call | solution.py:458
  46.4 0.7 %collective-permute-done.9.refs_3_ = f32[1,120,128]{2,1,0:T(8,128)S(1)} collective-permute-done((f32[1,120,128]{2,1,0:T(8,128)S(1)}, f32[1,120,128]{2,1,0:T(8,128)S(1)}, u32[]{:S(2)}, u32[]{:S(2)}) %collective-permute-start.9) | collective-permute-done | bytes 61472 | tf_op jit(solution)/shard_map/ppermute | solution.py:423
  47.1 0.9 %copy-done.5 = f32[240,256]{1,0:T(8,128)S(1)} copy-done((f32[240,256]{1,0:T(8,128)S(1)}, f32[240,256]{1,0:T(8,128)}, u32[]{:S(2)}) %copy-start.5) | copy-done | bytes 245784
  48.0 1.0 %end_flux.1 = f32[240,256]{1,0:T(8,128)} custom-call(bf16[512,512]{1,0:T(8,128)(2,1)S(1)} %get-tuple-element.20.table_ref, f32[240,256]{1,0:T(8,128)S(1)} %copy-done.5, f32[1,120,128]{2,1,0:T(8,128)S(1)} %get-tuple-element.32.refs_0_, f32[1,120,128]{2,1,0:T(8,128)S(1)} %collective-permute-done.7.refs_1_, f32[1,120,128]{2,1,0:T(8,128)S(1)} %collective-permute-done.8.refs_2_, ...), custom_call_target="tpu_custom_call" | custom-call | flops 125829120 | bytes 737280 | tf_op jit(solution)/shard_map/end_flux/pallas_call | solution.py:481
  (33 shorter events, 1.1 us)
Async XLA Ops:
  0.6 7.2 %copy-start.9 = (f32[256]{0:T(256)S(1)}, f32[256]{0:T(256)}, u32[]{:S(2)}) copy-start(f32[256]{0:T(256)} %param.10) | copy-start | bytes 3076
  0.6 7.1 %copy-start.12 = (s32[1024]{0:T(1024)S(1)}, s32[1024]{0:T(1024)}, u32[]{:S(2)}) copy-start(s32[1024]{0:T(1024)} %param.13) | copy-start | bytes 12292
  0.7 1.5 %copy-start = (f32[4,480,256]{2,1,0:T(8,128)S(1)}, f32[4,480,256]{2,1,0:T(8,128)}, u32[]{:S(2)}) copy-start(f32[4,480,256]{2,1,0:T(8,128)} %ivar_ref.5) | copy-start | bytes 5898244
  2.3 0.9 %copy-start.3 = (s32[4,32,256]{2,1,0:T(8,128)S(1)}, s32[4,32,256]{2,1,0:T(8,128)}, u32[]{:S(2)}) copy-start(s32[4,32,256]{2,1,0:T(8,128)} %bits_ref.3) | copy-start | bytes 393220
  3.2 0.7 %copy-start.6 = (s32[4,256]{1,0:T(4,128)S(1)}, s32[4,256]{1,0:T(4,128)}, u32[]{:S(2)}) copy-start(s32[4,256]{1,0:T(4,128)} %good_ref.3) | copy-start | bytes 12292
  3.9 0.7 %copy-start.8 = (f32[256]{0:T(256)S(1)}, f32[256]{0:T(256)}, u32[]{:S(2)}) copy-start(f32[256]{0:T(256)} %param.10) | copy-start | bytes 3076
  4.6 0.7 %copy-start.10 = (s32[256]{0:T(256)S(1)}, s32[256]{0:T(256)}, u32[]{:S(2)}) copy-start(s32[256]{0:T(256)} %param.11) | copy-start | bytes 3076
  5.2 2.6 %copy-start.1 = (f32[4,480,256]{2,1,0:T(8,128)S(1)}, f32[4,480,256]{2,1,0:T(8,128)}, u32[]{:S(2)}) copy-start(f32[4,480,256]{2,1,0:T(8,128)} %ivar_ref.5) | copy-start | bytes 5898244
  7.0 20.2 %collective-permute-start = (f32[2,240,256]{2,1,0:T(8,128)S(1)}, f32[2,240,256]{2,1,0:T(8,128)S(1)}, u32[]{:S(2)}, u32[]{:S(2)}) collective-permute-start(f32[2,240,256]{2,1,0:T(8,128)S(1)} %get-tuple-element.21), channel_id=1, source_target_pairs={{0,1},{1,0},{2,3},{3,2},{4,5},{5,4},{6,7},{7,6},{8,9},{9,8},{10,11... | collective-permute-start | bytes 1474568 | tf_op jit(solution)/shard_map/ppermute | solution.py:508
  7.8 1.5 %copy-start.2 = (f32[4,480,256]{2,1,0:T(8,128)S(1)}, f32[4,480,256]{2,1,0:T(8,128)}, u32[]{:S(2)}) copy-start(f32[4,480,256]{2,1,0:T(8,128)} %pixels_ref.3) | copy-start | bytes 5898244
  9.3 10.8 %copy-start.4 = (s32[4,32,256]{2,1,0:T(8,128)S(1)}, s32[4,32,256]{2,1,0:T(8,128)}, u32[]{:S(2)}) copy-start(s32[4,32,256]{2,1,0:T(8,128)} %bits_ref.3) | copy-start | bytes 393220
  9.3 10.8 %copy-start.7 = (s32[4,256]{1,0:T(4,128)S(1)}, s32[4,256]{1,0:T(4,128)}, u32[]{:S(2)}) copy-start(s32[4,256]{1,0:T(4,128)} %good_ref.3) | copy-start | bytes 12292
  9.3 10.8 %copy-start.11 = (s32[256]{0:T(256)S(1)}, s32[256]{0:T(256)}, u32[]{:S(2)}) copy-start(s32[256]{0:T(256)} %param.11) | copy-start | bytes 3076
  11.8 5.3 %collective-permute-start.5 = (f32[2,8,128]{2,1,0:T(8,128)S(1)}, f32[2,8,128]{2,1,0:T(8,128)S(1)}, u32[]{:S(2)}, u32[]{:S(2)}) collective-permute-start(f32[2,8,128]{2,1,0:T(8,128)S(1)} %get-tuple-element.37), channel_id=1, source_target_pairs={{2,0},{4,2},{6,4},{3,1},{5,3},{7,5},{10,8},{12,10},{14,12},{11,9},... | collective-permute-start | bytes 24584 | tf_op jit(solution)/shard_map/ppermute | solution.py:514
  14.8 5.3 %collective-permute-start.4 = (f32[2,8,128]{2,1,0:T(8,128)S(1)}, f32[2,8,128]{2,1,0:T(8,128)S(1)}, u32[]{:S(2)}, u32[]{:S(2)}) collective-permute-start(f32[2,8,128]{2,1,0:T(8,128)S(1)} %get-tuple-element.38), channel_id=1, source_target_pairs={{0,2},{2,4},{4,6},{1,3},{3,5},{5,7},{8,10},{10,12},{12,14},{9,11},... | collective-permute-start | bytes 24584 | tf_op jit(solution)/shard_map/ppermute | solution.py:513
  25.7 5.8 %collective-permute-start.6 = (f32[240,256]{1,0:T(8,128)S(1)}, f32[240,256]{1,0:T(8,128)S(1)}, u32[]{:S(2)}, u32[]{:S(2)}) collective-permute-start(f32[240,256]{1,0:T(8,128)S(1)} %get-tuple-element.30), channel_id=1, source_target_pairs={{0,1},{1,0},{2,3},{3,2},{4,5},{5,4},{6,7},{7,6},{8,9},{9,8},{10,11... | collective-permute-start | bytes 737288 | tf_op jit(solution)/shard_map/ppermute | solution.py:520
  27.7 7.4 %collective-permute-start.1 = (f32[2,120,128]{2,1,0:T(8,128)S(1)}, f32[2,120,128]{2,1,0:T(8,128)S(1)}, u32[]{:S(2)}, u32[]{:S(2)}) collective-permute-start(f32[2,120,128]{2,1,0:T(8,128)S(1)} %get-tuple-element.25), channel_id=1, source_target_pairs={{0,8},{8,16},{16,24},{24,0},{1,9},{9,17},{17,25},{25,1},{2,10},{10... | collective-permute-start | bytes 368648 | tf_op jit(solution)/shard_map/ppermute | solution.py:423
  29.0 13.3 %collective-permute-start.2 = (f32[2,120,128]{2,1,0:T(8,128)S(1)}, f32[2,120,128]{2,1,0:T(8,128)S(1)}, u32[]{:S(2)}, u32[]{:S(2)}) collective-permute-start(f32[2,120,128]{2,1,0:T(8,128)S(1)} %get-tuple-element.26), channel_id=1, source_target_pairs={{0,16},{8,24},{16,0},{24,8},{1,17},{9,25},{17,1},{25,9},{2,18},{10... | collective-permute-start | bytes 368648 | tf_op jit(solution)/shard_map/ppermute | solution.py:423
  30.1 14.3 %collective-permute-start.3 = (f32[2,120,128]{2,1,0:T(8,128)S(1)}, f32[2,120,128]{2,1,0:T(8,128)S(1)}, u32[]{:S(2)}, u32[]{:S(2)}) collective-permute-start(f32[2,120,128]{2,1,0:T(8,128)S(1)} %get-tuple-element.27), channel_id=1, source_target_pairs={{0,24},{8,0},{16,8},{24,16},{1,25},{9,1},{17,9},{25,17},{2,26},{10... | collective-permute-start | bytes 368648 | tf_op jit(solution)/shard_map/ppermute | solution.py:423
  31.9 14.5 %collective-permute-start.7 = (f32[1,120,128]{2,1,0:T(8,128)S(1)}, f32[1,120,128]{2,1,0:T(8,128)S(1)}, u32[]{:S(2)}, u32[]{:S(2)}) collective-permute-start(f32[1,120,128]{2,1,0:T(8,128)S(1)} %get-tuple-element.33), channel_id=1, source_target_pairs={{0,8},{8,16},{16,24},{24,0},{1,9},{9,17},{17,25},{25,1},{2,10},{10... | collective-permute-start | bytes 184328 | tf_op jit(solution)/shard_map/ppermute | solution.py:423
  32.0 14.4 %collective-permute-start.8 = (f32[1,120,128]{2,1,0:T(8,128)S(1)}, f32[1,120,128]{2,1,0:T(8,128)S(1)}, u32[]{:S(2)}, u32[]{:S(2)}) collective-permute-start(f32[1,120,128]{2,1,0:T(8,128)S(1)} %get-tuple-element.34), channel_id=1, source_target_pairs={{0,16},{8,24},{16,0},{24,8},{1,17},{9,25},{17,1},{25,9},{2,18},{10... | collective-permute-start | bytes 184328 | tf_op jit(solution)/shard_map/ppermute | solution.py:423
  35.1 12.0 %collective-permute-start.9 = (f32[1,120,128]{2,1,0:T(8,128)S(1)}, f32[1,120,128]{2,1,0:T(8,128)S(1)}, u32[]{:S(2)}, u32[]{:S(2)}) collective-permute-start(f32[1,120,128]{2,1,0:T(8,128)S(1)} %get-tuple-element.35), channel_id=1, source_target_pairs={{0,24},{8,0},{16,8},{24,16},{1,25},{9,1},{17,9},{25,17},{2,26},{10... | collective-permute-start | bytes 184328 | tf_op jit(solution)/shard_map/ppermute | solution.py:423
  47.1 0.9 %copy-start.5 = (f32[240,256]{1,0:T(8,128)S(1)}, f32[240,256]{1,0:T(8,128)}, u32[]{:S(2)}) copy-start(f32[240,256]{1,0:T(8,128)} %get-tuple-element.18.ivar_ref) | copy-start | bytes 737284
where the time goes:
time: 49.4 us; the launch traced here: 49 us
  starting transfers between devices  14.6 us (30%)
  Pallas kernels  13.5 us (27%)
  waiting for transfers between devices  13.1 us (27%)
  local copies, waits for them, and re-layouts  7.02 us (14%)
  between operations  0.77 us (2%)
    ppermute x6, waiting for transfers between devices, exchange(): lax.ppermute(pieces[d], 'fib', [(i, (i + d) % fib_count) for i in range(f...  10.1 us
    ppermute x6, starting transfers between devices, exchange(): lax.ppermute(pieces[d], 'fib', [(i, (i + d) % fib_count) for i in range(f...  7.02 us
    unnamed x26, local copies, waits for them, and re-layouts  7 us
    pallas_call x1, Pallas kernels, flux_sums(): pl.pallas_call(solve_kernel, in_specs=[in_smem] + [in_vmem] * 5 + [in_pla...  5.53 us
    ppermute x1, starting transfers between devices, per_device(): right = lax.ppermute(edges[1], 'wav', [(j, i) for i, j in up])  3.06 us
    ppermute x1, waiting for transfers between devices, per_device(): left = lax.ppermute(edges[0], 'wav', up)  3.06 us
    pallas_call x1, Pallas kernels, prepare(): pl.pallas_call(functools.partial(prep_kernel, fib_count, pack, per, rel),...  2.41 us
    ppermute x2, starting transfers between devices, per_device(): theirs = lax.ppermute(theirs, 'exp', swap)  2.27 us
  transfers between devices with their start and end apart: 10, of which 4 were waited for; matrix products, arithmetic and copies ran while one was open for 0% of the time, Pallas kernels for 22%

commit v1 on v0

v1 whole, which is shorter than its diff:
```python
import functools

import jax
import jax.numpy as jnp
from jax import lax
from jax.experimental import pallas as pl
from jax.experimental.pallas import tpu as pltpu
from jax.sharding import PartitionSpec as P

HALO = 50
BITS = 15
LANES = 128
ROWS = 8
GROUP = 120
VMEM_BYTES = 32 * 1024 * 1024
F32 = jnp.float32
BF16 = jnp.bfloat16
NT = (((1,), (1,)), ((), ()))

in_vmem = pl.BlockSpec(memory_space=pltpu.VMEM)
in_smem = pl.BlockSpec(memory_space=pltpu.SMEM)
in_hbm = pl.BlockSpec(memory_space=pltpu.HBM)


def params():
    return pltpu.CompilerParams(vmem_limit_bytes=VMEM_BYTES)


def cost(flops, moved):
    return pl.CostEstimate(flops=int(flops), bytes_accessed=int(moved), transcendentals=0)


def held_in_hbm(*arrays):
    return [pltpu.with_memory_space_constraint(array, pltpu.HBM) for array in arrays]


def shaped(shape, dtype=F32):
    return jax.ShapeDtypeStruct(shape, dtype)


def usable_rows(place_ref, counts_ref, good_ref):
    count = good_ref.shape[0]
    return [
        good_ref[e : e + 1, :].astype(F32)
        * jnp.where(place_ref[2] * count + e < counts_ref[...], 1.0, 0.0)
        for e in range(count)
    ]


def tile_bits(tile):
    first, last = (ROWS * tile) // BITS, (ROWS * tile + ROWS - 1) // BITS
    split = BITS * last - ROWS * tile
    row = lax.broadcasted_iota(jnp.int32, (ROWS, 1), 0)
    word = jnp.where(row >= split, last, first)
    return first, last, split, jnp.left_shift(1, ROWS * tile + row - BITS * word)


def tile_words(words, tile):
    first, last, split, mask = tile_bits(tile)
    picked = words[first : first + 1, :]
    if last != first:
        row = lax.broadcasted_iota(jnp.int32, (ROWS, 1), 0)
        picked = jnp.where(row >= split, words[last : last + 1, :], picked)
    return (picked & mask) != 0


def in_flight(pairs, sems, at=0):
    copies = [pltpu.make_async_copy(source, target, sems.at[at + i]) for i, (source, target) in enumerate(pairs)]
    for copy in copies:
        copy.start()
    return copies


def inverse_of(x):
    guess = pl.reciprocal(x, approx=True)
    return guess * (2.0 - x * guess)


def owners(slots_ref, fib_count, fibres):
    rows = [slots_ref[:, s * fibres : (s + 1) * fibres].astype(F32) for s in range(fib_count)]
    sources = -(-fib_count // ROWS) * ROWS
    if sources > fib_count:
        rows.append(jnp.full((sources - fib_count, fibres), -1.0, F32))
    slots = jnp.concatenate(rows, 0)
    owner = jnp.floor((slots + 0.5) * (1.0 / fibres))
    return owner, slots - owner * fibres


def earlier_fibres(fibres):
    row = lax.broadcasted_iota(jnp.int32, (fibres, fibres), 0)
    col = lax.broadcasted_iota(jnp.int32, (fibres, fibres), 1)
    return (row < col).astype(F32).astype(BF16)


def write_send_table(fib_count, pack, per, rel, me, slots_ref, table_ref):
    fibres = table_ref.shape[1] // pack
    lanes = pack * per
    owner, _ = owners(slots_ref, fib_count, fibres)
    source = lax.broadcasted_iota(jnp.int32, owner.shape, 0)
    my_owner = jnp.sum(jnp.where(source == me, owner, 0.0), axis=0, keepdims=True).astype(jnp.int32)
    to_owner = (source == my_owner).astype(F32)
    counted = jnp.dot(to_owner.astype(BF16), earlier_fibres(fibres), preferred_element_type=F32)
    rank = jnp.sum(to_owner * counted, axis=0, keepdims=True).astype(jnp.int32)
    target = my_owner
    if rel:
        target = jnp.where(my_owner >= me, my_owner - me, my_owner - me + fib_count)
    base = target * lanes + rank
    place_of = jnp.concatenate([base + h * per for h in range(pack)], 1)
    row = lax.broadcasted_iota(jnp.int32, table_ref.shape, 0)
    table_ref[...] = (row == place_of).astype(F32).astype(BF16)


def write_recv_table(fib_count, pack, per, rel, me, slots_ref, table_ref):
    fibres = table_ref.shape[0] // pack
    lanes = pack * per
    total_lanes = fib_count * lanes
    owner, column = owners(slots_ref, fib_count, fibres)
    source = lax.broadcasted_iota(jnp.int32, owner.shape, 0)
    mine = (owner == me.astype(F32)).astype(F32)
    rank_in = jnp.dot(mine.astype(BF16), earlier_fibres(fibres), preferred_element_type=F32).astype(jnp.int32)
    order = source
    if rel:
        order = jnp.where(me >= source, me - source, me - source + fib_count)
    arrival = jnp.where(mine > 0.0, order * lanes + rank_in, -total_lanes)
    tall = lax.broadcasted_iota(jnp.int32, (total_lanes, fibres), 0)
    landing = jnp.zeros((ROWS, total_lanes), F32)
    for s in range(fib_count):
        hit = tall == arrival[s : s + 1, :]
        for h in range(1, pack):
            hit = hit | (tall == arrival[s : s + 1, :] + h * per)
        values = jnp.broadcast_to(column[s : s + 1, :], (ROWS, fibres)).astype(BF16)
        landing = landing + lax.dot_general(
            values, hit.astype(F32).astype(BF16), NT, preferred_element_type=F32
        )
    lane = lax.broadcasted_iota(jnp.int32, (1, total_lanes), 1)
    landing = landing[0:1, :].astype(jnp.int32)
    for h in range(1, pack):
        inside = (lane % lanes >= h * per) & (lane % lanes < (h + 1) * per)
        landing = jnp.where(inside, landing + h * fibres, landing)
    row = lax.broadcasted_iota(jnp.int32, table_ref.shape, 0)
    table_ref[...] = (row == landing).astype(F32).astype(BF16)


def weights_kernel(
    write_table, mine, wav_count, place_ref, slots_ref, coupling_ref, counts_ref, good_ref, ivar_ref, bits_ref,
    sums_ref, weight_ref, table_ref, slots_v, coupling_v, counts_v, good_v, ivar_v, bits_v, sems,
):
    expos, width, _ = ivar_ref.shape
    half = width // 2
    groups = half // GROUP
    which = place_ref[2] if mine else 1 - place_ref[2]
    first = pl.multiple_of(which * half, ROWS)
    first_word = pl.multiple_of(which * (half // BITS), ROWS)
    waits = in_flight(
        [
            (slots_ref, slots_v),
            (coupling_ref, coupling_v),
            (counts_ref, counts_v),
            (good_ref, good_v),
            (bits_ref.at[:, pl.ds(first_word, half // BITS), :], bits_v),
        ]
        + [
            (ivar_ref.at[:, pl.ds(first + g * GROUP, GROUP), :], ivar_v.at[:, pl.ds(g * GROUP, GROUP), :])
            for g in range(groups)
        ],
        sems,
    )
    waits[0].wait()
    write_table(place_ref[0], slots_v, table_ref)
    for wait in waits[1:5]:
        wait.wait()
    coupling = coupling_v[...]
    usable = usable_rows(place_ref, counts_v, good_v)
    start = place_ref[1] * width + first
    tiles = half // ROWS
    tiles_in_group = GROUP // ROWS
    words_in_group = GROUP // BITS
    for tile in range(tiles):
        group, within = divmod(tile, tiles_in_group)
        if within == 0:
            waits[5 + group].wait()
        links = 4.0 * coupling
        if tile in (0, tiles - 1):
            row = start + ROWS * tile + lax.broadcasted_iota(jnp.int32, (ROWS, 1), 0)
            links = jnp.where((row == 0) | (row == wav_count * width - 1), 2.0, 4.0) * coupling
        at = slice(ROWS * tile, ROWS * (tile + 1))
        weight_sum = band_sum = None
        for e in range(expos):
            ivar = ivar_v[e, at, :]
            words = bits_v[e, words_in_group * group : words_in_group * (group + 1), :]
            weight = jnp.where(tile_words(words, within), ivar * usable[e], 0.0)
            weight_ref[e, at, :] = weight
            band = weight * inverse_of(ivar + links)
            weight_sum = weight if e == 0 else weight_sum + weight
            band_sum = band if e == 0 else band_sum + band
        sums_ref[0, at, :] = weight_sum
        sums_ref[1, at, :] = band_sum * coupling


def weight_sums(write_table, table_shape, mine, wav_count, place, slots, coupling, counts, good, ivar, bits):
    expos, width, fibres = ivar.shape
    half = width // 2
    return pl.pallas_call(
        functools.partial(weights_kernel, write_table, mine, wav_count),
        in_specs=[in_smem] + [in_hbm] * 6,
        out_specs=[in_vmem] * 3,
        out_shape=[shaped((2, half, fibres)), shaped((expos, half, fibres)), shaped(table_shape, BF16)],
        scratch_shapes=[
            pltpu.VMEM(slots.shape, jnp.int32),
            pltpu.VMEM(coupling.shape, F32),
            pltpu.VMEM(counts.shape, jnp.int32),
            pltpu.VMEM(good.shape, jnp.int32),
            pltpu.VMEM((expos, half, fibres), F32),
            pltpu.VMEM((expos, half // BITS, fibres), jnp.int32),
            pltpu.SemaphoreType.DMA((5 + half // GROUP,)),
        ],
        compiler_params=params(),
        cost_estimate=cost(20 * ivar.size, 6 * ivar.size),
        name="weights_kept" if mine else "weights_sent",
    )(place, *held_in_hbm(slots, coupling, counts, good, ivar, bits))


def stream_coupling(coupling_ref, expos):
    coupling = coupling_ref[...]
    blocks = coupling.shape[1] // LANES
    return jnp.concatenate(
        [jnp.broadcast_to(coupling[:, h * LANES : (h + 1) * LANES], (expos, LANES)) for h in range(blocks)], 0
    )


def advance(state, ivar, pixel, back_coupling):
    n, d, b = state
    d = d + n * back_coupling
    return (n + ivar * d, d, b + (ivar * pixel) * d)


def edges_kernel(place_ref, coupling_ref, pixels_ref, ivar_ref, edges_ref, pixel_out, ivar_out, sems):
    expos, width, fibres = pixels_ref.shape
    streams = expos * fibres // LANES
    count = -(-HALO // ROWS) * ROWS

    def copies(first, length):
        pairs = []
        for source, target in ((ivar_ref, ivar_out), (pixels_ref, pixel_out)):
            for stream in range(streams):
                h, e = divmod(stream, expos)
                pairs.append(
                    (
                        source.at[e, pl.ds(first, length), pl.ds(h * LANES, LANES)],
                        target.at[pl.ds(stream * width + first, length), :],
                    )
                )
        return pairs

    waits = in_flight(copies(0, count) + copies(width - count, count), sems)
    rest = in_flight(copies(count, width - 2 * count), sems, len(waits))
    for wait in waits:
        wait.wait()
    back = 1.0 / stream_coupling(coupling_ref, expos)
    zero = jnp.zeros((streams, LANES), F32)
    states = [(zero, zero + 1.0, zero), (zero, zero + 1.0, zero)]
    for i in range(HALO):
        for side, row in enumerate((width - HALO + i, HALO - 1 - i)):
            at = pl.ds(row, streams, stride=width)
            states[side] = advance(states[side], ivar_out[at, :], pixel_out[at, :], back)
            if i % 10 == 9:
                scale = inverse_of(states[side][1])
                states[side] = tuple(part * scale for part in states[side])
    for side in range(2):
        n, d, b = states[side]
        scale = 1.0 / (d + n * back)
        edges_ref[side, 0] = n * scale
        edges_ref[side, 1] = b * scale
    for wait in rest:
        wait.wait()


def edge_rows(place, coupling, pixels, ivar):
    expos, width, fibres = pixels.shape
    streams = expos * fibres // LANES
    laid = shaped((streams * width, LANES))
    return pl.pallas_call(
        edges_kernel,
        in_specs=[in_smem, in_vmem, in_hbm, in_hbm],
        out_specs=[in_vmem] * 3,
        out_shape=[shaped((2, 2, streams, LANES)), laid, laid],
        scratch_shapes=[pltpu.SemaphoreType.DMA((6 * streams,))],
        compiler_params=params(),
        cost_estimate=cost(0, 0),
        name="edge_rows",
    )(place, coupling, *held_in_hbm(pixels, ivar))


def solve_kernel(
    place_ref, coupling_ref, left_ref, right_ref, pixel_ref, ivar_ref, weight_t_ref, weight_m_ref,
    theirs_ref, mine_ref, solved_s, lead_s, rest_s,
):
    streams = left_ref.shape[1]
    expos, half, fibres = weight_t_ref.shape
    width = ivar_ref.shape[0] // streams
    middle = width // 2
    coupling = stream_coupling(coupling_ref, expos)
    back = 1.0 / coupling

    def row_at(i):
        return pl.ds(i, streams, stride=width)

    def begin(edge_ref):
        u = edge_ref[0]
        return (u, 1.0 - u * back, edge_ref[1])

    def keep(side, i, state):
        n, d, b = state
        inverse = inverse_of(d + n * back)
        lead_s[side, i] = d * inverse
        rest_s[side, i] = (b * back) * inverse

    def eliminate(it, states):
        states = list(states)
        for k in range(ROWS):
            i = it * ROWS + k
            for side, row in enumerate((i, width - 1 - i)):
                keep(side, i, states[side])
                states[side] = advance(states[side], ivar_ref[row_at(row), :], pixel_ref[row_at(row), :], back)
        scaled = []
        for n, d, b in states:
            scale = inverse_of(d)
            scaled.append((n * scale, d * scale, b * scale))
        return tuple(scaled)

    states = lax.fori_loop(0, middle // ROWS, eliminate, (begin(left_ref), begin(right_ref)))
    for side in range(2):
        keep(side, middle, states[side])
    lead, rest = lead_s[0, middle], rest_s[0, middle]
    lead_r, rest_r = lead_s[1, middle], rest_s[1, middle]
    left = (rest + lead * rest_r) / (1.0 - lead * lead_r)
    right = rest_r + lead_r * left

    def substitute(it, values):
        values = list(values)
        for k in range(ROWS):
            i = middle - 1 - (it * ROWS + k)
            for side, row in enumerate((i, width - 1 - i)):
                solved_s[row_at(row), :] = values[side]
                values[side] = rest_s[side, i] + lead_s[side, i] * values[side]
        return tuple(values)

    lax.fori_loop(0, middle // ROWS, substitute, (left, right))

    blocks = fibres // LANES
    unroll = 5

    def coadd(out_ref, weight_ref, which):
        start = which * half

        def body(g, carry):
            for k in range(unroll):
                row = pl.multiple_of((g * unroll + k) * ROWS, ROWS)
                for h in range(blocks):
                    cut = pl.ds(h * LANES, LANES)
                    total = None
                    for e in range(expos):
                        at = pl.ds(pl.multiple_of((h * expos + e) * width + start + row, ROWS), ROWS)
                        term = weight_ref[e, pl.ds(row, ROWS), cut] * solved_s[at, :]
                        total = term if e == 0 else total + term
                    out_ref[0, pl.ds(row, ROWS), cut] = total
            return carry

        lax.fori_loop(0, half // (unroll * ROWS), body, 0)

    coadd(theirs_ref, weight_t_ref, 1 - place_ref[2])
    coadd(mine_ref, weight_m_ref, place_ref[2])


def flux_sums(place, coupling, left, right, pixels, ivar, weight_t, weight_m):
    expos, half, fibres = weight_t.shape
    streams = left.shape[1]
    out = shaped((1, half, fibres))
    factor_scratch = pltpu.VMEM((2, half + 1, streams, LANES), F32)
    return pl.pallas_call(
        solve_kernel,
        in_specs=[in_smem] + [in_vmem] * 7,
        out_specs=[in_vmem, in_vmem],
        out_shape=[out, out],
        scratch_shapes=[pltpu.VMEM(pixels.shape, F32), factor_scratch, factor_scratch],
        compiler_params=params(),
        cost_estimate=cost(0, 0),
        name="flux_sums",
    )(place, coupling, left, right, pixels, ivar, weight_t, weight_m)


def split_dot(x, table, dims):
    top = x.astype(BF16)
    low = (x - top.astype(F32)).astype(BF16)
    both = lax.dot_general(jnp.concatenate([top, low], 0), table, dims, preferred_element_type=F32)
    return both[: x.shape[0]] + both[x.shape[0] :]


def sort_kernel(pack, scaled, theirs_ref, mine_ref, table_ref, *refs):
    values, rows, _ = mine_ref.shape
    part = rows // pack
    totals = [mine_ref[v] + theirs_ref[v] for v in range(values)]
    if scaled:
        scale_ref, *out_refs = refs
        totals = [t * scale_ref[...] for t in totals]
    else:
        *out_refs, scale_ref = refs
        scale = 1.0 / jnp.maximum(totals[0], 1.0)
        scale_ref[...] = scale
        totals[1] = totals[1] * scale
    x = jnp.concatenate(
        [jnp.concatenate([t[h * part : (h + 1) * part] for h in range(pack)], 1) for t in totals], 0
    )
    moved = split_dot(x, table_ref[...], NT)
    lanes = moved.shape[1] // len(out_refs)
    for d, out_ref in enumerate(out_refs):
        for v in range(values):
            out_ref[v] = moved[v * part : (v + 1) * part, d * lanes : (d + 1) * lanes]


def sort_fibres(theirs, mine, table, pack, pieces, scale=None):
    values, rows, fibres = mine.shape
    lanes = table.shape[0] // pieces
    scaled = scale is not None
    outs = [shaped((values, rows // pack, lanes))] * pieces + ([] if scaled else [shaped((rows, fibres))])
    args = (theirs, mine, table) + ((scale,) if scaled else ())
    return pl.pallas_call(
        functools.partial(sort_kernel, pack, scaled),
        in_specs=[in_vmem] * len(args),
        out_specs=[in_vmem] * len(outs),
        out_shape=outs,
        compiler_params=params(),
        cost_estimate=cost(0, 0),
        name="sort_flux" if scaled else "sort_weights",
    )(*args)


def exchange(pieces, fib_count):
    if len(pieces) == 1:
        return [lax.all_to_all(pieces[0], "fib", split_axis=2, concat_axis=2, tiled=True)]
    arrived = [pieces[0]]
    for d in range(1, fib_count):
        arrived.append(lax.ppermute(pieces[d], "fib", [(i, (i + d) % fib_count) for i in range(fib_count)]))
    return arrived


def landed(refs, table):
    values, part, _ = refs[0].shape
    x = jnp.concatenate(
        [jnp.concatenate([ref[v] for ref in refs], 1) if len(refs) > 1 else refs[0][v] for v in range(values)], 0
    )
    moved = split_dot(x, table, NT)
    return [moved[v * part : (v + 1) * part] for v in range(values)]


def weights_end_kernel(pack, total, place_ref, table_ref, *refs):
    *piece_refs, ivar_ref, res_ref = refs
    weight, band = landed(piece_refs, table_ref[...])
    rows, fibres = ivar_ref.shape
    part = rows // pack
    start = (place_ref[1] * 2 + place_ref[2]) * rows
    for h in range(pack):
        at = slice(h * part, (h + 1) * part)
        cut = slice(h * fibres, (h + 1) * fibres)
        row = start + h * part + lax.broadcasted_iota(jnp.int32, (part, 1), 0)
        w, b = weight[:, cut], band[:, cut]
        before = jnp.where(row == 0, 0.0, b)
        after = jnp.where(row == total - 1, 0.0, b)
        ivar_ref[at, :] = w
        res_ref[0, at, :] = before
        res_ref[1, at, :] = jnp.minimum(w, 1.0) - before - after
        res_ref[2, at, :] = after


def end_weights(place, table, pieces, pack, fibres, total):
    rows = pieces[0].shape[1] * pack
    return pl.pallas_call(
        functools.partial(weights_end_kernel, pack, total),
        in_specs=[in_smem] + [in_vmem] * (1 + len(pieces)),
        out_specs=[in_vmem] * 2,
        out_shape=[shaped((rows, fibres)), shaped((3, rows, fibres))],
        compiler_params=params(),
        cost_estimate=cost(4 * rows * table.size, 6 * rows * fibres * 4),
        name="end_weights",
    )(place, table, *pieces)


def flux_end_kernel(pack, table_ref, *refs):
    *piece_refs, flux_ref = refs
    (flux,) = landed(piece_refs, table_ref[...])
    rows, fibres = flux_ref.shape
    part = rows // pack
    for h in range(pack):
        flux_ref[h * part : (h + 1) * part, :] = flux[:, h * fibres : (h + 1) * fibres]


def end_flux(table, pieces, pack, fibres):
    rows = pieces[0].shape[1] * pack
    return pl.pallas_call(
        functools.partial(flux_end_kernel, pack),
        in_specs=[in_vmem] * (1 + len(pieces)),
        out_specs=in_vmem,
        out_shape=shaped((rows, fibres)),
        compiler_params=params(),
        cost_estimate=cost(2 * rows * table.size, 2 * rows * fibres * 4),
        name="end_flux",
    )(table, *pieces)


def after(value, done):
    return lax.optimization_barrier((value, done))[0]


def per_device(pixels, pixel_ivar, clip_bits, coupling, counts, good_flags, owner_slot):
    expos, width, fibres = pixels.shape
    fib_count, wav_count = lax.axis_size("fib"), lax.axis_size("wav")
    total = width * wav_count
    per = fibres // fib_count
    rows = width // 2
    pack = max(1, LANES // per)
    while pack > 1 and rows % (pack * ROWS):
        pack //= 2
    rel = pack * per == LANES
    pieces = fib_count if rel else 1
    place = jnp.stack([lax.axis_index(axis) for axis in ("fib", "wav", "exp")]).astype(jnp.int32)
    coupling, counts, slots = coupling[None], counts[None], owner_slot[None]
    swap = [(0, 1), (1, 0)]
    moves = (fib_count, pack, per, rel)
    send_shape = (fib_count * pack * per, pack * fibres)

    theirs, weight_t, send_table = weight_sums(
        functools.partial(write_send_table, *moves), send_shape, False, wav_count,
        place, slots, coupling, counts, good_flags, pixel_ivar, clip_bits,
    )
    arriving = lax.ppermute(theirs, "exp", swap)
    mine, weight_m, recv_table = weight_sums(
        functools.partial(write_recv_table, *moves), send_shape[::-1], True, wav_count,
        after(place, theirs), slots, coupling, counts, good_flags, pixel_ivar, clip_bits,
    )
    *sorted_pieces, scale = sort_fibres(arriving, mine, send_table, pack, pieces)
    weight_pieces = exchange(sorted_pieces, fib_count)

    edges, pixel_s, ivar_s = edge_rows(after(place, scale), coupling, pixels, pixel_ivar)
    up = [(i, i + 1) for i in range(wav_count - 1)]
    left = lax.ppermute(edges[0], "wav", up)
    right = lax.ppermute(edges[1], "wav", [(j, i) for i, j in up])
    if rel:
        left = after(left, weight_pieces[fib_count // 2])
    theirs, mine = flux_sums(place, coupling, left, right, pixel_s, ivar_s, weight_t, weight_m)
    if rel:
        theirs = after(theirs, weight_pieces[1])
    theirs = lax.ppermute(theirs, "exp", swap)
    flux_pieces = exchange(sort_fibres(theirs, mine, send_table, pack, pieces, scale), fib_count)

    ivar, res = end_weights(place, recv_table, weight_pieces, pack, fibres, total)
    flux = end_flux(recv_table, flux_pieces, pack, fibres)
    return (flux, ivar, res)


def solution(mesh):
    return jax.shard_map(
        per_device,
        mesh=mesh,
        in_specs=(
            P("exp", "wav", "fib"),
            P("exp", "wav", "fib"),
            P("exp", "wav", "fib"),
            P("fib"),
            P("fib"),
            P("exp", "fib"),
            P(),
        ),
        out_specs=(
            P(("wav", "exp"), "fib"),
            P(("wav", "exp"), "fib"),
            P(None, ("wav", "exp"), "fib"),
        ),
        check_vma=False,
    )
```

time: 49.4 us -> 41.2 us (0.83)
  the two profiles are of different devices: /device:TPU:13 before, /device:TPU:0 now
where the time goes in v1:
time: 41.2 us; the launch traced here: 41 us
  starting transfers between devices  16.7 us (41%)
  Pallas kernels  16.6 us (40%)
  waiting for transfers between devices  6.88 us (17%)
  between operations  0.75 us (2%)
    ppermute x6, starting transfers between devices, exchange(): lax.ppermute(pieces[d], 'fib', [(i, (i + d) % fib_count) for i in range(f...  11.4 us
    pallas_call x1, Pallas kernels, flux_sums(): pl.pallas_call(solve_kernel, in_specs=[in_smem] + [in_vmem] * 7, out_spec...  4.95 us
    pallas_call x2, Pallas kernels, weight_sums(): pl.pallas_call(functools.partial(weights_kernel, write_table, mine, wav_c...  4.74 us
    ppermute x1, waiting for transfers between devices, per_device(): right = lax.ppermute(edges[1], 'wav', [(j, i) for i, j in up])  4.19 us
    ppermute x1, starting transfers between devices, per_device(): left = lax.ppermute(edges[0], 'wav', up)  3.39 us
    pallas_call x1, Pallas kernels, edge_rows(): pl.pallas_call(edges_kernel, in_specs=[in_smem, in_vmem, in_hbm, in_hbm],...  3.17 us
    ppermute x6, waiting for transfers between devices, exchange(): lax.ppermute(pieces[d], 'fib', [(i, (i + d) % fib_count) for i in range(f...  2.64 us
    pallas_call x1, Pallas kernels, end_weights(): pl.pallas_call(functools.partial(weights_end_kernel, pack, total), in_spe...  1.92 us
  transfers between devices with their start and end apart: 10, of which 3 were waited for; matrix products, arithmetic and copies ran while one was open for 0% of the time, Pallas kernels for 32%

profile of v1, /device:TPU:0, one launch (start us, length us, event | category | flops | bytes accessed | tf_op | source)
XLA Modules:
  0.0 41.0 jit_solution(16748215682987917878)
XLA Ops:
  0.6 0.1 pad_add_fusion.place_ref
  0.7 2.2 %weights_sent.1 = (f32[2,240,256]{2,1,0:T(8,128)S(1)}, f32[4,240,256]{2,1,0:T(8,128)S(1)}, bf16[512,512]{1,0:T(8,128)(2,1)S(1)}) custom-call(s32[3]{0:T(128)S(1)} %pad_add_fusion.place_ref, s32[1,1024]{1,0:T(1,128)} %bitcast.14, f32[1,256]{1,0:T(1,128)} %bitcast.10, s32[1,256]{1,0:T(1,128)} %bitcast.16, s32[4,256]{1,0:T(4,128)} %good_ref.3, ...), custom_call_target="tpu_custom_call" | custom-call | flops 9830400 | bytes 2949120 | tf_op jit(solution)/shard_map/weights_sent/pallas_call | solution.py:203
  2.9 0.0 copy-start
  2.9 0.5 %collective-permute-start = (f32[2,240,256]{2,1,0:T(8,128)S(1)}, f32[2,240,256]{2,1,0:T(8,128)S(1)}, u32[]{:S(2)}, u32[]{:S(2)}) collective-permute-start(f32[2,240,256]{2,1,0:T(8,128)S(1)} %get-tuple-element.29), channel_id=1, source_target_pairs={{0,1},{1,0},{2,3},{3,2},{4,5},{5,4},{6,7},{7,6},{8,9},{9,8},{10,11... | collective-permute-start | bytes 1474568 | tf_op jit(solution)/shard_map/ppermute | solution.py:535
  3.4 2.6 %weights_kept.1 = (f32[2,240,256]{2,1,0:T(8,128)S(1)}, f32[4,240,256]{2,1,0:T(8,128)S(1)}, bf16[512,512]{1,0:T(8,128)(2,1)S(1)}) custom-call(s32[3]{0:T(128)S(1)} %pad_add_fusion.place_ref, s32[1,1024]{1,0:T(1,128)} %bitcast.15, f32[1,256]{1,0:T(1,128)} %bitcast.11, s32[1,256]{1,0:T(1,128)} %bitcast.17, s32[4,256]{1,0:T(4,128)} %good_ref.3, ...), custom_call_target="tpu_custom_call" | custom-call | flops 9830400 | bytes 2949120 | tf_op jit(solution)/shard_map/weights_kept/pallas_call | solution.py:203
  6.0 0.5 %sort_weights.1 = (f32[2,120,128]{2,1,0:T(8,128)S(1)}, f32[2,120,128]{2,1,0:T(8,128)S(1)}, f32[2,120,128]{2,1,0:T(8,128)S(1)}, f32[2,120,128]{2,1,0:T(8,128)S(1)}, f32[240,256]{1,0:T(8,128)S(1)}) custom-call(f32[2,240,256]{2,1,0:T(8,128)S(1)} %collective-permute-done.theirs_ref, f32[2,240,256]{2,1,0:T(8,128)S(1)} %get-tuple-element.32.mine_ref, ...), custom_call_target="tpu_custom_call" | custom-call | tf_op jit(solution)/shard_map/sort_weights/pallas_call | solution.py:427
  6.5 3.7 %collective-permute-start.2 = (f32[2,120,128]{2,1,0:T(8,128)S(1)}, f32[2,120,128]{2,1,0:T(8,128)S(1)}, u32[]{:S(2)}, u32[]{:S(2)}) collective-permute-start(f32[2,120,128]{2,1,0:T(8,128)S(1)} %get-tuple-element.37), channel_id=1, source_target_pairs={{0,16},{8,24},{16,0},{24,8},{1,17},{9,25},{17,1},{25,9},{2,18},{10... | collective-permute-start | bytes 368648 | tf_op jit(solution)/shard_map/ppermute | solution.py:443
  10.2 1.6 %collective-permute-start.4 = (f32[2,120,128]{2,1,0:T(8,128)S(1)}, f32[2,120,128]{2,1,0:T(8,128)S(1)}, u32[]{:S(2)}, u32[]{:S(2)}) collective-permute-start(f32[2,120,128]{2,1,0:T(8,128)S(1)} %get-tuple-element.44), channel_id=1, source_target_pairs={{0,8},{8,16},{16,24},{24,0},{1,9},{9,17},{17,25},{25,1},{2,10},{10... | collective-permute-start | bytes 368648 | tf_op jit(solution)/shard_map/ppermute | solution.py:443
  11.7 3.2 %edge_rows.1 = (f32[2,2,8,128]{3,2,1,0:T(8,128)S(1)}, f32[3840,128]{1,0:T(8,128)S(1)}, f32[3840,128]{1,0:T(8,128)S(1)}) custom-call(s32[3]{0:T(128)S(1)} %pad_add_fusion.place_ref, f32[1,256]{1,0:T(1,128)S(1)} %bitcast.12, f32[4,480,256]{2,1,0:T(8,128)} %pixels_ref.1, f32[4,480,256]{2,1,0:T(8,128)} %ivar_ref.5), custom_call_target="tpu_custom_call" | custom-call | tf_op jit(solution)/shard_map/edge_rows/pallas_call | solution.py:282
  14.9 3.4 %collective-permute-start.1 = (f32[2,8,128]{2,1,0:T(8,128)S(1)}, f32[2,8,128]{2,1,0:T(8,128)S(1)}, u32[]{:S(2)}, u32[]{:S(2)}) collective-permute-start(f32[2,8,128]{2,1,0:T(8,128)S(1)} %get-tuple-element.56), channel_id=1, source_target_pairs={{0,2},{2,4},{4,6},{1,3},{3,5},{5,7},{8,10},{10,12},{12,14},{9,11},... | collective-permute-start | bytes 24584 | tf_op jit(solution)/shard_map/ppermute | solution.py:545
  18.3 1.3 %collective-permute-start.3 = (f32[2,8,128]{2,1,0:T(8,128)S(1)}, f32[2,8,128]{2,1,0:T(8,128)S(1)}, u32[]{:S(2)}, u32[]{:S(2)}) collective-permute-start(f32[2,8,128]{2,1,0:T(8,128)S(1)} %get-tuple-element.55), channel_id=1, source_target_pairs={{2,0},{4,2},{6,4},{3,1},{5,3},{7,5},{10,8},{12,10},{14,12},{11,9},... | collective-permute-start | bytes 24584 | tf_op jit(solution)/shard_map/ppermute | solution.py:546
  19.6 0.0 collective-permute-done.1.left_ref
  19.7 4.2 %collective-permute-done.3.right_ref = f32[2,8,128]{2,1,0:T(8,128)S(1)} collective-permute-done((f32[2,8,128]{2,1,0:T(8,128)S(1)}, f32[2,8,128]{2,1,0:T(8,128)S(1)}, u32[]{:S(2)}, u32[]{:S(2)}) %collective-permute-start.3) | collective-permute-done | bytes 8224 | tf_op jit(solution)/shard_map/ppermute | solution.py:546
  23.9 4.9 %flux_sums.1 = (f32[1,240,256]{2,1,0:T(8,128)S(1)}, f32[1,240,256]{2,1,0:T(8,128)S(1)}) custom-call(s32[3]{0:T(128)S(1)} %pad_add_fusion.place_ref, f32[1,256]{1,0:T(1,128)S(1)} %bitcast.13, f32[2,8,128]{2,1,0:T(8,128)S(1)} %collective-permute-done.1.left_ref, f32[2,8,128]{2,1,0:T(8,128)S(1)} %collective-permute-done.3.right_ref, ...), custom_call_target="tpu_custom_call" | custom-call | tf_op jit(solution)/shard_map/flux_sums/pallas_call | solution.py:380
  28.8 0.1 collective-permute-start.5
  28.9 2.3 %collective-permute-start.9 = (f32[2,120,128]{2,1,0:T(8,128)S(1)}, f32[2,120,128]{2,1,0:T(8,128)S(1)}, u32[]{:S(2)}, u32[]{:S(2)}) collective-permute-start(f32[2,120,128]{2,1,0:T(8,128)S(1)} %get-tuple-element.52), channel_id=1, source_target_pairs={{0,24},{8,0},{16,8},{24,16},{1,25},{9,1},{17,9},{25,17},{2,26},{10... | collective-permute-start | bytes 368648 | tf_op jit(solution)/shard_map/ppermute | solution.py:443
  31.2 0.3 sort_flux.1
  31.6 0.1 collective-permute-start.6
  31.6 2.0 %collective-permute-start.7 = (f32[1,120,128]{2,1,0:T(8,128)S(1)}, f32[1,120,128]{2,1,0:T(8,128)S(1)}, u32[]{:S(2)}, u32[]{:S(2)}) collective-permute-start(f32[1,120,128]{2,1,0:T(8,128)S(1)} %get-tuple-element.49), channel_id=1, source_target_pairs={{0,16},{8,24},{16,0},{24,8},{1,17},{9,25},{17,1},{25,9},{2,18},{10... | collective-permute-start | bytes 184328 | tf_op jit(solution)/shard_map/ppermute | solution.py:443
  33.6 1.8 %collective-permute-start.8 = (f32[1,120,128]{2,1,0:T(8,128)S(1)}, f32[1,120,128]{2,1,0:T(8,128)S(1)}, u32[]{:S(2)}, u32[]{:S(2)}) collective-permute-start(f32[1,120,128]{2,1,0:T(8,128)S(1)} %get-tuple-element.50), channel_id=1, source_target_pairs={{0,24},{8,0},{16,8},{24,16},{1,25},{9,1},{17,9},{25,17},{2,26},{10... | collective-permute-start | bytes 184328 | tf_op jit(solution)/shard_map/ppermute | solution.py:443
  35.4 1.9 %end_weights.1 = (f32[240,256]{1,0:T(8,128)}, f32[3,240,256]{2,1,0:T(8,128)}) custom-call(s32[3]{0:T(128)S(1)} %pad_add_fusion.place_ref, bf16[512,512]{1,0:T(8,128)(2,1)S(1)} %get-tuple-element.31.table_ref, f32[2,120,128]{2,1,0:T(8,128)S(1)} %get-tuple-element.51.refs_0_, f32[2,120,128]{2,1,0:T(8,128)S(1)} %collective-permute-done.4.refs_1_, ...), custom_call_target="tpu_custom_call" | custom-call | flops 251658240 | bytes 1474560 | tf_op jit(solution)/shard_map/end_weights/pallas_call | solution.py:477
  37.4 0.9 %collective-permute-done.6.refs_1_ = f32[1,120,128]{2,1,0:T(8,128)S(1)} collective-permute-done((f32[1,120,128]{2,1,0:T(8,128)S(1)}, f32[1,120,128]{2,1,0:T(8,128)S(1)}, u32[]{:S(2)}, u32[]{:S(2)}) %collective-permute-start.6) | collective-permute-done | bytes 61472 | tf_op jit(solution)/shard_map/ppermute | solution.py:443
  38.3 1.7 %collective-permute-done.7.refs_2_ = f32[1,120,128]{2,1,0:T(8,128)S(1)} collective-permute-done((f32[1,120,128]{2,1,0:T(8,128)S(1)}, f32[1,120,128]{2,1,0:T(8,128)S(1)}, u32[]{:S(2)}, u32[]{:S(2)}) %collective-permute-start.7) | collective-permute-done | bytes 61472 | tf_op jit(solution)/shard_map/ppermute | solution.py:443
  40.0 1.0 %end_flux.1 = f32[240,256]{1,0:T(8,128)} custom-call(bf16[512,512]{1,0:T(8,128)(2,1)S(1)} %get-tuple-element.31.table_ref, f32[1,120,128]{2,1,0:T(8,128)S(1)} %get-tuple-element.47.refs_0_, f32[1,120,128]{2,1,0:T(8,128)S(1)} %collective-permute-done.6.refs_1_, f32[1,120,128]{2,1,0:T(8,128)S(1)} %collective-permute-done.7.refs_2_, ...), custom_call_target="tpu_custom_call" | custom-call | flops 125829120 | bytes 491520 | tf_op jit(solution)/shard_map/end_flux/pallas_call | solution.py:499
  (8 shorter events, 0.0 us)
Async XLA Ops:
  2.9 8.9 %copy-start = (f32[256]{0:T(256)S(1)}, f32[256]{0:T(256)}, u32[]{:S(2)}) copy-start(f32[256]{0:T(256)} %param.10) | copy-start | bytes 3076
  2.9 3.1 %collective-permute-start = (f32[2,240,256]{2,1,0:T(8,128)S(1)}, f32[2,240,256]{2,1,0:T(8,128)S(1)}, u32[]{:S(2)}, u32[]{:S(2)}) collective-permute-start(f32[2,240,256]{2,1,0:T(8,128)S(1)} %get-tuple-element.29), channel_id=1, source_target_pairs={{0,1},{1,0},{2,3},{3,2},{4,5},{5,4},{6,7},{7,6},{8,9},{9,8},{10,11... | collective-permute-start | bytes 1474568 | tf_op jit(solution)/shard_map/ppermute | solution.py:535
  6.5 13.2 %collective-permute-start.2 = (f32[2,120,128]{2,1,0:T(8,128)S(1)}, f32[2,120,128]{2,1,0:T(8,128)S(1)}, u32[]{:S(2)}, u32[]{:S(2)}) collective-permute-start(f32[2,120,128]{2,1,0:T(8,128)S(1)} %get-tuple-element.37), channel_id=1, source_target_pairs={{0,16},{8,24},{16,0},{24,8},{1,17},{9,25},{17,1},{25,9},{2,18},{10... | collective-permute-start | bytes 368648 | tf_op jit(solution)/shard_map/ppermute | solution.py:443
  10.2 18.7 %collective-permute-start.4 = (f32[2,120,128]{2,1,0:T(8,128)S(1)}, f32[2,120,128]{2,1,0:T(8,128)S(1)}, u32[]{:S(2)}, u32[]{:S(2)}) collective-permute-start(f32[2,120,128]{2,1,0:T(8,128)S(1)} %get-tuple-element.44), channel_id=1, source_target_pairs={{0,8},{8,16},{16,24},{24,0},{1,9},{9,17},{17,25},{25,1},{2,10},{10... | collective-permute-start | bytes 368648 | tf_op jit(solution)/shard_map/ppermute | solution.py:443
  14.9 4.7 %collective-permute-start.1 = (f32[2,8,128]{2,1,0:T(8,128)S(1)}, f32[2,8,128]{2,1,0:T(8,128)S(1)}, u32[]{:S(2)}, u32[]{:S(2)}) collective-permute-start(f32[2,8,128]{2,1,0:T(8,128)S(1)} %get-tuple-element.56), channel_id=1, source_target_pairs={{0,2},{2,4},{4,6},{1,3},{3,5},{5,7},{8,10},{10,12},{12,14},{9,11},... | collective-permute-start | bytes 24584 | tf_op jit(solution)/shard_map/ppermute | solution.py:545
  18.3 5.5 %collective-permute-start.3 = (f32[2,8,128]{2,1,0:T(8,128)S(1)}, f32[2,8,128]{2,1,0:T(8,128)S(1)}, u32[]{:S(2)}, u32[]{:S(2)}) collective-permute-start(f32[2,8,128]{2,1,0:T(8,128)S(1)} %get-tuple-element.55), channel_id=1, source_target_pairs={{2,0},{4,2},{6,4},{3,1},{5,3},{7,5},{10,8},{12,10},{14,12},{11,9},... | collective-permute-start | bytes 24584 | tf_op jit(solution)/shard_map/ppermute | solution.py:546
  28.8 2.4 %collective-permute-start.5 = (f32[1,240,256]{2,1,0:T(8,128)S(1)}, f32[1,240,256]{2,1,0:T(8,128)S(1)}, u32[]{:S(2)}, u32[]{:S(2)}) collective-permute-start(f32[1,240,256]{2,1,0:T(8,128)S(1)} %get-tuple-element.45), channel_id=1, source_target_pairs={{0,1},{1,0},{2,3},{3,2},{4,5},{5,4},{6,7},{7,6},{8,9},{9,8},{10,11... | collective-permute-start | bytes 737288 | tf_op jit(solution)/shard_map/ppermute | solution.py:552
  28.9 6.5 %collective-permute-start.9 = (f32[2,120,128]{2,1,0:T(8,128)S(1)}, f32[2,120,128]{2,1,0:T(8,128)S(1)}, u32[]{:S(2)}, u32[]{:S(2)}) collective-permute-start(f32[2,120,128]{2,1,0:T(8,128)S(1)} %get-tuple-element.52), channel_id=1, source_target_pairs={{0,24},{8,0},{16,8},{24,16},{1,25},{9,1},{17,9},{25,17},{2,26},{10... | collective-permute-start | bytes 368648 | tf_op jit(solution)/shard_map/ppermute | solution.py:443
  31.6 6.7 %collective-permute-start.6 = (f32[1,120,128]{2,1,0:T(8,128)S(1)}, f32[1,120,128]{2,1,0:T(8,128)S(1)}, u32[]{:S(2)}, u32[]{:S(2)}) collective-permute-start(f32[1,120,128]{2,1,0:T(8,128)S(1)} %get-tuple-element.48), channel_id=1, source_target_pairs={{0,8},{8,16},{16,24},{24,0},{1,9},{9,17},{17,25},{25,1},{2,10},{10... | collective-permute-start | bytes 184328 | tf_op jit(solution)/shard_map/ppermute | solution.py:443
  31.6 8.4 %collective-permute-start.7 = (f32[1,120,128]{2,1,0:T(8,128)S(1)}, f32[1,120,128]{2,1,0:T(8,128)S(1)}, u32[]{:S(2)}, u32[]{:S(2)}) collective-permute-start(f32[1,120,128]{2,1,0:T(8,128)S(1)} %get-tuple-element.49), channel_id=1, source_target_pairs={{0,16},{8,24},{16,0},{24,8},{1,17},{9,25},{17,1},{25,9},{2,18},{10... | collective-permute-start | bytes 184328 | tf_op jit(solution)/shard_map/ppermute | solution.py:443
  33.6 6.4 %collective-permute-start.8 = (f32[1,120,128]{2,1,0:T(8,128)S(1)}, f32[1,120,128]{2,1,0:T(8,128)S(1)}, u32[]{:S(2)}, u32[]{:S(2)}) collective-permute-start(f32[1,120,128]{2,1,0:T(8,128)S(1)} %get-tuple-element.50), channel_id=1, source_target_pairs={{0,24},{8,0},{16,8},{24,16},{1,25},{9,1},{17,9},{25,17},{2,26},{10... | collective-permute-start | bytes 184328 | tf_op jit(solution)/shard_map/ppermute | solution.py:443

commit v2 on v1

--- a/solution.py
+++ b/solution.py
@@ -74,6 +74,21 @@
 def inverse_of(x):
     guess = pl.reciprocal(x, approx=True)
     return guess * (2.0 - x * guess)
+
+
+def advance(state, ivar, pixel, back_coupling):
+    n, d, b = state
+    next_d = d + n * back_coupling
+    return (n * (1.0 + ivar * back_coupling) + ivar * d, next_d, b + (ivar * pixel) * next_d)
+
+
+def rescaled(state):
+    scale = inverse_of(state[1])
+    return tuple(part * scale for part in state)
+
+
+def divisor_of(size, most):
+    return max(k for k in range(1, most + 1) if size % k == 0)
 
 
 def owners(slots_ref, fib_count, fibres):
@@ -141,154 +156,215 @@
     table_ref[...] = (row == landing).astype(F32).astype(BF16)
 
 
-def weights_kernel(
-    write_table, mine, wav_count, place_ref, slots_ref, coupling_ref, counts_ref, good_ref, ivar_ref, bits_ref,
-    sums_ref, weight_ref, table_ref, slots_v, coupling_v, counts_v, good_v, ivar_v, bits_v, sems,
-):
-    expos, width, _ = ivar_ref.shape
-    half = width // 2
-    groups = half // GROUP
-    which = place_ref[2] if mine else 1 - place_ref[2]
+def stream_coupling(coupling_ref, expos):
+    coupling = coupling_ref[...]
+    blocks = coupling.shape[1] // LANES
+    return jnp.concatenate(
+        [jnp.broadcast_to(coupling[:, h * LANES : (h + 1) * LANES], (expos, LANES)) for h in range(blocks)], 0
+    )
+
+
+def weight_tile(coupling, usable, words, ivars, within, scale_row):
+    links = scale_row * coupling
+    weights = []
+    weight_sum = band_sum = None
+    for e, ivar in enumerate(ivars):
+        weight = jnp.where(tile_words(words[e], within), ivar * usable[e], 0.0)
+        band = weight * inverse_of(ivar + links)
+        weights.append(weight)
+        weight_sum = weight if e == 0 else weight_sum + weight
+        band_sum = band if e == 0 else band_sum + band
+    return weights, weight_sum, band_sum * coupling
+
+
+def half_copies(which, ivar_ref, bits_ref, ivar_v, bits_v):
+    half = ivar_v.shape[1]
     first = pl.multiple_of(which * half, ROWS)
     first_word = pl.multiple_of(which * (half // BITS), ROWS)
-    waits = in_flight(
-        [
-            (slots_ref, slots_v),
-            (coupling_ref, coupling_v),
-            (counts_ref, counts_v),
-            (good_ref, good_v),
-            (bits_ref.at[:, pl.ds(first_word, half // BITS), :], bits_v),
-        ]
-        + [
-            (ivar_ref.at[:, pl.ds(first + g * GROUP, GROUP), :], ivar_v.at[:, pl.ds(g * GROUP, GROUP), :])
-            for g in range(groups)
-        ],
-        sems,
-    )
-    waits[0].wait()
-    write_table(place_ref[0], slots_v, table_ref)
-    for wait in waits[1:5]:
-        wait.wait()
+    return [
+        (bits_ref.at[:, pl.ds(first_word, half // BITS), :], bits_v),
+        (ivar_ref.at[:, pl.ds(first, half), :], ivar_v),
+    ]
+
+
+def write_weights(place_ref, wav_count, which, coupling_v, counts_v, good_v, ivar_v, bits_v, sums_ref, weight_ref, beside):
+    expos, half, _ = ivar_v.shape
     coupling = coupling_v[...]
     usable = usable_rows(place_ref, counts_v, good_v)
-    start = place_ref[1] * width + first
+    start = place_ref[1] * (2 * half) + which * half
     tiles = half // ROWS
     tiles_in_group = GROUP // ROWS
     words_in_group = GROUP // BITS
     for tile in range(tiles):
         group, within = divmod(tile, tiles_in_group)
-        if within == 0:
-            waits[5 + group].wait()
-        links = 4.0 * coupling
+        scale_row = 4.0
         if tile in (0, tiles - 1):
             row = start + ROWS * tile + lax.broadcasted_iota(jnp.int32, (ROWS, 1), 0)
-            links = jnp.where((row == 0) | (row == wav_count * width - 1), 2.0, 4.0) * coupling
+            scale_row = jnp.where((row == 0) | (row == wav_count * 2 * half - 1), 2.0, 4.0)
         at = slice(ROWS * tile, ROWS * (tile + 1))
-        weight_sum = band_sum = None
+        words = [bits_v[e, words_in_group * group : words_in_group * (group + 1), :] for e in range(expos)]
+        weights, weight_sum, band_sum = weight_tile(
+            coupling, usable, words, [ivar_v[e, at, :] for e in range(expos)], within, scale_row
+        )
         for e in range(expos):
-            ivar = ivar_v[e, at, :]
-            words = bits_v[e, words_in_group * group : words_in_group * (group + 1), :]
-            weight = jnp.where(tile_words(words, within), ivar * usable[e], 0.0)
-            weight_ref[e, at, :] = weight
-            band = weight * inverse_of(ivar + links)
-            weight_sum = weight if e == 0 else weight_sum + weight
-            band_sum = band if e == 0 else band_sum + band
+            weight_ref[e, at, :] = weights[e]
         sums_ref[0, at, :] = weight_sum
-        sums_ref[1, at, :] = band_sum * coupling
-
-
-def weight_sums(write_table, table_shape, mine, wav_count, place, slots, coupling, counts, good, ivar, bits):
+        sums_ref[1, at, :] = band_sum
+        beside(tile, tiles)
+
+
+def stream_copies(source_ref, target, first, length, pitch, offset):
+    expos, _, fibres = source_ref.shape
+    return [
+        (
+            source_ref.at[e, pl.ds(first, length), pl.ds(h * LANES, LANES)],
+            target.at[pl.ds((h * expos + e) * pitch + offset, length), :],
+        )
+        for h in range(fibres // LANES)
+        for e in range(expos)
+    ]
+
+
+def first_kernel(
+    moves, wav_count, place_ref, slots_ref, coupling_ref, counts_ref, good_ref, pixels_ref, ivar_ref, bits_ref,
+    sums_ref, weight_ref, table_ref, up_ref, down_ref,
+    slots_v, coupling_v, counts_v, good_v, ivar_v, bits_v, ivar_s, pixel_s, sems,
+):
+    expos, width, fibres = ivar_ref.shape
+    streams = expos * fibres // LANES
+    count = ivar_s.shape[0] // (2 * streams)
+    which = 1 - place_ref[2]
+    pairs = [(slots_ref, slots_v), (coupling_ref, coupling_v), (counts_ref, counts_v), (good_ref, good_v)]
+    for source, target in ((ivar_ref, ivar_s), (pixels_ref, pixel_s)):
+        pairs += stream_copies(source, target, 0, count, 2 * count, 0)
+        pairs += stream_copies(source, target, width - count, count, 2 * count, count)
+    pairs += half_copies(which, ivar_ref, bits_ref, ivar_v, bits_v)
+    waits = in_flight(pairs, sems)
+    waits[0].wait()
+    write_send_table(*moves, place_ref[0], slots_v, table_ref)
+    for wait in waits[1:]:
+        wait.wait()
+
+    back = 1.0 / stream_coupling(coupling_v, expos)
+    zero = jnp.zeros((streams, LANES), F32)
+    states = [(zero, zero + 1.0, zero), (zero, zero + 1.0, zero)]
+
+    def eliminate(tile, tiles):
+        for i in range(HALO * tile // tiles, HALO * (tile + 1) // tiles):
+            for side, row in enumerate((2 * count - HALO + i, HALO - 1 - i)):
+                at = pl.ds(row, streams, stride=2 * count)
+                states[side] = advance(states[side], ivar_s[at, :], pixel_s[at, :], back)
+                if i % 24 == 23:
+                    states[side] = rescaled(states[side])
+
+    write_weights(
+        place_ref, wav_count, which, coupling_v, counts_v, good_v, ivar_v, bits_v, sums_ref, weight_ref, eliminate
+    )
+    for (n, d, b), out_ref in zip(states, (up_ref, down_ref)):
+        scale = 1.0 / (d + n * back)
+        out_ref[0] = n * scale
+        out_ref[1] = b * scale
+
+
+def weights_scratch(slots, coupling, counts, good, ivar):
     expos, width, fibres = ivar.shape
     half = width // 2
+    return [
+        pltpu.VMEM(coupling.shape, F32),
+        pltpu.VMEM(counts.shape, jnp.int32),
+        pltpu.VMEM(good.shape, jnp.int32),
+        pltpu.VMEM((expos, half, fibres), F32),
+        pltpu.VMEM((expos, half // BITS, fibres), jnp.int32),
+    ]
+
+
+def sent_weights(moves, wav_count, place, slots, coupling, counts, good, pixels, ivar, bits):
+    expos, width, fibres = ivar.shape
+    half = width // 2
+    streams = expos * fibres // LANES
+    fib_count, pack, per, _ = moves
+    count = -(-HALO // ROWS) * ROWS
+    edge = shaped((2, streams, LANES))
     return pl.pallas_call(
-        functools.partial(weights_kernel, write_table, mine, wav_count),
-        in_specs=[in_smem] + [in_hbm] * 6,
-        out_specs=[in_vmem] * 3,
-        out_shape=[shaped((2, half, fibres)), shaped((expos, half, fibres)), shaped(table_shape, BF16)],
+        functools.partial(first_kernel, moves, wav_count),
+        in_specs=[in_smem] + [in_hbm] * 7,
+        out_specs=[in_vmem] * 5,
+        out_shape=[
+            shaped((2, half, fibres)),
+            shaped((expos, half, fibres)),
+            shaped((fib_count * pack * per, pack * fibres), BF16),
+            edge,
+            edge,
+        ],
         scratch_shapes=[
             pltpu.VMEM(slots.shape, jnp.int32),
-            pltpu.VMEM(coupling.shape, F32),
-            pltpu.VMEM(counts.shape, jnp.int32),
-            pltpu.VMEM(good.shape, jnp.int32),
-            pltpu.VMEM((expos, half, fibres), F32),
-            pltpu.VMEM((expos, half // BITS, fibres), jnp.int32),
-            pltpu.SemaphoreType.DMA((5 + half // GROUP,)),
+            *weights_scratch(slots, coupling, counts, good, ivar),
+            pltpu.VMEM((streams * 2 * count, LANES), F32),
+            pltpu.VMEM((streams * 2 * count, LANES), F32),
+            pltpu.SemaphoreType.DMA((6 + 4 * streams,)),
         ],
         compiler_params=params(),
         cost_estimate=cost(20 * ivar.size, 6 * ivar.size),
-        name="weights_kept" if mine else "weights_sent",
-    )(place, *held_in_hbm(slots, coupling, counts, good, ivar, bits))
-
-
-def stream_coupling(coupling_ref, expos):
-    coupling = coupling_ref[...]
-    blocks = coupling.shape[1] // LANES
-    return jnp.concatenate(
-        [jnp.broadcast_to(coupling[:, h * LANES : (h + 1) * LANES], (expos, LANES)) for h in range(blocks)], 0
-    )
-
-
-def advance(state, ivar, pixel, back_coupling):
-    n, d, b = state
-    d = d + n * back_coupling
-    return (n + ivar * d, d, b + (ivar * pixel) * d)
-
-
-def edges_kernel(place_ref, coupling_ref, pixels_ref, ivar_ref, edges_ref, pixel_out, ivar_out, sems):
-    expos, width, fibres = pixels_ref.shape
-    streams = expos * fibres // LANES
-    count = -(-HALO // ROWS) * ROWS
-
-    def copies(first, length):
-        pairs = []
-        for source, target in ((ivar_ref, ivar_out), (pixels_ref, pixel_out)):
-            for stream in range(streams):
-                h, e = divmod(stream, expos)
-                pairs.append(
-                    (
-                        source.at[e, pl.ds(first, length), pl.ds(h * LANES, LANES)],
-                        target.at[pl.ds(stream * width + first, length), :],
-                    )
-                )
-        return pairs
-
-    waits = in_flight(copies(0, count) + copies(width - count, count), sems)
-    rest = in_flight(copies(count, width - 2 * count), sems, len(waits))
+        name="sent_weights",
+    )(place, *held_in_hbm(slots, coupling, counts, good, pixels, ivar, bits))
+
+
+def second_kernel(
+    wav_count, place_ref, coupling_ref, counts_ref, good_ref, pixels_ref, ivar_ref, bits_ref,
+    sums_ref, weight_ref, pixel_out, ivar_out, coupling_v, counts_v, good_v, ivar_v, bits_v, sems,
+):
+    width = ivar_ref.shape[1]
+    which = place_ref[2]
+    pairs = [(coupling_ref, coupling_v), (counts_ref, counts_v), (good_ref, good_v)]
+    pairs += half_copies(which, ivar_ref, bits_ref, ivar_v, bits_v)
+    waits = in_flight(pairs, sems)
+    laid = stream_copies(ivar_ref, ivar_out, 0, width, width, 0) + stream_copies(pixels_ref, pixel_out, 0, width, width, 0)
+    rest = in_flight(laid, sems, len(waits))
     for wait in waits:
         wait.wait()
-    back = 1.0 / stream_coupling(coupling_ref, expos)
-    zero = jnp.zeros((streams, LANES), F32)
-    states = [(zero, zero + 1.0, zero), (zero, zero + 1.0, zero)]
-    for i in range(HALO):
-        for side, row in enumerate((width - HALO + i, HALO - 1 - i)):
-            at = pl.ds(row, streams, stride=width)
-            states[side] = advance(states[side], ivar_out[at, :], pixel_out[at, :], back)
-            if i % 10 == 9:
-                scale = inverse_of(states[side][1])
-                states[side] = tuple(part * scale for part in states[side])
-    for side in range(2):
-        n, d, b = states[side]
-        scale = 1.0 / (d + n * back)
-        edges_ref[side, 0] = n * scale
-        edges_ref[side, 1] = b * scale
+    write_weights(
+        place_ref, wav_count, which, coupling_v, counts_v, good_v, ivar_v, bits_v, sums_ref, weight_ref,
+        lambda tile, tiles: None,
+    )
     for wait in rest:
         wait.wait()
 
 
-def edge_rows(place, coupling, pixels, ivar):
-    expos, width, fibres = pixels.shape
+def kept_weights(wav_count, place, coupling, counts, good, pixels, ivar, bits):
+    expos, width, fibres = ivar.shape
+    half = width // 2
     streams = expos * fibres // LANES
     laid = shaped((streams * width, LANES))
     return pl.pallas_call(
-        edges_kernel,
-        in_specs=[in_smem, in_vmem, in_hbm, in_hbm],
-        out_specs=[in_vmem] * 3,
-        out_shape=[shaped((2, 2, streams, LANES)), laid, laid],
-        scratch_shapes=[pltpu.SemaphoreType.DMA((6 * streams,))],
+        functools.partial(second_kernel, wav_count),
+        in_specs=[in_smem] + [in_hbm] * 6,
+        out_specs=[in_vmem] * 4,
+        out_shape=[shaped((2, half, fibres)), shaped((expos, half, fibres)), laid, laid],
+        scratch_shapes=[
+            *weights_scratch(None, coupling, counts, good, ivar),
+            pltpu.SemaphoreType.DMA((5 + 2 * streams,)),
+        ],
         compiler_params=params(),
-        cost_estimate=cost(0, 0),
-        name="edge_rows",
-    )(place, coupling, *held_in_hbm(pixels, ivar))
+        cost_estimate=cost(20 * ivar.size, 6 * ivar.size),
+        name="kept_weights",
+    )(place, *held_in_hbm(coupling, counts, good, pixels, ivar, bits))
+
+
+def recv_kernel(moves, place_ref, slots_ref, table_ref):
+    write_recv_table(*moves, place_ref[0], slots_ref, table_ref)
+
+
+def recv_moves(moves, place, slots, fibres):
+    fib_count, pack, per, _ = moves
+    return pl.pallas_call(
+        functools.partial(recv_kernel, moves),
+        in_specs=[in_smem, in_vmem],
+        out_specs=in_vmem,
+        out_shape=shaped((pack * fibres, fib_count * pack * per), BF16),
+        compiler_params=params(),
+        cost_estimate=cost(1e6, 1e6),
+        name="recv_moves",
+    )(place, slots)
 
 
 def solve_kernel(
@@ -315,37 +391,49 @@
         lead_s[side, i] = d * inverse
         rest_s[side, i] = (b * back) * inverse
 
+    unrolled = divisor_of(middle, 24)
+
     def eliminate(it, states):
         states = list(states)
-        for k in range(ROWS):
-            i = it * ROWS + k
+        for k in range(unrolled):
+            i = it * unrolled + k
             for side, row in enumerate((i, width - 1 - i)):
                 keep(side, i, states[side])
                 states[side] = advance(states[side], ivar_ref[row_at(row), :], pixel_ref[row_at(row), :], back)
-        scaled = []
-        for n, d, b in states:
-            scale = inverse_of(d)
-            scaled.append((n * scale, d * scale, b * scale))
-        return tuple(scaled)
-
-    states = lax.fori_loop(0, middle // ROWS, eliminate, (begin(left_ref), begin(right_ref)))
+        return tuple(rescaled(state) for state in states)
+
+    states = lax.fori_loop(0, middle // unrolled, eliminate, (begin(left_ref), begin(right_ref)))
     for side in range(2):
         keep(side, middle, states[side])
     lead, rest = lead_s[0, middle], rest_s[0, middle]
     lead_r, rest_r = lead_s[1, middle], rest_s[1, middle]
     left = (rest + lead * rest_r) / (1.0 - lead * lead_r)
     right = rest_r + lead_r * left
+    several = divisor_of(middle, 48)
+
+    def after_both(near, far):
+        return far[0] * near[0], far[1] + far[0] * near[1]
+
+    def step(factors, value):
+        return factors[1] + factors[0] * value
 
     def substitute(it, values):
         values = list(values)
-        for k in range(ROWS):
-            i = middle - 1 - (it * ROWS + k)
-            for side, row in enumerate((i, width - 1 - i)):
-                solved_s[row_at(row), :] = values[side]
-                values[side] = rest_s[side, i] + lead_s[side, i] * values[side]
+        for k in range(0, several, 4):
+            for side in range(2):
+                rows = [middle - 1 - (it * several + k + m) for m in range(4)]
+                one, two, three, four = [(lead_s[side, i], rest_s[side, i]) for i in rows]
+                first_two = after_both(one, two)
+                all_four = after_both(first_two, after_both(three, four))
+                value = values[side]
+                third = step(first_two, value)
+                solved = [value, step(one, value), third, step(three, third)]
+                values[side] = step(all_four, value)
+                for i, x in zip(rows, solved):
+                    solved_s[row_at(i if side == 0 else width - 1 - i), :] = x
         return tuple(values)
 
-    lax.fori_loop(0, middle // ROWS, substitute, (left, right))
+    lax.fori_loop(0, middle // several, substitute, (left, right))
 
     blocks = fibres // LANES
     unroll = 5
@@ -526,29 +614,26 @@
     coupling, counts, slots = coupling[None], counts[None], owner_slot[None]
     swap = [(0, 1), (1, 0)]
     moves = (fib_count, pack, per, rel)
-    send_shape = (fib_count * pack * per, pack * fibres)
-
-    theirs, weight_t, send_table = weight_sums(
-        functools.partial(write_send_table, *moves), send_shape, False, wav_count,
-        place, slots, coupling, counts, good_flags, pixel_ivar, clip_bits,
+
+    theirs, weight_t, send_table, up, down = sent_weights(
+        moves, wav_count, place, slots, coupling, counts, good_flags, pixels, pixel_ivar, clip_bits
     )
     arriving = lax.ppermute(theirs, "exp", swap)
-    mine, weight_m, recv_table = weight_sums(
-        functools.partial(write_recv_table, *moves), send_shape[::-1], True, wav_count,
-        after(place, theirs), slots, coupling, counts, good_flags, pixel_ivar, clip_bits,
+    upward = [(i, i + 1) for i in range(wav_count - 1)]
+    left = lax.ppermute(up, "wav", upward)
+    right = lax.ppermute(down, "wav", [(j, i) for i, j in upward])
+    mine, weight_m, pixel_s, ivar_s = kept_weights(
+        wav_count, after(place, theirs), coupling, counts, good_flags, pixels, pixel_ivar, clip_bits
     )
     *sorted_pieces, scale = sort_fibres(arriving, mine, send_table, pack, pieces)
+    if rel:
+        sorted_pieces[1] = after(sorted_pieces[1], (left, right))
     weight_pieces = exchange(sorted_pieces, fib_count)
 
-    edges, pixel_s, ivar_s = edge_rows(after(place, scale), coupling, pixels, pixel_ivar)
-    up = [(i, i + 1) for i in range(wav_count - 1)]
-    left = lax.ppermute(edges[0], "wav", up)
-    right = lax.ppermute(edges[1], "wav", [(j, i) for i, j in up])
+    theirs, mine = flux_sums(place, coupling, left, right, pixel_s, ivar_s, weight_t, weight_m)
+    recv_table = recv_moves(moves, after(place, theirs), slots, fibres)
     if rel:
-        left = after(left, weight_pieces[fib_count // 2])
-    theirs, mine = flux_sums(place, coupling, left, right, pixel_s, ivar_s, weight_t, weight_m)
-    if rel:
-        theirs = after(theirs, weight_pieces[1])
+        theirs = after(theirs, (weight_pieces[1], weight_pieces[-1]))
     theirs = lax.ppermute(theirs, "exp", swap)
     flux_pieces = exchange(sort_fibres(theirs, mine, send_table, pack, pieces, scale), fib_count)
 

time: 41.2 us -> 39.2 us (0.951); the launches traced: 41 us -> 38.6 us
  waiting for transfers between devices: 6.88 us -> 5.52 us
  starting transfers between devices: 16.7 us -> 15.7 us
    ppermute x2, waiting for transfers between devices: 4.24 us -> 0.52 us  [the longest x1 0.52 us: per_device(): right = lax.ppermute(down, 'wav', [(j, i) for i, j in upward])]
    ppermute x6, waiting for transfers between devices: 2.64 us -> 4.79 us  [exchange(): lax.ppermute(pieces[d], 'fib', [(i, (i + d) % fib_count) for i in range(f...]
    ppermute x6, starting transfers between devices: 11.4 us -> 9.52 us  [exchange(): lax.ppermute(pieces[d], 'fib', [(i, (i + d) % fib_count) for i in range(f...]
    ppermute x2, starting transfers between devices: 4.68 us -> 5.7 us  [the longest x1 4.4 us: per_device(): left = lax.ppermute(up, 'wav', upward)]
  transfers between devices with their start and end apart: 10 -> 10, of which waited for: 3 -> 4; matrix products, arithmetic and copies ran while one was open for 0% -> 0% of each run, Pallas kernels for 32% -> 32%
where the time goes in v2:
time: 39.2 us; the launch traced here: 38.6 us
  Pallas kernels  16.5 us (42%)
  starting transfers between devices  15.7 us (40%)
  waiting for transfers between devices  5.52 us (14%)
  between operations  0.74 us (2%)
    ppermute x6, starting transfers between devices, exchange(): lax.ppermute(pieces[d], 'fib', [(i, (i + d) % fib_count) for i in range(f...  9.52 us
    pallas_call x1, Pallas kernels, flux_sums(): pl.pallas_call(solve_kernel, in_specs=[in_smem] + [in_vmem] * 7, out_spec...  4.86 us
    ppermute x6, waiting for transfers between devices, exchange(): lax.ppermute(pieces[d], 'fib', [(i, (i + d) % fib_count) for i in range(f...  4.79 us
    ppermute x1, starting transfers between devices, per_device(): left = lax.ppermute(up, 'wav', upward)  4.4 us
    pallas_call x1, Pallas kernels, sent_weights(): pl.pallas_call(functools.partial(first_kernel, moves, wav_count), in_spec...  3.26 us
    pallas_call x1, Pallas kernels, kept_weights(): pl.pallas_call(functools.partial(second_kernel, wav_count), in_specs=[in_...  3.23 us
    pallas_call x1, Pallas kernels, end_weights(): pl.pallas_call(functools.partial(weights_end_kernel, pack, total), in_spe...  1.92 us
    pallas_call x1, Pallas kernels, recv_moves(): pl.pallas_call(functools.partial(recv_kernel, moves), in_specs=[in_smem,...  1.4 us
  transfers between devices with their start and end apart: 10, of which 4 were waited for; matrix products, arithmetic and copies ran while one was open for 0% of the time, Pallas kernels for 32%

profile of v2, /device:TPU:0, one launch (start us, length us, event | category | flops | bytes accessed | tf_op | source)
XLA Modules:
  0.0 38.6 jit_solution(17843957680948470797)
XLA Ops:
  0.6 0.1 pad_add_fusion.place_ref
  0.7 3.3 %sent_weights.1 = (f32[2,240,256]{2,1,0:T(8,128)S(1)}, f32[4,240,256]{2,1,0:T(8,128)S(1)}, bf16[512,512]{1,0:T(8,128)(2,1)S(1)}, f32[2,8,128]{2,1,0:T(8,128)S(1)}, f32[2,8,128]{2,1,0:T(8,128)S(1)}) custom-call(s32[3]{0:T(128)S(1)} %pad_add_fusion.place_ref, s32[1,1024]{1,0:T(1,128)} %bitcast.6, f32[1,256]{1,0:T(1,128)} %bitcast.8, s32[1,256]{1,0:T(1,128)} %bitcast.11, ...), custom_call_target="tpu_custom_call" | custom-call | flops 9830400 | bytes 2949120 | tf_op jit(solution)/shard_map/sent_weights/pallas_call | solution.py:288
  4.0 0.5 %collective-permute-start.2 = (f32[2,240,256]{2,1,0:T(8,128)S(1)}, f32[2,240,256]{2,1,0:T(8,128)S(1)}, u32[]{:S(2)}, u32[]{:S(2)}) collective-permute-start(f32[2,240,256]{2,1,0:T(8,128)S(1)} %get-tuple-element.31), channel_id=1, source_target_pairs={{0,1},{1,0},{2,3},{3,2},{4,5},{5,4},{6,7},{7,6},{8,9},{9,8},{10,11... | collective-permute-start | bytes 1474568 | tf_op jit(solution)/shard_map/ppermute | solution.py:621
  4.5 4.4 %collective-permute-start = (f32[2,8,128]{2,1,0:T(8,128)S(1)}, f32[2,8,128]{2,1,0:T(8,128)S(1)}, u32[]{:S(2)}, u32[]{:S(2)}) collective-permute-start(f32[2,8,128]{2,1,0:T(8,128)S(1)} %get-tuple-element.29), channel_id=1, source_target_pairs={{0,2},{2,4},{4,6},{1,3},{3,5},{5,7},{8,10},{10,12},{12,14},{9,11},... | collective-permute-start | bytes 24584 | tf_op jit(solution)/shard_map/ppermute | solution.py:623
  8.9 0.0 copy-start.1
  8.9 1.3 %collective-permute-start.1 = (f32[2,8,128]{2,1,0:T(8,128)S(1)}, f32[2,8,128]{2,1,0:T(8,128)S(1)}, u32[]{:S(2)}, u32[]{:S(2)}) collective-permute-start(f32[2,8,128]{2,1,0:T(8,128)S(1)} %get-tuple-element.30), channel_id=1, source_target_pairs={{2,0},{4,2},{6,4},{3,1},{5,3},{7,5},{10,8},{12,10},{14,12},{11,9},... | collective-permute-start | bytes 24584 | tf_op jit(solution)/shard_map/ppermute | solution.py:624
  10.2 3.2 %kept_weights.1 = (f32[2,240,256]{2,1,0:T(8,128)S(1)}, f32[4,240,256]{2,1,0:T(8,128)S(1)}, f32[3840,128]{1,0:T(8,128)S(1)}, f32[3840,128]{1,0:T(8,128)S(1)}) custom-call(s32[3]{0:T(128)S(1)} %pad_add_fusion.place_ref, f32[1,256]{1,0:T(1,128)} %bitcast.9, s32[1,256]{1,0:T(1,128)} %bitcast.12, s32[4,256]{1,0:T(4,128)} %good_ref.3, f32[4,480,256]{2,1,0:T(8,128)} %pixels_ref.3, ...), custom_call_target="tpu_custom_call" | custom-call | flops 9830400 | bytes 2949120 | tf_op jit(solution)/shard_map/kept_weights/pallas_call | solution.py:338
  13.5 0.0 collective-permute-done.2.theirs_ref
  13.5 0.5 %sort_weights.1 = (f32[2,120,128]{2,1,0:T(8,128)S(1)}, f32[2,120,128]{2,1,0:T(8,128)S(1)}, f32[2,120,128]{2,1,0:T(8,128)S(1)}, f32[2,120,128]{2,1,0:T(8,128)S(1)}, f32[240,256]{1,0:T(8,128)S(1)}) custom-call(f32[2,240,256]{2,1,0:T(8,128)S(1)} %collective-permute-done.2.theirs_ref, f32[2,240,256]{2,1,0:T(8,128)S(1)} %get-tuple-element.39.mine_ref, ...), custom_call_target="tpu_custom_call" | custom-call | tf_op jit(solution)/shard_map/sort_weights/pallas_call | solution.py:515
  13.9 0.5 %collective-permute-done.1.right_ref = f32[2,8,128]{2,1,0:T(8,128)S(1)} collective-permute-done((f32[2,8,128]{2,1,0:T(8,128)S(1)}, f32[2,8,128]{2,1,0:T(8,128)S(1)}, u32[]{:S(2)}, u32[]{:S(2)}) %collective-permute-start.1) | collective-permute-done | bytes 8224 | tf_op jit(solution)/shard_map/ppermute | solution.py:624
  14.5 1.6 %collective-permute-start.3 = (f32[2,120,128]{2,1,0:T(8,128)S(1)}, f32[2,120,128]{2,1,0:T(8,128)S(1)}, u32[]{:S(2)}, u32[]{:S(2)}) collective-permute-start(f32[2,120,128]{2,1,0:T(8,128)S(1)} %get-tuple-element.42), channel_id=1, source_target_pairs={{0,8},{8,16},{16,24},{24,0},{1,9},{9,17},{17,25},{25,1},{2,10},{10... | collective-permute-start | bytes 368648 | tf_op jit(solution)/shard_map/ppermute | solution.py:531
  16.0 2.2 %collective-permute-start.4 = (f32[2,120,128]{2,1,0:T(8,128)S(1)}, f32[2,120,128]{2,1,0:T(8,128)S(1)}, u32[]{:S(2)}, u32[]{:S(2)}) collective-permute-start(f32[2,120,128]{2,1,0:T(8,128)S(1)} %get-tuple-element.43), channel_id=1, source_target_pairs={{0,24},{8,0},{16,8},{24,16},{1,25},{9,1},{17,9},{25,17},{2,26},{10... | collective-permute-start | bytes 368648 | tf_op jit(solution)/shard_map/ppermute | solution.py:531
  18.3 4.9 %flux_sums.1 = (f32[1,240,256]{2,1,0:T(8,128)S(1)}, f32[1,240,256]{2,1,0:T(8,128)S(1)}) custom-call(s32[3]{0:T(128)S(1)} %pad_add_fusion.place_ref, f32[1,256]{1,0:T(1,128)S(1)} %bitcast.10, f32[2,8,128]{2,1,0:T(8,128)S(1)} %collective-permute-done.left_ref, f32[2,8,128]{2,1,0:T(8,128)S(1)} %collective-permute-done.1.right_ref, ...), custom_call_target="tpu_custom_call" | custom-call | tf_op jit(solution)/shard_map/flux_sums/pallas_call | solution.py:468
  23.2 0.2 collective-permute-done.4.refs_3_
  23.3 1.3 %collective-permute-start.9 = (f32[2,120,128]{2,1,0:T(8,128)S(1)}, f32[2,120,128]{2,1,0:T(8,128)S(1)}, u32[]{:S(2)}, u32[]{:S(2)}) collective-permute-start(f32[2,120,128]{2,1,0:T(8,128)S(1)} %get-tuple-element.52), channel_id=1, source_target_pairs={{0,16},{8,24},{16,0},{24,8},{1,17},{9,25},{17,1},{25,9},{2,18},{10... | collective-permute-start | bytes 368648 | tf_op jit(solution)/shard_map/ppermute | solution.py:531
  24.6 0.2 collective-permute-done.5.theirs_ref
  24.8 0.3 sort_flux.1
  25.2 1.4 %collective-permute-start.6 = (f32[1,120,128]{2,1,0:T(8,128)S(1)}, f32[1,120,128]{2,1,0:T(8,128)S(1)}, u32[]{:S(2)}, u32[]{:S(2)}) collective-permute-start(f32[1,120,128]{2,1,0:T(8,128)S(1)} %get-tuple-element.48), channel_id=1, source_target_pairs={{0,8},{8,16},{16,24},{24,0},{1,9},{9,17},{17,25},{25,1},{2,10},{10... | collective-permute-start | bytes 184328 | tf_op jit(solution)/shard_map/ppermute | solution.py:531
  26.6 1.5 %collective-permute-start.7 = (f32[1,120,128]{2,1,0:T(8,128)S(1)}, f32[1,120,128]{2,1,0:T(8,128)S(1)}, u32[]{:S(2)}, u32[]{:S(2)}) collective-permute-start(f32[1,120,128]{2,1,0:T(8,128)S(1)} %get-tuple-element.49), channel_id=1, source_target_pairs={{0,16},{8,24},{16,0},{24,8},{1,17},{9,25},{17,1},{25,9},{2,18},{10... | collective-permute-start | bytes 184328 | tf_op jit(solution)/shard_map/ppermute | solution.py:531
  28.1 1.5 %collective-permute-start.8 = (f32[1,120,128]{2,1,0:T(8,128)S(1)}, f32[1,120,128]{2,1,0:T(8,128)S(1)}, u32[]{:S(2)}, u32[]{:S(2)}) collective-permute-start(f32[1,120,128]{2,1,0:T(8,128)S(1)} %get-tuple-element.50), channel_id=1, source_target_pairs={{0,24},{8,0},{16,8},{24,16},{1,25},{9,1},{17,9},{25,17},{2,26},{10... | collective-permute-start | bytes 184328 | tf_op jit(solution)/shard_map/ppermute | solution.py:531
  29.6 1.4 %recv_moves.1.table_ref = bf16[512,512]{1,0:T(8,128)(2,1)S(1)} custom-call(s32[3]{0:T(128)S(1)} %pad_add_fusion.place_ref, s32[1,1024]{1,0:T(1,128)S(1)} %bitcast.7), custom_call_target="tpu_custom_call" | custom-call | flops 1000000 | bytes 1000000 | tf_op jit(solution)/shard_map/recv_moves/pallas_call | solution.py:359
  31.0 4.6 %collective-permute-done.9.refs_2_ = f32[2,120,128]{2,1,0:T(8,128)S(1)} collective-permute-done((f32[2,120,128]{2,1,0:T(8,128)S(1)}, f32[2,120,128]{2,1,0:T(8,128)S(1)}, u32[]{:S(2)}, u32[]{:S(2)}) %collective-permute-start.9) | collective-permute-done | bytes 122912 | tf_op jit(solution)/shard_map/ppermute | solution.py:531
  35.6 1.9 %end_weights.1 = (f32[240,256]{1,0:T(8,128)}, f32[3,240,256]{2,1,0:T(8,128)}) custom-call(s32[3]{0:T(128)S(1)} %pad_add_fusion.place_ref, bf16[512,512]{1,0:T(8,128)(2,1)S(1)} %recv_moves.1.table_ref, f32[2,120,128]{2,1,0:T(8,128)S(1)} %get-tuple-element.51.refs_0_, f32[2,120,128]{2,1,0:T(8,128)S(1)} %collective-permute-done.3.refs_1_, ...), custom_call_target="tpu_custom_call" | custom-call | flops 251658240 | bytes 1474560 | tf_op jit(solution)/shard_map/end_weights/pallas_call | solution.py:565
  37.5 1.0 %end_flux.1 = f32[240,256]{1,0:T(8,128)} custom-call(bf16[512,512]{1,0:T(8,128)(2,1)S(1)} %recv_moves.1.table_ref, f32[1,120,128]{2,1,0:T(8,128)S(1)} %get-tuple-element.47.refs_0_, f32[1,120,128]{2,1,0:T(8,128)S(1)} %collective-permute-done.6.refs_1_, f32[1,120,128]{2,1,0:T(8,128)S(1)} %collective-permute-done.7.refs_2_, ...), custom_call_target="tpu_custom_call" | custom-call | flops 125829120 | bytes 491520 | tf_op jit(solution)/shard_map/end_flux/pallas_call | solution.py:587
  (9 shorter events, 0.0 us)
Async XLA Ops:
  4.0 9.5 %collective-permute-start.2 = (f32[2,240,256]{2,1,0:T(8,128)S(1)}, f32[2,240,256]{2,1,0:T(8,128)S(1)}, u32[]{:S(2)}, u32[]{:S(2)}) collective-permute-start(f32[2,240,256]{2,1,0:T(8,128)S(1)} %get-tuple-element.31), channel_id=1, source_target_pairs={{0,1},{1,0},{2,3},{3,2},{4,5},{5,4},{6,7},{7,6},{8,9},{9,8},{10,11... | collective-permute-start | bytes 1474568 | tf_op jit(solution)/shard_map/ppermute | solution.py:621
  4.5 9.4 %collective-permute-start = (f32[2,8,128]{2,1,0:T(8,128)S(1)}, f32[2,8,128]{2,1,0:T(8,128)S(1)}, u32[]{:S(2)}, u32[]{:S(2)}) collective-permute-start(f32[2,8,128]{2,1,0:T(8,128)S(1)} %get-tuple-element.29), channel_id=1, source_target_pairs={{0,2},{2,4},{4,6},{1,3},{3,5},{5,7},{8,10},{10,12},{12,14},{9,11},... | collective-permute-start | bytes 24584 | tf_op jit(solution)/shard_map/ppermute | solution.py:623
  8.9 9.4 %copy-start.1 = (f32[256]{0:T(256)S(1)}, f32[256]{0:T(256)}, u32[]{:S(2)}) copy-start(f32[256]{0:T(256)} %param.10) | copy-start | bytes 3076
  8.9 5.5 %collective-permute-start.1 = (f32[2,8,128]{2,1,0:T(8,128)S(1)}, f32[2,8,128]{2,1,0:T(8,128)S(1)}, u32[]{:S(2)}, u32[]{:S(2)}) collective-permute-start(f32[2,8,128]{2,1,0:T(8,128)S(1)} %get-tuple-element.30), channel_id=1, source_target_pairs={{2,0},{4,2},{6,4},{3,1},{5,3},{7,5},{10,8},{12,10},{14,12},{11,9},... | collective-permute-start | bytes 24584 | tf_op jit(solution)/shard_map/ppermute | solution.py:624
  14.5 8.7 %collective-permute-start.3 = (f32[2,120,128]{2,1,0:T(8,128)S(1)}, f32[2,120,128]{2,1,0:T(8,128)S(1)}, u32[]{:S(2)}, u32[]{:S(2)}) collective-permute-start(f32[2,120,128]{2,1,0:T(8,128)S(1)} %get-tuple-element.42), channel_id=1, source_target_pairs={{0,8},{8,16},{16,24},{24,0},{1,9},{9,17},{17,25},{25,1},{2,10},{10... | collective-permute-start | bytes 368648 | tf_op jit(solution)/shard_map/ppermute | solution.py:531
  16.0 7.3 %collective-permute-start.4 = (f32[2,120,128]{2,1,0:T(8,128)S(1)}, f32[2,120,128]{2,1,0:T(8,128)S(1)}, u32[]{:S(2)}, u32[]{:S(2)}) collective-permute-start(f32[2,120,128]{2,1,0:T(8,128)S(1)} %get-tuple-element.43), channel_id=1, source_target_pairs={{0,24},{8,0},{16,8},{24,16},{1,25},{9,1},{17,9},{25,17},{2,26},{10... | collective-permute-start | bytes 368648 | tf_op jit(solution)/shard_map/ppermute | solution.py:531
  18.3 11.3 %copy-start = (s32[1024]{0:T(1024)S(1)}, s32[1024]{0:T(1024)}, u32[]{:S(2)}) copy-start(s32[1024]{0:T(1024)} %param.13) | copy-start | bytes 12292
  23.3 1.5 %collective-permute-start.5 = (f32[1,240,256]{2,1,0:T(8,128)S(1)}, f32[1,240,256]{2,1,0:T(8,128)S(1)}, u32[]{:S(2)}, u32[]{:S(2)}) collective-permute-start(f32[1,240,256]{2,1,0:T(8,128)S(1)} %get-tuple-element.44), channel_id=1, source_target_pairs={{0,1},{1,0},{2,3},{3,2},{4,5},{5,4},{6,7},{7,6},{8,9},{9,8},{10,11... | collective-permute-start | bytes 737288 | tf_op jit(solution)/shard_map/ppermute | solution.py:637
  23.3 12.3 %collective-permute-start.9 = (f32[2,120,128]{2,1,0:T(8,128)S(1)}, f32[2,120,128]{2,1,0:T(8,128)S(1)}, u32[]{:S(2)}, u32[]{:S(2)}) collective-permute-start(f32[2,120,128]{2,1,0:T(8,128)S(1)} %get-tuple-element.52), channel_id=1, source_target_pairs={{0,16},{8,24},{16,0},{24,8},{1,17},{9,25},{17,1},{25,9},{2,18},{10... | collective-permute-start | bytes 368648 | tf_op jit(solution)/shard_map/ppermute | solution.py:531
  25.2 12.4 %collective-permute-start.6 = (f32[1,120,128]{2,1,0:T(8,128)S(1)}, f32[1,120,128]{2,1,0:T(8,128)S(1)}, u32[]{:S(2)}, u32[]{:S(2)}) collective-permute-start(f32[1,120,128]{2,1,0:T(8,128)S(1)} %get-tuple-element.48), channel_id=1, source_target_pairs={{0,8},{8,16},{16,24},{24,0},{1,9},{9,17},{17,25},{25,1},{2,10},{10... | collective-permute-start | bytes 184328 | tf_op jit(solution)/shard_map/ppermute | solution.py:531
  26.6 10.9 %collective-permute-start.7 = (f32[1,120,128]{2,1,0:T(8,128)S(1)}, f32[1,120,128]{2,1,0:T(8,128)S(1)}, u32[]{:S(2)}, u32[]{:S(2)}) collective-permute-start(f32[1,120,128]{2,1,0:T(8,128)S(1)} %get-tuple-element.49), channel_id=1, source_target_pairs={{0,16},{8,24},{16,0},{24,8},{1,17},{9,25},{17,1},{25,9},{2,18},{10... | collective-permute-start | bytes 184328 | tf_op jit(solution)/shard_map/ppermute | solution.py:531
  28.1 9.4 %collective-permute-start.8 = (f32[1,120,128]{2,1,0:T(8,128)S(1)}, f32[1,120,128]{2,1,0:T(8,128)S(1)}, u32[]{:S(2)}, u32[]{:S(2)}) collective-permute-start(f32[1,120,128]{2,1,0:T(8,128)S(1)} %get-tuple-element.50), channel_id=1, source_target_pairs={{0,24},{8,0},{16,8},{24,16},{1,25},{9,1},{17,9},{25,17},{2,26},{10... | collective-permute-start | bytes 184328 | tf_op jit(solution)/shard_map/ppermute | solution.py:531

commit v3 on v2

--- a/solution.py
+++ b/solution.py
@@ -85,6 +85,10 @@
 def rescaled(state):
     scale = inverse_of(state[1])
     return tuple(part * scale for part in state)
+
+
+def odd(rows):
+    return rows + 1 - rows % 2
 
 
 def divisor_of(size, most):
@@ -232,12 +236,13 @@
 ):
     expos, width, fibres = ivar_ref.shape
     streams = expos * fibres // LANES
-    count = ivar_s.shape[0] // (2 * streams)
+    count = -(-HALO // ROWS) * ROWS
+    pitch = odd(2 * count)
     which = 1 - place_ref[2]
     pairs = [(slots_ref, slots_v), (coupling_ref, coupling_v), (counts_ref, counts_v), (good_ref, good_v)]
     for source, target in ((ivar_ref, ivar_s), (pixels_ref, pixel_s)):
-        pairs += stream_copies(source, target, 0, count, 2 * count, 0)
-        pairs += stream_copies(source, target, width - count, count, 2 * count, count)
+        pairs += stream_copies(source, target, 0, count, pitch, 0)
+        pairs += stream_copies(source, target, width - count, count, pitch, count)
     pairs += half_copies(which, ivar_ref, bits_ref, ivar_v, bits_v)
     waits = in_flight(pairs, sems)
     waits[0].wait()
@@ -252,7 +257,7 @@
     def eliminate(tile, tiles):
         for i in range(HALO * tile // tiles, HALO * (tile + 1) // tiles):
             for side, row in enumerate((2 * count - HALO + i, HALO - 1 - i)):
-                at = pl.ds(row, streams, stride=2 * count)
+                at = pl.ds(row, streams, stride=pitch)
                 states[side] = advance(states[side], ivar_s[at, :], pixel_s[at, :], back)
                 if i % 24 == 23:
                     states[side] = rescaled(states[side])
@@ -299,8 +304,8 @@
         scratch_shapes=[
             pltpu.VMEM(slots.shape, jnp.int32),
             *weights_scratch(slots, coupling, counts, good, ivar),
-            pltpu.VMEM((streams * 2 * count, LANES), F32),
-            pltpu.VMEM((streams * 2 * count, LANES), F32),
+            pltpu.VMEM((streams * odd(2 * count), LANES), F32),
+            pltpu.VMEM((streams * odd(2 * count), LANES), F32),
             pltpu.SemaphoreType.DMA((6 + 4 * streams,)),
         ],
         compiler_params=params(),
@@ -318,7 +323,8 @@
     pairs = [(coupling_ref, coupling_v), (counts_ref, counts_v), (good_ref, good_v)]
     pairs += half_copies(which, ivar_ref, bits_ref, ivar_v, bits_v)
     waits = in_flight(pairs, sems)
-    laid = stream_copies(ivar_ref, ivar_out, 0, width, width, 0) + stream_copies(pixels_ref, pixel_out, 0, width, width, 0)
+    laid = stream_copies(ivar_ref, ivar_out, 0, width, odd(width), 0)
+    laid += stream_copies(pixels_ref, pixel_out, 0, width, odd(width), 0)
     rest = in_flight(laid, sems, len(waits))
     for wait in waits:
         wait.wait()
@@ -334,7 +340,7 @@
     expos, width, fibres = ivar.shape
     half = width // 2
     streams = expos * fibres // LANES
-    laid = shaped((streams * width, LANES))
+    laid = shaped((streams * odd(width), LANES))
     return pl.pallas_call(
         functools.partial(second_kernel, wav_count),
         in_specs=[in_smem] + [in_hbm] * 6,
@@ -373,13 +379,14 @@
 ):
     streams = left_ref.shape[1]
     expos, half, fibres = weight_t_ref.shape
-    width = ivar_ref.shape[0] // streams
-    middle = width // 2
+    width = 2 * half
+    pitch = odd(width)
+    middle = half
     coupling = stream_coupling(coupling_ref, expos)
     back = 1.0 / coupling
 
     def row_at(i):
-        return pl.ds(i, streams, stride=width)
+        return pl.ds(i, streams, stride=pitch)
 
     def begin(edge_ref):
         u = edge_ref[0]
@@ -448,7 +455,7 @@
                     cut = pl.ds(h * LANES, LANES)
                     total = None
                     for e in range(expos):
-                        at = pl.ds(pl.multiple_of((h * expos + e) * width + start + row, ROWS), ROWS)
+                        at = pl.ds((h * expos + e) * pitch + start + row, ROWS)
                         term = weight_ref[e, pl.ds(row, ROWS), cut] * solved_s[at, :]
                         total = term if e == 0 else total + term
                     out_ref[0, pl.ds(row, ROWS), cut] = total

time: 39.2 us -> 39 us (level)
  Pallas kernels: 16.5 us -> 14.2 us
  waiting for transfers between devices: 5.52 us -> 7.78 us
    ppermute x6, waiting for transfers between devices: 4.79 us -> 7.07 us  [exchange(): lax.ppermute(pieces[d], 'fib', [(i, (i + d) % fib_count) for i in range(f...]
    pallas_call x1, Pallas kernels: 4.86 us -> 2.6 us  [flux_sums(): pl.pallas_call(solve_kernel, in_specs=[in_smem] + [in_vmem] * 7, out_spec...]
  transfers between devices with their start and end apart: 10 -> 10, of which waited for: 4 -> 5; matrix products, arithmetic and copies ran while one was open for 0% -> 0% of each run, Pallas kernels for 32% -> 26%
where the time goes in v3:
time: 39 us; the launch traced here: 38.5 us
  starting transfers between devices  15.7 us (40%)
  Pallas kernels  14.2 us (36%)
  waiting for transfers between devices  7.78 us (20%)
  between operations  0.73 us (2%)
    ppermute x6, starting transfers between devices, exchange(): lax.ppermute(pieces[d], 'fib', [(i, (i + d) % fib_count) for i in range(f...  9.53 us
    ppermute x6, waiting for transfers between devices, exchange(): lax.ppermute(pieces[d], 'fib', [(i, (i + d) % fib_count) for i in range(f...  7.07 us
    ppermute x1, starting transfers between devices, per_device(): left = lax.ppermute(up, 'wav', upward)  4.4 us
    pallas_call x1, Pallas kernels, kept_weights(): pl.pallas_call(functools.partial(second_kernel, wav_count), in_specs=[in_...  3.23 us
    pallas_call x1, Pallas kernels, sent_weights(): pl.pallas_call(functools.partial(first_kernel, moves, wav_count), in_spec...  3.15 us
    pallas_call x1, Pallas kernels, flux_sums(): pl.pallas_call(solve_kernel, in_specs=[in_smem] + [in_vmem] * 7, out_spec...  2.6 us
    pallas_call x1, Pallas kernels, end_weights(): pl.pallas_call(functools.partial(weights_end_kernel, pack, total), in_spe...  1.92 us
    pallas_call x1, Pallas kernels, recv_moves(): pl.pallas_call(functools.partial(recv_kernel, moves), in_specs=[in_smem,...  1.4 us
  transfers between devices with their start and end apart: 10, of which 5 were waited for; matrix products, arithmetic and copies ran while one was open for 0% of the time, Pallas kernels for 26%

profile of v3, /device:TPU:0, one launch (start us, length us, event | category | flops | bytes accessed | tf_op | source)
XLA Modules:
  0.0 38.5 jit_solution(790328091176018027)
XLA Ops:
  0.6 0.1 pad_add_fusion.place_ref
  0.7 3.1 %sent_weights.1 = (f32[2,240,256]{2,1,0:T(8,128)S(1)}, f32[4,240,256]{2,1,0:T(8,128)S(1)}, bf16[512,512]{1,0:T(8,128)(2,1)S(1)}, f32[2,8,128]{2,1,0:T(8,128)S(1)}, f32[2,8,128]{2,1,0:T(8,128)S(1)}) custom-call(s32[3]{0:T(128)S(1)} %pad_add_fusion.place_ref, s32[1,1024]{1,0:T(1,128)} %bitcast.6, f32[1,256]{1,0:T(1,128)} %bitcast.8, s32[1,256]{1,0:T(1,128)} %bitcast.11, ...), custom_call_target="tpu_custom_call" | custom-call | flops 9830400 | bytes 2949120 | tf_op jit(solution)/shard_map/sent_weights/pallas_call | solution.py:293
  3.9 0.5 %collective-permute-start.2 = (f32[2,240,256]{2,1,0:T(8,128)S(1)}, f32[2,240,256]{2,1,0:T(8,128)S(1)}, u32[]{:S(2)}, u32[]{:S(2)}) collective-permute-start(f32[2,240,256]{2,1,0:T(8,128)S(1)} %get-tuple-element.31), channel_id=1, source_target_pairs={{0,1},{1,0},{2,3},{3,2},{4,5},{5,4},{6,7},{7,6},{8,9},{9,8},{10,11... | collective-permute-start | bytes 1474568 | tf_op jit(solution)/shard_map/ppermute | solution.py:628
  4.4 4.4 %collective-permute-start = (f32[2,8,128]{2,1,0:T(8,128)S(1)}, f32[2,8,128]{2,1,0:T(8,128)S(1)}, u32[]{:S(2)}, u32[]{:S(2)}) collective-permute-start(f32[2,8,128]{2,1,0:T(8,128)S(1)} %get-tuple-element.29), channel_id=1, source_target_pairs={{0,2},{2,4},{4,6},{1,3},{3,5},{5,7},{8,10},{10,12},{12,14},{9,11},... | collective-permute-start | bytes 24584 | tf_op jit(solution)/shard_map/ppermute | solution.py:630
  8.8 0.0 copy-start.1
  8.8 1.3 %collective-permute-start.1 = (f32[2,8,128]{2,1,0:T(8,128)S(1)}, f32[2,8,128]{2,1,0:T(8,128)S(1)}, u32[]{:S(2)}, u32[]{:S(2)}) collective-permute-start(f32[2,8,128]{2,1,0:T(8,128)S(1)} %get-tuple-element.30), channel_id=1, source_target_pairs={{2,0},{4,2},{6,4},{3,1},{5,3},{7,5},{10,8},{12,10},{14,12},{11,9},... | collective-permute-start | bytes 24584 | tf_op jit(solution)/shard_map/ppermute | solution.py:631
  10.1 3.2 %kept_weights.1 = (f32[2,240,256]{2,1,0:T(8,128)S(1)}, f32[4,240,256]{2,1,0:T(8,128)S(1)}, f32[3848,128]{1,0:T(8,128)S(1)}, f32[3848,128]{1,0:T(8,128)S(1)}) custom-call(s32[3]{0:T(128)S(1)} %pad_add_fusion.place_ref, f32[1,256]{1,0:T(1,128)} %bitcast.9, s32[1,256]{1,0:T(1,128)} %bitcast.12, s32[4,256]{1,0:T(4,128)} %good_ref.3, f32[4,480,256]{2,1,0:T(8,128)} %pixels_ref.3, ...), custom_call_target="tpu_custom_call" | custom-call | flops 9830400 | bytes 2949120 | tf_op jit(solution)/shard_map/kept_weights/pallas_call | solution.py:344
  13.4 0.5 %sort_weights.1 = (f32[2,120,128]{2,1,0:T(8,128)S(1)}, f32[2,120,128]{2,1,0:T(8,128)S(1)}, f32[2,120,128]{2,1,0:T(8,128)S(1)}, f32[2,120,128]{2,1,0:T(8,128)S(1)}, f32[240,256]{1,0:T(8,128)S(1)}) custom-call(f32[2,240,256]{2,1,0:T(8,128)S(1)} %collective-permute-done.2.theirs_ref, f32[2,240,256]{2,1,0:T(8,128)S(1)} %get-tuple-element.39.mine_ref, ...), custom_call_target="tpu_custom_call" | custom-call | tf_op jit(solution)/shard_map/sort_weights/pallas_call | solution.py:522
  13.9 0.5 %collective-permute-done.1.right_ref = f32[2,8,128]{2,1,0:T(8,128)S(1)} collective-permute-done((f32[2,8,128]{2,1,0:T(8,128)S(1)}, f32[2,8,128]{2,1,0:T(8,128)S(1)}, u32[]{:S(2)}, u32[]{:S(2)}) %collective-permute-start.1) | collective-permute-done | bytes 8224 | tf_op jit(solution)/shard_map/ppermute | solution.py:631
  14.4 1.6 %collective-permute-start.3 = (f32[2,120,128]{2,1,0:T(8,128)S(1)}, f32[2,120,128]{2,1,0:T(8,128)S(1)}, u32[]{:S(2)}, u32[]{:S(2)}) collective-permute-start(f32[2,120,128]{2,1,0:T(8,128)S(1)} %get-tuple-element.42), channel_id=1, source_target_pairs={{0,8},{8,16},{16,24},{24,0},{1,9},{9,17},{17,25},{25,1},{2,10},{10... | collective-permute-start | bytes 368648 | tf_op jit(solution)/shard_map/ppermute | solution.py:538
  15.9 2.2 %collective-permute-start.4 = (f32[2,120,128]{2,1,0:T(8,128)S(1)}, f32[2,120,128]{2,1,0:T(8,128)S(1)}, u32[]{:S(2)}, u32[]{:S(2)}) collective-permute-start(f32[2,120,128]{2,1,0:T(8,128)S(1)} %get-tuple-element.43), channel_id=1, source_target_pairs={{0,24},{8,0},{16,8},{24,16},{1,25},{9,1},{17,9},{25,17},{2,26},{10... | collective-permute-start | bytes 368648 | tf_op jit(solution)/shard_map/ppermute | solution.py:538
  18.2 2.6 %flux_sums.1 = (f32[1,240,256]{2,1,0:T(8,128)S(1)}, f32[1,240,256]{2,1,0:T(8,128)S(1)}) custom-call(s32[3]{0:T(128)S(1)} %pad_add_fusion.place_ref, f32[1,256]{1,0:T(1,128)S(1)} %bitcast.10, f32[2,8,128]{2,1,0:T(8,128)S(1)} %collective-permute-done.left_ref, f32[2,8,128]{2,1,0:T(8,128)S(1)} %collective-permute-done.1.right_ref, ...), custom_call_target="tpu_custom_call" | custom-call | tf_op jit(solution)/shard_map/flux_sums/pallas_call | solution.py:475
  20.8 1.6 %collective-permute-done.3.refs_1_ = f32[2,120,128]{2,1,0:T(8,128)S(1)} collective-permute-done((f32[2,120,128]{2,1,0:T(8,128)S(1)}, f32[2,120,128]{2,1,0:T(8,128)S(1)}, u32[]{:S(2)}, u32[]{:S(2)}) %collective-permute-start.3) | collective-permute-done | bytes 122912 | tf_op jit(solution)/shard_map/ppermute | solution.py:538
  22.3 0.9 %collective-permute-done.4.refs_3_ = f32[2,120,128]{2,1,0:T(8,128)S(1)} collective-permute-done((f32[2,120,128]{2,1,0:T(8,128)S(1)}, f32[2,120,128]{2,1,0:T(8,128)S(1)}, u32[]{:S(2)}, u32[]{:S(2)}) %collective-permute-start.4) | collective-permute-done | bytes 122912 | tf_op jit(solution)/shard_map/ppermute | solution.py:538
  23.2 1.3 %collective-permute-start.9 = (f32[2,120,128]{2,1,0:T(8,128)S(1)}, f32[2,120,128]{2,1,0:T(8,128)S(1)}, u32[]{:S(2)}, u32[]{:S(2)}) collective-permute-start(f32[2,120,128]{2,1,0:T(8,128)S(1)} %get-tuple-element.52), channel_id=1, source_target_pairs={{0,16},{8,24},{16,0},{24,8},{1,17},{9,25},{17,1},{25,9},{2,18},{10... | collective-permute-start | bytes 368648 | tf_op jit(solution)/shard_map/ppermute | solution.py:538
  24.5 0.2 collective-permute-done.5.theirs_ref
  24.7 0.3 sort_flux.1
  25.1 1.4 %collective-permute-start.6 = (f32[1,120,128]{2,1,0:T(8,128)S(1)}, f32[1,120,128]{2,1,0:T(8,128)S(1)}, u32[]{:S(2)}, u32[]{:S(2)}) collective-permute-start(f32[1,120,128]{2,1,0:T(8,128)S(1)} %get-tuple-element.48), channel_id=1, source_target_pairs={{0,8},{8,16},{16,24},{24,0},{1,9},{9,17},{17,25},{25,1},{2,10},{10... | collective-permute-start | bytes 184328 | tf_op jit(solution)/shard_map/ppermute | solution.py:538
  26.5 1.5 %collective-permute-start.7 = (f32[1,120,128]{2,1,0:T(8,128)S(1)}, f32[1,120,128]{2,1,0:T(8,128)S(1)}, u32[]{:S(2)}, u32[]{:S(2)}) collective-permute-start(f32[1,120,128]{2,1,0:T(8,128)S(1)} %get-tuple-element.49), channel_id=1, source_target_pairs={{0,16},{8,24},{16,0},{24,8},{1,17},{9,25},{17,1},{25,9},{2,18},{10... | collective-permute-start | bytes 184328 | tf_op jit(solution)/shard_map/ppermute | solution.py:538
  28.0 1.5 %collective-permute-start.8 = (f32[1,120,128]{2,1,0:T(8,128)S(1)}, f32[1,120,128]{2,1,0:T(8,128)S(1)}, u32[]{:S(2)}, u32[]{:S(2)}) collective-permute-start(f32[1,120,128]{2,1,0:T(8,128)S(1)} %get-tuple-element.50), channel_id=1, source_target_pairs={{0,24},{8,0},{16,8},{24,16},{1,25},{9,1},{17,9},{25,17},{2,26},{10... | collective-permute-start | bytes 184328 | tf_op jit(solution)/shard_map/ppermute | solution.py:538
  29.5 1.4 %recv_moves.1.table_ref = bf16[512,512]{1,0:T(8,128)(2,1)S(1)} custom-call(s32[3]{0:T(128)S(1)} %pad_add_fusion.place_ref, s32[1,1024]{1,0:T(1,128)S(1)} %bitcast.7), custom_call_target="tpu_custom_call" | custom-call | flops 1000000 | bytes 1000000 | tf_op jit(solution)/shard_map/recv_moves/pallas_call | solution.py:365
  30.9 4.6 %collective-permute-done.9.refs_2_ = f32[2,120,128]{2,1,0:T(8,128)S(1)} collective-permute-done((f32[2,120,128]{2,1,0:T(8,128)S(1)}, f32[2,120,128]{2,1,0:T(8,128)S(1)}, u32[]{:S(2)}, u32[]{:S(2)}) %collective-permute-start.9) | collective-permute-done | bytes 122912 | tf_op jit(solution)/shard_map/ppermute | solution.py:538
  35.5 1.9 %end_weights.1 = (f32[240,256]{1,0:T(8,128)}, f32[3,240,256]{2,1,0:T(8,128)}) custom-call(s32[3]{0:T(128)S(1)} %pad_add_fusion.place_ref, bf16[512,512]{1,0:T(8,128)(2,1)S(1)} %recv_moves.1.table_ref, f32[2,120,128]{2,1,0:T(8,128)S(1)} %get-tuple-element.51.refs_0_, f32[2,120,128]{2,1,0:T(8,128)S(1)} %collective-permute-done.3.refs_1_, ...), custom_call_target="tpu_custom_call" | custom-call | flops 251658240 | bytes 1474560 | tf_op jit(solution)/shard_map/end_weights/pallas_call | solution.py:572
  37.5 1.0 %end_flux.1 = f32[240,256]{1,0:T(8,128)} custom-call(bf16[512,512]{1,0:T(8,128)(2,1)S(1)} %recv_moves.1.table_ref, f32[1,120,128]{2,1,0:T(8,128)S(1)} %get-tuple-element.47.refs_0_, f32[1,120,128]{2,1,0:T(8,128)S(1)} %collective-permute-done.6.refs_1_, f32[1,120,128]{2,1,0:T(8,128)S(1)} %collective-permute-done.7.refs_2_, ...), custom_call_target="tpu_custom_call" | custom-call | flops 125829120 | bytes 491520 | tf_op jit(solution)/shard_map/end_flux/pallas_call | solution.py:594
  (9 shorter events, 0.0 us)
Async XLA Ops:
  3.9 9.5 %collective-permute-start.2 = (f32[2,240,256]{2,1,0:T(8,128)S(1)}, f32[2,240,256]{2,1,0:T(8,128)S(1)}, u32[]{:S(2)}, u32[]{:S(2)}) collective-permute-start(f32[2,240,256]{2,1,0:T(8,128)S(1)} %get-tuple-element.31), channel_id=1, source_target_pairs={{0,1},{1,0},{2,3},{3,2},{4,5},{5,4},{6,7},{7,6},{8,9},{9,8},{10,11... | collective-permute-start | bytes 1474568 | tf_op jit(solution)/shard_map/ppermute | solution.py:628
  4.4 9.5 %collective-permute-start = (f32[2,8,128]{2,1,0:T(8,128)S(1)}, f32[2,8,128]{2,1,0:T(8,128)S(1)}, u32[]{:S(2)}, u32[]{:S(2)}) collective-permute-start(f32[2,8,128]{2,1,0:T(8,128)S(1)} %get-tuple-element.29), channel_id=1, source_target_pairs={{0,2},{2,4},{4,6},{1,3},{3,5},{5,7},{8,10},{10,12},{12,14},{9,11},... | collective-permute-start | bytes 24584 | tf_op jit(solution)/shard_map/ppermute | solution.py:630
  8.8 9.4 %copy-start.1 = (f32[256]{0:T(256)S(1)}, f32[256]{0:T(256)}, u32[]{:S(2)}) copy-start(f32[256]{0:T(256)} %param.10) | copy-start | bytes 3076
  8.8 5.5 %collective-permute-start.1 = (f32[2,8,128]{2,1,0:T(8,128)S(1)}, f32[2,8,128]{2,1,0:T(8,128)S(1)}, u32[]{:S(2)}, u32[]{:S(2)}) collective-permute-start(f32[2,8,128]{2,1,0:T(8,128)S(1)} %get-tuple-element.30), channel_id=1, source_target_pairs={{2,0},{4,2},{6,4},{3,1},{5,3},{7,5},{10,8},{12,10},{14,12},{11,9},... | collective-permute-start | bytes 24584 | tf_op jit(solution)/shard_map/ppermute | solution.py:631
  14.4 8.0 %collective-permute-start.3 = (f32[2,120,128]{2,1,0:T(8,128)S(1)}, f32[2,120,128]{2,1,0:T(8,128)S(1)}, u32[]{:S(2)}, u32[]{:S(2)}) collective-permute-start(f32[2,120,128]{2,1,0:T(8,128)S(1)} %get-tuple-element.42), channel_id=1, source_target_pairs={{0,8},{8,16},{16,24},{24,0},{1,9},{9,17},{17,25},{25,1},{2,10},{10... | collective-permute-start | bytes 368648 | tf_op jit(solution)/shard_map/ppermute | solution.py:538
  15.9 7.3 %collective-permute-start.4 = (f32[2,120,128]{2,1,0:T(8,128)S(1)}, f32[2,120,128]{2,1,0:T(8,128)S(1)}, u32[]{:S(2)}, u32[]{:S(2)}) collective-permute-start(f32[2,120,128]{2,1,0:T(8,128)S(1)} %get-tuple-element.43), channel_id=1, source_target_pairs={{0,24},{8,0},{16,8},{24,16},{1,25},{9,1},{17,9},{25,17},{2,26},{10... | collective-permute-start | bytes 368648 | tf_op jit(solution)/shard_map/ppermute | solution.py:538
  18.2 11.3 %copy-start = (s32[1024]{0:T(1024)S(1)}, s32[1024]{0:T(1024)}, u32[]{:S(2)}) copy-start(s32[1024]{0:T(1024)} %param.13) | copy-start | bytes 12292
  23.2 1.5 %collective-permute-start.5 = (f32[1,240,256]{2,1,0:T(8,128)S(1)}, f32[1,240,256]{2,1,0:T(8,128)S(1)}, u32[]{:S(2)}, u32[]{:S(2)}) collective-permute-start(f32[1,240,256]{2,1,0:T(8,128)S(1)} %get-tuple-element.44), channel_id=1, source_target_pairs={{0,1},{1,0},{2,3},{3,2},{4,5},{5,4},{6,7},{7,6},{8,9},{9,8},{10,11... | collective-permute-start | bytes 737288 | tf_op jit(solution)/shard_map/ppermute | solution.py:644
  23.2 12.3 %collective-permute-start.9 = (f32[2,120,128]{2,1,0:T(8,128)S(1)}, f32[2,120,128]{2,1,0:T(8,128)S(1)}, u32[]{:S(2)}, u32[]{:S(2)}) collective-permute-start(f32[2,120,128]{2,1,0:T(8,128)S(1)} %get-tuple-element.52), channel_id=1, source_target_pairs={{0,16},{8,24},{16,0},{24,8},{1,17},{9,25},{17,1},{25,9},{2,18},{10... | collective-permute-start | bytes 368648 | tf_op jit(solution)/shard_map/ppermute | solution.py:538
  25.1 12.4 %collective-permute-start.6 = (f32[1,120,128]{2,1,0:T(8,128)S(1)}, f32[1,120,128]{2,1,0:T(8,128)S(1)}, u32[]{:S(2)}, u32[]{:S(2)}) collective-permute-start(f32[1,120,128]{2,1,0:T(8,128)S(1)} %get-tuple-element.48), channel_id=1, source_target_pairs={{0,8},{8,16},{16,24},{24,0},{1,9},{9,17},{17,25},{25,1},{2,10},{10... | collective-permute-start | bytes 184328 | tf_op jit(solution)/shard_map/ppermute | solution.py:538
  26.5 10.9 %collective-permute-start.7 = (f32[1,120,128]{2,1,0:T(8,128)S(1)}, f32[1,120,128]{2,1,0:T(8,128)S(1)}, u32[]{:S(2)}, u32[]{:S(2)}) collective-permute-start(f32[1,120,128]{2,1,0:T(8,128)S(1)} %get-tuple-element.49), channel_id=1, source_target_pairs={{0,16},{8,24},{16,0},{24,8},{1,17},{9,25},{17,1},{25,9},{2,18},{10... | collective-permute-start | bytes 184328 | tf_op jit(solution)/shard_map/ppermute | solution.py:538
  28.0 9.4 %collective-permute-start.8 = (f32[1,120,128]{2,1,0:T(8,128)S(1)}, f32[1,120,128]{2,1,0:T(8,128)S(1)}, u32[]{:S(2)}, u32[]{:S(2)}) collective-permute-start(f32[1,120,128]{2,1,0:T(8,128)S(1)} %get-tuple-element.50), channel_id=1, source_target_pairs={{0,24},{8,0},{16,8},{24,16},{1,25},{9,1},{17,9},{25,17},{2,26},{10... | collective-permute-start | bytes 184328 | tf_op jit(solution)/shard_map/ppermute | solution.py:538

commit v4 on v3

--- a/solution.py
+++ b/solution.py
@@ -229,49 +229,25 @@
     ]
 
 
-def first_kernel(
-    moves, wav_count, place_ref, slots_ref, coupling_ref, counts_ref, good_ref, pixels_ref, ivar_ref, bits_ref,
-    sums_ref, weight_ref, table_ref, up_ref, down_ref,
-    slots_v, coupling_v, counts_v, good_v, ivar_v, bits_v, ivar_s, pixel_s, sems,
+def sent_kernel(
+    moves, wav_count, place_ref, slots_ref, coupling_ref, counts_ref, good_ref, ivar_ref, bits_ref,
+    sums_ref, weight_ref, table_ref, slots_v, coupling_v, counts_v, good_v, ivar_v, bits_v, sems,
 ):
-    expos, width, fibres = ivar_ref.shape
-    streams = expos * fibres // LANES
-    count = -(-HALO // ROWS) * ROWS
-    pitch = odd(2 * count)
     which = 1 - place_ref[2]
     pairs = [(slots_ref, slots_v), (coupling_ref, coupling_v), (counts_ref, counts_v), (good_ref, good_v)]
-    for source, target in ((ivar_ref, ivar_s), (pixels_ref, pixel_s)):
-        pairs += stream_copies(source, target, 0, count, pitch, 0)
-        pairs += stream_copies(source, target, width - count, count, pitch, count)
     pairs += half_copies(which, ivar_ref, bits_ref, ivar_v, bits_v)
     waits = in_flight(pairs, sems)
     waits[0].wait()
     write_send_table(*moves, place_ref[0], slots_v, table_ref)
     for wait in waits[1:]:
         wait.wait()
-
-    back = 1.0 / stream_coupling(coupling_v, expos)
-    zero = jnp.zeros((streams, LANES), F32)
-    states = [(zero, zero + 1.0, zero), (zero, zero + 1.0, zero)]
-
-    def eliminate(tile, tiles):
-        for i in range(HALO * tile // tiles, HALO * (tile + 1) // tiles):
-            for side, row in enumerate((2 * count - HALO + i, HALO - 1 - i)):
-                at = pl.ds(row, streams, stride=pitch)
-                states[side] = advance(states[side], ivar_s[at, :], pixel_s[at, :], back)
-                if i % 24 == 23:
-                    states[side] = rescaled(states[side])
-
     write_weights(
-        place_ref, wav_count, which, coupling_v, counts_v, good_v, ivar_v, bits_v, sums_ref, weight_ref, eliminate
-    )
-    for (n, d, b), out_ref in zip(states, (up_ref, down_ref)):
-        scale = 1.0 / (d + n * back)
-        out_ref[0] = n * scale
-        out_ref[1] = b * scale
-
-
-def weights_scratch(slots, coupling, counts, good, ivar):
+        place_ref, wav_count, which, coupling_v, counts_v, good_v, ivar_v, bits_v, sums_ref, weight_ref,
+        lambda tile, tiles: None,
+    )
+
+
+def weights_scratch(coupling, counts, good, ivar):
     expos, width, fibres = ivar.shape
     half = width // 2
     return [
@@ -283,77 +259,113 @@
     ]
 
 
-def sent_weights(moves, wav_count, place, slots, coupling, counts, good, pixels, ivar, bits):
+def sent_weights(moves, wav_count, place, slots, coupling, counts, good, ivar, bits):
     expos, width, fibres = ivar.shape
     half = width // 2
-    streams = expos * fibres // LANES
     fib_count, pack, per, _ = moves
-    count = -(-HALO // ROWS) * ROWS
-    edge = shaped((2, streams, LANES))
-    return pl.pallas_call(
-        functools.partial(first_kernel, moves, wav_count),
-        in_specs=[in_smem] + [in_hbm] * 7,
-        out_specs=[in_vmem] * 5,
+    return pl.pallas_call(
+        functools.partial(sent_kernel, moves, wav_count),
+        in_specs=[in_smem] + [in_hbm] * 6,
+        out_specs=[in_vmem] * 3,
         out_shape=[
             shaped((2, half, fibres)),
             shaped((expos, half, fibres)),
             shaped((fib_count * pack * per, pack * fibres), BF16),
-            edge,
-            edge,
         ],
         scratch_shapes=[
             pltpu.VMEM(slots.shape, jnp.int32),
-            *weights_scratch(slots, coupling, counts, good, ivar),
-            pltpu.VMEM((streams * odd(2 * count), LANES), F32),
-            pltpu.VMEM((streams * odd(2 * count), LANES), F32),
-            pltpu.SemaphoreType.DMA((6 + 4 * streams,)),
+            *weights_scratch(coupling, counts, good, ivar),
+            pltpu.SemaphoreType.DMA((6,)),
         ],
         compiler_params=params(),
         cost_estimate=cost(20 * ivar.size, 6 * ivar.size),
         name="sent_weights",
-    )(place, *held_in_hbm(slots, coupling, counts, good, pixels, ivar, bits))
-
-
-def second_kernel(
+    )(place, *held_in_hbm(slots, coupling, counts, good, ivar, bits))
+
+
+def kept_kernel(
     wav_count, place_ref, coupling_ref, counts_ref, good_ref, pixels_ref, ivar_ref, bits_ref,
-    sums_ref, weight_ref, pixel_out, ivar_out, coupling_v, counts_v, good_v, ivar_v, bits_v, sems,
+    sums_ref, weight_ref, up_ref, down_ref, coupling_v, counts_v, good_v, ivar_v, bits_v, ivar_s, pixel_s, sems,
 ):
-    width = ivar_ref.shape[1]
+    expos, width, fibres = ivar_ref.shape
+    streams = expos * fibres // LANES
+    count = -(-HALO // ROWS) * ROWS
+    pitch = odd(2 * count)
     which = place_ref[2]
     pairs = [(coupling_ref, coupling_v), (counts_ref, counts_v), (good_ref, good_v)]
     pairs += half_copies(which, ivar_ref, bits_ref, ivar_v, bits_v)
-    waits = in_flight(pairs, sems)
-    laid = stream_copies(ivar_ref, ivar_out, 0, width, odd(width), 0)
-    laid += stream_copies(pixels_ref, pixel_out, 0, width, odd(width), 0)
-    rest = in_flight(laid, sems, len(waits))
-    for wait in waits:
+    for source, target in ((ivar_ref, ivar_s), (pixels_ref, pixel_s)):
+        pairs += stream_copies(source, target, 0, count, pitch, 0)
+        pairs += stream_copies(source, target, width - count, count, pitch, count)
+    for wait in in_flight(pairs, sems):
         wait.wait()
+
+    back = 1.0 / stream_coupling(coupling_v, expos)
+    zero = jnp.zeros((streams, LANES), F32)
+    states = [(zero, zero + 1.0, zero), (zero, zero + 1.0, zero)]
+
+    def eliminate(tile, tiles):
+        for i in range(HALO * tile // tiles, HALO * (tile + 1) // tiles):
+            for side, row in enumerate((2 * count - HALO + i, HALO - 1 - i)):
+                at = pl.ds(row, streams, stride=pitch)
+                states[side] = advance(states[side], ivar_s[at, :], pixel_s[at, :], back)
+                if i % 24 == 23:
+                    states[side] = rescaled(states[side])
+
     write_weights(
-        place_ref, wav_count, which, coupling_v, counts_v, good_v, ivar_v, bits_v, sums_ref, weight_ref,
-        lambda tile, tiles: None,
-    )
-    for wait in rest:
-        wait.wait()
+        place_ref, wav_count, which, coupling_v, counts_v, good_v, ivar_v, bits_v, sums_ref, weight_ref, eliminate
+    )
+    for (n, d, b), out_ref in zip(states, (up_ref, down_ref)):
+        scale = 1.0 / (d + n * back)
+        out_ref[0] = n * scale
+        out_ref[1] = b * scale
 
 
 def kept_weights(wav_count, place, coupling, counts, good, pixels, ivar, bits):
     expos, width, fibres = ivar.shape
     half = width // 2
     streams = expos * fibres // LANES
-    laid = shaped((streams * odd(width), LANES))
-    return pl.pallas_call(
-        functools.partial(second_kernel, wav_count),
+    count = -(-HALO // ROWS) * ROWS
+    edge = shaped((2, streams, LANES))
+    return pl.pallas_call(
+        functools.partial(kept_kernel, wav_count),
         in_specs=[in_smem] + [in_hbm] * 6,
         out_specs=[in_vmem] * 4,
-        out_shape=[shaped((2, half, fibres)), shaped((expos, half, fibres)), laid, laid],
+        out_shape=[shaped((2, half, fibres)), shaped((expos, half, fibres)), edge, edge],
         scratch_shapes=[
-            *weights_scratch(None, coupling, counts, good, ivar),
-            pltpu.SemaphoreType.DMA((5 + 2 * streams,)),
+            *weights_scratch(coupling, counts, good, ivar),
+            pltpu.VMEM((streams * odd(2 * count), LANES), F32),
+            pltpu.VMEM((streams * odd(2 * count), LANES), F32),
+            pltpu.SemaphoreType.DMA((5 + 4 * streams,)),
         ],
         compiler_params=params(),
         cost_estimate=cost(20 * ivar.size, 6 * ivar.size),
         name="kept_weights",
     )(place, *held_in_hbm(coupling, counts, good, pixels, ivar, bits))
+
+
+def layout_kernel(place_ref, pixels_ref, ivar_ref, pixel_out, ivar_out, sems):
+    width = ivar_ref.shape[1]
+    pairs = stream_copies(ivar_ref, ivar_out, 0, width, odd(width), 0)
+    pairs += stream_copies(pixels_ref, pixel_out, 0, width, odd(width), 0)
+    for wait in in_flight(pairs, sems):
+        wait.wait()
+
+
+def stream_layout(place, pixels, ivar):
+    expos, width, fibres = ivar.shape
+    streams = expos * fibres // LANES
+    laid = shaped((streams * odd(width), LANES))
+    return pl.pallas_call(
+        layout_kernel,
+        in_specs=[in_smem] + [in_hbm] * 2,
+        out_specs=[in_vmem] * 2,
+        out_shape=[laid, laid],
+        scratch_shapes=[pltpu.SemaphoreType.DMA((2 * streams,))],
+        compiler_params=params(),
+        cost_estimate=cost(0, 16 * ivar.size),
+        name="stream_layout",
+    )(place, *held_in_hbm(pixels, ivar))
 
 
 def recv_kernel(moves, place_ref, slots_ref, table_ref):
@@ -622,25 +634,25 @@
     swap = [(0, 1), (1, 0)]
     moves = (fib_count, pack, per, rel)
 
-    theirs, weight_t, send_table, up, down = sent_weights(
-        moves, wav_count, place, slots, coupling, counts, good_flags, pixels, pixel_ivar, clip_bits
+    theirs, weight_t, send_table = sent_weights(
+        moves, wav_count, place, slots, coupling, counts, good_flags, pixel_ivar, clip_bits
     )
     arriving = lax.ppermute(theirs, "exp", swap)
+    mine, weight_m, up, down = kept_weights(
+        wav_count, after(place, theirs), coupling, counts, good_flags, pixels, pixel_ivar, clip_bits
+    )
+    *sorted_pieces, scale = sort_fibres(arriving, mine, send_table, pack, pieces)
+    weight_pieces = exchange(sorted_pieces, fib_count)
+
+    up, down = after((up, down), scale)
     upward = [(i, i + 1) for i in range(wav_count - 1)]
     left = lax.ppermute(up, "wav", upward)
     right = lax.ppermute(down, "wav", [(j, i) for i, j in upward])
-    mine, weight_m, pixel_s, ivar_s = kept_weights(
-        wav_count, after(place, theirs), coupling, counts, good_flags, pixels, pixel_ivar, clip_bits
-    )
-    *sorted_pieces, scale = sort_fibres(arriving, mine, send_table, pack, pieces)
-    if rel:
-        sorted_pieces[1] = after(sorted_pieces[1], (left, right))
-    weight_pieces = exchange(sorted_pieces, fib_count)
-
+    pixel_s, ivar_s = stream_layout(after(place, scale), pixels, pixel_ivar)
     theirs, mine = flux_sums(place, coupling, left, right, pixel_s, ivar_s, weight_t, weight_m)
     recv_table = recv_moves(moves, after(place, theirs), slots, fibres)
     if rel:
-        theirs = after(theirs, (weight_pieces[1], weight_pieces[-1]))
+        theirs = after(theirs, (weight_pieces[1], weight_pieces[2]))
     theirs = lax.ppermute(theirs, "exp", swap)
     flux_pieces = exchange(sort_fibres(theirs, mine, send_table, pack, pieces, scale), fib_count)
 

time: 39 us -> 35.6 us (0.913)
  waiting for transfers between devices: 7.78 us -> 2.85 us
  Pallas kernels: 14.2 us -> 15.8 us
    ppermute x6, waiting for transfers between devices: 7.07 us -> 1.4 us  [exchange(): lax.ppermute(pieces[d], 'fib', [(i, (i + d) % fib_count) for i in range(f...]
    pallas_call x2 -> x3, Pallas kernels: 6.38 us -> 8.04 us  [the longest x1 2.88 us: stream_layout(): pl.pallas_call(layout_kernel, in_specs=[in_smem] + [in_hbm] * 2, out_spec...]
    ppermute x6, starting transfers between devices: 9.53 us -> 10.5 us  [exchange(): lax.ppermute(pieces[d], 'fib', [(i, (i + d) % fib_count) for i in range(f...]
    ppermute x1, starting transfers between devices: 4.4 us -> 3.52 us  [per_device(): left = lax.ppermute(up, 'wav', upward)]
    ppermute x1, waiting for transfers between devices: 0.5 us -> 1.35 us  [per_device(): right = lax.ppermute(down, 'wav', [(j, i) for i, j in upward])]
  transfers between devices with their start and end apart: 10 -> 10, of which waited for: 5 -> 3; matrix products, arithmetic and copies ran while one was open for 0% -> 0% of each run, Pallas kernels for 26% -> 34%
where the time goes in v4:
time: 35.6 us; the launch traced here: 35.4 us
  starting transfers between devices  15.9 us (45%)
  Pallas kernels  15.8 us (44%)
  waiting for transfers between devices  2.85 us (8%)
  between operations  0.76 us (2%)
    ppermute x6, starting transfers between devices, exchange(): lax.ppermute(pieces[d], 'fib', [(i, (i + d) % fib_count) for i in range(f...  10.5 us
    ppermute x1, starting transfers between devices, per_device(): left = lax.ppermute(up, 'wav', upward)  3.52 us
    pallas_call x1, Pallas kernels, stream_layout(): pl.pallas_call(layout_kernel, in_specs=[in_smem] + [in_hbm] * 2, out_spec...  2.88 us
    pallas_call x1, Pallas kernels, kept_weights(): pl.pallas_call(functools.partial(kept_kernel, wav_count), in_specs=[in_sm...  2.85 us
    pallas_call x1, Pallas kernels, flux_sums(): pl.pallas_call(solve_kernel, in_specs=[in_smem] + [in_vmem] * 7, out_spec...  2.6 us
    pallas_call x1, Pallas kernels, sent_weights(): pl.pallas_call(functools.partial(sent_kernel, moves, wav_count), in_specs...  2.31 us
    pallas_call x1, Pallas kernels, end_weights(): pl.pallas_call(functools.partial(weights_end_kernel, pack, total), in_spe...  1.92 us
    pallas_call x1, Pallas kernels, recv_moves(): pl.pallas_call(functools.partial(recv_kernel, moves), in_specs=[in_smem,...  1.4 us
  transfers between devices with their start and end apart: 10, of which 3 were waited for; matrix products, arithmetic and copies ran while one was open for 0% of the time, Pallas kernels for 34%

profile of v4, /device:TPU:0, one launch (start us, length us, event | category | flops | bytes accessed | tf_op | source)
XLA Modules:
  0.0 35.4 jit_solution(18101012282901321253)
XLA Ops:
  0.6 0.1 pad_add_fusion.place_ref
  0.7 2.3 %sent_weights.1 = (f32[2,240,256]{2,1,0:T(8,128)S(1)}, f32[4,240,256]{2,1,0:T(8,128)S(1)}, bf16[512,512]{1,0:T(8,128)(2,1)S(1)}) custom-call(s32[3]{0:T(128)S(1)} %pad_add_fusion.place_ref, s32[1,1024]{1,0:T(1,128)} %bitcast.6, f32[1,256]{1,0:T(1,128)} %bitcast.8, s32[1,256]{1,0:T(1,128)} %bitcast.11, s32[4,256]{1,0:T(4,128)} %good_ref.3, ...), custom_call_target="tpu_custom_call" | custom-call | flops 9830400 | bytes 2949120 | tf_op jit(solution)/shard_map/sent_weights/pallas_call | solution.py:266
  3.0 0.5 %collective-permute-start = (f32[2,240,256]{2,1,0:T(8,128)S(1)}, f32[2,240,256]{2,1,0:T(8,128)S(1)}, u32[]{:S(2)}, u32[]{:S(2)}) collective-permute-start(f32[2,240,256]{2,1,0:T(8,128)S(1)} %get-tuple-element.31), channel_id=1, source_target_pairs={{0,1},{1,0},{2,3},{3,2},{4,5},{5,4},{6,7},{7,6},{8,9},{9,8},{10,11... | collective-permute-start | bytes 1474568 | tf_op jit(solution)/shard_map/ppermute | solution.py:640
  3.5 2.8 %kept_weights.1 = (f32[2,240,256]{2,1,0:T(8,128)S(1)}, f32[4,240,256]{2,1,0:T(8,128)S(1)}, f32[2,8,128]{2,1,0:T(8,128)S(1)}, f32[2,8,128]{2,1,0:T(8,128)S(1)}) custom-call(s32[3]{0:T(128)S(1)} %pad_add_fusion.place_ref, f32[1,256]{1,0:T(1,128)} %bitcast.9, s32[1,256]{1,0:T(1,128)} %bitcast.12, s32[4,256]{1,0:T(4,128)} %good_ref.3, ...), custom_call_target="tpu_custom_call" | custom-call | flops 9830400 | bytes 2949120 | tf_op jit(solution)/shard_map/kept_weights/pallas_call | solution.py:330
  6.4 0.0 collective-permute-done.theirs_ref
  6.4 0.5 %sort_weights.1 = (f32[2,120,128]{2,1,0:T(8,128)S(1)}, f32[2,120,128]{2,1,0:T(8,128)S(1)}, f32[2,120,128]{2,1,0:T(8,128)S(1)}, f32[2,120,128]{2,1,0:T(8,128)S(1)}, f32[240,256]{1,0:T(8,128)S(1)}) custom-call(f32[2,240,256]{2,1,0:T(8,128)S(1)} %collective-permute-done.theirs_ref, f32[2,240,256]{2,1,0:T(8,128)S(1)} %get-tuple-element.35.mine_ref, ...), custom_call_target="tpu_custom_call" | custom-call | tf_op jit(solution)/shard_map/sort_weights/pallas_call | solution.py:534
  6.9 2.6 %collective-permute-start.3 = (f32[2,120,128]{2,1,0:T(8,128)S(1)}, f32[2,120,128]{2,1,0:T(8,128)S(1)}, u32[]{:S(2)}, u32[]{:S(2)}) collective-permute-start(f32[2,120,128]{2,1,0:T(8,128)S(1)} %get-tuple-element.47), channel_id=1, source_target_pairs={{0,8},{8,16},{16,24},{24,0},{1,9},{9,17},{17,25},{25,1},{2,10},{10... | collective-permute-start | bytes 368648 | tf_op jit(solution)/shard_map/ppermute | solution.py:550
  9.5 2.6 %collective-permute-start.4 = (f32[2,120,128]{2,1,0:T(8,128)S(1)}, f32[2,120,128]{2,1,0:T(8,128)S(1)}, u32[]{:S(2)}, u32[]{:S(2)}) collective-permute-start(f32[2,120,128]{2,1,0:T(8,128)S(1)} %get-tuple-element.48), channel_id=1, source_target_pairs={{0,16},{8,24},{16,0},{24,8},{1,17},{9,25},{17,1},{25,9},{2,18},{10... | collective-permute-start | bytes 368648 | tf_op jit(solution)/shard_map/ppermute | solution.py:550
  12.1 3.5 %collective-permute-start.1 = (f32[2,8,128]{2,1,0:T(8,128)S(1)}, f32[2,8,128]{2,1,0:T(8,128)S(1)}, u32[]{:S(2)}, u32[]{:S(2)}) collective-permute-start(f32[2,8,128]{2,1,0:T(8,128)S(1)} %get-tuple-element.38), channel_id=1, source_target_pairs={{0,2},{2,4},{4,6},{1,3},{3,5},{5,7},{8,10},{10,12},{12,14},{9,11},... | collective-permute-start | bytes 24584 | tf_op jit(solution)/shard_map/ppermute | solution.py:649
  15.7 1.3 %collective-permute-start.2 = (f32[2,8,128]{2,1,0:T(8,128)S(1)}, f32[2,8,128]{2,1,0:T(8,128)S(1)}, u32[]{:S(2)}, u32[]{:S(2)}) collective-permute-start(f32[2,8,128]{2,1,0:T(8,128)S(1)} %get-tuple-element.39), channel_id=1, source_target_pairs={{2,0},{4,2},{6,4},{3,1},{5,3},{7,5},{10,8},{12,10},{14,12},{11,9},... | collective-permute-start | bytes 24584 | tf_op jit(solution)/shard_map/ppermute | solution.py:650
  17.0 2.9 %stream_layout.1 = (f32[3848,128]{1,0:T(8,128)S(1)}, f32[3848,128]{1,0:T(8,128)S(1)}) custom-call(s32[3]{0:T(128)S(1)} %pad_add_fusion.place_ref, f32[4,480,256]{2,1,0:T(8,128)} %pixels_ref.3, f32[4,480,256]{2,1,0:T(8,128)} %ivar_ref.5), custom_call_target="tpu_custom_call" | custom-call | bytes 7864320 | tf_op jit(solution)/shard_map/stream_layout/pallas_call | solution.py:359
  19.9 1.3 %collective-permute-done.2.right_ref = f32[2,8,128]{2,1,0:T(8,128)S(1)} collective-permute-done((f32[2,8,128]{2,1,0:T(8,128)S(1)}, f32[2,8,128]{2,1,0:T(8,128)S(1)}, u32[]{:S(2)}, u32[]{:S(2)}) %collective-permute-start.2) | collective-permute-done | bytes 8224 | tf_op jit(solution)/shard_map/ppermute | solution.py:650
  21.2 2.6 %flux_sums.1 = (f32[1,240,256]{2,1,0:T(8,128)S(1)}, f32[1,240,256]{2,1,0:T(8,128)S(1)}) custom-call(s32[3]{0:T(128)S(1)} %pad_add_fusion.place_ref, f32[1,256]{1,0:T(1,128)S(1)} %bitcast.10, f32[2,8,128]{2,1,0:T(8,128)S(1)} %collective-permute-done.1.left_ref, f32[2,8,128]{2,1,0:T(8,128)S(1)} %collective-permute-done.2.right_ref, ...), custom_call_target="tpu_custom_call" | custom-call | tf_op jit(solution)/shard_map/flux_sums/pallas_call | solution.py:487
  23.8 0.1 collective-permute-start.5
  23.9 1.4 %collective-permute-start.9 = (f32[2,120,128]{2,1,0:T(8,128)S(1)}, f32[2,120,128]{2,1,0:T(8,128)S(1)}, u32[]{:S(2)}, u32[]{:S(2)}) collective-permute-start(f32[2,120,128]{2,1,0:T(8,128)S(1)} %get-tuple-element.56), channel_id=1, source_target_pairs={{0,24},{8,0},{16,8},{24,16},{1,25},{9,1},{17,9},{25,17},{2,26},{10... | collective-permute-start | bytes 368648 | tf_op jit(solution)/shard_map/ppermute | solution.py:550
  25.3 0.1 collective-permute-done.5.theirs_ref
  25.4 0.3 sort_flux.1
  25.8 0.6 %collective-permute-start.6 = (f32[1,120,128]{2,1,0:T(8,128)S(1)}, f32[1,120,128]{2,1,0:T(8,128)S(1)}, u32[]{:S(2)}, u32[]{:S(2)}) collective-permute-start(f32[1,120,128]{2,1,0:T(8,128)S(1)} %get-tuple-element.52), channel_id=1, source_target_pairs={{0,8},{8,16},{16,24},{24,0},{1,9},{9,17},{17,25},{25,1},{2,10},{10... | collective-permute-start | bytes 184328 | tf_op jit(solution)/shard_map/ppermute | solution.py:550
  26.4 1.3 %collective-permute-start.7 = (f32[1,120,128]{2,1,0:T(8,128)S(1)}, f32[1,120,128]{2,1,0:T(8,128)S(1)}, u32[]{:S(2)}, u32[]{:S(2)}) collective-permute-start(f32[1,120,128]{2,1,0:T(8,128)S(1)} %get-tuple-element.53), channel_id=1, source_target_pairs={{0,16},{8,24},{16,0},{24,8},{1,17},{9,25},{17,1},{25,9},{2,18},{10... | collective-permute-start | bytes 184328 | tf_op jit(solution)/shard_map/ppermute | solution.py:550
  27.7 1.9 %collective-permute-start.8 = (f32[1,120,128]{2,1,0:T(8,128)S(1)}, f32[1,120,128]{2,1,0:T(8,128)S(1)}, u32[]{:S(2)}, u32[]{:S(2)}) collective-permute-start(f32[1,120,128]{2,1,0:T(8,128)S(1)} %get-tuple-element.54), channel_id=1, source_target_pairs={{0,24},{8,0},{16,8},{24,16},{1,25},{9,1},{17,9},{25,17},{2,26},{10... | collective-permute-start | bytes 184328 | tf_op jit(solution)/shard_map/ppermute | solution.py:550
  29.6 1.4 %recv_moves.1.table_ref = bf16[512,512]{1,0:T(8,128)(2,1)S(1)} custom-call(s32[3]{0:T(128)S(1)} %pad_add_fusion.place_ref, s32[1,1024]{1,0:T(1,128)S(1)} %bitcast.7), custom_call_target="tpu_custom_call" | custom-call | flops 1000000 | bytes 1000000 | tf_op jit(solution)/shard_map/recv_moves/pallas_call | solution.py:377
  31.1 1.9 %end_weights.1 = (f32[240,256]{1,0:T(8,128)}, f32[3,240,256]{2,1,0:T(8,128)}) custom-call(s32[3]{0:T(128)S(1)} %pad_add_fusion.place_ref, bf16[512,512]{1,0:T(8,128)(2,1)S(1)} %recv_moves.1.table_ref, f32[2,120,128]{2,1,0:T(8,128)S(1)} %get-tuple-element.55.refs_0_, f32[2,120,128]{2,1,0:T(8,128)S(1)} %collective-permute-done.3.refs_1_, ...), custom_call_target="tpu_custom_call" | custom-call | flops 251658240 | bytes 1474560 | tf_op jit(solution)/shard_map/end_weights/pallas_call | solution.py:584
  33.0 1.4 %collective-permute-done.7.refs_2_ = f32[1,120,128]{2,1,0:T(8,128)S(1)} collective-permute-done((f32[1,120,128]{2,1,0:T(8,128)S(1)}, f32[1,120,128]{2,1,0:T(8,128)S(1)}, u32[]{:S(2)}, u32[]{:S(2)}) %collective-permute-start.7) | collective-permute-done | bytes 61472 | tf_op jit(solution)/shard_map/ppermute | solution.py:550
  34.4 1.0 %end_flux.1 = f32[240,256]{1,0:T(8,128)} custom-call(bf16[512,512]{1,0:T(8,128)(2,1)S(1)} %recv_moves.1.table_ref, f32[1,120,128]{2,1,0:T(8,128)S(1)} %get-tuple-element.51.refs_0_, f32[1,120,128]{2,1,0:T(8,128)S(1)} %collective-permute-done.6.refs_1_, f32[1,120,128]{2,1,0:T(8,128)S(1)} %collective-permute-done.7.refs_2_, ...), custom_call_target="tpu_custom_call" | custom-call | flops 125829120 | bytes 491520 | tf_op jit(solution)/shard_map/end_flux/pallas_call | solution.py:606
  (10 shorter events, 0.0 us)
Async XLA Ops:
  3.0 3.4 %collective-permute-start = (f32[2,240,256]{2,1,0:T(8,128)S(1)}, f32[2,240,256]{2,1,0:T(8,128)S(1)}, u32[]{:S(2)}, u32[]{:S(2)}) collective-permute-start(f32[2,240,256]{2,1,0:T(8,128)S(1)} %get-tuple-element.31), channel_id=1, source_target_pairs={{0,1},{1,0},{2,3},{3,2},{4,5},{5,4},{6,7},{7,6},{8,9},{9,8},{10,11... | collective-permute-start | bytes 1474568 | tf_op jit(solution)/shard_map/ppermute | solution.py:640
  6.9 16.9 %collective-permute-start.3 = (f32[2,120,128]{2,1,0:T(8,128)S(1)}, f32[2,120,128]{2,1,0:T(8,128)S(1)}, u32[]{:S(2)}, u32[]{:S(2)}) collective-permute-start(f32[2,120,128]{2,1,0:T(8,128)S(1)} %get-tuple-element.47), channel_id=1, source_target_pairs={{0,8},{8,16},{16,24},{24,0},{1,9},{9,17},{17,25},{25,1},{2,10},{10... | collective-permute-start | bytes 368648 | tf_op jit(solution)/shard_map/ppermute | solution.py:550
  9.5 14.3 %collective-permute-start.4 = (f32[2,120,128]{2,1,0:T(8,128)S(1)}, f32[2,120,128]{2,1,0:T(8,128)S(1)}, u32[]{:S(2)}, u32[]{:S(2)}) collective-permute-start(f32[2,120,128]{2,1,0:T(8,128)S(1)} %get-tuple-element.48), channel_id=1, source_target_pairs={{0,16},{8,24},{16,0},{24,8},{1,17},{9,25},{17,1},{25,9},{2,18},{10... | collective-permute-start | bytes 368648 | tf_op jit(solution)/shard_map/ppermute | solution.py:550
  12.1 9.1 %copy-start.1 = (f32[256]{0:T(256)S(1)}, f32[256]{0:T(256)}, u32[]{:S(2)}) copy-start(f32[256]{0:T(256)} %param.10) | copy-start | bytes 3076
  12.1 7.7 %collective-permute-start.1 = (f32[2,8,128]{2,1,0:T(8,128)S(1)}, f32[2,8,128]{2,1,0:T(8,128)S(1)}, u32[]{:S(2)}, u32[]{:S(2)}) collective-permute-start(f32[2,8,128]{2,1,0:T(8,128)S(1)} %get-tuple-element.38), channel_id=1, source_target_pairs={{0,2},{2,4},{4,6},{1,3},{3,5},{5,7},{8,10},{10,12},{12,14},{9,11},... | collective-permute-start | bytes 24584 | tf_op jit(solution)/shard_map/ppermute | solution.py:649
  15.7 5.5 %collective-permute-start.2 = (f32[2,8,128]{2,1,0:T(8,128)S(1)}, f32[2,8,128]{2,1,0:T(8,128)S(1)}, u32[]{:S(2)}, u32[]{:S(2)}) collective-permute-start(f32[2,8,128]{2,1,0:T(8,128)S(1)} %get-tuple-element.39), channel_id=1, source_target_pairs={{2,0},{4,2},{6,4},{3,1},{5,3},{7,5},{10,8},{12,10},{14,12},{11,9},... | collective-permute-start | bytes 24584 | tf_op jit(solution)/shard_map/ppermute | solution.py:650
  21.2 8.4 %copy-start = (s32[1024]{0:T(1024)S(1)}, s32[1024]{0:T(1024)}, u32[]{:S(2)}) copy-start(s32[1024]{0:T(1024)} %param.13) | copy-start | bytes 12292
  23.8 1.6 %collective-permute-start.5 = (f32[1,240,256]{2,1,0:T(8,128)S(1)}, f32[1,240,256]{2,1,0:T(8,128)S(1)}, u32[]{:S(2)}, u32[]{:S(2)}) collective-permute-start(f32[1,240,256]{2,1,0:T(8,128)S(1)} %get-tuple-element.49), channel_id=1, source_target_pairs={{0,1},{1,0},{2,3},{3,2},{4,5},{5,4},{6,7},{7,6},{8,9},{9,8},{10,11... | collective-permute-start | bytes 737288 | tf_op jit(solution)/shard_map/ppermute | solution.py:656
  23.9 7.1 %collective-permute-start.9 = (f32[2,120,128]{2,1,0:T(8,128)S(1)}, f32[2,120,128]{2,1,0:T(8,128)S(1)}, u32[]{:S(2)}, u32[]{:S(2)}) collective-permute-start(f32[2,120,128]{2,1,0:T(8,128)S(1)} %get-tuple-element.56), channel_id=1, source_target_pairs={{0,24},{8,0},{16,8},{24,16},{1,25},{9,1},{17,9},{25,17},{2,26},{10... | collective-permute-start | bytes 368648 | tf_op jit(solution)/shard_map/ppermute | solution.py:550
  25.8 7.2 %collective-permute-start.6 = (f32[1,120,128]{2,1,0:T(8,128)S(1)}, f32[1,120,128]{2,1,0:T(8,128)S(1)}, u32[]{:S(2)}, u32[]{:S(2)}) collective-permute-start(f32[1,120,128]{2,1,0:T(8,128)S(1)} %get-tuple-element.52), channel_id=1, source_target_pairs={{0,8},{8,16},{16,24},{24,0},{1,9},{9,17},{17,25},{25,1},{2,10},{10... | collective-permute-start | bytes 184328 | tf_op jit(solution)/shard_map/ppermute | solution.py:550
  26.4 8.0 %collective-permute-start.7 = (f32[1,120,128]{2,1,0:T(8,128)S(1)}, f32[1,120,128]{2,1,0:T(8,128)S(1)}, u32[]{:S(2)}, u32[]{:S(2)}) collective-permute-start(f32[1,120,128]{2,1,0:T(8,128)S(1)} %get-tuple-element.53), channel_id=1, source_target_pairs={{0,16},{8,24},{16,0},{24,8},{1,17},{9,25},{17,1},{25,9},{2,18},{10... | collective-permute-start | bytes 184328 | tf_op jit(solution)/shard_map/ppermute | solution.py:550
  27.7 6.7 %collective-permute-start.8 = (f32[1,120,128]{2,1,0:T(8,128)S(1)}, f32[1,120,128]{2,1,0:T(8,128)S(1)}, u32[]{:S(2)}, u32[]{:S(2)}) collective-permute-start(f32[1,120,128]{2,1,0:T(8,128)S(1)} %get-tuple-element.54), channel_id=1, source_target_pairs={{0,24},{8,0},{16,8},{24,16},{1,25},{9,1},{17,9},{25,17},{2,26},{10... | collective-permute-start | bytes 184328 | tf_op jit(solution)/shard_map/ppermute | solution.py:550

commit v5 on v4

--- a/solution.py
+++ b/solution.py
@@ -181,126 +181,127 @@
     return weights, weight_sum, band_sum * coupling
 
 
-def half_copies(which, ivar_ref, bits_ref, ivar_v, bits_v):
-    half = ivar_v.shape[1]
-    first = pl.multiple_of(which * half, ROWS)
-    first_word = pl.multiple_of(which * (half // BITS), ROWS)
-    return [
-        (bits_ref.at[:, pl.ds(first_word, half // BITS), :], bits_v),
-        (ivar_ref.at[:, pl.ds(first, half), :], ivar_v),
-    ]
-
-
-def write_weights(place_ref, wav_count, which, coupling_v, counts_v, good_v, ivar_v, bits_v, sums_ref, weight_ref, beside):
-    expos, half, _ = ivar_v.shape
+def write_weights(place_ref, wav_count, which, coupling_v, counts_v, good_v, ivar_of, words_of, sums_ref, weight_ref, beside):
+    expos, half, _ = weight_ref.shape
     coupling = coupling_v[...]
     usable = usable_rows(place_ref, counts_v, good_v)
     start = place_ref[1] * (2 * half) + which * half
     tiles = half // ROWS
     tiles_in_group = GROUP // ROWS
-    words_in_group = GROUP // BITS
     for tile in range(tiles):
+        beside(tile, tiles)
         group, within = divmod(tile, tiles_in_group)
         scale_row = 4.0
         if tile in (0, tiles - 1):
             row = start + ROWS * tile + lax.broadcasted_iota(jnp.int32, (ROWS, 1), 0)
             scale_row = jnp.where((row == 0) | (row == wav_count * 2 * half - 1), 2.0, 4.0)
         at = slice(ROWS * tile, ROWS * (tile + 1))
-        words = [bits_v[e, words_in_group * group : words_in_group * (group + 1), :] for e in range(expos)]
         weights, weight_sum, band_sum = weight_tile(
-            coupling, usable, words, [ivar_v[e, at, :] for e in range(expos)], within, scale_row
+            coupling,
+            usable,
+            [words_of(e, group) for e in range(expos)],
+            [ivar_of(e, tile) for e in range(expos)],
+            within,
+            scale_row,
         )
         for e in range(expos):
             weight_ref[e, at, :] = weights[e]
         sums_ref[0, at, :] = weight_sum
         sums_ref[1, at, :] = band_sum
-        beside(tile, tiles)
-
-
-def stream_copies(source_ref, target, first, length, pitch, offset):
-    expos, _, fibres = source_ref.shape
-    return [
-        (
-            source_ref.at[e, pl.ds(first, length), pl.ds(h * LANES, LANES)],
-            target.at[pl.ds((h * expos + e) * pitch + offset, length), :],
-        )
-        for h in range(fibres // LANES)
-        for e in range(expos)
-    ]
 
 
 def sent_kernel(
-    moves, wav_count, place_ref, slots_ref, coupling_ref, counts_ref, good_ref, ivar_ref, bits_ref,
-    sums_ref, weight_ref, table_ref, slots_v, coupling_v, counts_v, good_v, ivar_v, bits_v, sems,
+    moves, wav_count, place_ref, slots_ref, coupling_ref, counts_ref, good_ref, bits_ref, ivar_ref, pixels_ref,
+    sums_ref, weight_ref, table_ref, slots_v, coupling_v, counts_v, good_v, bits_v, ivar_v, pixels_v, sems,
 ):
+    expos, width, _ = ivar_ref.shape
+    half = width // 2
     which = 1 - place_ref[2]
-    pairs = [(slots_ref, slots_v), (coupling_ref, coupling_v), (counts_ref, counts_v), (good_ref, good_v)]
-    pairs += half_copies(which, ivar_ref, bits_ref, ivar_v, bits_v)
-    waits = in_flight(pairs, sems)
+    words = GROUP // BITS
+
+    def part(source, target, first):
+        at = pl.ds(pl.multiple_of(first, ROWS), GROUP)
+        return source.at[:, at, :], target.at[:, at, :]
+
+    waits = in_flight(
+        [
+            (slots_ref, slots_v),
+            (coupling_ref, coupling_v),
+            (counts_ref, counts_v),
+            (good_ref, good_v),
+            (bits_ref, bits_v),
+        ]
+        + [part(ivar_ref, ivar_v, which * half + g) for g in range(0, half, GROUP)]
+        + [part(ivar_ref, ivar_v, (1 - which) * half + g) for g in range(0, half, GROUP)]
+        + [(pixels_ref, pixels_v)],
+        sems,
+    )
     waits[0].wait()
     write_send_table(*moves, place_ref[0], slots_v, table_ref)
-    for wait in waits[1:]:
+    for wait in waits[1:5]:
         wait.wait()
+
+    def arrive(tile, tiles):
+        if ROWS * tile % GROUP == 0:
+            waits[5 + ROWS * tile // GROUP].wait()
+
     write_weights(
-        place_ref, wav_count, which, coupling_v, counts_v, good_v, ivar_v, bits_v, sums_ref, weight_ref,
-        lambda tile, tiles: None,
-    )
-
-
-def weights_scratch(coupling, counts, good, ivar):
-    expos, width, fibres = ivar.shape
-    half = width // 2
-    return [
-        pltpu.VMEM(coupling.shape, F32),
-        pltpu.VMEM(counts.shape, jnp.int32),
-        pltpu.VMEM(good.shape, jnp.int32),
-        pltpu.VMEM((expos, half, fibres), F32),
-        pltpu.VMEM((expos, half // BITS, fibres), jnp.int32),
-    ]
-
-
-def sent_weights(moves, wav_count, place, slots, coupling, counts, good, ivar, bits):
+        place_ref, wav_count, which, coupling_v, counts_v, good_v,
+        lambda e, tile: ivar_v[e, pl.ds(pl.multiple_of(which * half + ROWS * tile, ROWS), ROWS), :],
+        lambda e, group: bits_v[e, pl.ds(pl.multiple_of(which * (half // BITS) + words * group, words), words), :],
+        sums_ref, weight_ref, arrive,
+    )
+    for wait in waits[5 + half // GROUP :]:
+        wait.wait()
+
+
+def sent_weights(moves, wav_count, place, slots, coupling, counts, good, bits, ivar, pixels):
     expos, width, fibres = ivar.shape
     half = width // 2
     fib_count, pack, per, _ = moves
+    inputs = (slots, coupling, counts, good, bits, ivar, pixels)
     return pl.pallas_call(
         functools.partial(sent_kernel, moves, wav_count),
-        in_specs=[in_smem] + [in_hbm] * 6,
-        out_specs=[in_vmem] * 3,
+        in_specs=[in_smem] + [in_hbm] * 7,
+        out_specs=[in_vmem] * 10,
         out_shape=[
             shaped((2, half, fibres)),
             shaped((expos, half, fibres)),
             shaped((fib_count * pack * per, pack * fibres), BF16),
-        ],
-        scratch_shapes=[
-            pltpu.VMEM(slots.shape, jnp.int32),
-            *weights_scratch(coupling, counts, good, ivar),
-            pltpu.SemaphoreType.DMA((6,)),
-        ],
+        ]
+        + [shaped(x.shape, x.dtype) for x in inputs],
+        scratch_shapes=[pltpu.SemaphoreType.DMA((6 + width // GROUP,))],
         compiler_params=params(),
         cost_estimate=cost(20 * ivar.size, 6 * ivar.size),
         name="sent_weights",
-    )(place, *held_in_hbm(slots, coupling, counts, good, ivar, bits))
+    )(place, *held_in_hbm(*inputs))
+
+
+def lay_out(source_ref, target_ref, pieces, pitch):
+    expos, _, fibres = source_ref.shape
+    for h in range(fibres // LANES):
+        for e in range(expos):
+            for first, length, at in pieces:
+                target_ref[pl.ds((h * expos + e) * pitch + at, length), :] = source_ref[
+                    e, pl.ds(first, length), pl.ds(h * LANES, LANES)
+                ]
 
 
 def kept_kernel(
     wav_count, place_ref, coupling_ref, counts_ref, good_ref, pixels_ref, ivar_ref, bits_ref,
-    sums_ref, weight_ref, up_ref, down_ref, coupling_v, counts_v, good_v, ivar_v, bits_v, ivar_s, pixel_s, sems,
+    sums_ref, weight_ref, up_ref, down_ref, ivar_s, pixel_s,
 ):
     expos, width, fibres = ivar_ref.shape
+    half = width // 2
     streams = expos * fibres // LANES
     count = -(-HALO // ROWS) * ROWS
     pitch = odd(2 * count)
     which = place_ref[2]
-    pairs = [(coupling_ref, coupling_v), (counts_ref, counts_v), (good_ref, good_v)]
-    pairs += half_copies(which, ivar_ref, bits_ref, ivar_v, bits_v)
-    for source, target in ((ivar_ref, ivar_s), (pixels_ref, pixel_s)):
-        pairs += stream_copies(source, target, 0, count, pitch, 0)
-        pairs += stream_copies(source, target, width - count, count, pitch, count)
-    for wait in in_flight(pairs, sems):
-        wait.wait()
-
-    back = 1.0 / stream_coupling(coupling_v, expos)
+    words = GROUP // BITS
+    edges = [(0, count, 0), (width - count, count, count)]
+    lay_out(ivar_ref, ivar_s, edges, pitch)
+    lay_out(pixels_ref, pixel_s, edges, pitch)
+    back = 1.0 / stream_coupling(coupling_ref, expos)
     zero = jnp.zeros((streams, LANES), F32)
     states = [(zero, zero + 1.0, zero), (zero, zero + 1.0, zero)]
 
@@ -313,7 +314,10 @@
                     states[side] = rescaled(states[side])
 
     write_weights(
-        place_ref, wav_count, which, coupling_v, counts_v, good_v, ivar_v, bits_v, sums_ref, weight_ref, eliminate
+        place_ref, wav_count, which, coupling_ref, counts_ref, good_ref,
+        lambda e, tile: ivar_ref[e, pl.ds(pl.multiple_of(which * half + ROWS * tile, ROWS), ROWS), :],
+        lambda e, group: bits_ref[e, pl.ds(pl.multiple_of(which * (half // BITS) + words * group, words), words), :],
+        sums_ref, weight_ref, eliminate,
     )
     for (n, d, b), out_ref in zip(states, (up_ref, down_ref)):
         scale = 1.0 / (d + n * back)
@@ -327,66 +331,44 @@
     streams = expos * fibres // LANES
     count = -(-HALO // ROWS) * ROWS
     edge = shaped((2, streams, LANES))
+    edge_scratch = pltpu.VMEM((streams * odd(2 * count), LANES), F32)
     return pl.pallas_call(
         functools.partial(kept_kernel, wav_count),
-        in_specs=[in_smem] + [in_hbm] * 6,
+        in_specs=[in_smem] + [in_vmem] * 6,
         out_specs=[in_vmem] * 4,
         out_shape=[shaped((2, half, fibres)), shaped((expos, half, fibres)), edge, edge],
-        scratch_shapes=[
-            *weights_scratch(coupling, counts, good, ivar),
-            pltpu.VMEM((streams * odd(2 * count), LANES), F32),
-            pltpu.VMEM((streams * odd(2 * count), LANES), F32),
-            pltpu.SemaphoreType.DMA((5 + 4 * streams,)),
-        ],
+        scratch_shapes=[edge_scratch, edge_scratch],
         compiler_params=params(),
         cost_estimate=cost(20 * ivar.size, 6 * ivar.size),
         name="kept_weights",
-    )(place, *held_in_hbm(coupling, counts, good, pixels, ivar, bits))
-
-
-def layout_kernel(place_ref, pixels_ref, ivar_ref, pixel_out, ivar_out, sems):
+    )(place, coupling, counts, good, pixels, ivar, bits)
+
+
+def layout_kernel(moves, place_ref, slots_ref, pixels_ref, ivar_ref, table_ref, pixel_out, ivar_out):
     width = ivar_ref.shape[1]
-    pairs = stream_copies(ivar_ref, ivar_out, 0, width, odd(width), 0)
-    pairs += stream_copies(pixels_ref, pixel_out, 0, width, odd(width), 0)
-    for wait in in_flight(pairs, sems):
-        wait.wait()
-
-
-def stream_layout(place, pixels, ivar):
+    lay_out(ivar_ref, ivar_out, [(0, width, 0)], odd(width))
+    lay_out(pixels_ref, pixel_out, [(0, width, 0)], odd(width))
+    write_recv_table(*moves, place_ref[0], slots_ref, table_ref)
+
+
+def stream_layout(moves, place, slots, pixels, ivar):
     expos, width, fibres = ivar.shape
     streams = expos * fibres // LANES
+    fib_count, pack, per, _ = moves
     laid = shaped((streams * odd(width), LANES))
     return pl.pallas_call(
-        layout_kernel,
-        in_specs=[in_smem] + [in_hbm] * 2,
-        out_specs=[in_vmem] * 2,
-        out_shape=[laid, laid],
-        scratch_shapes=[pltpu.SemaphoreType.DMA((2 * streams,))],
+        functools.partial(layout_kernel, moves),
+        in_specs=[in_smem] + [in_vmem] * 3,
+        out_specs=[in_vmem] * 3,
+        out_shape=[shaped((pack * fibres, fib_count * pack * per), BF16), laid, laid],
         compiler_params=params(),
         cost_estimate=cost(0, 16 * ivar.size),
         name="stream_layout",
-    )(place, *held_in_hbm(pixels, ivar))
-
-
-def recv_kernel(moves, place_ref, slots_ref, table_ref):
-    write_recv_table(*moves, place_ref[0], slots_ref, table_ref)
-
-
-def recv_moves(moves, place, slots, fibres):
-    fib_count, pack, per, _ = moves
-    return pl.pallas_call(
-        functools.partial(recv_kernel, moves),
-        in_specs=[in_smem, in_vmem],
-        out_specs=in_vmem,
-        out_shape=shaped((pack * fibres, fib_count * pack * per), BF16),
-        compiler_params=params(),
-        cost_estimate=cost(1e6, 1e6),
-        name="recv_moves",
-    )(place, slots)
+    )(place, slots, pixels, ivar)
 
 
 def solve_kernel(
-    place_ref, coupling_ref, left_ref, right_ref, pixel_ref, ivar_ref, weight_t_ref, weight_m_ref,
+    wav_count, place_ref, coupling_ref, left_ref, right_ref, pixel_ref, ivar_ref, weight_t_ref, weight_m_ref,
     theirs_ref, mine_ref, solved_s, lead_s, rest_s,
 ):
     streams = left_ref.shape[1]
@@ -400,9 +382,9 @@
     def row_at(i):
         return pl.ds(i, streams, stride=pitch)
 
-    def begin(edge_ref):
-        u = edge_ref[0]
-        return (u, 1.0 - u * back, edge_ref[1])
+    def begin(edge_ref, outermost):
+        u = jnp.where(place_ref[1] == outermost, 0.0, edge_ref[0])
+        return (u, 1.0 - u * back, jnp.where(place_ref[1] == outermost, 0.0, edge_ref[1]))
 
     def keep(side, i, state):
         n, d, b = state
@@ -421,7 +403,7 @@
                 states[side] = advance(states[side], ivar_ref[row_at(row), :], pixel_ref[row_at(row), :], back)
         return tuple(rescaled(state) for state in states)
 
-    states = lax.fori_loop(0, middle // unrolled, eliminate, (begin(left_ref), begin(right_ref)))
+    states = lax.fori_loop(0, middle // unrolled, eliminate, (begin(left_ref, 0), begin(right_ref, wav_count - 1)))
     for side in range(2):
         keep(side, middle, states[side])
     lead, rest = lead_s[0, middle], rest_s[0, middle]
@@ -479,13 +461,13 @@
     coadd(mine_ref, weight_m_ref, place_ref[2])
 
 
-def flux_sums(place, coupling, left, right, pixels, ivar, weight_t, weight_m):
+def flux_sums(wav_count, place, coupling, left, right, pixels, ivar, weight_t, weight_m):
     expos, half, fibres = weight_t.shape
     streams = left.shape[1]
     out = shaped((1, half, fibres))
     factor_scratch = pltpu.VMEM((2, half + 1, streams, LANES), F32)
     return pl.pallas_call(
-        solve_kernel,
+        functools.partial(solve_kernel, wav_count),
         in_specs=[in_smem] + [in_vmem] * 7,
         out_specs=[in_vmem, in_vmem],
         out_shape=[out, out],
@@ -634,25 +616,24 @@
     swap = [(0, 1), (1, 0)]
     moves = (fib_count, pack, per, rel)
 
-    theirs, weight_t, send_table = sent_weights(
-        moves, wav_count, place, slots, coupling, counts, good_flags, pixel_ivar, clip_bits
+    theirs, weight_t, send_table, slots, coupling, counts, good, bits, ivar, counted = sent_weights(
+        moves, wav_count, place, slots, coupling, counts, good_flags, clip_bits, pixel_ivar, pixels
     )
     arriving = lax.ppermute(theirs, "exp", swap)
     mine, weight_m, up, down = kept_weights(
-        wav_count, after(place, theirs), coupling, counts, good_flags, pixels, pixel_ivar, clip_bits
+        wav_count, place, coupling, counts, good, counted, ivar, bits
     )
     *sorted_pieces, scale = sort_fibres(arriving, mine, send_table, pack, pieces)
     weight_pieces = exchange(sorted_pieces, fib_count)
 
     up, down = after((up, down), scale)
-    upward = [(i, i + 1) for i in range(wav_count - 1)]
+    upward = [(i, (i + 1) % wav_count) for i in range(wav_count)]
     left = lax.ppermute(up, "wav", upward)
     right = lax.ppermute(down, "wav", [(j, i) for i, j in upward])
-    pixel_s, ivar_s = stream_layout(after(place, scale), pixels, pixel_ivar)
-    theirs, mine = flux_sums(place, coupling, left, right, pixel_s, ivar_s, weight_t, weight_m)
-    recv_table = recv_moves(moves, after(place, theirs), slots, fibres)
+    recv_table, pixel_s, ivar_s = stream_layout(moves, after(place, scale), slots, counted, ivar)
+    theirs, mine = flux_sums(wav_count, place, coupling, left, right, pixel_s, ivar_s, weight_t, weight_m)
     if rel:
-        theirs = after(theirs, (weight_pieces[1], weight_pieces[2]))
+        theirs = after(theirs, weight_pieces[1:])
     theirs = lax.ppermute(theirs, "exp", swap)
     flux_pieces = exchange(sort_fibres(theirs, mine, send_table, pack, pieces, scale), fib_count)
 

time: 35.6 us -> 33.2 us (0.933)
  Pallas kernels: 15.8 us -> 12 us
  waiting for transfers between devices: 2.85 us -> 4.92 us
  starting transfers between devices: 15.9 us -> 15.3 us
    pallas_call x3 -> x2, Pallas kernels: 6.88 us -> 4.25 us  [the longest x1 2.6 us: flux_sums(): pl.pallas_call(functools.partial(solve_kernel, wav_count), in_specs=[in_s...]
    ppermute x1, starting transfers between devices: 3.52 us -> 1.49 us  [per_device(): left = lax.ppermute(up, 'wav', upward)]
    pallas_call x1, Pallas kernels: 2.85 us -> 1.15 us  [kept_weights(): pl.pallas_call(functools.partial(kept_kernel, wav_count), in_specs=[in_sm...]
    ppermute x1, waiting for transfers between devices: 0.1 us -> 1.5 us  [per_device(): theirs = lax.ppermute(theirs, 'exp', swap)]
    ppermute x6, starting transfers between devices: 10.5 us -> 11.8 us  [exchange(): lax.ppermute(pieces[d], 'fib', [(i, (i + d) % fib_count) for i in range(f...]
    ppermute x6, waiting for transfers between devices: 1.4 us -> 2.53 us  [exchange(): lax.ppermute(pieces[d], 'fib', [(i, (i + d) % fib_count) for i in range(f...]
    ppermute x1, waiting for transfers between devices: 1.35 us -> 0.55 us  [per_device(): right = lax.ppermute(down, 'wav', [(j, i) for i, j in upward])]
    pallas_call x1, Pallas kernels: 2.31 us -> 2.91 us  [sent_weights(): pl.pallas_call(functools.partial(sent_kernel, moves, wav_count), in_specs...]
  transfers between devices with their start and end apart: 10 -> 10, of which waited for: 3 -> 5; matrix products, arithmetic and copies ran while one was open for 0% -> 0% of each run, Pallas kernels for 34% -> 22%
where the time goes in v5:
time: 33.2 us; the launch traced here: 33 us
  starting transfers between devices  15.3 us (46%)
  Pallas kernels  12 us (36%)
  waiting for transfers between devices  4.92 us (15%)
  between operations  0.72 us (2%)
    ppermute x6, starting transfers between devices, exchange(): lax.ppermute(pieces[d], 'fib', [(i, (i + d) % fib_count) for i in range(f...  11.8 us
    pallas_call x1, Pallas kernels, sent_weights(): pl.pallas_call(functools.partial(sent_kernel, moves, wav_count), in_specs...  2.91 us
    pallas_call x1, Pallas kernels, flux_sums(): pl.pallas_call(functools.partial(solve_kernel, wav_count), in_specs=[in_s...  2.6 us
    ppermute x6, waiting for transfers between devices, exchange(): lax.ppermute(pieces[d], 'fib', [(i, (i + d) % fib_count) for i in range(f...  2.53 us
    pallas_call x1, Pallas kernels, end_weights(): pl.pallas_call(functools.partial(weights_end_kernel, pack, total), in_spe...  1.91 us
    pallas_call x1, Pallas kernels, stream_layout(): pl.pallas_call(functools.partial(layout_kernel, moves), in_specs=[in_smem...  1.65 us
    ppermute x1, waiting for transfers between devices, per_device(): theirs = lax.ppermute(theirs, 'exp', swap)  1.5 us
    ppermute x1, starting transfers between devices, per_device(): left = lax.ppermute(up, 'wav', upward)  1.49 us
  transfers between devices with their start and end apart: 10, of which 5 were waited for; matrix products, arithmetic and copies ran while one was open for 0% of the time, Pallas kernels for 22%

profile of v5, /device:TPU:0, one launch (start us, length us, event | category | flops | bytes accessed | tf_op | source)
XLA Modules:
  0.0 33.0 jit_solution(7554418095318923314)
XLA Ops:
  0.6 0.1 pad_add_fusion.place_ref
  0.7 2.9 %sent_weights.1 = (f32[2,240,256]{2,1,0:T(8,128)S(1)}, f32[4,240,256]{2,1,0:T(8,128)S(1)}, bf16[512,512]{1,0:T(8,128)(2,1)S(1)}, s32[1,1024]{1,0:T(1,128)S(1)}, ...) custom-call(s32[3]{0:T(128)S(1)} %pad_add_fusion.place_ref, ...), custom_call_target="tpu_custom_call" | custom-call | flops 9830400 | bytes 2949120 | tf_op jit(solution)/shard_map/sent_weights/pallas_call | solution.py:263
  3.6 0.5 %collective-permute-start = (f32[2,240,256]{2,1,0:T(8,128)S(1)}, f32[2,240,256]{2,1,0:T(8,128)S(1)}, u32[]{:S(2)}, u32[]{:S(2)}) collective-permute-start(f32[2,240,256]{2,1,0:T(8,128)S(1)} %get-tuple-element.37), channel_id=1, source_target_pairs={{0,1},{1,0},{2,3},{3,2},{4,5},{5,4},{6,7},{7,6},{8,9},{9,8},{10,11... | collective-permute-start | bytes 1474568 | tf_op jit(solution)/shard_map/ppermute | solution.py:622
  4.1 1.1 %kept_weights.1 = (f32[2,240,256]{2,1,0:T(8,128)S(1)}, f32[4,240,256]{2,1,0:T(8,128)S(1)}, f32[2,8,128]{2,1,0:T(8,128)S(1)}, f32[2,8,128]{2,1,0:T(8,128)S(1)}) custom-call(s32[3]{0:T(128)S(1)} %pad_add_fusion.place_ref, f32[1,256]{1,0:T(1,128)S(1)} %get-tuple-element.38.coupling_ref, s32[1,256]{1,0:T(1,128)S(1)} %get-tuple-element.39.counts_ref, ...), custom_call_target="tpu_custom_call" | custom-call | flops 9830400 | bytes 2949120 | tf_op jit(solution)/shard_map/kept_weights/pallas_call | solution.py:335
  5.3 0.3 %collective-permute-done.theirs_ref = f32[2,240,256]{2,1,0:T(8,128)S(1)} collective-permute-done((f32[2,240,256]{2,1,0:T(8,128)S(1)}, f32[2,240,256]{2,1,0:T(8,128)S(1)}, u32[]{:S(2)}, u32[]{:S(2)}) %collective-permute-start) | collective-permute-done | bytes 491552 | tf_op jit(solution)/shard_map/ppermute | solution.py:622
  5.6 0.5 %sort_weights.1 = (f32[2,120,128]{2,1,0:T(8,128)S(1)}, f32[2,120,128]{2,1,0:T(8,128)S(1)}, f32[2,120,128]{2,1,0:T(8,128)S(1)}, f32[2,120,128]{2,1,0:T(8,128)S(1)}, f32[240,256]{1,0:T(8,128)S(1)}) custom-call(f32[2,240,256]{2,1,0:T(8,128)S(1)} %collective-permute-done.theirs_ref, f32[2,240,256]{2,1,0:T(8,128)S(1)} %get-tuple-element.44.mine_ref, ...), custom_call_target="tpu_custom_call" | custom-call | tf_op jit(solution)/shard_map/sort_weights/pallas_call | solution.py:516
  6.1 3.0 %collective-permute-start.3 = (f32[2,120,128]{2,1,0:T(8,128)S(1)}, f32[2,120,128]{2,1,0:T(8,128)S(1)}, u32[]{:S(2)}, u32[]{:S(2)}) collective-permute-start(f32[2,120,128]{2,1,0:T(8,128)S(1)} %get-tuple-element.59), channel_id=1, source_target_pairs={{0,8},{8,16},{16,24},{24,0},{1,9},{9,17},{17,25},{25,1},{2,10},{10... | collective-permute-start | bytes 368648 | tf_op jit(solution)/shard_map/ppermute | solution.py:532
  9.1 2.6 %collective-permute-start.4 = (f32[2,120,128]{2,1,0:T(8,128)S(1)}, f32[2,120,128]{2,1,0:T(8,128)S(1)}, u32[]{:S(2)}, u32[]{:S(2)}) collective-permute-start(f32[2,120,128]{2,1,0:T(8,128)S(1)} %get-tuple-element.60), channel_id=1, source_target_pairs={{0,16},{8,24},{16,0},{24,8},{1,17},{9,25},{17,1},{25,9},{2,18},{10... | collective-permute-start | bytes 368648 | tf_op jit(solution)/shard_map/ppermute | solution.py:532
  11.7 1.3 %collective-permute-start.5 = (f32[2,120,128]{2,1,0:T(8,128)S(1)}, f32[2,120,128]{2,1,0:T(8,128)S(1)}, u32[]{:S(2)}, u32[]{:S(2)}) collective-permute-start(f32[2,120,128]{2,1,0:T(8,128)S(1)} %get-tuple-element.61), channel_id=1, source_target_pairs={{0,24},{8,0},{16,8},{24,16},{1,25},{9,1},{17,9},{25,17},{2,26},{10... | collective-permute-start | bytes 368648 | tf_op jit(solution)/shard_map/ppermute | solution.py:532
  13.0 1.5 %collective-permute-start.1 = (f32[2,8,128]{2,1,0:T(8,128)S(1)}, f32[2,8,128]{2,1,0:T(8,128)S(1)}, u32[]{:S(2)}, u32[]{:S(2)}) collective-permute-start(f32[2,8,128]{2,1,0:T(8,128)S(1)} %get-tuple-element.52), channel_id=1, source_target_pairs={{0,2},{2,4},{4,6},{6,0},{1,3},{3,5},{5,7},{7,1},{8,10},{10,12},{12... | collective-permute-start | bytes 24584 | tf_op jit(solution)/shard_map/ppermute | solution.py:631
  14.5 1.4 %collective-permute-start.2 = (f32[2,8,128]{2,1,0:T(8,128)S(1)}, f32[2,8,128]{2,1,0:T(8,128)S(1)}, u32[]{:S(2)}, u32[]{:S(2)}) collective-permute-start(f32[2,8,128]{2,1,0:T(8,128)S(1)} %get-tuple-element.53), channel_id=1, source_target_pairs={{2,0},{4,2},{6,4},{0,6},{3,1},{5,3},{7,5},{1,7},{10,8},{12,10},{14... | collective-permute-start | bytes 24584 | tf_op jit(solution)/shard_map/ppermute | solution.py:632
  16.0 1.7 %stream_layout.1 = (bf16[512,512]{1,0:T(8,128)(2,1)S(1)}, f32[3848,128]{1,0:T(8,128)S(1)}, f32[3848,128]{1,0:T(8,128)S(1)}) custom-call(s32[3]{0:T(128)S(1)} %pad_add_fusion.place_ref, s32[1,1024]{1,0:T(1,128)S(1)} %get-tuple-element.48.slots_ref, f32[4,480,256]{2,1,0:T(8,128)S(1)} %get-tuple-element.41.pixels_ref, f32[4,480,256]{2,1,0:T(8,128)S(1)} %get-tuple-element.42.ivar_ref), custom_call_target="tpu_custom_call" | custom-call | bytes 7864320 | tf_op jit(solution)/shard_map/stream_layout/pallas_call | solution.py:359
  17.6 0.5 %collective-permute-done.2.right_ref = f32[2,8,128]{2,1,0:T(8,128)S(1)} collective-permute-done((f32[2,8,128]{2,1,0:T(8,128)S(1)}, f32[2,8,128]{2,1,0:T(8,128)S(1)}, u32[]{:S(2)}, u32[]{:S(2)}) %collective-permute-start.2) | collective-permute-done | bytes 8224 | tf_op jit(solution)/shard_map/ppermute | solution.py:632
  18.2 2.6 %flux_sums.1 = (f32[1,240,256]{2,1,0:T(8,128)S(1)}, f32[1,240,256]{2,1,0:T(8,128)S(1)}) custom-call(s32[3]{0:T(128)S(1)} %pad_add_fusion.place_ref, f32[1,256]{1,0:T(1,128)S(1)} %get-tuple-element.38.coupling_ref, f32[2,8,128]{2,1,0:T(8,128)S(1)} %collective-permute-done.1.left_ref, f32[2,8,128]{2,1,0:T(8,128)S(1)} %collective-permute-done.2.right_ref, ...), custom_call_target="tpu_custom_call" | custom-call | tf_op jit(solution)/shard_map/flux_sums/pallas_call | solution.py:469
  20.8 0.1 collective-permute-start.6
  20.9 1.5 %collective-permute-done.6.theirs_ref = f32[1,240,256]{2,1,0:T(8,128)S(1)} collective-permute-done((f32[1,240,256]{2,1,0:T(8,128)S(1)}, f32[1,240,256]{2,1,0:T(8,128)S(1)}, u32[]{:S(2)}, u32[]{:S(2)}) %collective-permute-start.6) | collective-permute-done | bytes 245792 | tf_op jit(solution)/shard_map/ppermute | solution.py:637
  22.4 0.3 %sort_flux.1 = (f32[1,120,128]{2,1,0:T(8,128)S(1)}, f32[1,120,128]{2,1,0:T(8,128)S(1)}, f32[1,120,128]{2,1,0:T(8,128)S(1)}, f32[1,120,128]{2,1,0:T(8,128)S(1)}) custom-call(f32[1,240,256]{2,1,0:T(8,128)S(1)} %collective-permute-done.6.theirs_ref, f32[1,240,256]{2,1,0:T(8,128)S(1)} %get-tuple-element.63.mine_ref, ...), custom_call_target="tpu_custom_call" | custom-call | tf_op jit(solution)/shard_map/sort_flux/pallas_call | solution.py:516
  22.7 2.4 %collective-permute-start.7 = (f32[1,120,128]{2,1,0:T(8,128)S(1)}, f32[1,120,128]{2,1,0:T(8,128)S(1)}, u32[]{:S(2)}, u32[]{:S(2)}) collective-permute-start(f32[1,120,128]{2,1,0:T(8,128)S(1)} %get-tuple-element.65), channel_id=1, source_target_pairs={{0,8},{8,16},{16,24},{24,0},{1,9},{9,17},{17,25},{25,1},{2,10},{10... | collective-permute-start | bytes 184328 | tf_op jit(solution)/shard_map/ppermute | solution.py:532
  25.1 1.6 %collective-permute-start.8 = (f32[1,120,128]{2,1,0:T(8,128)S(1)}, f32[1,120,128]{2,1,0:T(8,128)S(1)}, u32[]{:S(2)}, u32[]{:S(2)}) collective-permute-start(f32[1,120,128]{2,1,0:T(8,128)S(1)} %get-tuple-element.66), channel_id=1, source_target_pairs={{0,16},{8,24},{16,0},{24,8},{1,17},{9,25},{17,1},{25,9},{2,18},{10... | collective-permute-start | bytes 184328 | tf_op jit(solution)/shard_map/ppermute | solution.py:532
  26.8 0.8 %collective-permute-start.9 = (f32[1,120,128]{2,1,0:T(8,128)S(1)}, f32[1,120,128]{2,1,0:T(8,128)S(1)}, u32[]{:S(2)}, u32[]{:S(2)}) collective-permute-start(f32[1,120,128]{2,1,0:T(8,128)S(1)} %get-tuple-element.67), channel_id=1, source_target_pairs={{0,24},{8,0},{16,8},{24,16},{1,25},{9,1},{17,9},{25,17},{2,26},{10... | collective-permute-start | bytes 184328 | tf_op jit(solution)/shard_map/ppermute | solution.py:532
  27.6 1.9 %end_weights.1 = (f32[240,256]{1,0:T(8,128)}, f32[3,240,256]{2,1,0:T(8,128)}) custom-call(s32[3]{0:T(128)S(1)} %pad_add_fusion.place_ref, bf16[512,512]{1,0:T(8,128)(2,1)S(1)} %get-tuple-element.49.table_ref, f32[2,120,128]{2,1,0:T(8,128)S(1)} %get-tuple-element.68.refs_0_, f32[2,120,128]{2,1,0:T(8,128)S(1)} %collective-permute-done.3.refs_1_, ...), custom_call_target="tpu_custom_call" | custom-call | flops 251658240 | bytes 1474560 | tf_op jit(solution)/shard_map/end_weights/pallas_call | solution.py:566
  29.5 2.1 %collective-permute-done.8.refs_2_ = f32[1,120,128]{2,1,0:T(8,128)S(1)} collective-permute-done((f32[1,120,128]{2,1,0:T(8,128)S(1)}, f32[1,120,128]{2,1,0:T(8,128)S(1)}, u32[]{:S(2)}, u32[]{:S(2)}) %collective-permute-start.8) | collective-permute-done | bytes 61472 | tf_op jit(solution)/shard_map/ppermute | solution.py:532
  31.6 0.4 %collective-permute-done.9.refs_3_ = f32[1,120,128]{2,1,0:T(8,128)S(1)} collective-permute-done((f32[1,120,128]{2,1,0:T(8,128)S(1)}, f32[1,120,128]{2,1,0:T(8,128)S(1)}, u32[]{:S(2)}, u32[]{:S(2)}) %collective-permute-start.9) | collective-permute-done | bytes 61472 | tf_op jit(solution)/shard_map/ppermute | solution.py:532
  32.0 1.0 %end_flux.1 = f32[240,256]{1,0:T(8,128)} custom-call(bf16[512,512]{1,0:T(8,128)(2,1)S(1)} %get-tuple-element.49.table_ref, f32[1,120,128]{2,1,0:T(8,128)S(1)} %get-tuple-element.64.refs_0_, f32[1,120,128]{2,1,0:T(8,128)S(1)} %collective-permute-done.7.refs_1_, f32[1,120,128]{2,1,0:T(8,128)S(1)} %collective-permute-done.8.refs_2_, ...), custom_call_target="tpu_custom_call" | custom-call | flops 125829120 | bytes 491520 | tf_op jit(solution)/shard_map/end_flux/pallas_call | solution.py:588
  (5 shorter events, 0.0 us)
Async XLA Ops:
  3.6 2.0 %collective-permute-start = (f32[2,240,256]{2,1,0:T(8,128)S(1)}, f32[2,240,256]{2,1,0:T(8,128)S(1)}, u32[]{:S(2)}, u32[]{:S(2)}) collective-permute-start(f32[2,240,256]{2,1,0:T(8,128)S(1)} %get-tuple-element.37), channel_id=1, source_target_pairs={{0,1},{1,0},{2,3},{3,2},{4,5},{5,4},{6,7},{7,6},{8,9},{9,8},{10,11... | collective-permute-start | bytes 1474568 | tf_op jit(solution)/shard_map/ppermute | solution.py:622
  6.1 14.7 %collective-permute-start.3 = (f32[2,120,128]{2,1,0:T(8,128)S(1)}, f32[2,120,128]{2,1,0:T(8,128)S(1)}, u32[]{:S(2)}, u32[]{:S(2)}) collective-permute-start(f32[2,120,128]{2,1,0:T(8,128)S(1)} %get-tuple-element.59), channel_id=1, source_target_pairs={{0,8},{8,16},{16,24},{24,0},{1,9},{9,17},{17,25},{25,1},{2,10},{10... | collective-permute-start | bytes 368648 | tf_op jit(solution)/shard_map/ppermute | solution.py:532
  9.1 11.7 %collective-permute-start.4 = (f32[2,120,128]{2,1,0:T(8,128)S(1)}, f32[2,120,128]{2,1,0:T(8,128)S(1)}, u32[]{:S(2)}, u32[]{:S(2)}) collective-permute-start(f32[2,120,128]{2,1,0:T(8,128)S(1)} %get-tuple-element.60), channel_id=1, source_target_pairs={{0,16},{8,24},{16,0},{24,8},{1,17},{9,25},{17,1},{25,9},{2,18},{10... | collective-permute-start | bytes 368648 | tf_op jit(solution)/shard_map/ppermute | solution.py:532
  11.7 9.1 %collective-permute-start.5 = (f32[2,120,128]{2,1,0:T(8,128)S(1)}, f32[2,120,128]{2,1,0:T(8,128)S(1)}, u32[]{:S(2)}, u32[]{:S(2)}) collective-permute-start(f32[2,120,128]{2,1,0:T(8,128)S(1)} %get-tuple-element.61), channel_id=1, source_target_pairs={{0,24},{8,0},{16,8},{24,16},{1,25},{9,1},{17,9},{25,17},{2,26},{10... | collective-permute-start | bytes 368648 | tf_op jit(solution)/shard_map/ppermute | solution.py:532
  13.0 4.6 %collective-permute-start.1 = (f32[2,8,128]{2,1,0:T(8,128)S(1)}, f32[2,8,128]{2,1,0:T(8,128)S(1)}, u32[]{:S(2)}, u32[]{:S(2)}) collective-permute-start(f32[2,8,128]{2,1,0:T(8,128)S(1)} %get-tuple-element.52), channel_id=1, source_target_pairs={{0,2},{2,4},{4,6},{6,0},{1,3},{3,5},{5,7},{7,1},{8,10},{10,12},{12... | collective-permute-start | bytes 24584 | tf_op jit(solution)/shard_map/ppermute | solution.py:631
  14.5 3.7 %collective-permute-start.2 = (f32[2,8,128]{2,1,0:T(8,128)S(1)}, f32[2,8,128]{2,1,0:T(8,128)S(1)}, u32[]{:S(2)}, u32[]{:S(2)}) collective-permute-start(f32[2,8,128]{2,1,0:T(8,128)S(1)} %get-tuple-element.53), channel_id=1, source_target_pairs={{2,0},{4,2},{6,4},{0,6},{3,1},{5,3},{7,5},{1,7},{10,8},{12,10},{14... | collective-permute-start | bytes 24584 | tf_op jit(solution)/shard_map/ppermute | solution.py:632
  20.8 1.6 %collective-permute-start.6 = (f32[1,240,256]{2,1,0:T(8,128)S(1)}, f32[1,240,256]{2,1,0:T(8,128)S(1)}, u32[]{:S(2)}, u32[]{:S(2)}) collective-permute-start(f32[1,240,256]{2,1,0:T(8,128)S(1)} %get-tuple-element.62), channel_id=1, source_target_pairs={{0,1},{1,0},{2,3},{3,2},{4,5},{5,4},{6,7},{7,6},{8,9},{9,8},{10,11... | collective-permute-start | bytes 737288 | tf_op jit(solution)/shard_map/ppermute | solution.py:637
  22.7 6.7 %collective-permute-start.7 = (f32[1,120,128]{2,1,0:T(8,128)S(1)}, f32[1,120,128]{2,1,0:T(8,128)S(1)}, u32[]{:S(2)}, u32[]{:S(2)}) collective-permute-start(f32[1,120,128]{2,1,0:T(8,128)S(1)} %get-tuple-element.65), channel_id=1, source_target_pairs={{0,8},{8,16},{16,24},{24,0},{1,9},{9,17},{17,25},{25,1},{2,10},{10... | collective-permute-start | bytes 184328 | tf_op jit(solution)/shard_map/ppermute | solution.py:532
  25.1 6.4 %collective-permute-start.8 = (f32[1,120,128]{2,1,0:T(8,128)S(1)}, f32[1,120,128]{2,1,0:T(8,128)S(1)}, u32[]{:S(2)}, u32[]{:S(2)}) collective-permute-start(f32[1,120,128]{2,1,0:T(8,128)S(1)} %get-tuple-element.66), channel_id=1, source_target_pairs={{0,16},{8,24},{16,0},{24,8},{1,17},{9,25},{17,1},{25,9},{2,18},{10... | collective-permute-start | bytes 184328 | tf_op jit(solution)/shard_map/ppermute | solution.py:532
  26.8 5.2 %collective-permute-start.9 = (f32[1,120,128]{2,1,0:T(8,128)S(1)}, f32[1,120,128]{2,1,0:T(8,128)S(1)}, u32[]{:S(2)}, u32[]{:S(2)}) collective-permute-start(f32[1,120,128]{2,1,0:T(8,128)S(1)} %get-tuple-element.67), channel_id=1, source_target_pairs={{0,24},{8,0},{16,8},{24,16},{1,25},{9,1},{17,9},{25,17},{2,26},{10... | collective-permute-start | bytes 184328 | tf_op jit(solution)/shard_map/ppermute | solution.py:532

commit v6 on v5

--- a/solution.py
+++ b/solution.py
@@ -78,8 +78,9 @@
 
 def advance(state, ivar, pixel, back_coupling):
     n, d, b = state
-    next_d = d + n * back_coupling
-    return (n * (1.0 + ivar * back_coupling) + ivar * d, next_d, b + (ivar * pixel) * next_d)
+    ratio = ivar * back_coupling
+    next_d = d + n
+    return (n * (1.0 + ratio) + ratio * d, next_d, b + (ivar * pixel) * next_d)
 
 
 def rescaled(state):
@@ -211,8 +212,8 @@
 
 
 def sent_kernel(
-    moves, wav_count, place_ref, slots_ref, coupling_ref, counts_ref, good_ref, bits_ref, ivar_ref, pixels_ref,
-    sums_ref, weight_ref, table_ref, slots_v, coupling_v, counts_v, good_v, bits_v, ivar_v, pixels_v, sems,
+    moves, wav_count, place_ref, slots_ref, coupling_ref, counts_ref, good_ref, bits_ref, ivar_ref,
+    sums_ref, weight_ref, table_ref, slots_v, coupling_v, counts_v, good_v, bits_v, ivar_v, sems,
 ):
     expos, width, _ = ivar_ref.shape
     half = width // 2
@@ -232,8 +233,7 @@
             (bits_ref, bits_v),
         ]
         + [part(ivar_ref, ivar_v, which * half + g) for g in range(0, half, GROUP)]
-        + [part(ivar_ref, ivar_v, (1 - which) * half + g) for g in range(0, half, GROUP)]
-        + [(pixels_ref, pixels_v)],
+        + [part(ivar_ref, ivar_v, (1 - which) * half + g) for g in range(0, half, GROUP)],
         sems,
     )
     waits[0].wait()
@@ -255,22 +255,22 @@
         wait.wait()
 
 
-def sent_weights(moves, wav_count, place, slots, coupling, counts, good, bits, ivar, pixels):
+def sent_weights(moves, wav_count, place, slots, coupling, counts, good, bits, ivar):
     expos, width, fibres = ivar.shape
     half = width // 2
     fib_count, pack, per, _ = moves
-    inputs = (slots, coupling, counts, good, bits, ivar, pixels)
+    inputs = (slots, coupling, counts, good, bits, ivar)
     return pl.pallas_call(
         functools.partial(sent_kernel, moves, wav_count),
-        in_specs=[in_smem] + [in_hbm] * 7,
-        out_specs=[in_vmem] * 10,
+        in_specs=[in_smem] + [in_hbm] * 6,
+        out_specs=[in_vmem] * 9,
         out_shape=[
             shaped((2, half, fibres)),
             shaped((expos, half, fibres)),
             shaped((fib_count * pack * per, pack * fibres), BF16),
         ]
         + [shaped(x.shape, x.dtype) for x in inputs],
-        scratch_shapes=[pltpu.SemaphoreType.DMA((6 + width // GROUP,))],
+        scratch_shapes=[pltpu.SemaphoreType.DMA((5 + width // GROUP,))],
         compiler_params=params(),
         cost_estimate=cost(20 * ivar.size, 6 * ivar.size),
         name="sent_weights",
@@ -301,7 +301,8 @@
     edges = [(0, count, 0), (width - count, count, count)]
     lay_out(ivar_ref, ivar_s, edges, pitch)
     lay_out(pixels_ref, pixel_s, edges, pitch)
-    back = 1.0 / stream_coupling(coupling_ref, expos)
+    coupling = stream_coupling(coupling_ref, expos)
+    back = 1.0 / coupling
     zero = jnp.zeros((streams, LANES), F32)
     states = [(zero, zero + 1.0, zero), (zero, zero + 1.0, zero)]
 
@@ -320,8 +321,8 @@
         sums_ref, weight_ref, eliminate,
     )
     for (n, d, b), out_ref in zip(states, (up_ref, down_ref)):
-        scale = 1.0 / (d + n * back)
-        out_ref[0] = n * scale
+        scale = 1.0 / (d + n)
+        out_ref[0] = coupling * (n * scale)
         out_ref[1] = b * scale
 
 
@@ -368,11 +369,11 @@
 
 
 def solve_kernel(
-    wav_count, place_ref, coupling_ref, left_ref, right_ref, pixel_ref, ivar_ref, weight_t_ref, weight_m_ref,
-    theirs_ref, mine_ref, solved_s, lead_s, rest_s,
+    wav_count, place_ref, coupling_ref, left_ref, right_ref, pixel_ref, ivar_ref, weight_ref,
+    theirs_ref, solved_s, lead_s, rest_s,
 ):
     streams = left_ref.shape[1]
-    expos, half, fibres = weight_t_ref.shape
+    expos, half, fibres = weight_ref.shape
     width = 2 * half
     pitch = odd(width)
     middle = half
@@ -383,14 +384,14 @@
         return pl.ds(i, streams, stride=pitch)
 
     def begin(edge_ref, outermost):
-        u = jnp.where(place_ref[1] == outermost, 0.0, edge_ref[0])
-        return (u, 1.0 - u * back, jnp.where(place_ref[1] == outermost, 0.0, edge_ref[1]))
+        n = jnp.where(place_ref[1] == outermost, 0.0, edge_ref[0]) * back
+        return (n, 1.0 - n, jnp.where(place_ref[1] == outermost, 0.0, edge_ref[1]))
 
     def keep(side, i, state):
         n, d, b = state
-        inverse = inverse_of(d + n * back)
+        inverse = inverse_of(d + n)
         lead_s[side, i] = d * inverse
-        rest_s[side, i] = (b * back) * inverse
+        rest_s[side, i] = b * inverse
 
     unrolled = divisor_of(middle, 24)
 
@@ -436,46 +437,62 @@
 
     lax.fori_loop(0, middle // several, substitute, (left, right))
 
-    blocks = fibres // LANES
-    unroll = 5
-
-    def coadd(out_ref, weight_ref, which):
-        start = which * half
-
-        def body(g, carry):
-            for k in range(unroll):
-                row = pl.multiple_of((g * unroll + k) * ROWS, ROWS)
-                for h in range(blocks):
-                    cut = pl.ds(h * LANES, LANES)
-                    total = None
-                    for e in range(expos):
-                        at = pl.ds((h * expos + e) * pitch + start + row, ROWS)
-                        term = weight_ref[e, pl.ds(row, ROWS), cut] * solved_s[at, :]
-                        total = term if e == 0 else total + term
-                    out_ref[0, pl.ds(row, ROWS), cut] = total
-            return carry
-
-        lax.fori_loop(0, half // (unroll * ROWS), body, 0)
-
-    coadd(theirs_ref, weight_t_ref, 1 - place_ref[2])
-    coadd(mine_ref, weight_m_ref, place_ref[2])
-
-
-def flux_sums(wav_count, place, coupling, left, right, pixels, ivar, weight_t, weight_m):
-    expos, half, fibres = weight_t.shape
+    add_up(theirs_ref, weight_ref, solved_s, coupling_ref, 1 - place_ref[2])
+
+
+def add_up(out_ref, weight_ref, solved_ref, coupling_ref, which):
+    expos, half, fibres = weight_ref.shape
+    pitch = odd(2 * half)
+    start = which * half
+    back = 1.0 / coupling_ref[...]
+    unrolled = divisor_of(half // ROWS, 5)
+
+    def body(g, carry):
+        for k in range(unrolled):
+            row = pl.multiple_of((g * unrolled + k) * ROWS, ROWS)
+            for h in range(fibres // LANES):
+                total = None
+                for e in range(expos):
+                    at = pl.ds((h * expos + e) * pitch + start + row, ROWS)
+                    term = weight_ref[e, pl.ds(row, ROWS), pl.ds(h * LANES, LANES)] * solved_ref[at, :]
+                    total = term if e == 0 else total + term
+                out_ref[0, pl.ds(row, ROWS), pl.ds(h * LANES, LANES)] = total * back[:, h * LANES : (h + 1) * LANES]
+        return carry
+
+    lax.fori_loop(0, half // ROWS // unrolled, body, 0)
+
+
+def flux_sums(wav_count, place, coupling, left, right, pixels, ivar, weight):
+    expos, half, fibres = weight.shape
     streams = left.shape[1]
-    out = shaped((1, half, fibres))
     factor_scratch = pltpu.VMEM((2, half + 1, streams, LANES), F32)
     return pl.pallas_call(
         functools.partial(solve_kernel, wav_count),
-        in_specs=[in_smem] + [in_vmem] * 7,
+        in_specs=[in_smem] + [in_vmem] * 6,
         out_specs=[in_vmem, in_vmem],
-        out_shape=[out, out],
-        scratch_shapes=[pltpu.VMEM(pixels.shape, F32), factor_scratch, factor_scratch],
+        out_shape=[shaped((1, half, fibres)), shaped(pixels.shape)],
+        scratch_shapes=[factor_scratch, factor_scratch],
         compiler_params=params(),
         cost_estimate=cost(0, 0),
         name="flux_sums",
-    )(place, coupling, left, right, pixels, ivar, weight_t, weight_m)
+    )(place, coupling, left, right, pixels, ivar, weight)
+
+
+def kept_flux_kernel(place_ref, coupling_ref, solved_ref, weight_ref, out_ref):
+    add_up(out_ref, weight_ref, solved_ref, coupling_ref, place_ref[2])
+
+
+def kept_flux(place, coupling, solved, weight):
+    expos, half, fibres = weight.shape
+    return pl.pallas_call(
+        kept_flux_kernel,
+        in_specs=[in_smem] + [in_vmem] * 3,
+        out_specs=in_vmem,
+        out_shape=shaped((1, half, fibres)),
+        compiler_params=params(),
+        cost_estimate=cost(2 * weight.size, 8 * weight.size),
+        name="kept_flux",
+    )(place, coupling, solved, weight)
 
 
 def split_dot(x, table, dims):
@@ -616,12 +633,12 @@
     swap = [(0, 1), (1, 0)]
     moves = (fib_count, pack, per, rel)
 
-    theirs, weight_t, send_table, slots, coupling, counts, good, bits, ivar, counted = sent_weights(
-        moves, wav_count, place, slots, coupling, counts, good_flags, clip_bits, pixel_ivar, pixels
+    theirs, weight_t, send_table, slots, coupling, counts, good, bits, ivar = sent_weights(
+        moves, wav_count, place, slots, coupling, counts, good_flags, clip_bits, pixel_ivar
     )
     arriving = lax.ppermute(theirs, "exp", swap)
     mine, weight_m, up, down = kept_weights(
-        wav_count, place, coupling, counts, good, counted, ivar, bits
+        wav_count, place, coupling, counts, good, pixels, ivar, bits
     )
     *sorted_pieces, scale = sort_fibres(arriving, mine, send_table, pack, pieces)
     weight_pieces = exchange(sorted_pieces, fib_count)
@@ -630,12 +647,13 @@
     upward = [(i, (i + 1) % wav_count) for i in range(wav_count)]
     left = lax.ppermute(up, "wav", upward)
     right = lax.ppermute(down, "wav", [(j, i) for i, j in upward])
-    recv_table, pixel_s, ivar_s = stream_layout(moves, after(place, scale), slots, counted, ivar)
-    theirs, mine = flux_sums(wav_count, place, coupling, left, right, pixel_s, ivar_s, weight_t, weight_m)
+    recv_table, pixel_s, ivar_s = stream_layout(moves, after(place, scale), slots, pixels, ivar)
+    theirs, solved = flux_sums(wav_count, place, coupling, left, right, pixel_s, ivar_s, weight_t)
     if rel:
-        theirs = after(theirs, weight_pieces[1:])
-    theirs = lax.ppermute(theirs, "exp", swap)
-    flux_pieces = exchange(sort_fibres(theirs, mine, send_table, pack, pieces, scale), fib_count)
+        theirs = after(theirs, weight_pieces[1:-1])
+    arriving = lax.ppermute(theirs, "exp", swap)
+    mine = kept_flux(after(place, theirs), coupling, solved, weight_m)
+    flux_pieces = exchange(sort_fibres(arriving, mine, send_table, pack, pieces, scale), fib_count)
 
     ivar, res = end_weights(place, recv_table, weight_pieces, pack, fibres, total)
     flux = end_flux(recv_table, flux_pieces, pack, fibres)

time: 33.2 us -> 31.8 us (0.958)
  starting transfers between devices: 15.3 us -> 14.5 us
  waiting for transfers between devices: 4.92 us -> 4.47 us
    ppermute x1 -> x0, waiting for transfers between devices: 1.5 us -> none  [per_device(): theirs = lax.ppermute(theirs, 'exp', swap)]
    ppermute x6, waiting for transfers between devices: 2.53 us -> 3.56 us  [exchange(): lax.ppermute(pieces[d], 'fib', [(i, (i + d) % fib_count) for i in range(f...]
    pallas_call x0 -> x1, Pallas kernels: none -> 0.72 us  [kept_flux(): pl.pallas_call(kept_flux_kernel, in_specs=[in_smem] + [in_vmem] * 3, out_...]
    pallas_call x1, Pallas kernels: 2.91 us -> 2.22 us  [sent_weights(): pl.pallas_call(functools.partial(sent_kernel, moves, wav_count), in_specs...]
    ppermute x6, starting transfers between devices: 11.8 us -> 11.1 us  [exchange(): lax.ppermute(pieces[d], 'fib', [(i, (i + d) % fib_count) for i in range(f...]
  transfers between devices with their start and end apart: 10 -> 10, of which waited for: 5 -> 5; matrix products, arithmetic and copies ran while one was open for 0% -> 0% of each run, Pallas kernels for 22% -> 26%
where the time goes in v6:
time: 31.8 us; the launch traced here: 31.6 us
  starting transfers between devices  14.5 us (46%)
  Pallas kernels  11.8 us (37%)
  waiting for transfers between devices  4.47 us (14%)
  between operations  0.72 us (2%)
    ppermute x6, starting transfers between devices, exchange(): lax.ppermute(pieces[d], 'fib', [(i, (i + d) % fib_count) for i in range(f...  11.1 us
    ppermute x6, waiting for transfers between devices, exchange(): lax.ppermute(pieces[d], 'fib', [(i, (i + d) % fib_count) for i in range(f...  3.56 us
    pallas_call x1, Pallas kernels, flux_sums(): pl.pallas_call(functools.partial(solve_kernel, wav_count), in_specs=[in_s...  2.34 us
    pallas_call x1, Pallas kernels, sent_weights(): pl.pallas_call(functools.partial(sent_kernel, moves, wav_count), in_specs...  2.22 us
    pallas_call x1, Pallas kernels, end_weights(): pl.pallas_call(functools.partial(weights_end_kernel, pack, total), in_spe...  1.91 us
    pallas_call x1, Pallas kernels, stream_layout(): pl.pallas_call(functools.partial(layout_kernel, moves), in_specs=[in_smem...  1.65 us
    ppermute x1, starting transfers between devices, per_device(): left = lax.ppermute(up, 'wav', upward)  1.49 us
    ppermute x1, starting transfers between devices, per_device(): right = lax.ppermute(down, 'wav', [(j, i) for i, j in upward])  1.43 us
  transfers between devices with their start and end apart: 10, of which 5 were waited for; matrix products, arithmetic and copies ran while one was open for 0% of the time, Pallas kernels for 26%

profile of v6, /device:TPU:0, one launch (start us, length us, event | category | flops | bytes accessed | tf_op | source)
XLA Modules:
  0.0 31.6 jit_solution(8140154835812939595)
XLA Ops:
  0.6 0.1 pad_add_fusion.place_ref
  0.7 2.2 %sent_weights.1 = (f32[2,240,256]{2,1,0:T(8,128)S(1)}, f32[4,240,256]{2,1,0:T(8,128)S(1)}, bf16[512,512]{1,0:T(8,128)(2,1)S(1)}, s32[1,1024]{1,0:T(1,128)S(1)}, ...) custom-call(s32[3]{0:T(128)S(1)} %pad_add_fusion.place_ref, ...), custom_call_target="tpu_custom_call" | custom-call | flops 9830400 | bytes 2949120 | tf_op jit(solution)/shard_map/sent_weights/pallas_call | solution.py:263
  2.9 0.5 %collective-permute-start = (f32[2,240,256]{2,1,0:T(8,128)S(1)}, f32[2,240,256]{2,1,0:T(8,128)S(1)}, u32[]{:S(2)}, u32[]{:S(2)}) collective-permute-start(f32[2,240,256]{2,1,0:T(8,128)S(1)} %get-tuple-element.37), channel_id=1, source_target_pairs={{0,1},{1,0},{2,3},{3,2},{4,5},{5,4},{6,7},{7,6},{8,9},{9,8},{10,11... | collective-permute-start | bytes 1474568 | tf_op jit(solution)/shard_map/ppermute | solution.py:639
  3.5 1.1 %kept_weights.1 = (f32[2,240,256]{2,1,0:T(8,128)S(1)}, f32[4,240,256]{2,1,0:T(8,128)S(1)}, f32[2,8,128]{2,1,0:T(8,128)S(1)}, f32[2,8,128]{2,1,0:T(8,128)S(1)}) custom-call(s32[3]{0:T(128)S(1)} %pad_add_fusion.place_ref, f32[1,256]{1,0:T(1,128)S(1)} %get-tuple-element.38.coupling_ref, s32[1,256]{1,0:T(1,128)S(1)} %get-tuple-element.39.counts_ref, ...), custom_call_target="tpu_custom_call" | custom-call | flops 9830400 | bytes 2949120 | tf_op jit(solution)/shard_map/kept_weights/pallas_call | solution.py:336
  4.6 0.4 %collective-permute-done.theirs_ref = f32[2,240,256]{2,1,0:T(8,128)S(1)} collective-permute-done((f32[2,240,256]{2,1,0:T(8,128)S(1)}, f32[2,240,256]{2,1,0:T(8,128)S(1)}, u32[]{:S(2)}, u32[]{:S(2)}) %collective-permute-start) | collective-permute-done | bytes 491552 | tf_op jit(solution)/shard_map/ppermute | solution.py:639
  5.0 0.5 %sort_weights.1 = (f32[2,120,128]{2,1,0:T(8,128)S(1)}, f32[2,120,128]{2,1,0:T(8,128)S(1)}, f32[2,120,128]{2,1,0:T(8,128)S(1)}, f32[2,120,128]{2,1,0:T(8,128)S(1)}, f32[240,256]{1,0:T(8,128)S(1)}) custom-call(f32[2,240,256]{2,1,0:T(8,128)S(1)} %collective-permute-done.theirs_ref, f32[2,240,256]{2,1,0:T(8,128)S(1)} %get-tuple-element.43.mine_ref, ...), custom_call_target="tpu_custom_call" | custom-call | tf_op jit(solution)/shard_map/sort_weights/pallas_call | solution.py:533
  5.4 3.0 %collective-permute-start.3 = (f32[2,120,128]{2,1,0:T(8,128)S(1)}, f32[2,120,128]{2,1,0:T(8,128)S(1)}, u32[]{:S(2)}, u32[]{:S(2)}) collective-permute-start(f32[2,120,128]{2,1,0:T(8,128)S(1)} %get-tuple-element.57), channel_id=1, source_target_pairs={{0,8},{8,16},{16,24},{24,0},{1,9},{9,17},{17,25},{25,1},{2,10},{10... | collective-permute-start | bytes 368648 | tf_op jit(solution)/shard_map/ppermute | solution.py:549
  8.4 2.6 %collective-permute-start.4 = (f32[2,120,128]{2,1,0:T(8,128)S(1)}, f32[2,120,128]{2,1,0:T(8,128)S(1)}, u32[]{:S(2)}, u32[]{:S(2)}) collective-permute-start(f32[2,120,128]{2,1,0:T(8,128)S(1)} %get-tuple-element.58), channel_id=1, source_target_pairs={{0,16},{8,24},{16,0},{24,8},{1,17},{9,25},{17,1},{25,9},{2,18},{10... | collective-permute-start | bytes 368648 | tf_op jit(solution)/shard_map/ppermute | solution.py:549
  11.0 1.5 %collective-permute-start.1 = (f32[2,8,128]{2,1,0:T(8,128)S(1)}, f32[2,8,128]{2,1,0:T(8,128)S(1)}, u32[]{:S(2)}, u32[]{:S(2)}) collective-permute-start(f32[2,8,128]{2,1,0:T(8,128)S(1)} %get-tuple-element.51), channel_id=1, source_target_pairs={{0,2},{2,4},{4,6},{6,0},{1,3},{3,5},{5,7},{7,1},{8,10},{10,12},{12... | collective-permute-start | bytes 24584 | tf_op jit(solution)/shard_map/ppermute | solution.py:648
  12.5 1.4 %collective-permute-start.2 = (f32[2,8,128]{2,1,0:T(8,128)S(1)}, f32[2,8,128]{2,1,0:T(8,128)S(1)}, u32[]{:S(2)}, u32[]{:S(2)}) collective-permute-start(f32[2,8,128]{2,1,0:T(8,128)S(1)} %get-tuple-element.52), channel_id=1, source_target_pairs={{2,0},{4,2},{6,4},{0,6},{3,1},{5,3},{7,5},{1,7},{10,8},{12,10},{14... | collective-permute-start | bytes 24584 | tf_op jit(solution)/shard_map/ppermute | solution.py:649
  13.9 1.7 %stream_layout.1 = (bf16[512,512]{1,0:T(8,128)(2,1)S(1)}, f32[3848,128]{1,0:T(8,128)S(1)}, f32[3848,128]{1,0:T(8,128)S(1)}) custom-call(s32[3]{0:T(128)S(1)} %pad_add_fusion.place_ref, s32[1,1024]{1,0:T(1,128)S(1)} %get-tuple-element.47.slots_ref, f32[4,480,256]{2,1,0:T(8,128)S(1)} %copy-done, f32[4,480,256]{2,1,0:T(8,128)S(1)} %get-tuple-element.41.ivar_ref), custom_call_target="tpu_custom_call" | custom-call | bytes 7864320 | tf_op jit(solution)/shard_map/stream_layout/pallas_call | solution.py:360
  15.6 0.5 %collective-permute-done.2.right_ref = f32[2,8,128]{2,1,0:T(8,128)S(1)} collective-permute-done((f32[2,8,128]{2,1,0:T(8,128)S(1)}, f32[2,8,128]{2,1,0:T(8,128)S(1)}, u32[]{:S(2)}, u32[]{:S(2)}) %collective-permute-start.2) | collective-permute-done | bytes 8224 | tf_op jit(solution)/shard_map/ppermute | solution.py:649
  16.2 2.3 %flux_sums.1 = (f32[1,240,256]{2,1,0:T(8,128)S(1)}, f32[3848,128]{1,0:T(8,128)S(1)}) custom-call(s32[3]{0:T(128)S(1)} %pad_add_fusion.place_ref, f32[1,256]{1,0:T(1,128)S(1)} %get-tuple-element.38.coupling_ref, f32[2,8,128]{2,1,0:T(8,128)S(1)} %collective-permute-done.1.left_ref, f32[2,8,128]{2,1,0:T(8,128)S(1)} %collective-permute-done.2.right_ref, ...), custom_call_target="tpu_custom_call" | custom-call | tf_op jit(solution)/shard_map/flux_sums/pallas_call | solution.py:469
  18.5 0.8 %collective-permute-done.4.refs_2_ = f32[2,120,128]{2,1,0:T(8,128)S(1)} collective-permute-done((f32[2,120,128]{2,1,0:T(8,128)S(1)}, f32[2,120,128]{2,1,0:T(8,128)S(1)}, u32[]{:S(2)}, u32[]{:S(2)}) %collective-permute-start.4) | collective-permute-done | bytes 122912 | tf_op jit(solution)/shard_map/ppermute | solution.py:549
  19.4 1.6 %collective-permute-start.9 = (f32[2,120,128]{2,1,0:T(8,128)S(1)}, f32[2,120,128]{2,1,0:T(8,128)S(1)}, u32[]{:S(2)}, u32[]{:S(2)}) collective-permute-start(f32[2,120,128]{2,1,0:T(8,128)S(1)} %get-tuple-element.68), channel_id=1, source_target_pairs={{0,24},{8,0},{16,8},{24,16},{1,25},{9,1},{17,9},{25,17},{2,26},{10... | collective-permute-start | bytes 368648 | tf_op jit(solution)/shard_map/ppermute | solution.py:549
  21.0 0.7 %kept_flux.1.mine_ref = f32[1,240,256]{2,1,0:T(8,128)S(1)} custom-call(s32[3]{0:T(128)S(1)} %pad_add_fusion.place_ref, f32[1,256]{1,0:T(1,128)S(1)} %get-tuple-element.38.coupling_ref, f32[3848,128]{1,0:T(8,128)S(1)} %get-tuple-element.61.solved_ref, f32[4,240,256]{2,1,0:T(8,128)S(1)} %get-tuple-element.62.weight_ref), custom_call_target="tpu_custom_call" | custom-call | flops 491520 | bytes 1966080 | tf_op jit(solution)/shard_map/kept_flux/pallas_call | solution.py:487
  21.7 0.3 %sort_flux.1 = (f32[1,120,128]{2,1,0:T(8,128)S(1)}, f32[1,120,128]{2,1,0:T(8,128)S(1)}, f32[1,120,128]{2,1,0:T(8,128)S(1)}, f32[1,120,128]{2,1,0:T(8,128)S(1)}) custom-call(f32[1,240,256]{2,1,0:T(8,128)S(1)} %collective-permute-done.5.theirs_ref, f32[1,240,256]{2,1,0:T(8,128)S(1)} %kept_flux.1.mine_ref, bf16[512,512]{1,0:T(8,128)(2,1)S(1)} %get-tuple-element.44.table_ref, ...), custom_call_target="tpu_custom_call" | custom-call | tf_op jit(solution)/shard_map/sort_flux/pallas_call | solution.py:533
  22.1 0.5 %collective-permute-start.6 = (f32[1,120,128]{2,1,0:T(8,128)S(1)}, f32[1,120,128]{2,1,0:T(8,128)S(1)}, u32[]{:S(2)}, u32[]{:S(2)}) collective-permute-start(f32[1,120,128]{2,1,0:T(8,128)S(1)} %get-tuple-element.64), channel_id=1, source_target_pairs={{0,8},{8,16},{16,24},{24,0},{1,9},{9,17},{17,25},{25,1},{2,10},{10... | collective-permute-start | bytes 184328 | tf_op jit(solution)/shard_map/ppermute | solution.py:549
  22.5 0.9 %collective-permute-start.7 = (f32[1,120,128]{2,1,0:T(8,128)S(1)}, f32[1,120,128]{2,1,0:T(8,128)S(1)}, u32[]{:S(2)}, u32[]{:S(2)}) collective-permute-start(f32[1,120,128]{2,1,0:T(8,128)S(1)} %get-tuple-element.65), channel_id=1, source_target_pairs={{0,16},{8,24},{16,0},{24,8},{1,17},{9,25},{17,1},{25,9},{2,18},{10... | collective-permute-start | bytes 184328 | tf_op jit(solution)/shard_map/ppermute | solution.py:549
  23.4 2.5 %collective-permute-start.8 = (f32[1,120,128]{2,1,0:T(8,128)S(1)}, f32[1,120,128]{2,1,0:T(8,128)S(1)}, u32[]{:S(2)}, u32[]{:S(2)}) collective-permute-start(f32[1,120,128]{2,1,0:T(8,128)S(1)} %get-tuple-element.66), channel_id=1, source_target_pairs={{0,24},{8,0},{16,8},{24,16},{1,25},{9,1},{17,9},{25,17},{2,26},{10... | collective-permute-start | bytes 184328 | tf_op jit(solution)/shard_map/ppermute | solution.py:549
  25.9 1.9 %end_weights.1 = (f32[240,256]{1,0:T(8,128)}, f32[3,240,256]{2,1,0:T(8,128)}) custom-call(s32[3]{0:T(128)S(1)} %pad_add_fusion.place_ref, bf16[512,512]{1,0:T(8,128)(2,1)S(1)} %get-tuple-element.48.table_ref, f32[2,120,128]{2,1,0:T(8,128)S(1)} %get-tuple-element.67.refs_0_, f32[2,120,128]{2,1,0:T(8,128)S(1)} %collective-permute-done.3.refs_1_, ...), custom_call_target="tpu_custom_call" | custom-call | flops 251658240 | bytes 1474560 | tf_op jit(solution)/shard_map/end_weights/pallas_call | solution.py:583
  27.8 1.0 %collective-permute-done.6.refs_1_ = f32[1,120,128]{2,1,0:T(8,128)S(1)} collective-permute-done((f32[1,120,128]{2,1,0:T(8,128)S(1)}, f32[1,120,128]{2,1,0:T(8,128)S(1)}, u32[]{:S(2)}, u32[]{:S(2)}) %collective-permute-start.6) | collective-permute-done | bytes 61472 | tf_op jit(solution)/shard_map/ppermute | solution.py:549
  28.8 1.8 %collective-permute-done.7.refs_2_ = f32[1,120,128]{2,1,0:T(8,128)S(1)} collective-permute-done((f32[1,120,128]{2,1,0:T(8,128)S(1)}, f32[1,120,128]{2,1,0:T(8,128)S(1)}, u32[]{:S(2)}, u32[]{:S(2)}) %collective-permute-start.7) | collective-permute-done | bytes 61472 | tf_op jit(solution)/shard_map/ppermute | solution.py:549
  30.6 1.0 %end_flux.1 = f32[240,256]{1,0:T(8,128)} custom-call(bf16[512,512]{1,0:T(8,128)(2,1)S(1)} %get-tuple-element.48.table_ref, f32[1,120,128]{2,1,0:T(8,128)S(1)} %get-tuple-element.63.refs_0_, f32[1,120,128]{2,1,0:T(8,128)S(1)} %collective-permute-done.6.refs_1_, f32[1,120,128]{2,1,0:T(8,128)S(1)} %collective-permute-done.7.refs_2_, ...), custom_call_target="tpu_custom_call" | custom-call | flops 125829120 | bytes 491520 | tf_op jit(solution)/shard_map/end_flux/pallas_call | solution.py:605
  (8 shorter events, 0.0 us)
Async XLA Ops:
  0.6 2.8 %copy-start = (f32[4,480,256]{2,1,0:T(8,128)S(1)}, f32[4,480,256]{2,1,0:T(8,128)}, u32[]{:S(2)}) copy-start(f32[4,480,256]{2,1,0:T(8,128)} %pixels_ref.3) | copy-start | bytes 5898244
  2.9 2.0 %collective-permute-start = (f32[2,240,256]{2,1,0:T(8,128)S(1)}, f32[2,240,256]{2,1,0:T(8,128)S(1)}, u32[]{:S(2)}, u32[]{:S(2)}) collective-permute-start(f32[2,240,256]{2,1,0:T(8,128)S(1)} %get-tuple-element.37), channel_id=1, source_target_pairs={{0,1},{1,0},{2,3},{3,2},{4,5},{5,4},{6,7},{7,6},{8,9},{9,8},{10,11... | collective-permute-start | bytes 1474568 | tf_op jit(solution)/shard_map/ppermute | solution.py:639
  5.4 13.1 %collective-permute-start.3 = (f32[2,120,128]{2,1,0:T(8,128)S(1)}, f32[2,120,128]{2,1,0:T(8,128)S(1)}, u32[]{:S(2)}, u32[]{:S(2)}) collective-permute-start(f32[2,120,128]{2,1,0:T(8,128)S(1)} %get-tuple-element.57), channel_id=1, source_target_pairs={{0,8},{8,16},{16,24},{24,0},{1,9},{9,17},{17,25},{25,1},{2,10},{10... | collective-permute-start | bytes 368648 | tf_op jit(solution)/shard_map/ppermute | solution.py:549
  8.4 10.9 %collective-permute-start.4 = (f32[2,120,128]{2,1,0:T(8,128)S(1)}, f32[2,120,128]{2,1,0:T(8,128)S(1)}, u32[]{:S(2)}, u32[]{:S(2)}) collective-permute-start(f32[2,120,128]{2,1,0:T(8,128)S(1)} %get-tuple-element.58), channel_id=1, source_target_pairs={{0,16},{8,24},{16,0},{24,8},{1,17},{9,25},{17,1},{25,9},{2,18},{10... | collective-permute-start | bytes 368648 | tf_op jit(solution)/shard_map/ppermute | solution.py:549
  11.0 4.6 %collective-permute-start.1 = (f32[2,8,128]{2,1,0:T(8,128)S(1)}, f32[2,8,128]{2,1,0:T(8,128)S(1)}, u32[]{:S(2)}, u32[]{:S(2)}) collective-permute-start(f32[2,8,128]{2,1,0:T(8,128)S(1)} %get-tuple-element.51), channel_id=1, source_target_pairs={{0,2},{2,4},{4,6},{6,0},{1,3},{3,5},{5,7},{7,1},{8,10},{10,12},{12... | collective-permute-start | bytes 24584 | tf_op jit(solution)/shard_map/ppermute | solution.py:648
  12.5 3.7 %collective-permute-start.2 = (f32[2,8,128]{2,1,0:T(8,128)S(1)}, f32[2,8,128]{2,1,0:T(8,128)S(1)}, u32[]{:S(2)}, u32[]{:S(2)}) collective-permute-start(f32[2,8,128]{2,1,0:T(8,128)S(1)} %get-tuple-element.52), channel_id=1, source_target_pairs={{2,0},{4,2},{6,4},{0,6},{3,1},{5,3},{7,5},{1,7},{10,8},{12,10},{14... | collective-permute-start | bytes 24584 | tf_op jit(solution)/shard_map/ppermute | solution.py:649
  19.3 2.4 %collective-permute-start.5 = (f32[1,240,256]{2,1,0:T(8,128)S(1)}, f32[1,240,256]{2,1,0:T(8,128)S(1)}, u32[]{:S(2)}, u32[]{:S(2)}) collective-permute-start(f32[1,240,256]{2,1,0:T(8,128)S(1)} %get-tuple-element.59), channel_id=1, source_target_pairs={{0,1},{1,0},{2,3},{3,2},{4,5},{5,4},{6,7},{7,6},{8,9},{9,8},{10,11... | collective-permute-start | bytes 737288 | tf_op jit(solution)/shard_map/ppermute | solution.py:654
  19.4 6.6 %collective-permute-start.9 = (f32[2,120,128]{2,1,0:T(8,128)S(1)}, f32[2,120,128]{2,1,0:T(8,128)S(1)}, u32[]{:S(2)}, u32[]{:S(2)}) collective-permute-start(f32[2,120,128]{2,1,0:T(8,128)S(1)} %get-tuple-element.68), channel_id=1, source_target_pairs={{0,24},{8,0},{16,8},{24,16},{1,25},{9,1},{17,9},{25,17},{2,26},{10... | collective-permute-start | bytes 368648 | tf_op jit(solution)/shard_map/ppermute | solution.py:549
  22.1 6.7 %collective-permute-start.6 = (f32[1,120,128]{2,1,0:T(8,128)S(1)}, f32[1,120,128]{2,1,0:T(8,128)S(1)}, u32[]{:S(2)}, u32[]{:S(2)}) collective-permute-start(f32[1,120,128]{2,1,0:T(8,128)S(1)} %get-tuple-element.64), channel_id=1, source_target_pairs={{0,8},{8,16},{16,24},{24,0},{1,9},{9,17},{17,25},{25,1},{2,10},{10... | collective-permute-start | bytes 184328 | tf_op jit(solution)/shard_map/ppermute | solution.py:549
  22.5 8.1 %collective-permute-start.7 = (f32[1,120,128]{2,1,0:T(8,128)S(1)}, f32[1,120,128]{2,1,0:T(8,128)S(1)}, u32[]{:S(2)}, u32[]{:S(2)}) collective-permute-start(f32[1,120,128]{2,1,0:T(8,128)S(1)} %get-tuple-element.65), channel_id=1, source_target_pairs={{0,16},{8,24},{16,0},{24,8},{1,17},{9,25},{17,1},{25,9},{2,18},{10... | collective-permute-start | bytes 184328 | tf_op jit(solution)/shard_map/ppermute | solution.py:549
  23.4 7.1 %collective-permute-start.8 = (f32[1,120,128]{2,1,0:T(8,128)S(1)}, f32[1,120,128]{2,1,0:T(8,128)S(1)}, u32[]{:S(2)}, u32[]{:S(2)}) collective-permute-start(f32[1,120,128]{2,1,0:T(8,128)S(1)} %get-tuple-element.66), channel_id=1, source_target_pairs={{0,24},{8,0},{16,8},{24,16},{1,25},{9,1},{17,9},{25,17},{2,26},{10... | collective-permute-start | bytes 184328 | tf_op jit(solution)/shard_map/ppermute | solution.py:549

commit v7 on v6

--- a/solution.py
+++ b/solution.py
@@ -507,7 +507,7 @@
     part = rows // pack
     totals = [mine_ref[v] + theirs_ref[v] for v in range(values)]
     if scaled:
-        scale_ref, *out_refs = refs
+        scale_ref, _, *out_refs = refs
         totals = [t * scale_ref[...] for t in totals]
     else:
         *out_refs, scale_ref = refs
@@ -524,12 +524,12 @@
             out_ref[v] = moved[v * part : (v + 1) * part, d * lanes : (d + 1) * lanes]
 
 
-def sort_fibres(theirs, mine, table, pack, pieces, scale=None):
+def sort_fibres(theirs, mine, table, pack, pieces, scale=None, ahead=None):
     values, rows, fibres = mine.shape
     lanes = table.shape[0] // pieces
     scaled = scale is not None
     outs = [shaped((values, rows // pack, lanes))] * pieces + ([] if scaled else [shaped((rows, fibres))])
-    args = (theirs, mine, table) + ((scale,) if scaled else ())
+    args = (theirs, mine, table) + ((scale, ahead) if scaled else ())
     return pl.pallas_call(
         functools.partial(sort_kernel, pack, scaled),
         in_specs=[in_vmem] * len(args),
@@ -640,20 +640,18 @@
     mine, weight_m, up, down = kept_weights(
         wav_count, place, coupling, counts, good, pixels, ivar, bits
     )
-    *sorted_pieces, scale = sort_fibres(arriving, mine, send_table, pack, pieces)
-    weight_pieces = exchange(sorted_pieces, fib_count)
-
-    up, down = after((up, down), scale)
     upward = [(i, (i + 1) % wav_count) for i in range(wav_count)]
     left = lax.ppermute(up, "wav", upward)
     right = lax.ppermute(down, "wav", [(j, i) for i, j in upward])
+    *sorted_pieces, scale = sort_fibres(arriving, mine, send_table, pack, pieces)
+    weight_pieces = exchange(sorted_pieces, fib_count)
+
     recv_table, pixel_s, ivar_s = stream_layout(moves, after(place, scale), slots, pixels, ivar)
     theirs, solved = flux_sums(wav_count, place, coupling, left, right, pixel_s, ivar_s, weight_t)
-    if rel:
-        theirs = after(theirs, weight_pieces[1:-1])
+    ahead = sum(piece[0, :ROWS, :] for piece in weight_pieces[1:] or weight_pieces)
     arriving = lax.ppermute(theirs, "exp", swap)
     mine = kept_flux(after(place, theirs), coupling, solved, weight_m)
-    flux_pieces = exchange(sort_fibres(arriving, mine, send_table, pack, pieces, scale), fib_count)
+    flux_pieces = exchange(sort_fibres(arriving, mine, send_table, pack, pieces, scale, ahead), fib_count)
 
     ivar, res = end_weights(place, recv_table, weight_pieces, pack, fibres, total)
     flux = end_flux(recv_table, flux_pieces, pack, fibres)

time: 31.8 us -> 31.4 us (0.987)
  waiting for transfers between devices: 4.47 us -> 3.68 us
  starting transfers between devices: 14.5 us -> 14.9 us
    ppermute x6, waiting for transfers between devices: 3.56 us -> 2.78 us  [exchange(): lax.ppermute(pieces[d], 'fib', [(i, (i + d) % fib_count) for i in range(f...]
  transfers between devices with their start and end apart: 10 -> 10, of which waited for: 5 -> 4; matrix products, arithmetic and copies ran while one was open for 0% -> 0% of each run, Pallas kernels for 26% -> 25%
where the time goes in v7:
time: 31.4 us; the launch traced here: 31.2 us
  starting transfers between devices  14.9 us (47%)
  Pallas kernels  11.8 us (38%)
  waiting for transfers between devices  3.68 us (12%)
  between operations  0.72 us (2%)
    ppermute x6, starting transfers between devices, exchange(): lax.ppermute(pieces[d], 'fib', [(i, (i + d) % fib_count) for i in range(f...  11.4 us
    ppermute x6, waiting for transfers between devices, exchange(): lax.ppermute(pieces[d], 'fib', [(i, (i + d) % fib_count) for i in range(f...  2.78 us
    pallas_call x1, Pallas kernels, flux_sums(): pl.pallas_call(functools.partial(solve_kernel, wav_count), in_specs=[in_s...  2.34 us
    pallas_call x1, Pallas kernels, sent_weights(): pl.pallas_call(functools.partial(sent_kernel, moves, wav_count), in_specs...  2.22 us
    pallas_call x1, Pallas kernels, end_weights(): pl.pallas_call(functools.partial(weights_end_kernel, pack, total), in_spe...  1.91 us
    pallas_call x1, Pallas kernels, stream_layout(): pl.pallas_call(functools.partial(layout_kernel, moves), in_specs=[in_smem...  1.65 us
    ppermute x1, starting transfers between devices, per_device(): left = lax.ppermute(up, 'wav', upward)  1.49 us
    ppermute x1, starting transfers between devices, per_device(): right = lax.ppermute(down, 'wav', [(j, i) for i, j in upward])  1.43 us
  transfers between devices with their start and end apart: 10, of which 4 were waited for; matrix products, arithmetic and copies ran while one was open for 0% of the time, Pallas kernels for 25%

profile of v7, /device:TPU:0, one launch (start us, length us, event | category | flops | bytes accessed | tf_op | source)
XLA Modules:
  0.0 31.2 jit_solution(10391218546705018315)
XLA Ops:
  0.6 0.1 pad_add_fusion.place_ref
  0.7 2.2 %sent_weights.1 = (f32[2,240,256]{2,1,0:T(8,128)S(1)}, f32[4,240,256]{2,1,0:T(8,128)S(1)}, bf16[512,512]{1,0:T(8,128)(2,1)S(1)}, s32[1,1024]{1,0:T(1,128)S(1)}, ...) custom-call(s32[3]{0:T(128)S(1)} %pad_add_fusion.place_ref, ...), custom_call_target="tpu_custom_call" | custom-call | flops 9830400 | bytes 2949120 | tf_op jit(solution)/shard_map/sent_weights/pallas_call | solution.py:263
  2.9 0.5 %collective-permute-start = (f32[2,240,256]{2,1,0:T(8,128)S(1)}, f32[2,240,256]{2,1,0:T(8,128)S(1)}, u32[]{:S(2)}, u32[]{:S(2)}) collective-permute-start(f32[2,240,256]{2,1,0:T(8,128)S(1)} %get-tuple-element.34), channel_id=1, source_target_pairs={{0,1},{1,0},{2,3},{3,2},{4,5},{5,4},{6,7},{7,6},{8,9},{9,8},{10,11... | collective-permute-start | bytes 1474568 | tf_op jit(solution)/shard_map/ppermute | solution.py:639
  3.5 1.1 %kept_weights.1 = (f32[2,240,256]{2,1,0:T(8,128)S(1)}, f32[4,240,256]{2,1,0:T(8,128)S(1)}, f32[2,8,128]{2,1,0:T(8,128)S(1)}, f32[2,8,128]{2,1,0:T(8,128)S(1)}) custom-call(s32[3]{0:T(128)S(1)} %pad_add_fusion.place_ref, f32[1,256]{1,0:T(1,128)S(1)} %get-tuple-element.35.coupling_ref, s32[1,256]{1,0:T(1,128)S(1)} %get-tuple-element.36.counts_ref, ...), custom_call_target="tpu_custom_call" | custom-call | flops 9830400 | bytes 2949120 | tf_op jit(solution)/shard_map/kept_weights/pallas_call | solution.py:336
  4.6 0.4 %collective-permute-done.theirs_ref = f32[2,240,256]{2,1,0:T(8,128)S(1)} collective-permute-done((f32[2,240,256]{2,1,0:T(8,128)S(1)}, f32[2,240,256]{2,1,0:T(8,128)S(1)}, u32[]{:S(2)}, u32[]{:S(2)}) %collective-permute-start) | collective-permute-done | bytes 491552 | tf_op jit(solution)/shard_map/ppermute | solution.py:639
  5.0 0.5 %sort_weights.1 = (f32[2,120,128]{2,1,0:T(8,128)S(1)}, f32[2,120,128]{2,1,0:T(8,128)S(1)}, f32[2,120,128]{2,1,0:T(8,128)S(1)}, f32[2,120,128]{2,1,0:T(8,128)S(1)}, f32[240,256]{1,0:T(8,128)S(1)}) custom-call(f32[2,240,256]{2,1,0:T(8,128)S(1)} %collective-permute-done.theirs_ref, f32[2,240,256]{2,1,0:T(8,128)S(1)} %get-tuple-element.40.mine_ref, ...), custom_call_target="tpu_custom_call" | custom-call | tf_op jit(solution)/shard_map/sort_weights/pallas_call | solution.py:533
  5.4 5.0 %collective-permute-start.6 = (f32[2,120,128]{2,1,0:T(8,128)S(1)}, f32[2,120,128]{2,1,0:T(8,128)S(1)}, u32[]{:S(2)}, u32[]{:S(2)}) collective-permute-start(f32[2,120,128]{2,1,0:T(8,128)S(1)} %get-tuple-element.57), channel_id=1, source_target_pairs={{0,24},{8,0},{16,8},{24,16},{1,25},{9,1},{17,9},{25,17},{2,26},{10... | collective-permute-start | bytes 368648 | tf_op jit(solution)/shard_map/ppermute | solution.py:549
  10.4 1.0 %collective-permute-start.4 = (f32[2,120,128]{2,1,0:T(8,128)S(1)}, f32[2,120,128]{2,1,0:T(8,128)S(1)}, u32[]{:S(2)}, u32[]{:S(2)}) collective-permute-start(f32[2,120,128]{2,1,0:T(8,128)S(1)} %get-tuple-element.55), channel_id=1, source_target_pairs={{0,8},{8,16},{16,24},{24,0},{1,9},{9,17},{17,25},{25,1},{2,10},{10... | collective-permute-start | bytes 368648 | tf_op jit(solution)/shard_map/ppermute | solution.py:549
  11.5 1.5 %collective-permute-start.1 = (f32[2,8,128]{2,1,0:T(8,128)S(1)}, f32[2,8,128]{2,1,0:T(8,128)S(1)}, u32[]{:S(2)}, u32[]{:S(2)}) collective-permute-start(f32[2,8,128]{2,1,0:T(8,128)S(1)} %get-tuple-element.46), channel_id=1, source_target_pairs={{0,2},{2,4},{4,6},{6,0},{1,3},{3,5},{5,7},{7,1},{8,10},{10,12},{12... | collective-permute-start | bytes 24584 | tf_op jit(solution)/shard_map/ppermute | solution.py:644
  13.0 1.4 %collective-permute-start.2 = (f32[2,8,128]{2,1,0:T(8,128)S(1)}, f32[2,8,128]{2,1,0:T(8,128)S(1)}, u32[]{:S(2)}, u32[]{:S(2)}) collective-permute-start(f32[2,8,128]{2,1,0:T(8,128)S(1)} %get-tuple-element.47), channel_id=1, source_target_pairs={{2,0},{4,2},{6,4},{0,6},{3,1},{5,3},{7,5},{1,7},{10,8},{12,10},{14... | collective-permute-start | bytes 24584 | tf_op jit(solution)/shard_map/ppermute | solution.py:645
  14.4 1.7 %stream_layout.1 = (bf16[512,512]{1,0:T(8,128)(2,1)S(1)}, f32[3848,128]{1,0:T(8,128)S(1)}, f32[3848,128]{1,0:T(8,128)S(1)}) custom-call(s32[3]{0:T(128)S(1)} %pad_add_fusion.place_ref, s32[1,1024]{1,0:T(1,128)S(1)} %get-tuple-element.44.slots_ref, f32[4,480,256]{2,1,0:T(8,128)S(1)} %copy-done, f32[4,480,256]{2,1,0:T(8,128)S(1)} %get-tuple-element.38.ivar_ref), custom_call_target="tpu_custom_call" | custom-call | bytes 7864320 | tf_op jit(solution)/shard_map/stream_layout/pallas_call | solution.py:360
  16.0 0.0 collective-permute-done.1.left_ref
  16.1 0.5 %collective-permute-done.2.right_ref = f32[2,8,128]{2,1,0:T(8,128)S(1)} collective-permute-done((f32[2,8,128]{2,1,0:T(8,128)S(1)}, f32[2,8,128]{2,1,0:T(8,128)S(1)}, u32[]{:S(2)}, u32[]{:S(2)}) %collective-permute-start.2) | collective-permute-done | bytes 8224 | tf_op jit(solution)/shard_map/ppermute | solution.py:645
  16.6 2.3 %flux_sums.1 = (f32[1,240,256]{2,1,0:T(8,128)S(1)}, f32[3848,128]{1,0:T(8,128)S(1)}) custom-call(s32[3]{0:T(128)S(1)} %pad_add_fusion.place_ref, f32[1,256]{1,0:T(1,128)S(1)} %get-tuple-element.35.coupling_ref, f32[2,8,128]{2,1,0:T(8,128)S(1)} %collective-permute-done.1.left_ref, f32[2,8,128]{2,1,0:T(8,128)S(1)} %collective-permute-done.2.right_ref, ...), custom_call_target="tpu_custom_call" | custom-call | tf_op jit(solution)/shard_map/flux_sums/pallas_call | solution.py:469
  18.9 0.1 collective-permute-start.3
  19.0 0.7 %kept_flux.1.mine_ref = f32[1,240,256]{2,1,0:T(8,128)S(1)} custom-call(s32[3]{0:T(128)S(1)} %pad_add_fusion.place_ref, f32[1,256]{1,0:T(1,128)S(1)} %get-tuple-element.35.coupling_ref, f32[3848,128]{1,0:T(8,128)S(1)} %get-tuple-element.53.solved_ref, f32[4,240,256]{2,1,0:T(8,128)S(1)} %get-tuple-element.54.weight_ref), custom_call_target="tpu_custom_call" | custom-call | flops 491520 | bytes 1966080 | tf_op jit(solution)/shard_map/kept_flux/pallas_call | solution.py:487
  19.8 1.7 %collective-permute-done.5.refs_2_ = f32[2,120,128]{2,1,0:T(8,128)S(1)} collective-permute-done((f32[2,120,128]{2,1,0:T(8,128)S(1)}, f32[2,120,128]{2,1,0:T(8,128)S(1)}, u32[]{:S(2)}, u32[]{:S(2)}) %collective-permute-start.5) | collective-permute-done | bytes 122912 | tf_op jit(solution)/shard_map/ppermute | solution.py:549
  21.5 0.3 %sort_flux.1 = (f32[1,120,128]{2,1,0:T(8,128)S(1)}, f32[1,120,128]{2,1,0:T(8,128)S(1)}, f32[1,120,128]{2,1,0:T(8,128)S(1)}, f32[1,120,128]{2,1,0:T(8,128)S(1)}) custom-call(f32[1,240,256]{2,1,0:T(8,128)S(1)} %collective-permute-done.3.theirs_ref, f32[1,240,256]{2,1,0:T(8,128)S(1)} %kept_flux.1.mine_ref, bf16[512,512]{1,0:T(8,128)(2,1)S(1)} %get-tuple-element.41.table_ref, ...), custom_call_target="tpu_custom_call" | custom-call | tf_op jit(solution)/shard_map/sort_flux/pallas_call | solution.py:533
  21.9 1.5 %collective-permute-start.7 = (f32[1,120,128]{2,1,0:T(8,128)S(1)}, f32[1,120,128]{2,1,0:T(8,128)S(1)}, u32[]{:S(2)}, u32[]{:S(2)}) collective-permute-start(f32[1,120,128]{2,1,0:T(8,128)S(1)} %get-tuple-element.59), channel_id=1, source_target_pairs={{0,8},{8,16},{16,24},{24,0},{1,9},{9,17},{17,25},{25,1},{2,10},{10... | collective-permute-start | bytes 184328 | tf_op jit(solution)/shard_map/ppermute | solution.py:549
  23.4 1.0 %collective-permute-start.8 = (f32[1,120,128]{2,1,0:T(8,128)S(1)}, f32[1,120,128]{2,1,0:T(8,128)S(1)}, u32[]{:S(2)}, u32[]{:S(2)}) collective-permute-start(f32[1,120,128]{2,1,0:T(8,128)S(1)} %get-tuple-element.60), channel_id=1, source_target_pairs={{0,16},{8,24},{16,0},{24,8},{1,17},{9,25},{17,1},{25,9},{2,18},{10... | collective-permute-start | bytes 184328 | tf_op jit(solution)/shard_map/ppermute | solution.py:549
  24.4 2.8 %collective-permute-start.9 = (f32[1,120,128]{2,1,0:T(8,128)S(1)}, f32[1,120,128]{2,1,0:T(8,128)S(1)}, u32[]{:S(2)}, u32[]{:S(2)}) collective-permute-start(f32[1,120,128]{2,1,0:T(8,128)S(1)} %get-tuple-element.61), channel_id=1, source_target_pairs={{0,24},{8,0},{16,8},{24,16},{1,25},{9,1},{17,9},{25,17},{2,26},{10... | collective-permute-start | bytes 184328 | tf_op jit(solution)/shard_map/ppermute | solution.py:549
  27.2 1.9 %end_weights.1 = (f32[240,256]{1,0:T(8,128)}, f32[3,240,256]{2,1,0:T(8,128)}) custom-call(s32[3]{0:T(128)S(1)} %pad_add_fusion.place_ref, bf16[512,512]{1,0:T(8,128)(2,1)S(1)} %get-tuple-element.45.table_ref, f32[2,120,128]{2,1,0:T(8,128)S(1)} %get-tuple-element.62.refs_0_, f32[2,120,128]{2,1,0:T(8,128)S(1)} %collective-permute-done.4.refs_1_, ...), custom_call_target="tpu_custom_call" | custom-call | flops 251658240 | bytes 1474560 | tf_op jit(solution)/shard_map/end_weights/pallas_call | solution.py:583
  29.1 1.0 %collective-permute-done.8.refs_2_ = f32[1,120,128]{2,1,0:T(8,128)S(1)} collective-permute-done((f32[1,120,128]{2,1,0:T(8,128)S(1)}, f32[1,120,128]{2,1,0:T(8,128)S(1)}, u32[]{:S(2)}, u32[]{:S(2)}) %collective-permute-start.8) | collective-permute-done | bytes 61472 | tf_op jit(solution)/shard_map/ppermute | solution.py:549
  30.2 1.0 %end_flux.1 = f32[240,256]{1,0:T(8,128)} custom-call(bf16[512,512]{1,0:T(8,128)(2,1)S(1)} %get-tuple-element.45.table_ref, f32[1,120,128]{2,1,0:T(8,128)S(1)} %get-tuple-element.58.refs_0_, f32[1,120,128]{2,1,0:T(8,128)S(1)} %collective-permute-done.7.refs_1_, f32[1,120,128]{2,1,0:T(8,128)S(1)} %collective-permute-done.8.refs_2_, ...), custom_call_target="tpu_custom_call" | custom-call | flops 125829120 | bytes 491520 | tf_op jit(solution)/shard_map/end_flux/pallas_call | solution.py:605
  (9 shorter events, 0.0 us)
Async XLA Ops:
  0.6 2.8 %copy-start = (f32[4,480,256]{2,1,0:T(8,128)S(1)}, f32[4,480,256]{2,1,0:T(8,128)}, u32[]{:S(2)}) copy-start(f32[4,480,256]{2,1,0:T(8,128)} %pixels_ref.3) | copy-start | bytes 5898244
  2.9 2.0 %collective-permute-start = (f32[2,240,256]{2,1,0:T(8,128)S(1)}, f32[2,240,256]{2,1,0:T(8,128)S(1)}, u32[]{:S(2)}, u32[]{:S(2)}) collective-permute-start(f32[2,240,256]{2,1,0:T(8,128)S(1)} %get-tuple-element.34), channel_id=1, source_target_pairs={{0,1},{1,0},{2,3},{3,2},{4,5},{5,4},{6,7},{7,6},{8,9},{9,8},{10,11... | collective-permute-start | bytes 1474568 | tf_op jit(solution)/shard_map/ppermute | solution.py:639
  5.4 14.3 %collective-permute-start.6 = (f32[2,120,128]{2,1,0:T(8,128)S(1)}, f32[2,120,128]{2,1,0:T(8,128)S(1)}, u32[]{:S(2)}, u32[]{:S(2)}) collective-permute-start(f32[2,120,128]{2,1,0:T(8,128)S(1)} %get-tuple-element.57), channel_id=1, source_target_pairs={{0,24},{8,0},{16,8},{24,16},{1,25},{9,1},{17,9},{25,17},{2,26},{10... | collective-permute-start | bytes 368648 | tf_op jit(solution)/shard_map/ppermute | solution.py:549
  10.4 11.1 %collective-permute-start.5 = (f32[2,120,128]{2,1,0:T(8,128)S(1)}, f32[2,120,128]{2,1,0:T(8,128)S(1)}, u32[]{:S(2)}, u32[]{:S(2)}) collective-permute-start(f32[2,120,128]{2,1,0:T(8,128)S(1)} %get-tuple-element.56), channel_id=1, source_target_pairs={{0,16},{8,24},{16,0},{24,8},{1,17},{9,25},{17,1},{25,9},{2,18},{10... | collective-permute-start | bytes 368648 | tf_op jit(solution)/shard_map/ppermute | solution.py:549
  10.4 11.1 %collective-permute-start.4 = (f32[2,120,128]{2,1,0:T(8,128)S(1)}, f32[2,120,128]{2,1,0:T(8,128)S(1)}, u32[]{:S(2)}, u32[]{:S(2)}) collective-permute-start(f32[2,120,128]{2,1,0:T(8,128)S(1)} %get-tuple-element.55), channel_id=1, source_target_pairs={{0,8},{8,16},{16,24},{24,0},{1,9},{9,17},{17,25},{25,1},{2,10},{10... | collective-permute-start | bytes 368648 | tf_op jit(solution)/shard_map/ppermute | solution.py:549
  11.5 4.6 %collective-permute-start.1 = (f32[2,8,128]{2,1,0:T(8,128)S(1)}, f32[2,8,128]{2,1,0:T(8,128)S(1)}, u32[]{:S(2)}, u32[]{:S(2)}) collective-permute-start(f32[2,8,128]{2,1,0:T(8,128)S(1)} %get-tuple-element.46), channel_id=1, source_target_pairs={{0,2},{2,4},{4,6},{6,0},{1,3},{3,5},{5,7},{7,1},{8,10},{10,12},{12... | collective-permute-start | bytes 24584 | tf_op jit(solution)/shard_map/ppermute | solution.py:644
  13.0 3.7 %collective-permute-start.2 = (f32[2,8,128]{2,1,0:T(8,128)S(1)}, f32[2,8,128]{2,1,0:T(8,128)S(1)}, u32[]{:S(2)}, u32[]{:S(2)}) collective-permute-start(f32[2,8,128]{2,1,0:T(8,128)S(1)} %get-tuple-element.47), channel_id=1, source_target_pairs={{2,0},{4,2},{6,4},{0,6},{3,1},{5,3},{7,5},{1,7},{10,8},{12,10},{14... | collective-permute-start | bytes 24584 | tf_op jit(solution)/shard_map/ppermute | solution.py:645
  18.9 2.6 %collective-permute-start.3 = (f32[1,240,256]{2,1,0:T(8,128)S(1)}, f32[1,240,256]{2,1,0:T(8,128)S(1)}, u32[]{:S(2)}, u32[]{:S(2)}) collective-permute-start(f32[1,240,256]{2,1,0:T(8,128)S(1)} %get-tuple-element.51), channel_id=1, source_target_pairs={{0,1},{1,0},{2,3},{3,2},{4,5},{5,4},{6,7},{7,6},{8,9},{9,8},{10,11... | collective-permute-start | bytes 737288 | tf_op jit(solution)/shard_map/ppermute | solution.py:652
  21.9 7.3 %collective-permute-start.7 = (f32[1,120,128]{2,1,0:T(8,128)S(1)}, f32[1,120,128]{2,1,0:T(8,128)S(1)}, u32[]{:S(2)}, u32[]{:S(2)}) collective-permute-start(f32[1,120,128]{2,1,0:T(8,128)S(1)} %get-tuple-element.59), channel_id=1, source_target_pairs={{0,8},{8,16},{16,24},{24,0},{1,9},{9,17},{17,25},{25,1},{2,10},{10... | collective-permute-start | bytes 184328 | tf_op jit(solution)/shard_map/ppermute | solution.py:549
  23.4 6.8 %collective-permute-start.8 = (f32[1,120,128]{2,1,0:T(8,128)S(1)}, f32[1,120,128]{2,1,0:T(8,128)S(1)}, u32[]{:S(2)}, u32[]{:S(2)}) collective-permute-start(f32[1,120,128]{2,1,0:T(8,128)S(1)} %get-tuple-element.60), channel_id=1, source_target_pairs={{0,16},{8,24},{16,0},{24,8},{1,17},{9,25},{17,1},{25,9},{2,18},{10... | collective-permute-start | bytes 184328 | tf_op jit(solution)/shard_map/ppermute | solution.py:549
  24.4 5.8 %collective-permute-start.9 = (f32[1,120,128]{2,1,0:T(8,128)S(1)}, f32[1,120,128]{2,1,0:T(8,128)S(1)}, u32[]{:S(2)}, u32[]{:S(2)}) collective-permute-start(f32[1,120,128]{2,1,0:T(8,128)S(1)} %get-tuple-element.61), channel_id=1, source_target_pairs={{0,24},{8,0},{16,8},{24,16},{1,25},{9,1},{17,9},{25,17},{2,26},{10... | collective-permute-start | bytes 184328 | tf_op jit(solution)/shard_map/ppermute | solution.py:549

commit v8 on v7

--- a/solution.py
+++ b/solution.py
@@ -345,27 +345,42 @@
     )(place, coupling, counts, good, pixels, ivar, bits)
 
 
-def layout_kernel(moves, place_ref, slots_ref, pixels_ref, ivar_ref, table_ref, pixel_out, ivar_out):
+def layout_kernel(arrived_ref, pixels_ref, ivar_ref, pixel_out, ivar_out):
     width = ivar_ref.shape[1]
     lay_out(ivar_ref, ivar_out, [(0, width, 0)], odd(width))
     lay_out(pixels_ref, pixel_out, [(0, width, 0)], odd(width))
-    write_recv_table(*moves, place_ref[0], slots_ref, table_ref)
-
-
-def stream_layout(moves, place, slots, pixels, ivar):
+
+
+def stream_layout(arrived, pixels, ivar):
     expos, width, fibres = ivar.shape
     streams = expos * fibres // LANES
-    fib_count, pack, per, _ = moves
     laid = shaped((streams * odd(width), LANES))
     return pl.pallas_call(
-        functools.partial(layout_kernel, moves),
-        in_specs=[in_smem] + [in_vmem] * 3,
-        out_specs=[in_vmem] * 3,
-        out_shape=[shaped((pack * fibres, fib_count * pack * per), BF16), laid, laid],
+        layout_kernel,
+        in_specs=[in_vmem] * 3,
+        out_specs=[in_vmem] * 2,
+        out_shape=[laid, laid],
         compiler_params=params(),
         cost_estimate=cost(0, 16 * ivar.size),
         name="stream_layout",
-    )(place, slots, pixels, ivar)
+    )(arrived, pixels, ivar)
+
+
+def recv_kernel(moves, place_ref, slots_ref, table_ref):
+    write_recv_table(*moves, place_ref[0], slots_ref, table_ref)
+
+
+def recv_moves(moves, place, slots, fibres):
+    fib_count, pack, per, _ = moves
+    return pl.pallas_call(
+        functools.partial(recv_kernel, moves),
+        in_specs=[in_smem, in_vmem],
+        out_specs=in_vmem,
+        out_shape=shaped((pack * fibres, fib_count * pack * per), BF16),
+        compiler_params=params(),
+        cost_estimate=cost(1e6, 1e6),
+        name="recv_moves",
+    )(place, slots)
 
 
 def solve_kernel(
@@ -646,12 +661,14 @@
     *sorted_pieces, scale = sort_fibres(arriving, mine, send_table, pack, pieces)
     weight_pieces = exchange(sorted_pieces, fib_count)
 
-    recv_table, pixel_s, ivar_s = stream_layout(moves, after(place, scale), slots, pixels, ivar)
+    pixel_s, ivar_s = stream_layout(left[0] + right[0], pixels, ivar)
     theirs, solved = flux_sums(wav_count, place, coupling, left, right, pixel_s, ivar_s, weight_t)
-    ahead = sum(piece[0, :ROWS, :] for piece in weight_pieces[1:] or weight_pieces)
+    ahead = sum(piece[0, :ROWS, :] for piece in weight_pieces[1:-1] or weight_pieces)
     arriving = lax.ppermute(theirs, "exp", swap)
     mine = kept_flux(after(place, theirs), coupling, solved, weight_m)
-    flux_pieces = exchange(sort_fibres(arriving, mine, send_table, pack, pieces, scale, ahead), fib_count)
+    sorted_pieces = sort_fibres(arriving, mine, send_table, pack, pieces, scale, ahead)
+    flux_pieces = exchange(sorted_pieces, fib_count)
+    recv_table = recv_moves(moves, after(place, sorted_pieces[0]), slots, fibres)
 
     ivar, res = end_weights(place, recv_table, weight_pieces, pack, fibres, total)
     flux = end_flux(recv_table, flux_pieces, pack, fibres)

time: 31.4 us -> 31.3 us (level)
  starting transfers between devices: 14.9 us -> 14.1 us
  waiting for transfers between devices: 3.68 us -> 4.39 us
    ppermute x6, waiting for transfers between devices: 2.78 us -> 4.38 us  [exchange(): lax.ppermute(pieces[d], 'fib', [(i, (i + d) % fib_count) for i in range(f...]
    ppermute x6, starting transfers between devices: 11.4 us -> 9.9 us  [exchange(): lax.ppermute(pieces[d], 'fib', [(i, (i + d) % fib_count) for i in range(f...]
    ppermute x1, starting transfers between devices: 1.49 us -> 2.56 us  [per_device(): left = lax.ppermute(up, 'wav', upward)]
    ppermute x1, waiting for transfers between devices: 0.55 us -> 0.01 us  [per_device(): right = lax.ppermute(down, 'wav', [(j, i) for i, j in upward])]
    ppermute x1, starting transfers between devices: 1.43 us -> 1.02 us  [per_device(): right = lax.ppermute(down, 'wav', [(j, i) for i, j in upward])]
    ppermute x2, waiting for transfers between devices: 0.36 us -> 0.01 us  [per_device(): arriving = lax.ppermute(theirs, 'exp', swap)]
    pallas_call x1 -> x2, Pallas kernels: 1.65 us -> 1.66 us  [the longest x1 1.4 us: recv_moves(): pl.pallas_call(functools.partial(recv_kernel, moves), in_specs=[in_smem,...]
  transfers between devices with their start and end apart: 10 -> 10, of which waited for: 4 -> 2; matrix products, arithmetic and copies ran while one was open for 0% -> 0% of each run, Pallas kernels for 25% -> 28%
where the time goes in v8:
time: 31.3 us; the launch traced here: 31.1 us
  starting transfers between devices  14.1 us (45%)
  Pallas kernels  11.8 us (38%)
  waiting for transfers between devices  4.39 us (14%)
  between operations  0.73 us (2%)
    ppermute x6, starting transfers between devices, exchange(): lax.ppermute(pieces[d], 'fib', [(i, (i + d) % fib_count) for i in range(f...  9.9 us
    ppermute x6, waiting for transfers between devices, exchange(): lax.ppermute(pieces[d], 'fib', [(i, (i + d) % fib_count) for i in range(f...  4.38 us
    ppermute x1, starting transfers between devices, per_device(): left = lax.ppermute(up, 'wav', upward)  2.56 us
    pallas_call x1, Pallas kernels, flux_sums(): pl.pallas_call(functools.partial(solve_kernel, wav_count), in_specs=[in_s...  2.34 us
    pallas_call x1, Pallas kernels, sent_weights(): pl.pallas_call(functools.partial(sent_kernel, moves, wav_count), in_specs...  2.22 us
    pallas_call x1, Pallas kernels, end_weights(): pl.pallas_call(functools.partial(weights_end_kernel, pack, total), in_spe...  1.91 us
    pallas_call x1, Pallas kernels, recv_moves(): pl.pallas_call(functools.partial(recv_kernel, moves), in_specs=[in_smem,...  1.4 us
    pallas_call x1, Pallas kernels, kept_weights(): pl.pallas_call(functools.partial(kept_kernel, wav_count), in_specs=[in_sm...  1.14 us
  transfers between devices with their start and end apart: 10, of which 2 were waited for; matrix products, arithmetic and copies ran while one was open for 0% of the time, Pallas kernels for 28%

profile of v8, /device:TPU:0, one launch (start us, length us, event | category | flops | bytes accessed | tf_op | source)
XLA Modules:
  0.0 31.1 jit_solution(17160750847961644472)
XLA Ops:
  0.6 0.1 pad_add_fusion.place_ref
  0.7 2.2 %sent_weights.1 = (f32[2,240,256]{2,1,0:T(8,128)S(1)}, f32[4,240,256]{2,1,0:T(8,128)S(1)}, bf16[512,512]{1,0:T(8,128)(2,1)S(1)}, s32[1,1024]{1,0:T(1,128)S(1)}, ...) custom-call(s32[3]{0:T(128)S(1)} %pad_add_fusion.place_ref, ...), custom_call_target="tpu_custom_call" | custom-call | flops 9830400 | bytes 2949120 | tf_op jit(solution)/shard_map/sent_weights/pallas_call | solution.py:263
  2.9 0.5 %collective-permute-start.3 = (f32[2,240,256]{2,1,0:T(8,128)S(1)}, f32[2,240,256]{2,1,0:T(8,128)S(1)}, u32[]{:S(2)}, u32[]{:S(2)}) collective-permute-start(f32[2,240,256]{2,1,0:T(8,128)S(1)} %get-tuple-element.48), channel_id=1, source_target_pairs={{0,1},{1,0},{2,3},{3,2},{4,5},{5,4},{6,7},{7,6},{8,9},{9,8},{10,11... | collective-permute-start | bytes 1474568 | tf_op jit(solution)/shard_map/ppermute | solution.py:654
  3.5 1.1 %kept_weights.1 = (f32[2,240,256]{2,1,0:T(8,128)S(1)}, f32[4,240,256]{2,1,0:T(8,128)S(1)}, f32[2,8,128]{2,1,0:T(8,128)S(1)}, f32[2,8,128]{2,1,0:T(8,128)S(1)}) custom-call(s32[3]{0:T(128)S(1)} %pad_add_fusion.place_ref, f32[1,256]{1,0:T(1,128)S(1)} %get-tuple-element.33.coupling_ref, s32[1,256]{1,0:T(1,128)S(1)} %get-tuple-element.34.counts_ref, ...), custom_call_target="tpu_custom_call" | custom-call | flops 9830400 | bytes 2949120 | tf_op jit(solution)/shard_map/kept_weights/pallas_call | solution.py:336
  4.6 2.6 %collective-permute-start = (f32[2,8,128]{2,1,0:T(8,128)S(1)}, f32[2,8,128]{2,1,0:T(8,128)S(1)}, u32[]{:S(2)}, u32[]{:S(2)}) collective-permute-start(f32[2,8,128]{2,1,0:T(8,128)S(1)} %get-tuple-element.38), channel_id=1, source_target_pairs={{0,2},{2,4},{4,6},{6,0},{1,3},{3,5},{5,7},{7,1},{8,10},{10,12},{12... | collective-permute-start | bytes 24584 | tf_op jit(solution)/shard_map/ppermute | solution.py:659
  7.2 1.0 %collective-permute-start.1 = (f32[2,8,128]{2,1,0:T(8,128)S(1)}, f32[2,8,128]{2,1,0:T(8,128)S(1)}, u32[]{:S(2)}, u32[]{:S(2)}) collective-permute-start(f32[2,8,128]{2,1,0:T(8,128)S(1)} %get-tuple-element.39), channel_id=1, source_target_pairs={{2,0},{4,2},{6,4},{0,6},{3,1},{5,3},{7,5},{1,7},{10,8},{12,10},{14... | collective-permute-start | bytes 24584 | tf_op jit(solution)/shard_map/ppermute | solution.py:660
  8.2 0.5 %sort_weights.1 = (f32[2,120,128]{2,1,0:T(8,128)S(1)}, f32[2,120,128]{2,1,0:T(8,128)S(1)}, f32[2,120,128]{2,1,0:T(8,128)S(1)}, f32[2,120,128]{2,1,0:T(8,128)S(1)}, f32[240,256]{1,0:T(8,128)S(1)}) custom-call(f32[2,240,256]{2,1,0:T(8,128)S(1)} %collective-permute-done.3.theirs_ref, f32[2,240,256]{2,1,0:T(8,128)S(1)} %get-tuple-element.49.mine_ref, ...), custom_call_target="tpu_custom_call" | custom-call | tf_op jit(solution)/shard_map/sort_weights/pallas_call | solution.py:548
  8.7 2.0 %collective-permute-start.4 = (f32[2,120,128]{2,1,0:T(8,128)S(1)}, f32[2,120,128]{2,1,0:T(8,128)S(1)}, u32[]{:S(2)}, u32[]{:S(2)}) collective-permute-start(f32[2,120,128]{2,1,0:T(8,128)S(1)} %get-tuple-element.51), channel_id=1, source_target_pairs={{0,8},{8,16},{16,24},{24,0},{1,9},{9,17},{17,25},{25,1},{2,10},{10... | collective-permute-start | bytes 368648 | tf_op jit(solution)/shard_map/ppermute | solution.py:564
  10.7 2.6 %collective-permute-start.5 = (f32[2,120,128]{2,1,0:T(8,128)S(1)}, f32[2,120,128]{2,1,0:T(8,128)S(1)}, u32[]{:S(2)}, u32[]{:S(2)}) collective-permute-start(f32[2,120,128]{2,1,0:T(8,128)S(1)} %get-tuple-element.52), channel_id=1, source_target_pairs={{0,16},{8,24},{16,0},{24,8},{1,17},{9,25},{17,1},{25,9},{2,18},{10... | collective-permute-start | bytes 368648 | tf_op jit(solution)/shard_map/ppermute | solution.py:564
  13.3 0.3 stream_layout.1
  13.6 2.3 %flux_sums.1 = (f32[1,240,256]{2,1,0:T(8,128)S(1)}, f32[3848,128]{1,0:T(8,128)S(1)}) custom-call(s32[3]{0:T(128)S(1)} %pad_add_fusion.place_ref, f32[1,256]{1,0:T(1,128)S(1)} %get-tuple-element.33.coupling_ref, f32[2,8,128]{2,1,0:T(8,128)S(1)} %collective-permute-done.left_ref, f32[2,8,128]{2,1,0:T(8,128)S(1)} %collective-permute-done.1.right_ref, ...), custom_call_target="tpu_custom_call" | custom-call | tf_op jit(solution)/shard_map/flux_sums/pallas_call | solution.py:484
  15.9 0.1 collective-permute-start.2
  16.0 0.7 %kept_flux.1.mine_ref = f32[1,240,256]{2,1,0:T(8,128)S(1)} custom-call(s32[3]{0:T(128)S(1)} %pad_add_fusion.place_ref, f32[1,256]{1,0:T(1,128)S(1)} %get-tuple-element.33.coupling_ref, f32[3848,128]{1,0:T(8,128)S(1)} %get-tuple-element.45.solved_ref, f32[4,240,256]{2,1,0:T(8,128)S(1)} %get-tuple-element.46.weight_ref), custom_call_target="tpu_custom_call" | custom-call | flops 491520 | bytes 1966080 | tf_op jit(solution)/shard_map/kept_flux/pallas_call | solution.py:502
  16.7 1.4 %collective-permute-start.9 = (f32[2,120,128]{2,1,0:T(8,128)S(1)}, f32[2,120,128]{2,1,0:T(8,128)S(1)}, u32[]{:S(2)}, u32[]{:S(2)}) collective-permute-start(f32[2,120,128]{2,1,0:T(8,128)S(1)} %get-tuple-element.60), channel_id=1, source_target_pairs={{0,24},{8,0},{16,8},{24,16},{1,25},{9,1},{17,9},{25,17},{2,26},{10... | collective-permute-start | bytes 368648 | tf_op jit(solution)/shard_map/ppermute | solution.py:564
  18.1 3.4 %collective-permute-done.5.refs_2_ = f32[2,120,128]{2,1,0:T(8,128)S(1)} collective-permute-done((f32[2,120,128]{2,1,0:T(8,128)S(1)}, f32[2,120,128]{2,1,0:T(8,128)S(1)}, u32[]{:S(2)}, u32[]{:S(2)}) %collective-permute-start.5) | collective-permute-done | bytes 122912 | tf_op jit(solution)/shard_map/ppermute | solution.py:564
  21.5 0.0 collective-permute-done.2.theirs_ref
  21.5 0.3 %sort_flux.1 = (f32[1,120,128]{2,1,0:T(8,128)S(1)}, f32[1,120,128]{2,1,0:T(8,128)S(1)}, f32[1,120,128]{2,1,0:T(8,128)S(1)}, f32[1,120,128]{2,1,0:T(8,128)S(1)}) custom-call(f32[1,240,256]{2,1,0:T(8,128)S(1)} %collective-permute-done.2.theirs_ref, f32[1,240,256]{2,1,0:T(8,128)S(1)} %kept_flux.1.mine_ref, bf16[512,512]{1,0:T(8,128)(2,1)S(1)} %get-tuple-element.47.table_ref, ...), custom_call_target="tpu_custom_call" | custom-call | tf_op jit(solution)/shard_map/sort_flux/pallas_call | solution.py:548
  21.9 0.1 collective-permute-start.6
  22.0 2.1 %collective-permute-start.7 = (f32[1,120,128]{2,1,0:T(8,128)S(1)}, f32[1,120,128]{2,1,0:T(8,128)S(1)}, u32[]{:S(2)}, u32[]{:S(2)}) collective-permute-start(f32[1,120,128]{2,1,0:T(8,128)S(1)} %get-tuple-element.57), channel_id=1, source_target_pairs={{0,16},{8,24},{16,0},{24,8},{1,17},{9,25},{17,1},{25,9},{2,18},{10... | collective-permute-start | bytes 184328 | tf_op jit(solution)/shard_map/ppermute | solution.py:564
  24.0 1.7 %collective-permute-start.8 = (f32[1,120,128]{2,1,0:T(8,128)S(1)}, f32[1,120,128]{2,1,0:T(8,128)S(1)}, u32[]{:S(2)}, u32[]{:S(2)}) collective-permute-start(f32[1,120,128]{2,1,0:T(8,128)S(1)} %get-tuple-element.58), channel_id=1, source_target_pairs={{0,24},{8,0},{16,8},{24,16},{1,25},{9,1},{17,9},{25,17},{2,26},{10... | collective-permute-start | bytes 184328 | tf_op jit(solution)/shard_map/ppermute | solution.py:564
  25.8 1.4 %recv_moves.1.table_ref = bf16[512,512]{1,0:T(8,128)(2,1)S(1)} custom-call(s32[3]{0:T(128)S(1)} %pad_add_fusion.place_ref, s32[1,1024]{1,0:T(1,128)S(1)} %get-tuple-element.55.slots_ref), custom_call_target="tpu_custom_call" | custom-call | flops 1000000 | bytes 1000000 | tf_op jit(solution)/shard_map/recv_moves/pallas_call | solution.py:375
  27.2 1.9 %end_weights.1 = (f32[240,256]{1,0:T(8,128)}, f32[3,240,256]{2,1,0:T(8,128)}) custom-call(s32[3]{0:T(128)S(1)} %pad_add_fusion.place_ref, bf16[512,512]{1,0:T(8,128)(2,1)S(1)} %recv_moves.1.table_ref, f32[2,120,128]{2,1,0:T(8,128)S(1)} %get-tuple-element.59.refs_0_, f32[2,120,128]{2,1,0:T(8,128)S(1)} %collective-permute-done.4.refs_1_, ...), custom_call_target="tpu_custom_call" | custom-call | flops 251658240 | bytes 1474560 | tf_op jit(solution)/shard_map/end_weights/pallas_call | solution.py:598
  29.1 1.0 %collective-permute-done.7.refs_2_ = f32[1,120,128]{2,1,0:T(8,128)S(1)} collective-permute-done((f32[1,120,128]{2,1,0:T(8,128)S(1)}, f32[1,120,128]{2,1,0:T(8,128)S(1)}, u32[]{:S(2)}, u32[]{:S(2)}) %collective-permute-start.7) | collective-permute-done | bytes 61472 | tf_op jit(solution)/shard_map/ppermute | solution.py:564
  30.1 1.0 %end_flux.1 = f32[240,256]{1,0:T(8,128)} custom-call(bf16[512,512]{1,0:T(8,128)(2,1)S(1)} %recv_moves.1.table_ref, f32[1,120,128]{2,1,0:T(8,128)S(1)} %get-tuple-element.53.refs_0_, f32[1,120,128]{2,1,0:T(8,128)S(1)} %collective-permute-done.6.refs_1_, f32[1,120,128]{2,1,0:T(8,128)S(1)} %collective-permute-done.7.refs_2_, ...), custom_call_target="tpu_custom_call" | custom-call | flops 125829120 | bytes 491520 | tf_op jit(solution)/shard_map/end_flux/pallas_call | solution.py:620
  (11 shorter events, 0.0 us)
Async XLA Ops:
  0.6 2.8 %copy-start = (f32[4,480,256]{2,1,0:T(8,128)S(1)}, f32[4,480,256]{2,1,0:T(8,128)}, u32[]{:S(2)}) copy-start(f32[4,480,256]{2,1,0:T(8,128)} %pixels_ref.3) | copy-start | bytes 5898244
  2.9 5.2 %collective-permute-start.3 = (f32[2,240,256]{2,1,0:T(8,128)S(1)}, f32[2,240,256]{2,1,0:T(8,128)S(1)}, u32[]{:S(2)}, u32[]{:S(2)}) collective-permute-start(f32[2,240,256]{2,1,0:T(8,128)S(1)} %get-tuple-element.48), channel_id=1, source_target_pairs={{0,1},{1,0},{2,3},{3,2},{4,5},{5,4},{6,7},{7,6},{8,9},{9,8},{10,11... | collective-permute-start | bytes 1474568 | tf_op jit(solution)/shard_map/ppermute | solution.py:654
  4.6 8.7 %collective-permute-start = (f32[2,8,128]{2,1,0:T(8,128)S(1)}, f32[2,8,128]{2,1,0:T(8,128)S(1)}, u32[]{:S(2)}, u32[]{:S(2)}) collective-permute-start(f32[2,8,128]{2,1,0:T(8,128)S(1)} %get-tuple-element.38), channel_id=1, source_target_pairs={{0,2},{2,4},{4,6},{6,0},{1,3},{3,5},{5,7},{7,1},{8,10},{10,12},{12... | collective-permute-start | bytes 24584 | tf_op jit(solution)/shard_map/ppermute | solution.py:659
  7.2 6.1 %collective-permute-start.1 = (f32[2,8,128]{2,1,0:T(8,128)S(1)}, f32[2,8,128]{2,1,0:T(8,128)S(1)}, u32[]{:S(2)}, u32[]{:S(2)}) collective-permute-start(f32[2,8,128]{2,1,0:T(8,128)S(1)} %get-tuple-element.39), channel_id=1, source_target_pairs={{2,0},{4,2},{6,4},{0,6},{3,1},{5,3},{7,5},{1,7},{10,8},{12,10},{14... | collective-permute-start | bytes 24584 | tf_op jit(solution)/shard_map/ppermute | solution.py:660
  8.7 9.5 %collective-permute-start.4 = (f32[2,120,128]{2,1,0:T(8,128)S(1)}, f32[2,120,128]{2,1,0:T(8,128)S(1)}, u32[]{:S(2)}, u32[]{:S(2)}) collective-permute-start(f32[2,120,128]{2,1,0:T(8,128)S(1)} %get-tuple-element.51), channel_id=1, source_target_pairs={{0,8},{8,16},{16,24},{24,0},{1,9},{9,17},{17,25},{25,1},{2,10},{10... | collective-permute-start | bytes 368648 | tf_op jit(solution)/shard_map/ppermute | solution.py:564
  10.7 10.8 %collective-permute-start.5 = (f32[2,120,128]{2,1,0:T(8,128)S(1)}, f32[2,120,128]{2,1,0:T(8,128)S(1)}, u32[]{:S(2)}, u32[]{:S(2)}) collective-permute-start(f32[2,120,128]{2,1,0:T(8,128)S(1)} %get-tuple-element.52), channel_id=1, source_target_pairs={{0,16},{8,24},{16,0},{24,8},{1,17},{9,25},{17,1},{25,9},{2,18},{10... | collective-permute-start | bytes 368648 | tf_op jit(solution)/shard_map/ppermute | solution.py:564
  15.9 5.6 %collective-permute-start.2 = (f32[1,240,256]{2,1,0:T(8,128)S(1)}, f32[1,240,256]{2,1,0:T(8,128)S(1)}, u32[]{:S(2)}, u32[]{:S(2)}) collective-permute-start(f32[1,240,256]{2,1,0:T(8,128)S(1)} %get-tuple-element.43), channel_id=1, source_target_pairs={{0,1},{1,0},{2,3},{3,2},{4,5},{5,4},{6,7},{7,6},{8,9},{9,8},{10,11... | collective-permute-start | bytes 737288 | tf_op jit(solution)/shard_map/ppermute | solution.py:667
  16.7 10.4 %collective-permute-start.9 = (f32[2,120,128]{2,1,0:T(8,128)S(1)}, f32[2,120,128]{2,1,0:T(8,128)S(1)}, u32[]{:S(2)}, u32[]{:S(2)}) collective-permute-start(f32[2,120,128]{2,1,0:T(8,128)S(1)} %get-tuple-element.60), channel_id=1, source_target_pairs={{0,24},{8,0},{16,8},{24,16},{1,25},{9,1},{17,9},{25,17},{2,26},{10... | collective-permute-start | bytes 368648 | tf_op jit(solution)/shard_map/ppermute | solution.py:564
  21.9 7.2 %collective-permute-start.6 = (f32[1,120,128]{2,1,0:T(8,128)S(1)}, f32[1,120,128]{2,1,0:T(8,128)S(1)}, u32[]{:S(2)}, u32[]{:S(2)}) collective-permute-start(f32[1,120,128]{2,1,0:T(8,128)S(1)} %get-tuple-element.56), channel_id=1, source_target_pairs={{0,8},{8,16},{16,24},{24,0},{1,9},{9,17},{17,25},{25,1},{2,10},{10... | collective-permute-start | bytes 184328 | tf_op jit(solution)/shard_map/ppermute | solution.py:564
  22.0 8.1 %collective-permute-start.7 = (f32[1,120,128]{2,1,0:T(8,128)S(1)}, f32[1,120,128]{2,1,0:T(8,128)S(1)}, u32[]{:S(2)}, u32[]{:S(2)}) collective-permute-start(f32[1,120,128]{2,1,0:T(8,128)S(1)} %get-tuple-element.57), channel_id=1, source_target_pairs={{0,16},{8,24},{16,0},{24,8},{1,17},{9,25},{17,1},{25,9},{2,18},{10... | collective-permute-start | bytes 184328 | tf_op jit(solution)/shard_map/ppermute | solution.py:564
  24.0 6.1 %collective-permute-start.8 = (f32[1,120,128]{2,1,0:T(8,128)S(1)}, f32[1,120,128]{2,1,0:T(8,128)S(1)}, u32[]{:S(2)}, u32[]{:S(2)}) collective-permute-start(f32[1,120,128]{2,1,0:T(8,128)S(1)} %get-tuple-element.58), channel_id=1, source_target_pairs={{0,24},{8,0},{16,8},{24,16},{1,25},{9,1},{17,9},{25,17},{2,26},{10... | collective-permute-start | bytes 184328 | tf_op jit(solution)/shard_map/ppermute | solution.py:564

commit v9 on v8

--- a/solution.py
+++ b/solution.py
@@ -663,7 +663,8 @@
 
     pixel_s, ivar_s = stream_layout(left[0] + right[0], pixels, ivar)
     theirs, solved = flux_sums(wav_count, place, coupling, left, right, pixel_s, ivar_s, weight_t)
-    ahead = sum(piece[0, :ROWS, :] for piece in weight_pieces[1:-1] or weight_pieces)
+    early = [piece for d, piece in enumerate(weight_pieces) if d not in (0, fib_count // 2)] or weight_pieces
+    ahead = sum(piece[0, :ROWS, :] for piece in early)
     arriving = lax.ppermute(theirs, "exp", swap)
     mine = kept_flux(after(place, theirs), coupling, solved, weight_m)
     sorted_pieces = sort_fibres(arriving, mine, send_table, pack, pieces, scale, ahead)

time: 31.3 us -> 30.7 us (0.981)
  starting transfers between devices: 14.1 us -> 13.6 us
    ppermute x6, starting transfers between devices: 9.9 us -> 9.42 us  [exchange(): lax.ppermute(pieces[d], 'fib', [(i, (i + d) % fib_count) for i in range(f...]
where the time goes in v9:
time: 30.7 us; the launch traced here: 30.6 us
  starting transfers between devices  13.6 us (44%)
  Pallas kernels  11.9 us (39%)
  waiting for transfers between devices  4.32 us (14%)
  between operations  0.72 us (2%)
    ppermute x6, starting transfers between devices, exchange(): lax.ppermute(pieces[d], 'fib', [(i, (i + d) % fib_count) for i in range(f...  9.42 us
    ppermute x6, waiting for transfers between devices, exchange(): lax.ppermute(pieces[d], 'fib', [(i, (i + d) % fib_count) for i in range(f...  4.31 us
    ppermute x1, starting transfers between devices, per_device(): left = lax.ppermute(up, 'wav', upward)  2.56 us
    pallas_call x1, Pallas kernels, flux_sums(): pl.pallas_call(functools.partial(solve_kernel, wav_count), in_specs=[in_s...  2.34 us
    pallas_call x1, Pallas kernels, sent_weights(): pl.pallas_call(functools.partial(sent_kernel, moves, wav_count), in_specs...  2.22 us
    pallas_call x1, Pallas kernels, end_weights(): pl.pallas_call(functools.partial(weights_end_kernel, pack, total), in_spe...  1.91 us
    pallas_call x1, Pallas kernels, recv_moves(): pl.pallas_call(functools.partial(recv_kernel, moves), in_specs=[in_smem,...  1.4 us
    pallas_call x1, Pallas kernels, kept_weights(): pl.pallas_call(functools.partial(kept_kernel, wav_count), in_specs=[in_sm...  1.14 us
  transfers between devices with their start and end apart: 10, of which 2 were waited for; matrix products, arithmetic and copies ran while one was open for 0% of the time, Pallas kernels for 28%

profile of v9, /device:TPU:0, one launch (start us, length us, event | category | flops | bytes accessed | tf_op | source)
XLA Modules:
  0.0 30.6 jit_solution(3068385587039848087)
XLA Ops:
  0.6 0.1 pad_add_fusion.place_ref
  0.7 2.2 %sent_weights.1 = (f32[2,240,256]{2,1,0:T(8,128)S(1)}, f32[4,240,256]{2,1,0:T(8,128)S(1)}, bf16[512,512]{1,0:T(8,128)(2,1)S(1)}, s32[1,1024]{1,0:T(1,128)S(1)}, ...) custom-call(s32[3]{0:T(128)S(1)} %pad_add_fusion.place_ref, ...), custom_call_target="tpu_custom_call" | custom-call | flops 9830400 | bytes 2949120 | tf_op jit(solution)/shard_map/sent_weights/pallas_call | solution.py:263
  2.9 0.5 %collective-permute-start.3 = (f32[2,240,256]{2,1,0:T(8,128)S(1)}, f32[2,240,256]{2,1,0:T(8,128)S(1)}, u32[]{:S(2)}, u32[]{:S(2)}) collective-permute-start(f32[2,240,256]{2,1,0:T(8,128)S(1)} %get-tuple-element.48), channel_id=1, source_target_pairs={{0,1},{1,0},{2,3},{3,2},{4,5},{5,4},{6,7},{7,6},{8,9},{9,8},{10,11... | collective-permute-start | bytes 1474568 | tf_op jit(solution)/shard_map/ppermute | solution.py:654
  3.5 1.1 %kept_weights.1 = (f32[2,240,256]{2,1,0:T(8,128)S(1)}, f32[4,240,256]{2,1,0:T(8,128)S(1)}, f32[2,8,128]{2,1,0:T(8,128)S(1)}, f32[2,8,128]{2,1,0:T(8,128)S(1)}) custom-call(s32[3]{0:T(128)S(1)} %pad_add_fusion.place_ref, f32[1,256]{1,0:T(1,128)S(1)} %get-tuple-element.33.coupling_ref, s32[1,256]{1,0:T(1,128)S(1)} %get-tuple-element.34.counts_ref, ...), custom_call_target="tpu_custom_call" | custom-call | flops 9830400 | bytes 2949120 | tf_op jit(solution)/shard_map/kept_weights/pallas_call | solution.py:336
  4.6 2.6 %collective-permute-start = (f32[2,8,128]{2,1,0:T(8,128)S(1)}, f32[2,8,128]{2,1,0:T(8,128)S(1)}, u32[]{:S(2)}, u32[]{:S(2)}) collective-permute-start(f32[2,8,128]{2,1,0:T(8,128)S(1)} %get-tuple-element.38), channel_id=1, source_target_pairs={{0,2},{2,4},{4,6},{6,0},{1,3},{3,5},{5,7},{7,1},{8,10},{10,12},{12... | collective-permute-start | bytes 24584 | tf_op jit(solution)/shard_map/ppermute | solution.py:659
  7.2 1.0 %collective-permute-start.1 = (f32[2,8,128]{2,1,0:T(8,128)S(1)}, f32[2,8,128]{2,1,0:T(8,128)S(1)}, u32[]{:S(2)}, u32[]{:S(2)}) collective-permute-start(f32[2,8,128]{2,1,0:T(8,128)S(1)} %get-tuple-element.39), channel_id=1, source_target_pairs={{2,0},{4,2},{6,4},{0,6},{3,1},{5,3},{7,5},{1,7},{10,8},{12,10},{14... | collective-permute-start | bytes 24584 | tf_op jit(solution)/shard_map/ppermute | solution.py:660
  8.2 0.5 %sort_weights.1 = (f32[2,120,128]{2,1,0:T(8,128)S(1)}, f32[2,120,128]{2,1,0:T(8,128)S(1)}, f32[2,120,128]{2,1,0:T(8,128)S(1)}, f32[2,120,128]{2,1,0:T(8,128)S(1)}, f32[240,256]{1,0:T(8,128)S(1)}) custom-call(f32[2,240,256]{2,1,0:T(8,128)S(1)} %collective-permute-done.3.theirs_ref, f32[2,240,256]{2,1,0:T(8,128)S(1)} %get-tuple-element.49.mine_ref, ...), custom_call_target="tpu_custom_call" | custom-call | tf_op jit(solution)/shard_map/sort_weights/pallas_call | solution.py:548
  8.7 2.0 %collective-permute-start.4 = (f32[2,120,128]{2,1,0:T(8,128)S(1)}, f32[2,120,128]{2,1,0:T(8,128)S(1)}, u32[]{:S(2)}, u32[]{:S(2)}) collective-permute-start(f32[2,120,128]{2,1,0:T(8,128)S(1)} %get-tuple-element.51), channel_id=1, source_target_pairs={{0,8},{8,16},{16,24},{24,0},{1,9},{9,17},{17,25},{25,1},{2,10},{10... | collective-permute-start | bytes 368648 | tf_op jit(solution)/shard_map/ppermute | solution.py:564
  10.7 2.1 %collective-permute-start.5 = (f32[2,120,128]{2,1,0:T(8,128)S(1)}, f32[2,120,128]{2,1,0:T(8,128)S(1)}, u32[]{:S(2)}, u32[]{:S(2)}) collective-permute-start(f32[2,120,128]{2,1,0:T(8,128)S(1)} %get-tuple-element.52), channel_id=1, source_target_pairs={{0,24},{8,0},{16,8},{24,16},{1,25},{9,1},{17,9},{25,17},{2,26},{10... | collective-permute-start | bytes 368648 | tf_op jit(solution)/shard_map/ppermute | solution.py:564
  12.8 0.0 collective-permute-done.left_ref
  12.8 0.3 stream_layout.1
  13.1 2.3 %flux_sums.1 = (f32[1,240,256]{2,1,0:T(8,128)S(1)}, f32[3848,128]{1,0:T(8,128)S(1)}) custom-call(s32[3]{0:T(128)S(1)} %pad_add_fusion.place_ref, f32[1,256]{1,0:T(1,128)S(1)} %get-tuple-element.33.coupling_ref, f32[2,8,128]{2,1,0:T(8,128)S(1)} %collective-permute-done.left_ref, f32[2,8,128]{2,1,0:T(8,128)S(1)} %collective-permute-done.1.right_ref, ...), custom_call_target="tpu_custom_call" | custom-call | tf_op jit(solution)/shard_map/flux_sums/pallas_call | solution.py:484
  15.4 0.1 collective-permute-start.2
  15.5 0.7 %kept_flux.1.mine_ref = f32[1,240,256]{2,1,0:T(8,128)S(1)} custom-call(s32[3]{0:T(128)S(1)} %pad_add_fusion.place_ref, f32[1,256]{1,0:T(1,128)S(1)} %get-tuple-element.33.coupling_ref, f32[3848,128]{1,0:T(8,128)S(1)} %get-tuple-element.45.solved_ref, f32[4,240,256]{2,1,0:T(8,128)S(1)} %get-tuple-element.46.weight_ref), custom_call_target="tpu_custom_call" | custom-call | flops 491520 | bytes 1966080 | tf_op jit(solution)/shard_map/kept_flux/pallas_call | solution.py:502
  16.2 1.0 %collective-permute-start.9 = (f32[2,120,128]{2,1,0:T(8,128)S(1)}, f32[2,120,128]{2,1,0:T(8,128)S(1)}, u32[]{:S(2)}, u32[]{:S(2)}) collective-permute-start(f32[2,120,128]{2,1,0:T(8,128)S(1)} %get-tuple-element.60), channel_id=1, source_target_pairs={{0,16},{8,24},{16,0},{24,8},{1,17},{9,25},{17,1},{25,9},{2,18},{10... | collective-permute-start | bytes 368648 | tf_op jit(solution)/shard_map/ppermute | solution.py:564
  17.3 1.0 %collective-permute-done.5.refs_3_ = f32[2,120,128]{2,1,0:T(8,128)S(1)} collective-permute-done((f32[2,120,128]{2,1,0:T(8,128)S(1)}, f32[2,120,128]{2,1,0:T(8,128)S(1)}, u32[]{:S(2)}, u32[]{:S(2)}) %collective-permute-start.5) | collective-permute-done | bytes 122912 | tf_op jit(solution)/shard_map/ppermute | solution.py:564
  18.2 0.3 %sort_flux.1 = (f32[1,120,128]{2,1,0:T(8,128)S(1)}, f32[1,120,128]{2,1,0:T(8,128)S(1)}, f32[1,120,128]{2,1,0:T(8,128)S(1)}, f32[1,120,128]{2,1,0:T(8,128)S(1)}) custom-call(f32[1,240,256]{2,1,0:T(8,128)S(1)} %collective-permute-done.2.theirs_ref, f32[1,240,256]{2,1,0:T(8,128)S(1)} %kept_flux.1.mine_ref, bf16[512,512]{1,0:T(8,128)(2,1)S(1)} %get-tuple-element.47.table_ref, ...), custom_call_target="tpu_custom_call" | custom-call | tf_op jit(solution)/shard_map/sort_flux/pallas_call | solution.py:548
  18.6 1.2 %collective-permute-start.6 = (f32[1,120,128]{2,1,0:T(8,128)S(1)}, f32[1,120,128]{2,1,0:T(8,128)S(1)}, u32[]{:S(2)}, u32[]{:S(2)}) collective-permute-start(f32[1,120,128]{2,1,0:T(8,128)S(1)} %get-tuple-element.56), channel_id=1, source_target_pairs={{0,8},{8,16},{16,24},{24,0},{1,9},{9,17},{17,25},{25,1},{2,10},{10... | collective-permute-start | bytes 184328 | tf_op jit(solution)/shard_map/ppermute | solution.py:564
  19.8 1.7 %collective-permute-start.7 = (f32[1,120,128]{2,1,0:T(8,128)S(1)}, f32[1,120,128]{2,1,0:T(8,128)S(1)}, u32[]{:S(2)}, u32[]{:S(2)}) collective-permute-start(f32[1,120,128]{2,1,0:T(8,128)S(1)} %get-tuple-element.57), channel_id=1, source_target_pairs={{0,16},{8,24},{16,0},{24,8},{1,17},{9,25},{17,1},{25,9},{2,18},{10... | collective-permute-start | bytes 184328 | tf_op jit(solution)/shard_map/ppermute | solution.py:564
  21.5 1.4 %collective-permute-start.8 = (f32[1,120,128]{2,1,0:T(8,128)S(1)}, f32[1,120,128]{2,1,0:T(8,128)S(1)}, u32[]{:S(2)}, u32[]{:S(2)}) collective-permute-start(f32[1,120,128]{2,1,0:T(8,128)S(1)} %get-tuple-element.58), channel_id=1, source_target_pairs={{0,24},{8,0},{16,8},{24,16},{1,25},{9,1},{17,9},{25,17},{2,26},{10... | collective-permute-start | bytes 184328 | tf_op jit(solution)/shard_map/ppermute | solution.py:564
  22.9 1.4 %recv_moves.1.table_ref = bf16[512,512]{1,0:T(8,128)(2,1)S(1)} custom-call(s32[3]{0:T(128)S(1)} %pad_add_fusion.place_ref, s32[1,1024]{1,0:T(1,128)S(1)} %get-tuple-element.55.slots_ref), custom_call_target="tpu_custom_call" | custom-call | flops 1000000 | bytes 1000000 | tf_op jit(solution)/shard_map/recv_moves/pallas_call | solution.py:375
  24.3 3.3 %collective-permute-done.9.refs_2_ = f32[2,120,128]{2,1,0:T(8,128)S(1)} collective-permute-done((f32[2,120,128]{2,1,0:T(8,128)S(1)}, f32[2,120,128]{2,1,0:T(8,128)S(1)}, u32[]{:S(2)}, u32[]{:S(2)}) %collective-permute-start.9) | collective-permute-done | bytes 122912 | tf_op jit(solution)/shard_map/ppermute | solution.py:564
  27.6 1.9 %end_weights.1 = (f32[240,256]{1,0:T(8,128)}, f32[3,240,256]{2,1,0:T(8,128)}) custom-call(s32[3]{0:T(128)S(1)} %pad_add_fusion.place_ref, bf16[512,512]{1,0:T(8,128)(2,1)S(1)} %recv_moves.1.table_ref, f32[2,120,128]{2,1,0:T(8,128)S(1)} %get-tuple-element.59.refs_0_, f32[2,120,128]{2,1,0:T(8,128)S(1)} %collective-permute-done.4.refs_1_, ...), custom_call_target="tpu_custom_call" | custom-call | flops 251658240 | bytes 1474560 | tf_op jit(solution)/shard_map/end_weights/pallas_call | solution.py:598
  29.5 1.0 %end_flux.1 = f32[240,256]{1,0:T(8,128)} custom-call(bf16[512,512]{1,0:T(8,128)(2,1)S(1)} %recv_moves.1.table_ref, f32[1,120,128]{2,1,0:T(8,128)S(1)} %get-tuple-element.53.refs_0_, f32[1,120,128]{2,1,0:T(8,128)S(1)} %collective-permute-done.6.refs_1_, f32[1,120,128]{2,1,0:T(8,128)S(1)} %collective-permute-done.7.refs_2_, ...), custom_call_target="tpu_custom_call" | custom-call | flops 125829120 | bytes 491520 | tf_op jit(solution)/shard_map/end_flux/pallas_call | solution.py:620
  (11 shorter events, 0.0 us)
Async XLA Ops:
  0.6 2.8 %copy-start = (f32[4,480,256]{2,1,0:T(8,128)S(1)}, f32[4,480,256]{2,1,0:T(8,128)}, u32[]{:S(2)}) copy-start(f32[4,480,256]{2,1,0:T(8,128)} %pixels_ref.3) | copy-start | bytes 5898244
  2.9 5.2 %collective-permute-start.3 = (f32[2,240,256]{2,1,0:T(8,128)S(1)}, f32[2,240,256]{2,1,0:T(8,128)S(1)}, u32[]{:S(2)}, u32[]{:S(2)}) collective-permute-start(f32[2,240,256]{2,1,0:T(8,128)S(1)} %get-tuple-element.48), channel_id=1, source_target_pairs={{0,1},{1,0},{2,3},{3,2},{4,5},{5,4},{6,7},{7,6},{8,9},{9,8},{10,11... | collective-permute-start | bytes 1474568 | tf_op jit(solution)/shard_map/ppermute | solution.py:654
  4.6 8.2 %collective-permute-start = (f32[2,8,128]{2,1,0:T(8,128)S(1)}, f32[2,8,128]{2,1,0:T(8,128)S(1)}, u32[]{:S(2)}, u32[]{:S(2)}) collective-permute-start(f32[2,8,128]{2,1,0:T(8,128)S(1)} %get-tuple-element.38), channel_id=1, source_target_pairs={{0,2},{2,4},{4,6},{6,0},{1,3},{3,5},{5,7},{7,1},{8,10},{10,12},{12... | collective-permute-start | bytes 24584 | tf_op jit(solution)/shard_map/ppermute | solution.py:659
  7.2 5.6 %collective-permute-start.1 = (f32[2,8,128]{2,1,0:T(8,128)S(1)}, f32[2,8,128]{2,1,0:T(8,128)S(1)}, u32[]{:S(2)}, u32[]{:S(2)}) collective-permute-start(f32[2,8,128]{2,1,0:T(8,128)S(1)} %get-tuple-element.39), channel_id=1, source_target_pairs={{2,0},{4,2},{6,4},{0,6},{3,1},{5,3},{7,5},{1,7},{10,8},{12,10},{14... | collective-permute-start | bytes 24584 | tf_op jit(solution)/shard_map/ppermute | solution.py:660
  8.7 8.6 %collective-permute-start.4 = (f32[2,120,128]{2,1,0:T(8,128)S(1)}, f32[2,120,128]{2,1,0:T(8,128)S(1)}, u32[]{:S(2)}, u32[]{:S(2)}) collective-permute-start(f32[2,120,128]{2,1,0:T(8,128)S(1)} %get-tuple-element.51), channel_id=1, source_target_pairs={{0,8},{8,16},{16,24},{24,0},{1,9},{9,17},{17,25},{25,1},{2,10},{10... | collective-permute-start | bytes 368648 | tf_op jit(solution)/shard_map/ppermute | solution.py:564
  10.7 7.5 %collective-permute-start.5 = (f32[2,120,128]{2,1,0:T(8,128)S(1)}, f32[2,120,128]{2,1,0:T(8,128)S(1)}, u32[]{:S(2)}, u32[]{:S(2)}) collective-permute-start(f32[2,120,128]{2,1,0:T(8,128)S(1)} %get-tuple-element.52), channel_id=1, source_target_pairs={{0,24},{8,0},{16,8},{24,16},{1,25},{9,1},{17,9},{25,17},{2,26},{10... | collective-permute-start | bytes 368648 | tf_op jit(solution)/shard_map/ppermute | solution.py:564
  15.4 2.8 %collective-permute-start.2 = (f32[1,240,256]{2,1,0:T(8,128)S(1)}, f32[1,240,256]{2,1,0:T(8,128)S(1)}, u32[]{:S(2)}, u32[]{:S(2)}) collective-permute-start(f32[1,240,256]{2,1,0:T(8,128)S(1)} %get-tuple-element.43), channel_id=1, source_target_pairs={{0,1},{1,0},{2,3},{3,2},{4,5},{5,4},{6,7},{7,6},{8,9},{9,8},{10,11... | collective-permute-start | bytes 737288 | tf_op jit(solution)/shard_map/ppermute | solution.py:668
  16.2 11.4 %collective-permute-start.9 = (f32[2,120,128]{2,1,0:T(8,128)S(1)}, f32[2,120,128]{2,1,0:T(8,128)S(1)}, u32[]{:S(2)}, u32[]{:S(2)}) collective-permute-start(f32[2,120,128]{2,1,0:T(8,128)S(1)} %get-tuple-element.60), channel_id=1, source_target_pairs={{0,16},{8,24},{16,0},{24,8},{1,17},{9,25},{17,1},{25,9},{2,18},{10... | collective-permute-start | bytes 368648 | tf_op jit(solution)/shard_map/ppermute | solution.py:564
  18.6 10.9 %collective-permute-start.6 = (f32[1,120,128]{2,1,0:T(8,128)S(1)}, f32[1,120,128]{2,1,0:T(8,128)S(1)}, u32[]{:S(2)}, u32[]{:S(2)}) collective-permute-start(f32[1,120,128]{2,1,0:T(8,128)S(1)} %get-tuple-element.56), channel_id=1, source_target_pairs={{0,8},{8,16},{16,24},{24,0},{1,9},{9,17},{17,25},{25,1},{2,10},{10... | collective-permute-start | bytes 184328 | tf_op jit(solution)/shard_map/ppermute | solution.py:564
  19.8 9.8 %collective-permute-start.7 = (f32[1,120,128]{2,1,0:T(8,128)S(1)}, f32[1,120,128]{2,1,0:T(8,128)S(1)}, u32[]{:S(2)}, u32[]{:S(2)}) collective-permute-start(f32[1,120,128]{2,1,0:T(8,128)S(1)} %get-tuple-element.57), channel_id=1, source_target_pairs={{0,16},{8,24},{16,0},{24,8},{1,17},{9,25},{17,1},{25,9},{2,18},{10... | collective-permute-start | bytes 184328 | tf_op jit(solution)/shard_map/ppermute | solution.py:564
  21.5 8.0 %collective-permute-start.8 = (f32[1,120,128]{2,1,0:T(8,128)S(1)}, f32[1,120,128]{2,1,0:T(8,128)S(1)}, u32[]{:S(2)}, u32[]{:S(2)}) collective-permute-start(f32[1,120,128]{2,1,0:T(8,128)S(1)} %get-tuple-element.58), channel_id=1, source_target_pairs={{0,24},{8,0},{16,8},{24,16},{1,25},{9,1},{17,9},{25,17},{2,26},{10... | collective-permute-start | bytes 184328 | tf_op jit(solution)/shard_map/ppermute | solution.py:564

commit v10 on v8

--- a/solution.py
+++ b/solution.py
@@ -121,9 +121,7 @@
     to_owner = (source == my_owner).astype(F32)
     counted = jnp.dot(to_owner.astype(BF16), earlier_fibres(fibres), preferred_element_type=F32)
     rank = jnp.sum(to_owner * counted, axis=0, keepdims=True).astype(jnp.int32)
-    target = my_owner
-    if rel:
-        target = jnp.where(my_owner >= me, my_owner - me, my_owner - me + fib_count)
+    target = my_owner ^ me if rel else my_owner
     base = target * lanes + rank
     place_of = jnp.concatenate([base + h * per for h in range(pack)], 1)
     row = lax.broadcasted_iota(jnp.int32, table_ref.shape, 0)
@@ -138,9 +136,7 @@
     source = lax.broadcasted_iota(jnp.int32, owner.shape, 0)
     mine = (owner == me.astype(F32)).astype(F32)
     rank_in = jnp.dot(mine.astype(BF16), earlier_fibres(fibres), preferred_element_type=F32).astype(jnp.int32)
-    order = source
-    if rel:
-        order = jnp.where(me >= source, me - source, me - source + fib_count)
+    order = source ^ me if rel else source
     arrival = jnp.where(mine > 0.0, order * lanes + rank_in, -total_lanes)
     tall = lax.broadcasted_iota(jnp.int32, (total_lanes, fibres), 0)
     landing = jnp.zeros((ROWS, total_lanes), F32)
@@ -366,23 +362,6 @@
     )(arrived, pixels, ivar)
 
 
-def recv_kernel(moves, place_ref, slots_ref, table_ref):
-    write_recv_table(*moves, place_ref[0], slots_ref, table_ref)
-
-
-def recv_moves(moves, place, slots, fibres):
-    fib_count, pack, per, _ = moves
-    return pl.pallas_call(
-        functools.partial(recv_kernel, moves),
-        in_specs=[in_smem, in_vmem],
-        out_specs=in_vmem,
-        out_shape=shaped((pack * fibres, fib_count * pack * per), BF16),
-        compiler_params=params(),
-        cost_estimate=cost(1e6, 1e6),
-        name="recv_moves",
-    )(place, slots)
-
-
 def solve_kernel(
     wav_count, place_ref, coupling_ref, left_ref, right_ref, pixel_ref, ivar_ref, weight_ref,
     theirs_ref, solved_s, lead_s, rest_s,
@@ -559,10 +538,8 @@
 def exchange(pieces, fib_count):
     if len(pieces) == 1:
         return [lax.all_to_all(pieces[0], "fib", split_axis=2, concat_axis=2, tiled=True)]
-    arrived = [pieces[0]]
-    for d in range(1, fib_count):
-        arrived.append(lax.ppermute(pieces[d], "fib", [(i, (i + d) % fib_count) for i in range(fib_count)]))
-    return arrived
+    swapped = [lax.ppermute(pieces[d], "fib", [(i, i ^ d) for i in range(fib_count)]) for d in range(1, fib_count)]
+    return [pieces[0]] + swapped
 
 
 def landed(refs, table):
@@ -574,58 +551,76 @@
     return [moved[v * part : (v + 1) * part] for v in range(values)]
 
 
-def weights_end_kernel(pack, total, place_ref, table_ref, *refs):
-    *piece_refs, ivar_ref, res_ref = refs
-    weight, band = landed(piece_refs, table_ref[...])
-    rows, fibres = ivar_ref.shape
+def columns_of(table, which, pieces):
+    lanes = table.shape[1] // pieces
+    return jnp.concatenate([table[:, d * lanes : (d + 1) * lanes] for d in which], 1)
+
+
+def early_kernel(moves, which, pieces, place_ref, slots_ref, *refs):
+    *piece_refs, table_ref, sums_ref = refs
+    write_recv_table(*moves, place_ref[0], slots_ref, table_ref)
+    for v, moved in enumerate(landed(piece_refs, columns_of(table_ref[...], which, pieces))):
+        sums_ref[v] = moved
+
+
+def place_early(moves, which, place, slots, weight_pieces, fibres):
+    fib_count, pack, per, _ = moves
+    early = [weight_pieces[d] for d in which]
+    values, part, _ = early[0].shape
+    return pl.pallas_call(
+        functools.partial(early_kernel, moves, which, len(weight_pieces)),
+        in_specs=[in_smem] + [in_vmem] * (1 + len(early)),
+        out_specs=[in_vmem] * 2,
+        out_shape=[
+            shaped((pack * fibres, fib_count * pack * per), BF16),
+            shaped((values, part, pack * fibres)),
+        ],
+        compiler_params=params(),
+        cost_estimate=cost(0, 0),
+        name="place_early",
+    )(place, slots, *early)
+
+
+def last_kernel(pack, total, late, pieces, place_ref, table_ref, sums_ref, *refs):
+    late_refs, refs = refs[: len(late)], refs[len(late) :]
+    flux_refs, (flux_v, ivar_v, res_v) = refs[:pieces], refs[pieces:]
+    table = table_ref[...]
+    sums = [sums_ref[v] for v in range(2)]
+    if late:
+        sums = [x + y for x, y in zip(sums, landed(late_refs, columns_of(table, late, pieces)))]
+    rows, fibres = ivar_v.shape
     part = rows // pack
     start = (place_ref[1] * 2 + place_ref[2]) * rows
     for h in range(pack):
         at = slice(h * part, (h + 1) * part)
         cut = slice(h * fibres, (h + 1) * fibres)
         row = start + h * part + lax.broadcasted_iota(jnp.int32, (part, 1), 0)
-        w, b = weight[:, cut], band[:, cut]
-        before = jnp.where(row == 0, 0.0, b)
-        after = jnp.where(row == total - 1, 0.0, b)
-        ivar_ref[at, :] = w
-        res_ref[0, at, :] = before
-        res_ref[1, at, :] = jnp.minimum(w, 1.0) - before - after
-        res_ref[2, at, :] = after
-
-
-def end_weights(place, table, pieces, pack, fibres, total):
-    rows = pieces[0].shape[1] * pack
-    return pl.pallas_call(
-        functools.partial(weights_end_kernel, pack, total),
-        in_specs=[in_smem] + [in_vmem] * (1 + len(pieces)),
-        out_specs=[in_vmem] * 2,
-        out_shape=[shaped((rows, fibres)), shaped((3, rows, fibres))],
-        compiler_params=params(),
-        cost_estimate=cost(4 * rows * table.size, 6 * rows * fibres * 4),
-        name="end_weights",
-    )(place, table, *pieces)
-
-
-def flux_end_kernel(pack, table_ref, *refs):
-    *piece_refs, flux_ref = refs
-    (flux,) = landed(piece_refs, table_ref[...])
-    rows, fibres = flux_ref.shape
-    part = rows // pack
+        weight, band = sums[0][:, cut], sums[1][:, cut]
+        before = jnp.where(row == 0, 0.0, band)
+        after = jnp.where(row == total - 1, 0.0, band)
+        ivar_v[at, :] = weight
+        res_v[0, at, :] = before
+        res_v[1, at, :] = jnp.minimum(weight, 1.0) - before - after
+        res_v[2, at, :] = after
+    (flux,) = landed(flux_refs, table)
     for h in range(pack):
-        flux_ref[h * part : (h + 1) * part, :] = flux[:, h * fibres : (h + 1) * fibres]
-
-
-def end_flux(table, pieces, pack, fibres):
-    rows = pieces[0].shape[1] * pack
-    return pl.pallas_call(
-        functools.partial(flux_end_kernel, pack),
-        in_specs=[in_vmem] * (1 + len(pieces)),
-        out_specs=in_vmem,
-        out_shape=shaped((rows, fibres)),
-        compiler_params=params(),
-        cost_estimate=cost(2 * rows * table.size, 2 * rows * fibres * 4),
-        name="end_flux",
-    )(table, *pieces)
+        flux_v[h * part : (h + 1) * part, :] = flux[:, h * fibres : (h + 1) * fibres]
+
+
+def place_last(place, table, sums, late, weight_pieces, flux_pieces, pack, fibres, total):
+    rows = flux_pieces[0].shape[1] * pack
+    late_pieces = [weight_pieces[d] for d in late]
+    args = (table, sums, *late_pieces, *flux_pieces)
+    outs = [shaped((rows, fibres)), shaped((rows, fibres)), shaped((3, rows, fibres))]
+    return pl.pallas_call(
+        functools.partial(last_kernel, pack, total, late, len(flux_pieces)),
+        in_specs=[in_smem] + [in_vmem] * len(args),
+        out_specs=[in_vmem] * 3,
+        out_shape=outs,
+        compiler_params=params(),
+        cost_estimate=cost(0, 0),
+        name="place_last",
+    )(place, *args)
 
 
 def after(value, done):
@@ -641,7 +636,7 @@
     pack = max(1, LANES // per)
     while pack > 1 and rows % (pack * ROWS):
         pack //= 2
-    rel = pack * per == LANES
+    rel = pack * per == LANES and fib_count & (fib_count - 1) == 0
     pieces = fib_count if rel else 1
     place = jnp.stack([lax.axis_index(axis) for axis in ("fib", "wav", "exp")]).astype(jnp.int32)
     coupling, counts, slots = coupling[None], counts[None], owner_slot[None]
@@ -663,16 +658,15 @@
 
     pixel_s, ivar_s = stream_layout(left[0] + right[0], pixels, ivar)
     theirs, solved = flux_sums(wav_count, place, coupling, left, right, pixel_s, ivar_s, weight_t)
-    ahead = sum(piece[0, :ROWS, :] for piece in weight_pieces[1:-1] or weight_pieces)
+    late = [fib_count // 2] if rel else []
+    early = [d for d in range(len(weight_pieces)) if d not in late]
+    ahead = sum(weight_pieces[d][0, :ROWS, :] for d in early[1:] or early)
     arriving = lax.ppermute(theirs, "exp", swap)
     mine = kept_flux(after(place, theirs), coupling, solved, weight_m)
     sorted_pieces = sort_fibres(arriving, mine, send_table, pack, pieces, scale, ahead)
     flux_pieces = exchange(sorted_pieces, fib_count)
-    recv_table = recv_moves(moves, after(place, sorted_pieces[0]), slots, fibres)
-
-    ivar, res = end_weights(place, recv_table, weight_pieces, pack, fibres, total)
-    flux = end_flux(recv_table, flux_pieces, pack, fibres)
-    return (flux, ivar, res)
+    recv_table, placed = place_early(moves, early, after(place, sorted_pieces[0]), slots, weight_pieces, fibres)
+    return place_last(place, recv_table, placed, late, weight_pieces, flux_pieces, pack, fibres, total)
 
 
 def solution(mesh):

time: 31.3 us -> 32.1 us (1.026)
  waiting for transfers between devices: 4.39 us -> 6.66 us
  Pallas kernels: 11.8 us -> 11.1 us
  starting transfers between devices: 14.1 us -> 13.4 us
    ppermute x6, waiting for transfers between devices: 4.38 us -> 6.65 us  [exchange(): lax.ppermute(pieces[d], 'fib', [(i, i ^ d) for i in range(fib_count)])]
    pallas_call x3 -> x2, Pallas kernels: 4.35 us -> 3.63 us  [the longest x1 1.88 us: place_last(): pl.pallas_call(functools.partial(last_kernel, pack, total, late, len(flux...]
    ppermute x6, starting transfers between devices: 9.9 us -> 9.24 us  [exchange(): lax.ppermute(pieces[d], 'fib', [(i, i ^ d) for i in range(fib_count)])]
  transfers between devices with their start and end apart: 10 -> 10, of which waited for: 2 -> 3; matrix products, arithmetic and copies ran while one was open for 0% -> 0% of each run, Pallas kernels for 28% -> 22%
where the time goes in v10:
time: 32.1 us; the launch traced here: 32 us
  starting transfers between devices  13.4 us (42%)
  Pallas kernels  11.1 us (35%)
  waiting for transfers between devices  6.66 us (21%)
  between operations  0.72 us (2%)
    ppermute x6, starting transfers between devices, exchange(): lax.ppermute(pieces[d], 'fib', [(i, i ^ d) for i in range(fib_count)])  9.24 us
    ppermute x6, waiting for transfers between devices, exchange(): lax.ppermute(pieces[d], 'fib', [(i, i ^ d) for i in range(fib_count)])  6.65 us
    ppermute x1, starting transfers between devices, per_device(): left = lax.ppermute(up, 'wav', upward)  2.56 us
    pallas_call x1, Pallas kernels, flux_sums(): pl.pallas_call(functools.partial(solve_kernel, wav_count), in_specs=[in_s...  2.34 us
    pallas_call x1, Pallas kernels, sent_weights(): pl.pallas_call(functools.partial(sent_kernel, moves, wav_count), in_specs...  2.22 us
    pallas_call x1, Pallas kernels, place_last(): pl.pallas_call(functools.partial(last_kernel, pack, total, late, len(flux...  1.88 us
    pallas_call x1, Pallas kernels, place_early(): pl.pallas_call(functools.partial(early_kernel, moves, which, len(weight_p...  1.75 us
    pallas_call x1, Pallas kernels, kept_weights(): pl.pallas_call(functools.partial(kept_kernel, wav_count), in_specs=[in_sm...  1.14 us
  transfers between devices with their start and end apart: 10, of which 3 were waited for; matrix products, arithmetic and copies ran while one was open for 0% of the time, Pallas kernels for 22%

profile of v10, /device:TPU:0, one launch (start us, length us, event | category | flops | bytes accessed | tf_op | source)
XLA Modules:
  0.0 32.0 jit_solution(8835453988811440158)
XLA Ops:
  0.6 0.1 pad_add_fusion.place_ref
  0.7 2.2 %sent_weights.1 = (f32[2,240,256]{2,1,0:T(8,128)S(1)}, f32[4,240,256]{2,1,0:T(8,128)S(1)}, bf16[512,512]{1,0:T(8,128)(2,1)S(1)}, s32[1,1024]{1,0:T(1,128)S(1)}, ...) custom-call(s32[3]{0:T(128)S(1)} %pad_add_fusion.place_ref, ...), custom_call_target="tpu_custom_call" | custom-call | flops 9830400 | bytes 2949120 | tf_op jit(solution)/shard_map/sent_weights/pallas_call | solution.py:259
  2.9 0.5 %collective-permute-start.3 = (f32[2,240,256]{2,1,0:T(8,128)S(1)}, f32[2,240,256]{2,1,0:T(8,128)S(1)}, u32[]{:S(2)}, u32[]{:S(2)}) collective-permute-start(f32[2,240,256]{2,1,0:T(8,128)S(1)} %get-tuple-element.48), channel_id=1, source_target_pairs={{0,1},{1,0},{2,3},{3,2},{4,5},{5,4},{6,7},{7,6},{8,9},{9,8},{10,11... | collective-permute-start | bytes 1474568 | tf_op jit(solution)/shard_map/ppermute | solution.py:649
  3.5 1.1 %kept_weights.1 = (f32[2,240,256]{2,1,0:T(8,128)S(1)}, f32[4,240,256]{2,1,0:T(8,128)S(1)}, f32[2,8,128]{2,1,0:T(8,128)S(1)}, f32[2,8,128]{2,1,0:T(8,128)S(1)}) custom-call(s32[3]{0:T(128)S(1)} %pad_add_fusion.place_ref, f32[1,256]{1,0:T(1,128)S(1)} %get-tuple-element.33.coupling_ref, s32[1,256]{1,0:T(1,128)S(1)} %get-tuple-element.34.counts_ref, ...), custom_call_target="tpu_custom_call" | custom-call | flops 9830400 | bytes 2949120 | tf_op jit(solution)/shard_map/kept_weights/pallas_call | solution.py:332
  4.6 2.6 %collective-permute-start = (f32[2,8,128]{2,1,0:T(8,128)S(1)}, f32[2,8,128]{2,1,0:T(8,128)S(1)}, u32[]{:S(2)}, u32[]{:S(2)}) collective-permute-start(f32[2,8,128]{2,1,0:T(8,128)S(1)} %get-tuple-element.38), channel_id=1, source_target_pairs={{0,2},{2,4},{4,6},{6,0},{1,3},{3,5},{5,7},{7,1},{8,10},{10,12},{12... | collective-permute-start | bytes 24584 | tf_op jit(solution)/shard_map/ppermute | solution.py:654
  7.2 1.0 %collective-permute-start.1 = (f32[2,8,128]{2,1,0:T(8,128)S(1)}, f32[2,8,128]{2,1,0:T(8,128)S(1)}, u32[]{:S(2)}, u32[]{:S(2)}) collective-permute-start(f32[2,8,128]{2,1,0:T(8,128)S(1)} %get-tuple-element.39), channel_id=1, source_target_pairs={{2,0},{4,2},{6,4},{0,6},{3,1},{5,3},{7,5},{1,7},{10,8},{12,10},{14... | collective-permute-start | bytes 24584 | tf_op jit(solution)/shard_map/ppermute | solution.py:655
  8.2 0.0 collective-permute-done.3.theirs_ref
  8.2 0.5 %sort_weights.1 = (f32[2,120,128]{2,1,0:T(8,128)S(1)}, f32[2,120,128]{2,1,0:T(8,128)S(1)}, f32[2,120,128]{2,1,0:T(8,128)S(1)}, f32[2,120,128]{2,1,0:T(8,128)S(1)}, f32[240,256]{1,0:T(8,128)S(1)}) custom-call(f32[2,240,256]{2,1,0:T(8,128)S(1)} %collective-permute-done.3.theirs_ref, f32[2,240,256]{2,1,0:T(8,128)S(1)} %get-tuple-element.49.mine_ref, ...), custom_call_target="tpu_custom_call" | custom-call | tf_op jit(solution)/shard_map/sort_weights/pallas_call | solution.py:527
  8.7 2.1 %collective-permute-start.4 = (f32[2,120,128]{2,1,0:T(8,128)S(1)}, f32[2,120,128]{2,1,0:T(8,128)S(1)}, u32[]{:S(2)}, u32[]{:S(2)}) collective-permute-start(f32[2,120,128]{2,1,0:T(8,128)S(1)} %get-tuple-element.51), channel_id=1, source_target_pairs={{0,8},{8,0},{16,24},{24,16},{1,9},{9,1},{17,25},{25,17},{2,10},{10... | collective-permute-start | bytes 368648 | tf_op jit(solution)/shard_map/ppermute | solution.py:541
  10.7 2.5 %collective-permute-start.5 = (f32[2,120,128]{2,1,0:T(8,128)S(1)}, f32[2,120,128]{2,1,0:T(8,128)S(1)}, u32[]{:S(2)}, u32[]{:S(2)}) collective-permute-start(f32[2,120,128]{2,1,0:T(8,128)S(1)} %get-tuple-element.52), channel_id=1, source_target_pairs={{0,24},{8,16},{16,8},{24,0},{1,25},{9,17},{17,9},{25,1},{2,26},{10... | collective-permute-start | bytes 368648 | tf_op jit(solution)/shard_map/ppermute | solution.py:541
  13.2 0.3 stream_layout.1
  13.5 2.3 %flux_sums.1 = (f32[1,240,256]{2,1,0:T(8,128)S(1)}, f32[3848,128]{1,0:T(8,128)S(1)}) custom-call(s32[3]{0:T(128)S(1)} %pad_add_fusion.place_ref, f32[1,256]{1,0:T(1,128)S(1)} %get-tuple-element.33.coupling_ref, f32[2,8,128]{2,1,0:T(8,128)S(1)} %collective-permute-done.left_ref, f32[2,8,128]{2,1,0:T(8,128)S(1)} %collective-permute-done.1.right_ref, ...), custom_call_target="tpu_custom_call" | custom-call | tf_op jit(solution)/shard_map/flux_sums/pallas_call | solution.py:463
  15.8 0.1 collective-permute-start.2
  15.9 0.7 %kept_flux.1.mine_ref = f32[1,240,256]{2,1,0:T(8,128)S(1)} custom-call(s32[3]{0:T(128)S(1)} %pad_add_fusion.place_ref, f32[1,256]{1,0:T(1,128)S(1)} %get-tuple-element.33.coupling_ref, f32[3848,128]{1,0:T(8,128)S(1)} %get-tuple-element.45.solved_ref, f32[4,240,256]{2,1,0:T(8,128)S(1)} %get-tuple-element.46.weight_ref), custom_call_target="tpu_custom_call" | custom-call | flops 491520 | bytes 1966080 | tf_op jit(solution)/shard_map/kept_flux/pallas_call | solution.py:481
  16.6 0.3 collective-permute-start.6
  16.9 2.2 %collective-permute-done.5.refs_2_ = f32[2,120,128]{2,1,0:T(8,128)S(1)} collective-permute-done((f32[2,120,128]{2,1,0:T(8,128)S(1)}, f32[2,120,128]{2,1,0:T(8,128)S(1)}, u32[]{:S(2)}, u32[]{:S(2)}) %collective-permute-start.5) | collective-permute-done | bytes 122912 | tf_op jit(solution)/shard_map/ppermute | solution.py:541
  19.1 0.3 %sort_flux.1 = (f32[1,120,128]{2,1,0:T(8,128)S(1)}, f32[1,120,128]{2,1,0:T(8,128)S(1)}, f32[1,120,128]{2,1,0:T(8,128)S(1)}, f32[1,120,128]{2,1,0:T(8,128)S(1)}) custom-call(f32[1,240,256]{2,1,0:T(8,128)S(1)} %collective-permute-done.2.theirs_ref, f32[1,240,256]{2,1,0:T(8,128)S(1)} %kept_flux.1.mine_ref, bf16[512,512]{1,0:T(8,128)(2,1)S(1)} %get-tuple-element.47.table_ref, ...), custom_call_target="tpu_custom_call" | custom-call | tf_op jit(solution)/shard_map/sort_flux/pallas_call | solution.py:527
  19.4 0.6 %collective-permute-start.7 = (f32[1,120,128]{2,1,0:T(8,128)S(1)}, f32[1,120,128]{2,1,0:T(8,128)S(1)}, u32[]{:S(2)}, u32[]{:S(2)}) collective-permute-start(f32[1,120,128]{2,1,0:T(8,128)S(1)} %get-tuple-element.60), channel_id=1, source_target_pairs={{0,8},{8,0},{16,24},{24,16},{1,9},{9,1},{17,25},{25,17},{2,10},{10... | collective-permute-start | bytes 184328 | tf_op jit(solution)/shard_map/ppermute | solution.py:541
  20.1 1.5 %collective-permute-start.8 = (f32[1,120,128]{2,1,0:T(8,128)S(1)}, f32[1,120,128]{2,1,0:T(8,128)S(1)}, u32[]{:S(2)}, u32[]{:S(2)}) collective-permute-start(f32[1,120,128]{2,1,0:T(8,128)S(1)} %get-tuple-element.61), channel_id=1, source_target_pairs={{0,16},{8,24},{16,0},{24,8},{1,17},{9,25},{17,1},{25,9},{2,18},{10... | collective-permute-start | bytes 184328 | tf_op jit(solution)/shard_map/ppermute | solution.py:541
  21.5 2.4 %collective-permute-start.9 = (f32[1,120,128]{2,1,0:T(8,128)S(1)}, f32[1,120,128]{2,1,0:T(8,128)S(1)}, u32[]{:S(2)}, u32[]{:S(2)}) collective-permute-start(f32[1,120,128]{2,1,0:T(8,128)S(1)} %get-tuple-element.62), channel_id=1, source_target_pairs={{0,24},{8,16},{16,8},{24,0},{1,25},{9,17},{17,9},{25,1},{2,26},{10... | collective-permute-start | bytes 184328 | tf_op jit(solution)/shard_map/ppermute | solution.py:541
  23.9 1.7 %place_early.1 = (bf16[512,512]{1,0:T(8,128)(2,1)S(1)}, f32[2,120,512]{2,1,0:T(8,128)S(1)}) custom-call(s32[3]{0:T(128)S(1)} %pad_add_fusion.place_ref, s32[1,1024]{1,0:T(1,128)S(1)} %get-tuple-element.55.slots_ref, f32[2,120,128]{2,1,0:T(8,128)S(1)} %get-tuple-element.56.refs_0_, f32[2,120,128]{2,1,0:T(8,128)S(1)} %collective-permute-done.4.refs_1_, ...), custom_call_target="tpu_custom_call" | custom-call | tf_op jit(solution)/shard_map/place_early/pallas_call | solution.py:570
  25.6 3.2 %collective-permute-done.6.refs_0_ = f32[2,120,128]{2,1,0:T(8,128)S(1)} collective-permute-done((f32[2,120,128]{2,1,0:T(8,128)S(1)}, f32[2,120,128]{2,1,0:T(8,128)S(1)}, u32[]{:S(2)}, u32[]{:S(2)}) %collective-permute-start.6) | collective-permute-done | bytes 122912 | tf_op jit(solution)/shard_map/ppermute | solution.py:541
  28.8 1.3 %collective-permute-done.8.refs_3_ = f32[1,120,128]{2,1,0:T(8,128)S(1)} collective-permute-done((f32[1,120,128]{2,1,0:T(8,128)S(1)}, f32[1,120,128]{2,1,0:T(8,128)S(1)}, u32[]{:S(2)}, u32[]{:S(2)}) %collective-permute-start.8) | collective-permute-done | bytes 61472 | tf_op jit(solution)/shard_map/ppermute | solution.py:541
  30.1 1.9 %place_last.1 = (f32[240,256]{1,0:T(8,128)}, f32[240,256]{1,0:T(8,128)}, f32[3,240,256]{2,1,0:T(8,128)}) custom-call(s32[3]{0:T(128)S(1)} %pad_add_fusion.place_ref, bf16[512,512]{1,0:T(8,128)(2,1)S(1)} %get-tuple-element.57.table_ref, f32[2,120,512]{2,1,0:T(8,128)S(1)} %get-tuple-element.58.sums_ref, f32[2,120,128]{2,1,0:T(8,128)S(1)} %collective-permute-done.6.refs_0_, ...), custom_call_target="tpu_custom_call" | custom-call | tf_op jit(solution)/shard_map/place_last/pallas_call | solution.py:615
  (10 shorter events, 0.0 us)
Async XLA Ops:
  0.6 2.8 %copy-start = (f32[4,480,256]{2,1,0:T(8,128)S(1)}, f32[4,480,256]{2,1,0:T(8,128)}, u32[]{:S(2)}) copy-start(f32[4,480,256]{2,1,0:T(8,128)} %pixels_ref.3) | copy-start | bytes 5898244
  2.9 5.2 %collective-permute-start.3 = (f32[2,240,256]{2,1,0:T(8,128)S(1)}, f32[2,240,256]{2,1,0:T(8,128)S(1)}, u32[]{:S(2)}, u32[]{:S(2)}) collective-permute-start(f32[2,240,256]{2,1,0:T(8,128)S(1)} %get-tuple-element.48), channel_id=1, source_target_pairs={{0,1},{1,0},{2,3},{3,2},{4,5},{5,4},{6,7},{7,6},{8,9},{9,8},{10,11... | collective-permute-start | bytes 1474568 | tf_op jit(solution)/shard_map/ppermute | solution.py:649
  4.6 8.6 %collective-permute-start = (f32[2,8,128]{2,1,0:T(8,128)S(1)}, f32[2,8,128]{2,1,0:T(8,128)S(1)}, u32[]{:S(2)}, u32[]{:S(2)}) collective-permute-start(f32[2,8,128]{2,1,0:T(8,128)S(1)} %get-tuple-element.38), channel_id=1, source_target_pairs={{0,2},{2,4},{4,6},{6,0},{1,3},{3,5},{5,7},{7,1},{8,10},{10,12},{12... | collective-permute-start | bytes 24584 | tf_op jit(solution)/shard_map/ppermute | solution.py:654
  7.2 6.0 %collective-permute-start.1 = (f32[2,8,128]{2,1,0:T(8,128)S(1)}, f32[2,8,128]{2,1,0:T(8,128)S(1)}, u32[]{:S(2)}, u32[]{:S(2)}) collective-permute-start(f32[2,8,128]{2,1,0:T(8,128)S(1)} %get-tuple-element.39), channel_id=1, source_target_pairs={{2,0},{4,2},{6,4},{0,6},{3,1},{5,3},{7,5},{1,7},{10,8},{12,10},{14... | collective-permute-start | bytes 24584 | tf_op jit(solution)/shard_map/ppermute | solution.py:655
  8.7 8.2 %collective-permute-start.4 = (f32[2,120,128]{2,1,0:T(8,128)S(1)}, f32[2,120,128]{2,1,0:T(8,128)S(1)}, u32[]{:S(2)}, u32[]{:S(2)}) collective-permute-start(f32[2,120,128]{2,1,0:T(8,128)S(1)} %get-tuple-element.51), channel_id=1, source_target_pairs={{0,8},{8,0},{16,24},{24,16},{1,9},{9,1},{17,25},{25,17},{2,10},{10... | collective-permute-start | bytes 368648 | tf_op jit(solution)/shard_map/ppermute | solution.py:541
  10.7 8.3 %collective-permute-start.5 = (f32[2,120,128]{2,1,0:T(8,128)S(1)}, f32[2,120,128]{2,1,0:T(8,128)S(1)}, u32[]{:S(2)}, u32[]{:S(2)}) collective-permute-start(f32[2,120,128]{2,1,0:T(8,128)S(1)} %get-tuple-element.52), channel_id=1, source_target_pairs={{0,24},{8,16},{16,8},{24,0},{1,25},{9,17},{17,9},{25,1},{2,26},{10... | collective-permute-start | bytes 368648 | tf_op jit(solution)/shard_map/ppermute | solution.py:541
  15.8 3.3 %collective-permute-start.2 = (f32[1,240,256]{2,1,0:T(8,128)S(1)}, f32[1,240,256]{2,1,0:T(8,128)S(1)}, u32[]{:S(2)}, u32[]{:S(2)}) collective-permute-start(f32[1,240,256]{2,1,0:T(8,128)S(1)} %get-tuple-element.43), channel_id=1, source_target_pairs={{0,1},{1,0},{2,3},{3,2},{4,5},{5,4},{6,7},{7,6},{8,9},{9,8},{10,11... | collective-permute-start | bytes 737288 | tf_op jit(solution)/shard_map/ppermute | solution.py:664
  16.6 12.2 %collective-permute-start.6 = (f32[2,120,128]{2,1,0:T(8,128)S(1)}, f32[2,120,128]{2,1,0:T(8,128)S(1)}, u32[]{:S(2)}, u32[]{:S(2)}) collective-permute-start(f32[2,120,128]{2,1,0:T(8,128)S(1)} %get-tuple-element.59), channel_id=1, source_target_pairs={{0,16},{8,24},{16,0},{24,8},{1,17},{9,25},{17,1},{25,9},{2,18},{10... | collective-permute-start | bytes 368648 | tf_op jit(solution)/shard_map/ppermute | solution.py:541
  19.4 9.4 %collective-permute-start.7 = (f32[1,120,128]{2,1,0:T(8,128)S(1)}, f32[1,120,128]{2,1,0:T(8,128)S(1)}, u32[]{:S(2)}, u32[]{:S(2)}) collective-permute-start(f32[1,120,128]{2,1,0:T(8,128)S(1)} %get-tuple-element.60), channel_id=1, source_target_pairs={{0,8},{8,0},{16,24},{24,16},{1,9},{9,1},{17,25},{25,17},{2,10},{10... | collective-permute-start | bytes 184328 | tf_op jit(solution)/shard_map/ppermute | solution.py:541
  20.1 10.0 %collective-permute-start.8 = (f32[1,120,128]{2,1,0:T(8,128)S(1)}, f32[1,120,128]{2,1,0:T(8,128)S(1)}, u32[]{:S(2)}, u32[]{:S(2)}) collective-permute-start(f32[1,120,128]{2,1,0:T(8,128)S(1)} %get-tuple-element.61), channel_id=1, source_target_pairs={{0,16},{8,24},{16,0},{24,8},{1,17},{9,25},{17,1},{25,9},{2,18},{10... | collective-permute-start | bytes 184328 | tf_op jit(solution)/shard_map/ppermute | solution.py:541
  21.5 8.6 %collective-permute-start.9 = (f32[1,120,128]{2,1,0:T(8,128)S(1)}, f32[1,120,128]{2,1,0:T(8,128)S(1)}, u32[]{:S(2)}, u32[]{:S(2)}) collective-permute-start(f32[1,120,128]{2,1,0:T(8,128)S(1)} %get-tuple-element.62), channel_id=1, source_target_pairs={{0,24},{8,16},{16,8},{24,0},{1,25},{9,17},{17,9},{25,1},{2,26},{10... | collective-permute-start | bytes 184328 | tf_op jit(solution)/shard_map/ppermute | solution.py:541

commit v11 on v8

--- a/solution.py
+++ b/solution.py
@@ -289,7 +289,7 @@
 
 def kept_kernel(
     wav_count, place_ref, coupling_ref, counts_ref, good_ref, pixels_ref, ivar_ref, bits_ref,
-    sums_ref, weight_ref, up_ref, down_ref, ivar_s, pixel_s,
+    sums_ref, weight_ref, edges_ref, ivar_s, pixel_s,
 ):
     expos, width, fibres = ivar_ref.shape
     half = width // 2
@@ -320,10 +320,13 @@
         lambda e, group: bits_ref[e, pl.ds(pl.multiple_of(which * (half // BITS) + words * group, words), words), :],
         sums_ref, weight_ref, eliminate,
     )
-    for (n, d, b), out_ref in zip(states, (up_ref, down_ref)):
+    ends = []
+    for n, d, b in states:
         scale = 1.0 / (d + n)
-        out_ref[0] = coupling * (n * scale)
-        out_ref[1] = b * scale
+        ends.append((coupling * (n * scale), b * scale))
+    for other in range(wav_count):
+        for value in range(2):
+            edges_ref[other, value] = jnp.where(place_ref[1] < other, ends[0][value], ends[1][value])
 
 
 def kept_weights(wav_count, place, coupling, counts, good, pixels, ivar, bits):
@@ -331,13 +334,16 @@
     half = width // 2
     streams = expos * fibres // LANES
     count = -(-HALO // ROWS) * ROWS
-    edge = shaped((2, streams, LANES))
     edge_scratch = pltpu.VMEM((streams * odd(2 * count), LANES), F32)
     return pl.pallas_call(
         functools.partial(kept_kernel, wav_count),
         in_specs=[in_smem] + [in_vmem] * 6,
-        out_specs=[in_vmem] * 4,
-        out_shape=[shaped((2, half, fibres)), shaped((expos, half, fibres)), edge, edge],
+        out_specs=[in_vmem] * 3,
+        out_shape=[
+            shaped((2, half, fibres)),
+            shaped((expos, half, fibres)),
+            shaped((wav_count, 2, streams, LANES)),
+        ],
         scratch_shapes=[edge_scratch, edge_scratch],
         compiler_params=params(),
         cost_estimate=cost(20 * ivar.size, 6 * ivar.size),
@@ -366,28 +372,11 @@
     )(arrived, pixels, ivar)
 
 
-def recv_kernel(moves, place_ref, slots_ref, table_ref):
-    write_recv_table(*moves, place_ref[0], slots_ref, table_ref)
-
-
-def recv_moves(moves, place, slots, fibres):
-    fib_count, pack, per, _ = moves
-    return pl.pallas_call(
-        functools.partial(recv_kernel, moves),
-        in_specs=[in_smem, in_vmem],
-        out_specs=in_vmem,
-        out_shape=shaped((pack * fibres, fib_count * pack * per), BF16),
-        compiler_params=params(),
-        cost_estimate=cost(1e6, 1e6),
-        name="recv_moves",
-    )(place, slots)
-
-
 def solve_kernel(
-    wav_count, place_ref, coupling_ref, left_ref, right_ref, pixel_ref, ivar_ref, weight_ref,
+    wav_count, place_ref, coupling_ref, edges_ref, pixel_ref, ivar_ref, weight_ref,
     theirs_ref, solved_s, lead_s, rest_s,
 ):
-    streams = left_ref.shape[1]
+    streams = edges_ref.shape[2]
     expos, half, fibres = weight_ref.shape
     width = 2 * half
     pitch = odd(width)
@@ -398,9 +387,11 @@
     def row_at(i):
         return pl.ds(i, streams, stride=pitch)
 
-    def begin(edge_ref, outermost):
-        n = jnp.where(place_ref[1] == outermost, 0.0, edge_ref[0]) * back
-        return (n, 1.0 - n, jnp.where(place_ref[1] == outermost, 0.0, edge_ref[1]))
+    def begin(neighbour):
+        there = (neighbour >= 0) & (neighbour < wav_count)
+        at = jnp.clip(neighbour, 0, wav_count - 1)
+        n = jnp.where(there, edges_ref[at, 0], 0.0) * back
+        return (n, 1.0 - n, jnp.where(there, edges_ref[at, 1], 0.0))
 
     def keep(side, i, state):
         n, d, b = state
@@ -419,7 +410,7 @@
                 states[side] = advance(states[side], ivar_ref[row_at(row), :], pixel_ref[row_at(row), :], back)
         return tuple(rescaled(state) for state in states)
 
-    states = lax.fori_loop(0, middle // unrolled, eliminate, (begin(left_ref, 0), begin(right_ref, wav_count - 1)))
+    states = lax.fori_loop(0, middle // unrolled, eliminate, (begin(place_ref[1] - 1), begin(place_ref[1] + 1)))
     for side in range(2):
         keep(side, middle, states[side])
     lead, rest = lead_s[0, middle], rest_s[0, middle]
@@ -477,20 +468,20 @@
     lax.fori_loop(0, half // ROWS // unrolled, body, 0)
 
 
-def flux_sums(wav_count, place, coupling, left, right, pixels, ivar, weight):
+def flux_sums(wav_count, place, coupling, edges, pixels, ivar, weight):
     expos, half, fibres = weight.shape
-    streams = left.shape[1]
+    streams = edges.shape[2]
     factor_scratch = pltpu.VMEM((2, half + 1, streams, LANES), F32)
     return pl.pallas_call(
         functools.partial(solve_kernel, wav_count),
-        in_specs=[in_smem] + [in_vmem] * 6,
+        in_specs=[in_smem] + [in_vmem] * 5,
         out_specs=[in_vmem, in_vmem],
         out_shape=[shaped((1, half, fibres)), shaped(pixels.shape)],
         scratch_shapes=[factor_scratch, factor_scratch],
         compiler_params=params(),
         cost_estimate=cost(0, 0),
         name="flux_sums",
-    )(place, coupling, left, right, pixels, ivar, weight)
+    )(place, coupling, edges, pixels, ivar, weight)
 
 
 def kept_flux_kernel(place_ref, coupling_ref, solved_ref, weight_ref, out_ref):
@@ -574,9 +565,42 @@
     return [moved[v * part : (v + 1) * part] for v in range(values)]
 
 
-def weights_end_kernel(pack, total, place_ref, table_ref, *refs):
-    *piece_refs, ivar_ref, res_ref = refs
-    weight, band = landed(piece_refs, table_ref[...])
+def columns_of(table, which, pieces):
+    lanes = table.shape[1] // pieces
+    return jnp.concatenate([table[:, d * lanes : (d + 1) * lanes] for d in which], 1)
+
+
+def early_kernel(moves, which, pieces, place_ref, slots_ref, *refs):
+    *piece_refs, table_ref, sums_ref = refs
+    write_recv_table(*moves, place_ref[0], slots_ref, table_ref)
+    for v, moved in enumerate(landed(piece_refs, columns_of(table_ref[...], which, pieces))):
+        sums_ref[v] = moved
+
+
+def place_early(moves, which, place, slots, weight_pieces, fibres):
+    fib_count, pack, per, _ = moves
+    early = [weight_pieces[d] for d in which]
+    values, part, _ = early[0].shape
+    return pl.pallas_call(
+        functools.partial(early_kernel, moves, which, len(weight_pieces)),
+        in_specs=[in_smem] + [in_vmem] * (1 + len(early)),
+        out_specs=[in_vmem] * 2,
+        out_shape=[
+            shaped((pack * fibres, fib_count * pack * per), BF16),
+            shaped((values, part, pack * fibres)),
+        ],
+        compiler_params=params(),
+        cost_estimate=cost(0, 0),
+        name="place_early",
+    )(place, slots, *early)
+
+
+def weights_end_kernel(pack, total, late, pieces, place_ref, table_ref, sums_ref, *refs):
+    *late_refs, ivar_ref, res_ref = refs
+    weight, band = sums_ref[0], sums_ref[1]
+    if late:
+        more_weight, more_band = landed(late_refs, columns_of(table_ref[...], late, pieces))
+        weight, band = weight + more_weight, band + more_band
     rows, fibres = ivar_ref.shape
     part = rows // pack
     start = (place_ref[1] * 2 + place_ref[2]) * rows
@@ -593,17 +617,18 @@
         res_ref[2, at, :] = after
 
 
-def end_weights(place, table, pieces, pack, fibres, total):
-    rows = pieces[0].shape[1] * pack
-    return pl.pallas_call(
-        functools.partial(weights_end_kernel, pack, total),
-        in_specs=[in_smem] + [in_vmem] * (1 + len(pieces)),
+def end_weights(place, table, sums, late, weight_pieces, pack, fibres, total):
+    rows = sums.shape[1] * pack
+    late_pieces = [weight_pieces[d] for d in late]
+    return pl.pallas_call(
+        functools.partial(weights_end_kernel, pack, total, late, len(weight_pieces)),
+        in_specs=[in_smem] + [in_vmem] * (2 + len(late)),
         out_specs=[in_vmem] * 2,
         out_shape=[shaped((rows, fibres)), shaped((3, rows, fibres))],
         compiler_params=params(),
-        cost_estimate=cost(4 * rows * table.size, 6 * rows * fibres * 4),
+        cost_estimate=cost(0, 0),
         name="end_weights",
-    )(place, table, *pieces)
+    )(place, table, sums, *late_pieces)
 
 
 def flux_end_kernel(pack, table_ref, *refs):
@@ -652,25 +677,24 @@
         moves, wav_count, place, slots, coupling, counts, good_flags, clip_bits, pixel_ivar
     )
     arriving = lax.ppermute(theirs, "exp", swap)
-    mine, weight_m, up, down = kept_weights(
+    mine, weight_m, edges = kept_weights(
         wav_count, place, coupling, counts, good, pixels, ivar, bits
     )
-    upward = [(i, (i + 1) % wav_count) for i in range(wav_count)]
-    left = lax.ppermute(up, "wav", upward)
-    right = lax.ppermute(down, "wav", [(j, i) for i, j in upward])
+    edges = lax.all_to_all(edges, "wav", split_axis=0, concat_axis=0, tiled=True)
     *sorted_pieces, scale = sort_fibres(arriving, mine, send_table, pack, pieces)
     weight_pieces = exchange(sorted_pieces, fib_count)
 
-    pixel_s, ivar_s = stream_layout(left[0] + right[0], pixels, ivar)
-    theirs, solved = flux_sums(wav_count, place, coupling, left, right, pixel_s, ivar_s, weight_t)
-    ahead = sum(piece[0, :ROWS, :] for piece in weight_pieces[1:-1] or weight_pieces)
+    pixel_s, ivar_s = stream_layout(edges[0, 0] + edges[-1, 0], pixels, ivar)
+    theirs, solved = flux_sums(wav_count, place, coupling, edges, pixel_s, ivar_s, weight_t)
+    late = [fib_count // 2] if rel else []
+    early = [d for d in range(len(weight_pieces)) if d not in late]
+    ahead = sum(weight_pieces[d][0, :ROWS, :] for d in early[1:] or early)
     arriving = lax.ppermute(theirs, "exp", swap)
     mine = kept_flux(after(place, theirs), coupling, solved, weight_m)
     sorted_pieces = sort_fibres(arriving, mine, send_table, pack, pieces, scale, ahead)
     flux_pieces = exchange(sorted_pieces, fib_count)
-    recv_table = recv_moves(moves, after(place, sorted_pieces[0]), slots, fibres)
-
-    ivar, res = end_weights(place, recv_table, weight_pieces, pack, fibres, total)
+    recv_table, placed = place_early(moves, early, after(place, sorted_pieces[0]), slots, weight_pieces, fibres)
+    ivar, res = end_weights(place, recv_table, placed, late, weight_pieces, pack, fibres, total)
     flux = end_flux(recv_table, flux_pieces, pack, fibres)
     return (flux, ivar, res)
 

time: 31.3 us -> 40.9 us (1.31)
  local copies, waits for them, and re-layouts: 0.01 us -> 6.38 us
  Pallas kernels: 11.8 us -> 15.5 us
  waiting for transfers between devices: 4.39 us -> 2 us
  starting transfers between devices: 14.1 us -> 15.1 us
  other arithmetic: 0.08 us -> 0.77 us
    unnamed x2 -> x26, local copies, waits for them, and re-layouts: 0.01 us -> 6.38 us
    all_to_all x0 -> x1, starting transfers between devices: none -> 4.74 us  [per_device(): lax.all_to_all(edges, 'wav', split_axis=0, concat_axis=0, tiled=True)]
    ppermute x2 -> x0, starting transfers between devices: 3.58 us -> none  [the longest x1 2.56 us: per_device(): left = lax.ppermute(up, 'wav', upward)]
    ppermute x6, waiting for transfers between devices: 4.38 us -> 1.99 us  [exchange(): lax.ppermute(pieces[d], 'fib', [(i, (i + d) % fib_count) for i in range(f...]
    pallas_call x2, Pallas kernels: 0.82 us -> 2.52 us  [sort_fibres(): pl.pallas_call(functools.partial(sort_kernel, pack, scaled), in_specs=[in...]
    pallas_call x1, Pallas kernels: 2.22 us -> 3 us  [sent_weights(): pl.pallas_call(functools.partial(sent_kernel, moves, wav_count), in_specs...]
    add x2, other arithmetic: 0.01 us -> 0.69 us  [the longest x1 0.69 us: per_device(): ahead = sum((weight_pieces[d][0, :ROWS, :] for d in early[1:] or early))]
    pallas_call x2, Pallas kernels: 3.31 us -> 3.93 us  [the longest x1 2.18 us: place_early(): pl.pallas_call(functools.partial(early_kernel, moves, which, len(weight_p...]
  transfers between devices with their start and end apart: 10 -> 9, of which waited for: 2 -> 1; matrix products, arithmetic and copies ran while one was open for 0% -> 2% of each run, Pallas kernels for 28% -> 28%
where the time goes in v11:
time: 40.9 us; the launch traced here: 40.5 us
  Pallas kernels  15.5 us (38%)
  starting transfers between devices  15.1 us (37%)
  local copies, waits for them, and re-layouts  6.38 us (16%)
  waiting for transfers between devices  2 us (5%)
  other arithmetic  0.77 us (2%)
  between operations  0.76 us (2%)
    ppermute x6, starting transfers between devices, exchange(): lax.ppermute(pieces[d], 'fib', [(i, (i + d) % fib_count) for i in range(f...  9.75 us
    unnamed x26, local copies, waits for them, and re-layouts  6.38 us
    all_to_all x1, starting transfers between devices, per_device(): lax.all_to_all(edges, 'wav', split_axis=0, concat_axis=0, tiled=True)  4.74 us
    pallas_call x1, Pallas kernels, sent_weights(): pl.pallas_call(functools.partial(sent_kernel, moves, wav_count), in_specs...  3 us
    pallas_call x2, Pallas kernels, sort_fibres(): pl.pallas_call(functools.partial(sort_kernel, pack, scaled), in_specs=[in...  2.52 us
    pallas_call x1, Pallas kernels, flux_sums(): pl.pallas_call(functools.partial(solve_kernel, wav_count), in_specs=[in_s...  2.35 us
    pallas_call x1, Pallas kernels, place_early(): pl.pallas_call(functools.partial(early_kernel, moves, which, len(weight_p...  2.18 us
    ppermute x6, waiting for transfers between devices, exchange(): lax.ppermute(pieces[d], 'fib', [(i, (i + d) % fib_count) for i in range(f...  1.99 us
  transfers between devices with their start and end apart: 9, of which 1 were waited for; matrix products, arithmetic and copies ran while one was open for 2% of the time, Pallas kernels for 28%

profile of v11, /device:TPU:0, one launch (start us, length us, event | category | flops | bytes accessed | tf_op | source)
XLA Modules:
  0.0 40.5 jit_solution(7151805219338162911)
XLA Ops:
  0.7 3.0 %sent_weights.1 = (f32[2,240,256]{2,1,0:T(8,128)}, f32[4,240,256]{2,1,0:T(8,128)S(1)}, bf16[512,512]{1,0:T(8,128)(2,1)S(1)}, s32[1,1024]{1,0:T(1,128)S(1)}, f32[...) custom-call(s32[3]{0:T(128)S(1)} %pad_add_fusion.place_ref, ...), custom_call_target="tpu_custom_call" | custom-call | flops 9830400 | bytes 2949120 | tf_op jit(solution)/shard_map/sent_weights/pallas_call | solution.py:263
  4.3 1.7 %kept_weights.1 = (f32[2,240,256]{2,1,0:T(8,128)S(1)}, f32[4,240,256]{2,1,0:T(8,128)S(1)}, f32[4,2,8,128]{3,2,1,0:T(8,128)}) custom-call(s32[3]{0:T(128)S(1)} %pad_add_fusion.place_ref, f32[1,256]{1,0:T(1,128)S(1)} %get-tuple-element.34.coupling_ref, s32[1,256]{1,0:T(1,128)S(1)} %get-tuple-element.35.counts_ref, s32[4,256]{1,0:T(4,128)S(1)} %get-tuple-element.36.good_ref, ...), custom_call_target="tpu_custom_call" | custom-call | flops 9830400 | bytes 2949120 | tf_op jit(solution)/shard_map/kept_weights/pallas_call | solution.py:338
  6.0 1.0 %copy-done.3 = f32[4,240,256]{2,1,0:T(8,128)} copy-done((f32[4,240,256]{2,1,0:T(8,128)}, f32[4,240,256]{2,1,0:T(8,128)S(1)}, u32[]{:S(2)}) %copy-start.3) | copy-done | bytes 983064
  7.0 0.8 %copy-done.5 = f32[2,240,256]{2,1,0:T(8,128)} copy-done((f32[2,240,256]{2,1,0:T(8,128)}, f32[2,240,256]{2,1,0:T(8,128)S(1)}, u32[]{:S(2)}) %copy-start.5) | copy-done | bytes 491544
  7.7 4.7 %all-to-all-start = ((f32[4,2,8,128]{3,2,1,0:T(8,128)}), f32[4,2,8,128]{3,2,1,0:T(8,128)S(1)}, u32[]{:S(2)}, u32[]{:S(2)}) async-start(f32[4,2,8,128]{3,2,1,0:T(8,128)} %get-tuple-element.39), calls=%async_computation | async-start | bytes 65536 | tf_op jit(solution)/shard_map/all_to_all | solution.py:683
  12.5 1.0 %copy-done.6 = f32[2,240,256]{2,1,0:T(8,128)S(1)} copy-done((f32[2,240,256]{2,1,0:T(8,128)S(1)}, f32[2,240,256]{2,1,0:T(8,128)}, u32[]{:S(2)}) %copy-start.6) | copy-done | bytes 491544
  13.5 2.2 %sort_weights.1 = (f32[2,120,128]{2,1,0:T(8,128)S(1)}, f32[2,120,128]{2,1,0:T(8,128)}, f32[2,120,128]{2,1,0:T(8,128)S(1)}, f32[2,120,128]{2,1,0:T(8,128)}, f32[240,256]{1,0:T(8,128)S(1)}) custom-call(f32[2,240,256]{2,1,0:T(8,128)} %collective-permute-done.1.theirs_ref, f32[2,240,256]{2,1,0:T(8,128)S(1)} %copy-done.6, ...), custom_call_target="tpu_custom_call" | custom-call | tf_op jit(solution)/shard_map/sort_weights/pallas_call | solution.py:539
  15.7 0.7 %copy-done.7 = f32[240,256]{1,0:T(8,128)} copy-done((f32[240,256]{1,0:T(8,128)}, f32[240,256]{1,0:T(8,128)S(1)}, u32[]{:S(2)}) %copy-start.7) | copy-done | bytes 245784
  16.4 0.7 %copy-done.9 = f32[2,120,128]{2,1,0:T(8,128)} copy-done((f32[2,120,128]{2,1,0:T(8,128)}, f32[2,120,128]{2,1,0:T(8,128)S(1)}, u32[]{:S(2)}) %copy-start.9) | copy-done | bytes 122904
  17.0 0.7 %copy-done.11 = f32[2,120,128]{2,1,0:T(8,128)} copy-done((f32[2,120,128]{2,1,0:T(8,128)}, f32[2,120,128]{2,1,0:T(8,128)S(1)}, u32[]{:S(2)}) %copy-start.11) | copy-done | bytes 122904
  17.7 1.6 %collective-permute-start.2 = (f32[2,120,128]{2,1,0:T(8,128)}, f32[2,120,128]{2,1,0:T(8,128)}, u32[]{:S(2)}, u32[]{:S(2)}) collective-permute-start(f32[2,120,128]{2,1,0:T(8,128)} %get-tuple-element.51), channel_id=1, source_target_pairs={{0,8},{8,16},{16,24},{24,0},{1,9},{9,17},{17,25},{25,1},{2,10},{10... | collective-permute-start | bytes 368648 | tf_op jit(solution)/shard_map/ppermute | solution.py:555
  19.3 2.2 %collective-permute-start.3 = (f32[2,120,128]{2,1,0:T(8,128)}, f32[2,120,128]{2,1,0:T(8,128)}, u32[]{:S(2)}, u32[]{:S(2)}) collective-permute-start(f32[2,120,128]{2,1,0:T(8,128)} %get-tuple-element.52), channel_id=1, source_target_pairs={{0,24},{8,0},{16,8},{24,16},{1,25},{9,1},{17,9},{25,17},{2,26},{10... | collective-permute-start | bytes 368648 | tf_op jit(solution)/shard_map/ppermute | solution.py:555
  21.5 1.5 %copy-done.2 = f32[4,480,256]{2,1,0:T(8,128)S(1)} copy-done((f32[4,480,256]{2,1,0:T(8,128)S(1)}, f32[4,480,256]{2,1,0:T(8,128)}, u32[]{:S(2)}) %copy-start.2) | copy-done | bytes 1966104
  23.3 2.3 %flux_sums.1 = (f32[1,240,256]{2,1,0:T(8,128)S(1)}, f32[3848,128]{1,0:T(8,128)S(1)}) custom-call(s32[3]{0:T(128)S(1)} %pad_add_fusion.place_ref, f32[1,256]{1,0:T(1,128)S(1)} %get-tuple-element.34.coupling_ref, f32[4,2,8,128]{3,2,1,0:T(8,128)S(1)} %all-to-all-done.edges_ref, f32[3848,128]{1,0:T(8,128)S(1)} %get-tuple-element.40.pixel_ref, ...), custom_call_target="tpu_custom_call" | custom-call | tf_op jit(solution)/shard_map/flux_sums/pallas_call | solution.py:475
  25.8 0.7 %kept_flux.1.mine_ref = f32[1,240,256]{2,1,0:T(8,128)S(1)} custom-call(s32[3]{0:T(128)S(1)} %pad_add_fusion.place_ref, f32[1,256]{1,0:T(1,128)S(1)} %get-tuple-element.34.coupling_ref, f32[3848,128]{1,0:T(8,128)S(1)} %get-tuple-element.45.solved_ref, f32[4,240,256]{2,1,0:T(8,128)S(1)} %copy-done.4), custom_call_target="tpu_custom_call" | custom-call | flops 491520 | bytes 1966080 | tf_op jit(solution)/shard_map/kept_flux/pallas_call | solution.py:493
  26.6 0.8 %collective-permute-start.7 = (f32[2,120,128]{2,1,0:T(8,128)S(1)}, f32[2,120,128]{2,1,0:T(8,128)S(1)}, u32[]{:S(2)}, u32[]{:S(2)}) collective-permute-start(f32[2,120,128]{2,1,0:T(8,128)S(1)} %copy-done.12), channel_id=1, source_target_pairs={{0,16},{8,24},{16,0},{24,8},{1,17},{9,25},{17,1},{25,9},{2,18},{10... | collective-permute-start | bytes 368648 | tf_op jit(solution)/shard_map/ppermute | solution.py:555
  27.4 0.7 %fusion.refs_1_ = f32[8,128]{1,0:T(8,128)S(1)} fusion(f32[2,120,128]{2,1,0:T(8,128)} %collective-permute-done.3.refs_2_, f32[2,120,128]{2,1,0:T(8,128)} %collective-permute-done.2.refs_1_), kind=kLoop, calls=%fused_computation.1 | loop fusion | flops 1024 | bytes 12288 | tf_op jit(solution)/shard_map/add | solution.py:691
  28.5 1.6 %collective-permute-start.4 = (f32[1,120,128]{2,1,0:T(8,128)S(1)}, f32[1,120,128]{2,1,0:T(8,128)S(1)}, u32[]{:S(2)}, u32[]{:S(2)}) collective-permute-start(f32[1,120,128]{2,1,0:T(8,128)S(1)} %get-tuple-element.58), channel_id=1, source_target_pairs={{0,8},{8,16},{16,24},{24,0},{1,9},{9,17},{17,25},{25,1},{2,10},{10... | collective-permute-start | bytes 184328 | tf_op jit(solution)/shard_map/ppermute | solution.py:555
  30.1 1.3 %collective-permute-start.5 = (f32[1,120,128]{2,1,0:T(8,128)S(1)}, f32[1,120,128]{2,1,0:T(8,128)S(1)}, u32[]{:S(2)}, u32[]{:S(2)}) collective-permute-start(f32[1,120,128]{2,1,0:T(8,128)S(1)} %get-tuple-element.59), channel_id=1, source_target_pairs={{0,16},{8,24},{16,0},{24,8},{1,17},{9,25},{17,1},{25,9},{2,18},{10... | collective-permute-start | bytes 184328 | tf_op jit(solution)/shard_map/ppermute | solution.py:555
  31.3 2.2 %collective-permute-start.6 = (f32[1,120,128]{2,1,0:T(8,128)S(1)}, f32[1,120,128]{2,1,0:T(8,128)S(1)}, u32[]{:S(2)}, u32[]{:S(2)}) collective-permute-start(f32[1,120,128]{2,1,0:T(8,128)S(1)} %get-tuple-element.60), channel_id=1, source_target_pairs={{0,24},{8,0},{16,8},{24,16},{1,25},{9,1},{17,9},{25,17},{2,26},{10... | collective-permute-start | bytes 184328 | tf_op jit(solution)/shard_map/ppermute | solution.py:555
  33.6 2.2 %place_early.1 = (bf16[512,512]{1,0:T(8,128)(2,1)S(1)}, f32[2,120,512]{2,1,0:T(8,128)S(1)}) custom-call(s32[3]{0:T(128)S(1)} %pad_add_fusion.place_ref, s32[1,1024]{1,0:T(1,128)S(1)} %get-tuple-element.55.slots_ref, f32[2,120,128]{2,1,0:T(8,128)S(1)} %copy-done.10, f32[2,120,128]{2,1,0:T(8,128)} %collective-permute-done.2.refs_1_, ...), custom_call_target="tpu_custom_call" | custom-call | tf_op jit(solution)/shard_map/place_early/pallas_call | solution.py:584
  35.8 2.0 %collective-permute-done.7.refs_0_ = f32[2,120,128]{2,1,0:T(8,128)S(1)} collective-permute-done((f32[2,120,128]{2,1,0:T(8,128)S(1)}, f32[2,120,128]{2,1,0:T(8,128)S(1)}, u32[]{:S(2)}, u32[]{:S(2)}) %collective-permute-start.7) | collective-permute-done | bytes 122912 | tf_op jit(solution)/shard_map/ppermute | solution.py:555
  37.7 1.8 %end_weights.1 = (f32[240,256]{1,0:T(8,128)}, f32[3,240,256]{2,1,0:T(8,128)}) custom-call(s32[3]{0:T(128)S(1)} %pad_add_fusion.place_ref, bf16[512,512]{1,0:T(8,128)(2,1)S(1)} %get-tuple-element.57.table_ref, f32[2,120,512]{2,1,0:T(8,128)S(1)} %get-tuple-element.61.sums_ref, f32[2,120,128]{2,1,0:T(8,128)S(1)} %collective-permute-done.7.refs_0_), custom_call_target="tpu_custom_call" | custom-call | tf_op jit(solution)/shard_map/end_weights/pallas_call | solution.py:623
  39.5 1.0 %end_flux.1 = f32[240,256]{1,0:T(8,128)} custom-call(bf16[512,512]{1,0:T(8,128)(2,1)S(1)} %get-tuple-element.57.table_ref, f32[1,120,128]{2,1,0:T(8,128)S(1)} %get-tuple-element.53.refs_0_, f32[1,120,128]{2,1,0:T(8,128)S(1)} %collective-permute-done.4.refs_1_, f32[1,120,128]{2,1,0:T(8,128)S(1)} %collective-permute-done.5.refs_2_, ...), custom_call_target="tpu_custom_call" | custom-call | flops 125829120 | bytes 491520 | tf_op jit(solution)/shard_map/end_flux/pallas_call | solution.py:645
  (33 shorter events, 1.4 us)
Async XLA Ops:
  0.6 3.6 %copy-start = (f32[4,480,256]{2,1,0:T(8,128)S(1)}, f32[4,480,256]{2,1,0:T(8,128)}, u32[]{:S(2)}) copy-start(f32[4,480,256]{2,1,0:T(8,128)} %pixels_ref.3) | copy-start | bytes 5898244
  3.7 2.3 %copy-start.1 = (f32[4,480,256]{2,1,0:T(8,128)}, f32[4,480,256]{2,1,0:T(8,128)S(1)}, u32[]{:S(2)}) copy-start(f32[4,480,256]{2,1,0:T(8,128)S(1)} %get-tuple-element.37.ivar_ref) | copy-start | bytes 5898244
  3.7 8.7 %collective-permute-start.1 = (f32[2,240,256]{2,1,0:T(8,128)}, f32[2,240,256]{2,1,0:T(8,128)}, u32[]{:S(2)}, u32[]{:S(2)}) collective-permute-start(f32[2,240,256]{2,1,0:T(8,128)} %get-tuple-element.48), channel_id=1, source_target_pairs={{0,1},{1,0},{2,3},{3,2},{4,5},{5,4},{6,7},{7,6},{8,9},{9,8},{10,11... | collective-permute-start | bytes 1474568 | tf_op jit(solution)/shard_map/ppermute | solution.py:679
  6.0 1.0 %copy-start.3 = (f32[4,240,256]{2,1,0:T(8,128)}, f32[4,240,256]{2,1,0:T(8,128)S(1)}, u32[]{:S(2)}) copy-start(f32[4,240,256]{2,1,0:T(8,128)S(1)} %get-tuple-element.46.weight_ref) | copy-start | bytes 2949124
  7.0 0.8 %copy-start.5 = (f32[2,240,256]{2,1,0:T(8,128)}, f32[2,240,256]{2,1,0:T(8,128)S(1)}, u32[]{:S(2)}) copy-start(f32[2,240,256]{2,1,0:T(8,128)S(1)} %get-tuple-element.49.mine_ref) | copy-start | bytes 1474564
  7.7 13.8 %all-to-all-start = ((f32[4,2,8,128]{3,2,1,0:T(8,128)}), f32[4,2,8,128]{3,2,1,0:T(8,128)S(1)}, u32[]{:S(2)}, u32[]{:S(2)}) async-start(f32[4,2,8,128]{3,2,1,0:T(8,128)} %get-tuple-element.39), calls=%async_computation | async-start | bytes 65536 | tf_op jit(solution)/shard_map/all_to_all | solution.py:683
  12.5 1.0 %copy-start.6 = (f32[2,240,256]{2,1,0:T(8,128)S(1)}, f32[2,240,256]{2,1,0:T(8,128)}, u32[]{:S(2)}) copy-start(f32[2,240,256]{2,1,0:T(8,128)} %copy-done.5) | copy-start | bytes 1474564
  15.7 0.7 %copy-start.7 = (f32[240,256]{1,0:T(8,128)}, f32[240,256]{1,0:T(8,128)S(1)}, u32[]{:S(2)}) copy-start(f32[240,256]{1,0:T(8,128)S(1)} %get-tuple-element.50.refs_0_) | copy-start | bytes 737284
  16.4 0.7 %copy-start.9 = (f32[2,120,128]{2,1,0:T(8,128)}, f32[2,120,128]{2,1,0:T(8,128)S(1)}, u32[]{:S(2)}) copy-start(f32[2,120,128]{2,1,0:T(8,128)S(1)} %get-tuple-element.56.refs_0_) | copy-start | bytes 368644
  17.0 0.7 %copy-start.11 = (f32[2,120,128]{2,1,0:T(8,128)}, f32[2,120,128]{2,1,0:T(8,128)S(1)}, u32[]{:S(2)}) copy-start(f32[2,120,128]{2,1,0:T(8,128)S(1)} %get-tuple-element.62) | copy-start | bytes 368644
  17.7 9.7 %collective-permute-start.2 = (f32[2,120,128]{2,1,0:T(8,128)}, f32[2,120,128]{2,1,0:T(8,128)}, u32[]{:S(2)}, u32[]{:S(2)}) collective-permute-start(f32[2,120,128]{2,1,0:T(8,128)} %get-tuple-element.51), channel_id=1, source_target_pairs={{0,8},{8,16},{16,24},{24,0},{1,9},{9,17},{17,25},{25,1},{2,10},{10... | collective-permute-start | bytes 368648 | tf_op jit(solution)/shard_map/ppermute | solution.py:555
  19.3 8.1 %collective-permute-start.3 = (f32[2,120,128]{2,1,0:T(8,128)}, f32[2,120,128]{2,1,0:T(8,128)}, u32[]{:S(2)}, u32[]{:S(2)}) collective-permute-start(f32[2,120,128]{2,1,0:T(8,128)} %get-tuple-element.52), channel_id=1, source_target_pairs={{0,24},{8,0},{16,8},{24,16},{1,25},{9,1},{17,9},{25,17},{2,26},{10... | collective-permute-start | bytes 368648 | tf_op jit(solution)/shard_map/ppermute | solution.py:555
  21.5 1.5 %copy-start.2 = (f32[4,480,256]{2,1,0:T(8,128)S(1)}, f32[4,480,256]{2,1,0:T(8,128)}, u32[]{:S(2)}) copy-start(f32[4,480,256]{2,1,0:T(8,128)} %copy-done.1) | copy-start | bytes 5898244
  23.3 2.5 %copy-start.4 = (f32[4,240,256]{2,1,0:T(8,128)S(1)}, f32[4,240,256]{2,1,0:T(8,128)}, u32[]{:S(2)}) copy-start(f32[4,240,256]{2,1,0:T(8,128)} %copy-done.3) | copy-start | bytes 2949124
  25.7 0.9 %copy-start.12 = (f32[2,120,128]{2,1,0:T(8,128)S(1)}, f32[2,120,128]{2,1,0:T(8,128)}, u32[]{:S(2)}) copy-start(f32[2,120,128]{2,1,0:T(8,128)} %copy-done.11) | copy-start | bytes 368644
  25.7 2.4 %copy-start.8 = (f32[240,256]{1,0:T(8,128)S(1)}, f32[240,256]{1,0:T(8,128)}, u32[]{:S(2)}) copy-start(f32[240,256]{1,0:T(8,128)} %copy-done.7) | copy-start | bytes 737284
  25.7 2.4 %collective-permute-start = (f32[1,240,256]{2,1,0:T(8,128)S(1)}, f32[1,240,256]{2,1,0:T(8,128)S(1)}, u32[]{:S(2)}, u32[]{:S(2)}) collective-permute-start(f32[1,240,256]{2,1,0:T(8,128)S(1)} %get-tuple-element.43), channel_id=1, source_target_pairs={{0,1},{1,0},{2,3},{3,2},{4,5},{5,4},{6,7},{7,6},{8,9},{9,8},{10,11... | collective-permute-start | bytes 737288 | tf_op jit(solution)/shard_map/ppermute | solution.py:692
  25.8 7.8 %copy-start.10 = (f32[2,120,128]{2,1,0:T(8,128)S(1)}, f32[2,120,128]{2,1,0:T(8,128)}, u32[]{:S(2)}) copy-start(f32[2,120,128]{2,1,0:T(8,128)} %copy-done.9) | copy-start | bytes 368644
  26.6 11.2 %collective-permute-start.7 = (f32[2,120,128]{2,1,0:T(8,128)S(1)}, f32[2,120,128]{2,1,0:T(8,128)S(1)}, u32[]{:S(2)}, u32[]{:S(2)}) collective-permute-start(f32[2,120,128]{2,1,0:T(8,128)S(1)} %copy-done.12), channel_id=1, source_target_pairs={{0,16},{8,24},{16,0},{24,8},{1,17},{9,25},{17,1},{25,9},{2,18},{10... | collective-permute-start | bytes 368648 | tf_op jit(solution)/shard_map/ppermute | solution.py:555
  28.5 11.0 %collective-permute-start.4 = (f32[1,120,128]{2,1,0:T(8,128)S(1)}, f32[1,120,128]{2,1,0:T(8,128)S(1)}, u32[]{:S(2)}, u32[]{:S(2)}) collective-permute-start(f32[1,120,128]{2,1,0:T(8,128)S(1)} %get-tuple-element.58), channel_id=1, source_target_pairs={{0,8},{8,16},{16,24},{24,0},{1,9},{9,17},{17,25},{25,1},{2,10},{10... | collective-permute-start | bytes 184328 | tf_op jit(solution)/shard_map/ppermute | solution.py:555
  30.1 9.4 %collective-permute-start.5 = (f32[1,120,128]{2,1,0:T(8,128)S(1)}, f32[1,120,128]{2,1,0:T(8,128)S(1)}, u32[]{:S(2)}, u32[]{:S(2)}) collective-permute-start(f32[1,120,128]{2,1,0:T(8,128)S(1)} %get-tuple-element.59), channel_id=1, source_target_pairs={{0,16},{8,24},{16,0},{24,8},{1,17},{9,25},{17,1},{25,9},{2,18},{10... | collective-permute-start | bytes 184328 | tf_op jit(solution)/shard_map/ppermute | solution.py:555
  31.3 8.2 %collective-permute-start.6 = (f32[1,120,128]{2,1,0:T(8,128)S(1)}, f32[1,120,128]{2,1,0:T(8,128)S(1)}, u32[]{:S(2)}, u32[]{:S(2)}) collective-permute-start(f32[1,120,128]{2,1,0:T(8,128)S(1)} %get-tuple-element.60), channel_id=1, source_target_pairs={{0,24},{8,0},{16,8},{24,16},{1,25},{9,1},{17,9},{25,17},{2,26},{10... | collective-permute-start | bytes 184328 | tf_op jit(solution)/shard_map/ppermute | solution.py:555

commit v12 on v11

--- a/solution.py
+++ b/solution.py
@@ -289,7 +289,7 @@
 
 def kept_kernel(
     wav_count, place_ref, coupling_ref, counts_ref, good_ref, pixels_ref, ivar_ref, bits_ref,
-    sums_ref, weight_ref, edges_ref, ivar_s, pixel_s,
+    sums_ref, weight_ref, up_ref, down_ref, ivar_s, pixel_s,
 ):
     expos, width, fibres = ivar_ref.shape
     half = width // 2
@@ -320,13 +320,10 @@
         lambda e, group: bits_ref[e, pl.ds(pl.multiple_of(which * (half // BITS) + words * group, words), words), :],
         sums_ref, weight_ref, eliminate,
     )
-    ends = []
-    for n, d, b in states:
+    for (n, d, b), out_ref in zip(states, (up_ref, down_ref)):
         scale = 1.0 / (d + n)
-        ends.append((coupling * (n * scale), b * scale))
-    for other in range(wav_count):
-        for value in range(2):
-            edges_ref[other, value] = jnp.where(place_ref[1] < other, ends[0][value], ends[1][value])
+        out_ref[0] = coupling * (n * scale)
+        out_ref[1] = b * scale
 
 
 def kept_weights(wav_count, place, coupling, counts, good, pixels, ivar, bits):
@@ -334,16 +331,13 @@
     half = width // 2
     streams = expos * fibres // LANES
     count = -(-HALO // ROWS) * ROWS
+    edge = shaped((2, streams, LANES))
     edge_scratch = pltpu.VMEM((streams * odd(2 * count), LANES), F32)
     return pl.pallas_call(
         functools.partial(kept_kernel, wav_count),
         in_specs=[in_smem] + [in_vmem] * 6,
-        out_specs=[in_vmem] * 3,
-        out_shape=[
-            shaped((2, half, fibres)),
-            shaped((expos, half, fibres)),
-            shaped((wav_count, 2, streams, LANES)),
-        ],
+        out_specs=[in_vmem] * 4,
+        out_shape=[shaped((2, half, fibres)), shaped((expos, half, fibres)), edge, edge],
         scratch_shapes=[edge_scratch, edge_scratch],
         compiler_params=params(),
         cost_estimate=cost(20 * ivar.size, 6 * ivar.size),
@@ -373,10 +367,10 @@
 
 
 def solve_kernel(
-    wav_count, place_ref, coupling_ref, edges_ref, pixel_ref, ivar_ref, weight_ref,
+    wav_count, place_ref, coupling_ref, left_ref, right_ref, pixel_ref, ivar_ref, weight_ref,
     theirs_ref, solved_s, lead_s, rest_s,
 ):
-    streams = edges_ref.shape[2]
+    streams = left_ref.shape[1]
     expos, half, fibres = weight_ref.shape
     width = 2 * half
     pitch = odd(width)
@@ -387,11 +381,9 @@
     def row_at(i):
         return pl.ds(i, streams, stride=pitch)
 
-    def begin(neighbour):
-        there = (neighbour >= 0) & (neighbour < wav_count)
-        at = jnp.clip(neighbour, 0, wav_count - 1)
-        n = jnp.where(there, edges_ref[at, 0], 0.0) * back
-        return (n, 1.0 - n, jnp.where(there, edges_ref[at, 1], 0.0))
+    def begin(edge_ref, outermost):
+        n = jnp.where(place_ref[1] == outermost, 0.0, edge_ref[0]) * back
+        return (n, 1.0 - n, jnp.where(place_ref[1] == outermost, 0.0, edge_ref[1]))
 
     def keep(side, i, state):
         n, d, b = state
@@ -410,7 +402,7 @@
                 states[side] = advance(states[side], ivar_ref[row_at(row), :], pixel_ref[row_at(row), :], back)
         return tuple(rescaled(state) for state in states)
 
-    states = lax.fori_loop(0, middle // unrolled, eliminate, (begin(place_ref[1] - 1), begin(place_ref[1] + 1)))
+    states = lax.fori_loop(0, middle // unrolled, eliminate, (begin(left_ref, 0), begin(right_ref, wav_count - 1)))
     for side in range(2):
         keep(side, middle, states[side])
     lead, rest = lead_s[0, middle], rest_s[0, middle]
@@ -468,20 +460,20 @@
     lax.fori_loop(0, half // ROWS // unrolled, body, 0)
 
 
-def flux_sums(wav_count, place, coupling, edges, pixels, ivar, weight):
+def flux_sums(wav_count, place, coupling, left, right, pixels, ivar, weight):
     expos, half, fibres = weight.shape
-    streams = edges.shape[2]
+    streams = left.shape[1]
     factor_scratch = pltpu.VMEM((2, half + 1, streams, LANES), F32)
     return pl.pallas_call(
         functools.partial(solve_kernel, wav_count),
-        in_specs=[in_smem] + [in_vmem] * 5,
+        in_specs=[in_smem] + [in_vmem] * 6,
         out_specs=[in_vmem, in_vmem],
         out_shape=[shaped((1, half, fibres)), shaped(pixels.shape)],
         scratch_shapes=[factor_scratch, factor_scratch],
         compiler_params=params(),
         cost_estimate=cost(0, 0),
         name="flux_sums",
-    )(place, coupling, edges, pixels, ivar, weight)
+    )(place, coupling, left, right, pixels, ivar, weight)
 
 
 def kept_flux_kernel(place_ref, coupling_ref, solved_ref, weight_ref, out_ref):
@@ -677,15 +669,17 @@
         moves, wav_count, place, slots, coupling, counts, good_flags, clip_bits, pixel_ivar
     )
     arriving = lax.ppermute(theirs, "exp", swap)
-    mine, weight_m, edges = kept_weights(
+    mine, weight_m, up, down = kept_weights(
         wav_count, place, coupling, counts, good, pixels, ivar, bits
     )
-    edges = lax.all_to_all(edges, "wav", split_axis=0, concat_axis=0, tiled=True)
+    upward = [(i, (i + 1) % wav_count) for i in range(wav_count)]
+    left = lax.ppermute(up, "wav", upward)
+    right = lax.ppermute(down, "wav", [(j, i) for i, j in upward])
     *sorted_pieces, scale = sort_fibres(arriving, mine, send_table, pack, pieces)
     weight_pieces = exchange(sorted_pieces, fib_count)
 
-    pixel_s, ivar_s = stream_layout(edges[0, 0] + edges[-1, 0], pixels, ivar)
-    theirs, solved = flux_sums(wav_count, place, coupling, edges, pixel_s, ivar_s, weight_t)
+    pixel_s, ivar_s = stream_layout(left[0] + right[0], pixels, ivar)
+    theirs, solved = flux_sums(wav_count, place, coupling, left, right, pixel_s, ivar_s, weight_t)
     late = [fib_count // 2] if rel else []
     early = [d for d in range(len(weight_pieces)) if d not in late]
     ahead = sum(weight_pieces[d][0, :ROWS, :] for d in early[1:] or early)

time: 40.9 us -> 30.5 us (0.75)
  local copies, waits for them, and re-layouts: 6.38 us -> 0.01 us
  Pallas kernels: 15.5 us -> 12 us
  waiting for transfers between devices: 2 us -> 3.98 us
  starting transfers between devices: 15.1 us -> 13.6 us
  other arithmetic: 0.77 us -> 0.08 us
    unnamed x26 -> x2, local copies, waits for them, and re-layouts: 6.38 us -> 0.01 us
    all_to_all x1 -> x0, starting transfers between devices: 4.74 us -> none  [per_device(): lax.all_to_all(edges, 'wav', split_axis=0, concat_axis=0, tiled=True)]
    ppermute x0 -> x2, starting transfers between devices: none -> 3.58 us  [the longest x1 2.56 us: per_device(): left = lax.ppermute(up, 'wav', upward)]
    ppermute x6, waiting for transfers between devices: 1.99 us -> 3.97 us  [exchange(): lax.ppermute(pieces[d], 'fib', [(i, (i + d) % fib_count) for i in range(f...]
    pallas_call x2, Pallas kernels: 2.52 us -> 0.82 us  [sort_fibres(): pl.pallas_call(functools.partial(sort_kernel, pack, scaled), in_specs=[in...]
    pallas_call x1, Pallas kernels: 3 us -> 2.22 us  [sent_weights(): pl.pallas_call(functools.partial(sent_kernel, moves, wav_count), in_specs...]
    add x1, other arithmetic: 0.69 us -> 0.01 us  [per_device(): ahead = sum((weight_pieces[d][0, :ROWS, :] for d in early[1:] or early))]
    pallas_call x1, Pallas kernels: 1.74 us -> 1.14 us  [kept_weights(): pl.pallas_call(functools.partial(kept_kernel, wav_count), in_specs=[in_sm...]
  transfers between devices with their start and end apart: 9 -> 10, of which waited for: 1 -> 2; matrix products, arithmetic and copies ran while one was open for 2% -> 0% of each run, Pallas kernels for 28% -> 29%
where the time goes in v12:
time: 30.5 us; the launch traced here: 30.4 us
  starting transfers between devices  13.6 us (45%)
  Pallas kernels  12 us (39%)
  waiting for transfers between devices  3.98 us (13%)
  between operations  0.72 us (2%)
    ppermute x6, starting transfers between devices, exchange(): lax.ppermute(pieces[d], 'fib', [(i, (i + d) % fib_count) for i in range(f...  9.41 us
    ppermute x6, waiting for transfers between devices, exchange(): lax.ppermute(pieces[d], 'fib', [(i, (i + d) % fib_count) for i in range(f...  3.97 us
    ppermute x1, starting transfers between devices, per_device(): left = lax.ppermute(up, 'wav', upward)  2.56 us
    pallas_call x1, Pallas kernels, flux_sums(): pl.pallas_call(functools.partial(solve_kernel, wav_count), in_specs=[in_s...  2.34 us
    pallas_call x1, Pallas kernels, sent_weights(): pl.pallas_call(functools.partial(sent_kernel, moves, wav_count), in_specs...  2.22 us
    pallas_call x1, Pallas kernels, end_weights(): pl.pallas_call(functools.partial(weights_end_kernel, pack, total, late, l...  1.75 us
    pallas_call x1, Pallas kernels, place_early(): pl.pallas_call(functools.partial(early_kernel, moves, which, len(weight_p...  1.74 us
    pallas_call x1, Pallas kernels, kept_weights(): pl.pallas_call(functools.partial(kept_kernel, wav_count), in_specs=[in_sm...  1.14 us
  transfers between devices with their start and end apart: 10, of which 2 were waited for; matrix products, arithmetic and copies ran while one was open for 0% of the time, Pallas kernels for 29%

profile of v12, /device:TPU:0, one launch (start us, length us, event | category | flops | bytes accessed | tf_op | source)
XLA Modules:
  0.0 30.4 jit_solution(1710875741608622660)
XLA Ops:
  0.6 0.1 pad_add_fusion.place_ref
  0.7 2.2 %sent_weights.1 = (f32[2,240,256]{2,1,0:T(8,128)S(1)}, f32[4,240,256]{2,1,0:T(8,128)S(1)}, bf16[512,512]{1,0:T(8,128)(2,1)S(1)}, s32[1,1024]{1,0:T(1,128)S(1)}, ...) custom-call(s32[3]{0:T(128)S(1)} %pad_add_fusion.place_ref, ...), custom_call_target="tpu_custom_call" | custom-call | flops 9830400 | bytes 2949120 | tf_op jit(solution)/shard_map/sent_weights/pallas_call | solution.py:263
  2.9 0.5 %collective-permute-start.3 = (f32[2,240,256]{2,1,0:T(8,128)S(1)}, f32[2,240,256]{2,1,0:T(8,128)S(1)}, u32[]{:S(2)}, u32[]{:S(2)}) collective-permute-start(f32[2,240,256]{2,1,0:T(8,128)S(1)} %get-tuple-element.50), channel_id=1, source_target_pairs={{0,1},{1,0},{2,3},{3,2},{4,5},{5,4},{6,7},{7,6},{8,9},{9,8},{10,11... | collective-permute-start | bytes 1474568 | tf_op jit(solution)/shard_map/ppermute | solution.py:671
  3.5 1.1 %kept_weights.1 = (f32[2,240,256]{2,1,0:T(8,128)S(1)}, f32[4,240,256]{2,1,0:T(8,128)S(1)}, f32[2,8,128]{2,1,0:T(8,128)S(1)}, f32[2,8,128]{2,1,0:T(8,128)S(1)}) custom-call(s32[3]{0:T(128)S(1)} %pad_add_fusion.place_ref, f32[1,256]{1,0:T(1,128)S(1)} %get-tuple-element.35.coupling_ref, s32[1,256]{1,0:T(1,128)S(1)} %get-tuple-element.36.counts_ref, ...), custom_call_target="tpu_custom_call" | custom-call | flops 9830400 | bytes 2949120 | tf_op jit(solution)/shard_map/kept_weights/pallas_call | solution.py:336
  4.6 2.6 %collective-permute-start = (f32[2,8,128]{2,1,0:T(8,128)S(1)}, f32[2,8,128]{2,1,0:T(8,128)S(1)}, u32[]{:S(2)}, u32[]{:S(2)}) collective-permute-start(f32[2,8,128]{2,1,0:T(8,128)S(1)} %get-tuple-element.40), channel_id=1, source_target_pairs={{0,2},{2,4},{4,6},{6,0},{1,3},{3,5},{5,7},{7,1},{8,10},{10,12},{12... | collective-permute-start | bytes 24584 | tf_op jit(solution)/shard_map/ppermute | solution.py:676
  7.2 1.0 %collective-permute-start.1 = (f32[2,8,128]{2,1,0:T(8,128)S(1)}, f32[2,8,128]{2,1,0:T(8,128)S(1)}, u32[]{:S(2)}, u32[]{:S(2)}) collective-permute-start(f32[2,8,128]{2,1,0:T(8,128)S(1)} %get-tuple-element.41), channel_id=1, source_target_pairs={{2,0},{4,2},{6,4},{0,6},{3,1},{5,3},{7,5},{1,7},{10,8},{12,10},{14... | collective-permute-start | bytes 24584 | tf_op jit(solution)/shard_map/ppermute | solution.py:677
  8.2 0.5 %sort_weights.1 = (f32[2,120,128]{2,1,0:T(8,128)S(1)}, f32[2,120,128]{2,1,0:T(8,128)S(1)}, f32[2,120,128]{2,1,0:T(8,128)S(1)}, f32[2,120,128]{2,1,0:T(8,128)S(1)}, f32[240,256]{1,0:T(8,128)S(1)}) custom-call(f32[2,240,256]{2,1,0:T(8,128)S(1)} %collective-permute-done.3.theirs_ref, f32[2,240,256]{2,1,0:T(8,128)S(1)} %get-tuple-element.51.mine_ref, ...), custom_call_target="tpu_custom_call" | custom-call | tf_op jit(solution)/shard_map/sort_weights/pallas_call | solution.py:531
  8.7 2.0 %collective-permute-start.4 = (f32[2,120,128]{2,1,0:T(8,128)S(1)}, f32[2,120,128]{2,1,0:T(8,128)S(1)}, u32[]{:S(2)}, u32[]{:S(2)}) collective-permute-start(f32[2,120,128]{2,1,0:T(8,128)S(1)} %get-tuple-element.53), channel_id=1, source_target_pairs={{0,8},{8,16},{16,24},{24,0},{1,9},{9,17},{17,25},{25,1},{2,10},{10... | collective-permute-start | bytes 368648 | tf_op jit(solution)/shard_map/ppermute | solution.py:547
  10.7 2.1 %collective-permute-start.5 = (f32[2,120,128]{2,1,0:T(8,128)S(1)}, f32[2,120,128]{2,1,0:T(8,128)S(1)}, u32[]{:S(2)}, u32[]{:S(2)}) collective-permute-start(f32[2,120,128]{2,1,0:T(8,128)S(1)} %get-tuple-element.54), channel_id=1, source_target_pairs={{0,24},{8,0},{16,8},{24,16},{1,25},{9,1},{17,9},{25,17},{2,26},{10... | collective-permute-start | bytes 368648 | tf_op jit(solution)/shard_map/ppermute | solution.py:547
  12.8 0.0 collective-permute-done.1.right_ref
  12.8 0.3 stream_layout.1
  13.1 2.3 %flux_sums.1 = (f32[1,240,256]{2,1,0:T(8,128)S(1)}, f32[3848,128]{1,0:T(8,128)S(1)}) custom-call(s32[3]{0:T(128)S(1)} %pad_add_fusion.place_ref, f32[1,256]{1,0:T(1,128)S(1)} %get-tuple-element.35.coupling_ref, f32[2,8,128]{2,1,0:T(8,128)S(1)} %collective-permute-done.left_ref, f32[2,8,128]{2,1,0:T(8,128)S(1)} %collective-permute-done.1.right_ref, ...), custom_call_target="tpu_custom_call" | custom-call | tf_op jit(solution)/shard_map/flux_sums/pallas_call | solution.py:467
  15.4 0.1 collective-permute-start.2
  15.5 0.7 %kept_flux.1.mine_ref = f32[1,240,256]{2,1,0:T(8,128)S(1)} custom-call(s32[3]{0:T(128)S(1)} %pad_add_fusion.place_ref, f32[1,256]{1,0:T(1,128)S(1)} %get-tuple-element.35.coupling_ref, f32[3848,128]{1,0:T(8,128)S(1)} %get-tuple-element.47.solved_ref, f32[4,240,256]{2,1,0:T(8,128)S(1)} %get-tuple-element.48.weight_ref), custom_call_target="tpu_custom_call" | custom-call | flops 491520 | bytes 1966080 | tf_op jit(solution)/shard_map/kept_flux/pallas_call | solution.py:485
  16.2 1.0 %collective-permute-start.9 = (f32[2,120,128]{2,1,0:T(8,128)S(1)}, f32[2,120,128]{2,1,0:T(8,128)S(1)}, u32[]{:S(2)}, u32[]{:S(2)}) collective-permute-start(f32[2,120,128]{2,1,0:T(8,128)S(1)} %get-tuple-element.64), channel_id=1, source_target_pairs={{0,16},{8,24},{16,0},{24,8},{1,17},{9,25},{17,1},{25,9},{2,18},{10... | collective-permute-start | bytes 368648 | tf_op jit(solution)/shard_map/ppermute | solution.py:547
  17.3 1.0 %collective-permute-done.5.refs_2_ = f32[2,120,128]{2,1,0:T(8,128)S(1)} collective-permute-done((f32[2,120,128]{2,1,0:T(8,128)S(1)}, f32[2,120,128]{2,1,0:T(8,128)S(1)}, u32[]{:S(2)}, u32[]{:S(2)}) %collective-permute-start.5) | collective-permute-done | bytes 122912 | tf_op jit(solution)/shard_map/ppermute | solution.py:547
  18.2 0.3 %sort_flux.1 = (f32[1,120,128]{2,1,0:T(8,128)S(1)}, f32[1,120,128]{2,1,0:T(8,128)S(1)}, f32[1,120,128]{2,1,0:T(8,128)S(1)}, f32[1,120,128]{2,1,0:T(8,128)S(1)}) custom-call(f32[1,240,256]{2,1,0:T(8,128)S(1)} %collective-permute-done.2.theirs_ref, f32[1,240,256]{2,1,0:T(8,128)S(1)} %kept_flux.1.mine_ref, bf16[512,512]{1,0:T(8,128)(2,1)S(1)} %get-tuple-element.49.table_ref, ...), custom_call_target="tpu_custom_call" | custom-call | tf_op jit(solution)/shard_map/sort_flux/pallas_call | solution.py:531
  18.6 1.2 %collective-permute-start.6 = (f32[1,120,128]{2,1,0:T(8,128)S(1)}, f32[1,120,128]{2,1,0:T(8,128)S(1)}, u32[]{:S(2)}, u32[]{:S(2)}) collective-permute-start(f32[1,120,128]{2,1,0:T(8,128)S(1)} %get-tuple-element.60), channel_id=1, source_target_pairs={{0,8},{8,16},{16,24},{24,0},{1,9},{9,17},{17,25},{25,1},{2,10},{10... | collective-permute-start | bytes 184328 | tf_op jit(solution)/shard_map/ppermute | solution.py:547
  19.8 1.7 %collective-permute-start.7 = (f32[1,120,128]{2,1,0:T(8,128)S(1)}, f32[1,120,128]{2,1,0:T(8,128)S(1)}, u32[]{:S(2)}, u32[]{:S(2)}) collective-permute-start(f32[1,120,128]{2,1,0:T(8,128)S(1)} %get-tuple-element.61), channel_id=1, source_target_pairs={{0,16},{8,24},{16,0},{24,8},{1,17},{9,25},{17,1},{25,9},{2,18},{10... | collective-permute-start | bytes 184328 | tf_op jit(solution)/shard_map/ppermute | solution.py:547
  21.5 1.3 %collective-permute-start.8 = (f32[1,120,128]{2,1,0:T(8,128)S(1)}, f32[1,120,128]{2,1,0:T(8,128)S(1)}, u32[]{:S(2)}, u32[]{:S(2)}) collective-permute-start(f32[1,120,128]{2,1,0:T(8,128)S(1)} %get-tuple-element.62), channel_id=1, source_target_pairs={{0,24},{8,0},{16,8},{24,16},{1,25},{9,1},{17,9},{25,17},{2,26},{10... | collective-permute-start | bytes 184328 | tf_op jit(solution)/shard_map/ppermute | solution.py:547
  22.9 1.7 %place_early.1 = (bf16[512,512]{1,0:T(8,128)(2,1)S(1)}, f32[2,120,512]{2,1,0:T(8,128)S(1)}) custom-call(s32[3]{0:T(128)S(1)} %pad_add_fusion.place_ref, s32[1,1024]{1,0:T(1,128)S(1)} %get-tuple-element.57.slots_ref, f32[2,120,128]{2,1,0:T(8,128)S(1)} %get-tuple-element.58.refs_0_, f32[2,120,128]{2,1,0:T(8,128)S(1)} %collective-permute-done.4.refs_1_, ...), custom_call_target="tpu_custom_call" | custom-call | tf_op jit(solution)/shard_map/place_early/pallas_call | solution.py:576
  24.6 3.0 %collective-permute-done.9.refs_0_ = f32[2,120,128]{2,1,0:T(8,128)S(1)} collective-permute-done((f32[2,120,128]{2,1,0:T(8,128)S(1)}, f32[2,120,128]{2,1,0:T(8,128)S(1)}, u32[]{:S(2)}, u32[]{:S(2)}) %collective-permute-start.9) | collective-permute-done | bytes 122912 | tf_op jit(solution)/shard_map/ppermute | solution.py:547
  27.6 1.8 %end_weights.1 = (f32[240,256]{1,0:T(8,128)}, f32[3,240,256]{2,1,0:T(8,128)}) custom-call(s32[3]{0:T(128)S(1)} %pad_add_fusion.place_ref, bf16[512,512]{1,0:T(8,128)(2,1)S(1)} %get-tuple-element.59.table_ref, f32[2,120,512]{2,1,0:T(8,128)S(1)} %get-tuple-element.63.sums_ref, f32[2,120,128]{2,1,0:T(8,128)S(1)} %collective-permute-done.9.refs_0_), custom_call_target="tpu_custom_call" | custom-call | tf_op jit(solution)/shard_map/end_weights/pallas_call | solution.py:615
  29.4 1.0 %end_flux.1 = f32[240,256]{1,0:T(8,128)} custom-call(bf16[512,512]{1,0:T(8,128)(2,1)S(1)} %get-tuple-element.59.table_ref, f32[1,120,128]{2,1,0:T(8,128)S(1)} %get-tuple-element.55.refs_0_, f32[1,120,128]{2,1,0:T(8,128)S(1)} %collective-permute-done.6.refs_1_, f32[1,120,128]{2,1,0:T(8,128)S(1)} %collective-permute-done.7.refs_2_, ...), custom_call_target="tpu_custom_call" | custom-call | flops 125829120 | bytes 491520 | tf_op jit(solution)/shard_map/end_flux/pallas_call | solution.py:637
  (11 shorter events, 0.0 us)
Async XLA Ops:
  0.6 2.8 %copy-start = (f32[4,480,256]{2,1,0:T(8,128)S(1)}, f32[4,480,256]{2,1,0:T(8,128)}, u32[]{:S(2)}) copy-start(f32[4,480,256]{2,1,0:T(8,128)} %pixels_ref.3) | copy-start | bytes 5898244
  2.9 5.2 %collective-permute-start.3 = (f32[2,240,256]{2,1,0:T(8,128)S(1)}, f32[2,240,256]{2,1,0:T(8,128)S(1)}, u32[]{:S(2)}, u32[]{:S(2)}) collective-permute-start(f32[2,240,256]{2,1,0:T(8,128)S(1)} %get-tuple-element.50), channel_id=1, source_target_pairs={{0,1},{1,0},{2,3},{3,2},{4,5},{5,4},{6,7},{7,6},{8,9},{9,8},{10,11... | collective-permute-start | bytes 1474568 | tf_op jit(solution)/shard_map/ppermute | solution.py:671
  4.6 8.2 %collective-permute-start = (f32[2,8,128]{2,1,0:T(8,128)S(1)}, f32[2,8,128]{2,1,0:T(8,128)S(1)}, u32[]{:S(2)}, u32[]{:S(2)}) collective-permute-start(f32[2,8,128]{2,1,0:T(8,128)S(1)} %get-tuple-element.40), channel_id=1, source_target_pairs={{0,2},{2,4},{4,6},{6,0},{1,3},{3,5},{5,7},{7,1},{8,10},{10,12},{12... | collective-permute-start | bytes 24584 | tf_op jit(solution)/shard_map/ppermute | solution.py:676
  7.2 5.6 %collective-permute-start.1 = (f32[2,8,128]{2,1,0:T(8,128)S(1)}, f32[2,8,128]{2,1,0:T(8,128)S(1)}, u32[]{:S(2)}, u32[]{:S(2)}) collective-permute-start(f32[2,8,128]{2,1,0:T(8,128)S(1)} %get-tuple-element.41), channel_id=1, source_target_pairs={{2,0},{4,2},{6,4},{0,6},{3,1},{5,3},{7,5},{1,7},{10,8},{12,10},{14... | collective-permute-start | bytes 24584 | tf_op jit(solution)/shard_map/ppermute | solution.py:677
  8.7 8.6 %collective-permute-start.4 = (f32[2,120,128]{2,1,0:T(8,128)S(1)}, f32[2,120,128]{2,1,0:T(8,128)S(1)}, u32[]{:S(2)}, u32[]{:S(2)}) collective-permute-start(f32[2,120,128]{2,1,0:T(8,128)S(1)} %get-tuple-element.53), channel_id=1, source_target_pairs={{0,8},{8,16},{16,24},{24,0},{1,9},{9,17},{17,25},{25,1},{2,10},{10... | collective-permute-start | bytes 368648 | tf_op jit(solution)/shard_map/ppermute | solution.py:547
  10.7 7.5 %collective-permute-start.5 = (f32[2,120,128]{2,1,0:T(8,128)S(1)}, f32[2,120,128]{2,1,0:T(8,128)S(1)}, u32[]{:S(2)}, u32[]{:S(2)}) collective-permute-start(f32[2,120,128]{2,1,0:T(8,128)S(1)} %get-tuple-element.54), channel_id=1, source_target_pairs={{0,24},{8,0},{16,8},{24,16},{1,25},{9,1},{17,9},{25,17},{2,26},{10... | collective-permute-start | bytes 368648 | tf_op jit(solution)/shard_map/ppermute | solution.py:547
  15.4 2.8 %collective-permute-start.2 = (f32[1,240,256]{2,1,0:T(8,128)S(1)}, f32[1,240,256]{2,1,0:T(8,128)S(1)}, u32[]{:S(2)}, u32[]{:S(2)}) collective-permute-start(f32[1,240,256]{2,1,0:T(8,128)S(1)} %get-tuple-element.45), channel_id=1, source_target_pairs={{0,1},{1,0},{2,3},{3,2},{4,5},{5,4},{6,7},{7,6},{8,9},{9,8},{10,11... | collective-permute-start | bytes 737288 | tf_op jit(solution)/shard_map/ppermute | solution.py:686
  16.2 11.4 %collective-permute-start.9 = (f32[2,120,128]{2,1,0:T(8,128)S(1)}, f32[2,120,128]{2,1,0:T(8,128)S(1)}, u32[]{:S(2)}, u32[]{:S(2)}) collective-permute-start(f32[2,120,128]{2,1,0:T(8,128)S(1)} %get-tuple-element.64), channel_id=1, source_target_pairs={{0,16},{8,24},{16,0},{24,8},{1,17},{9,25},{17,1},{25,9},{2,18},{10... | collective-permute-start | bytes 368648 | tf_op jit(solution)/shard_map/ppermute | solution.py:547
  18.6 10.8 %collective-permute-start.6 = (f32[1,120,128]{2,1,0:T(8,128)S(1)}, f32[1,120,128]{2,1,0:T(8,128)S(1)}, u32[]{:S(2)}, u32[]{:S(2)}) collective-permute-start(f32[1,120,128]{2,1,0:T(8,128)S(1)} %get-tuple-element.60), channel_id=1, source_target_pairs={{0,8},{8,16},{16,24},{24,0},{1,9},{9,17},{17,25},{25,1},{2,10},{10... | collective-permute-start | bytes 184328 | tf_op jit(solution)/shard_map/ppermute | solution.py:547
  19.8 9.6 %collective-permute-start.7 = (f32[1,120,128]{2,1,0:T(8,128)S(1)}, f32[1,120,128]{2,1,0:T(8,128)S(1)}, u32[]{:S(2)}, u32[]{:S(2)}) collective-permute-start(f32[1,120,128]{2,1,0:T(8,128)S(1)} %get-tuple-element.61), channel_id=1, source_target_pairs={{0,16},{8,24},{16,0},{24,8},{1,17},{9,25},{17,1},{25,9},{2,18},{10... | collective-permute-start | bytes 184328 | tf_op jit(solution)/shard_map/ppermute | solution.py:547
  21.5 7.8 %collective-permute-start.8 = (f32[1,120,128]{2,1,0:T(8,128)S(1)}, f32[1,120,128]{2,1,0:T(8,128)S(1)}, u32[]{:S(2)}, u32[]{:S(2)}) collective-permute-start(f32[1,120,128]{2,1,0:T(8,128)S(1)} %get-tuple-element.62), channel_id=1, source_target_pairs={{0,24},{8,0},{16,8},{24,16},{1,25},{9,1},{17,9},{25,17},{2,26},{10... | collective-permute-start | bytes 184328 | tf_op jit(solution)/shard_map/ppermute | solution.py:547

commit v13 on v12

--- a/solution.py
+++ b/solution.py
@@ -680,9 +680,9 @@
 
     pixel_s, ivar_s = stream_layout(left[0] + right[0], pixels, ivar)
     theirs, solved = flux_sums(wav_count, place, coupling, left, right, pixel_s, ivar_s, weight_t)
-    late = [fib_count // 2] if rel else []
-    early = [d for d in range(len(weight_pieces)) if d not in late]
-    ahead = sum(weight_pieces[d][0, :ROWS, :] for d in early[1:] or early)
+    early = [0, fib_count // 2] if rel else [0]
+    late = [d for d in range(pieces) if d not in early]
+    ahead = weight_pieces[early[-1]][0, :ROWS, :] * 0.5
     arriving = lax.ppermute(theirs, "exp", swap)
     mine = kept_flux(after(place, theirs), coupling, solved, weight_m)
     sorted_pieces = sort_fibres(arriving, mine, send_table, pack, pieces, scale, ahead)

time: 30.5 us -> 30.6 us (level)
  starting transfers between devices: 13.6 us -> 15 us
  waiting for transfers between devices: 3.98 us -> 2.69 us
    ppermute x6, starting transfers between devices: 9.41 us -> 10.8 us  [exchange(): lax.ppermute(pieces[d], 'fib', [(i, (i + d) % fib_count) for i in range(f...]
    ppermute x6, waiting for transfers between devices: 3.97 us -> 2.68 us  [exchange(): lax.ppermute(pieces[d], 'fib', [(i, (i + d) % fib_count) for i in range(f...]
where the time goes in v13:
time: 30.6 us; the launch traced here: 30.4 us
  starting transfers between devices  15 us (49%)
  Pallas kernels  11.9 us (39%)
  waiting for transfers between devices  2.69 us (9%)
  between operations  0.73 us (2%)
    ppermute x6, starting transfers between devices, exchange(): lax.ppermute(pieces[d], 'fib', [(i, (i + d) % fib_count) for i in range(f...  10.8 us
    ppermute x6, waiting for transfers between devices, exchange(): lax.ppermute(pieces[d], 'fib', [(i, (i + d) % fib_count) for i in range(f...  2.68 us
    ppermute x1, starting transfers between devices, per_device(): left = lax.ppermute(up, 'wav', upward)  2.56 us
    pallas_call x1, Pallas kernels, flux_sums(): pl.pallas_call(functools.partial(solve_kernel, wav_count), in_specs=[in_s...  2.34 us
    pallas_call x1, Pallas kernels, sent_weights(): pl.pallas_call(functools.partial(sent_kernel, moves, wav_count), in_specs...  2.22 us
    pallas_call x1, Pallas kernels, end_weights(): pl.pallas_call(functools.partial(weights_end_kernel, pack, total, late, l...  1.78 us
    pallas_call x1, Pallas kernels, place_early(): pl.pallas_call(functools.partial(early_kernel, moves, which, len(weight_p...  1.62 us
    pallas_call x1, Pallas kernels, kept_weights(): pl.pallas_call(functools.partial(kept_kernel, wav_count), in_specs=[in_sm...  1.14 us
  transfers between devices with their start and end apart: 10, of which 2 were waited for; matrix products, arithmetic and copies ran while one was open for 0% of the time, Pallas kernels for 29%

profile of v13, /device:TPU:0, one launch (start us, length us, event | category | flops | bytes accessed | tf_op | source)
XLA Modules:
  0.0 30.4 jit_solution(11040349522429333152)
XLA Ops:
  0.6 0.1 pad_add_fusion.place_ref
  0.7 2.2 %sent_weights.1 = (f32[2,240,256]{2,1,0:T(8,128)S(1)}, f32[4,240,256]{2,1,0:T(8,128)S(1)}, bf16[512,512]{1,0:T(8,128)(2,1)S(1)}, s32[1,1024]{1,0:T(1,128)S(1)}, ...) custom-call(s32[3]{0:T(128)S(1)} %pad_add_fusion.place_ref, ...), custom_call_target="tpu_custom_call" | custom-call | flops 9830400 | bytes 2949120 | tf_op jit(solution)/shard_map/sent_weights/pallas_call | solution.py:263
  2.9 0.5 %collective-permute-start.3 = (f32[2,240,256]{2,1,0:T(8,128)S(1)}, f32[2,240,256]{2,1,0:T(8,128)S(1)}, u32[]{:S(2)}, u32[]{:S(2)}) collective-permute-start(f32[2,240,256]{2,1,0:T(8,128)S(1)} %get-tuple-element.50), channel_id=1, source_target_pairs={{0,1},{1,0},{2,3},{3,2},{4,5},{5,4},{6,7},{7,6},{8,9},{9,8},{10,11... | collective-permute-start | bytes 1474568 | tf_op jit(solution)/shard_map/ppermute | solution.py:671
  3.5 1.1 %kept_weights.1 = (f32[2,240,256]{2,1,0:T(8,128)S(1)}, f32[4,240,256]{2,1,0:T(8,128)S(1)}, f32[2,8,128]{2,1,0:T(8,128)S(1)}, f32[2,8,128]{2,1,0:T(8,128)S(1)}) custom-call(s32[3]{0:T(128)S(1)} %pad_add_fusion.place_ref, f32[1,256]{1,0:T(1,128)S(1)} %get-tuple-element.35.coupling_ref, s32[1,256]{1,0:T(1,128)S(1)} %get-tuple-element.36.counts_ref, ...), custom_call_target="tpu_custom_call" | custom-call | flops 9830400 | bytes 2949120 | tf_op jit(solution)/shard_map/kept_weights/pallas_call | solution.py:336
  4.6 2.6 %collective-permute-start = (f32[2,8,128]{2,1,0:T(8,128)S(1)}, f32[2,8,128]{2,1,0:T(8,128)S(1)}, u32[]{:S(2)}, u32[]{:S(2)}) collective-permute-start(f32[2,8,128]{2,1,0:T(8,128)S(1)} %get-tuple-element.40), channel_id=1, source_target_pairs={{0,2},{2,4},{4,6},{6,0},{1,3},{3,5},{5,7},{7,1},{8,10},{10,12},{12... | collective-permute-start | bytes 24584 | tf_op jit(solution)/shard_map/ppermute | solution.py:676
  7.2 1.0 %collective-permute-start.1 = (f32[2,8,128]{2,1,0:T(8,128)S(1)}, f32[2,8,128]{2,1,0:T(8,128)S(1)}, u32[]{:S(2)}, u32[]{:S(2)}) collective-permute-start(f32[2,8,128]{2,1,0:T(8,128)S(1)} %get-tuple-element.41), channel_id=1, source_target_pairs={{2,0},{4,2},{6,4},{0,6},{3,1},{5,3},{7,5},{1,7},{10,8},{12,10},{14... | collective-permute-start | bytes 24584 | tf_op jit(solution)/shard_map/ppermute | solution.py:677
  8.2 0.0 collective-permute-done.3.theirs_ref
  8.2 0.5 %sort_weights.1 = (f32[2,120,128]{2,1,0:T(8,128)S(1)}, f32[2,120,128]{2,1,0:T(8,128)S(1)}, f32[2,120,128]{2,1,0:T(8,128)S(1)}, f32[2,120,128]{2,1,0:T(8,128)S(1)}, f32[240,256]{1,0:T(8,128)S(1)}) custom-call(f32[2,240,256]{2,1,0:T(8,128)S(1)} %collective-permute-done.3.theirs_ref, f32[2,240,256]{2,1,0:T(8,128)S(1)} %get-tuple-element.51.mine_ref, ...), custom_call_target="tpu_custom_call" | custom-call | tf_op jit(solution)/shard_map/sort_weights/pallas_call | solution.py:531
  8.7 3.1 %collective-permute-start.4 = (f32[2,120,128]{2,1,0:T(8,128)S(1)}, f32[2,120,128]{2,1,0:T(8,128)S(1)}, u32[]{:S(2)}, u32[]{:S(2)}) collective-permute-start(f32[2,120,128]{2,1,0:T(8,128)S(1)} %get-tuple-element.53), channel_id=1, source_target_pairs={{0,16},{8,24},{16,0},{24,8},{1,17},{9,25},{17,1},{25,9},{2,18},{10... | collective-permute-start | bytes 368648 | tf_op jit(solution)/shard_map/ppermute | solution.py:547
  11.8 0.3 stream_layout.1
  12.0 2.3 %flux_sums.1 = (f32[1,240,256]{2,1,0:T(8,128)S(1)}, f32[3848,128]{1,0:T(8,128)S(1)}) custom-call(s32[3]{0:T(128)S(1)} %pad_add_fusion.place_ref, f32[1,256]{1,0:T(1,128)S(1)} %get-tuple-element.35.coupling_ref, f32[2,8,128]{2,1,0:T(8,128)S(1)} %collective-permute-done.left_ref, f32[2,8,128]{2,1,0:T(8,128)S(1)} %collective-permute-done.1.right_ref, ...), custom_call_target="tpu_custom_call" | custom-call | tf_op jit(solution)/shard_map/flux_sums/pallas_call | solution.py:467
  14.4 0.1 collective-permute-start.2
  14.4 0.7 %kept_flux.1.mine_ref = f32[1,240,256]{2,1,0:T(8,128)S(1)} custom-call(s32[3]{0:T(128)S(1)} %pad_add_fusion.place_ref, f32[1,256]{1,0:T(1,128)S(1)} %get-tuple-element.35.coupling_ref, f32[3848,128]{1,0:T(8,128)S(1)} %get-tuple-element.47.solved_ref, f32[4,240,256]{2,1,0:T(8,128)S(1)} %get-tuple-element.48.weight_ref), custom_call_target="tpu_custom_call" | custom-call | flops 491520 | bytes 1966080 | tf_op jit(solution)/shard_map/kept_flux/pallas_call | solution.py:485
  15.2 1.6 %collective-permute-start.8 = (f32[2,120,128]{2,1,0:T(8,128)S(1)}, f32[2,120,128]{2,1,0:T(8,128)S(1)}, u32[]{:S(2)}, u32[]{:S(2)}) collective-permute-start(f32[2,120,128]{2,1,0:T(8,128)S(1)} %get-tuple-element.63), channel_id=1, source_target_pairs={{0,8},{8,16},{16,24},{24,0},{1,9},{9,17},{17,25},{25,1},{2,10},{10... | collective-permute-start | bytes 368648 | tf_op jit(solution)/shard_map/ppermute | solution.py:547
  16.8 2.2 %collective-permute-start.9 = (f32[2,120,128]{2,1,0:T(8,128)S(1)}, f32[2,120,128]{2,1,0:T(8,128)S(1)}, u32[]{:S(2)}, u32[]{:S(2)}) collective-permute-start(f32[2,120,128]{2,1,0:T(8,128)S(1)} %get-tuple-element.64), channel_id=1, source_target_pairs={{0,24},{8,0},{16,8},{24,16},{1,25},{9,1},{17,9},{25,17},{2,26},{10... | collective-permute-start | bytes 368648 | tf_op jit(solution)/shard_map/ppermute | solution.py:547
  19.1 0.3 %sort_flux.1 = (f32[1,120,128]{2,1,0:T(8,128)S(1)}, f32[1,120,128]{2,1,0:T(8,128)S(1)}, f32[1,120,128]{2,1,0:T(8,128)S(1)}, f32[1,120,128]{2,1,0:T(8,128)S(1)}) custom-call(f32[1,240,256]{2,1,0:T(8,128)S(1)} %collective-permute-done.2.theirs_ref, f32[1,240,256]{2,1,0:T(8,128)S(1)} %kept_flux.1.mine_ref, bf16[512,512]{1,0:T(8,128)(2,1)S(1)} %get-tuple-element.49.table_ref, ...), custom_call_target="tpu_custom_call" | custom-call | tf_op jit(solution)/shard_map/sort_flux/pallas_call | solution.py:531
  19.4 0.1 collective-permute-start.5
  19.5 2.9 %collective-permute-start.6 = (f32[1,120,128]{2,1,0:T(8,128)S(1)}, f32[1,120,128]{2,1,0:T(8,128)S(1)}, u32[]{:S(2)}, u32[]{:S(2)}) collective-permute-start(f32[1,120,128]{2,1,0:T(8,128)S(1)} %get-tuple-element.60), channel_id=1, source_target_pairs={{0,16},{8,24},{16,0},{24,8},{1,17},{9,25},{17,1},{25,9},{2,18},{10... | collective-permute-start | bytes 184328 | tf_op jit(solution)/shard_map/ppermute | solution.py:547
  22.4 0.9 %collective-permute-start.7 = (f32[1,120,128]{2,1,0:T(8,128)S(1)}, f32[1,120,128]{2,1,0:T(8,128)S(1)}, u32[]{:S(2)}, u32[]{:S(2)}) collective-permute-start(f32[1,120,128]{2,1,0:T(8,128)S(1)} %get-tuple-element.61), channel_id=1, source_target_pairs={{0,24},{8,0},{16,8},{24,16},{1,25},{9,1},{17,9},{25,17},{2,26},{10... | collective-permute-start | bytes 184328 | tf_op jit(solution)/shard_map/ppermute | solution.py:547
  23.3 1.6 %place_early.1 = (bf16[512,512]{1,0:T(8,128)(2,1)S(1)}, f32[2,120,512]{2,1,0:T(8,128)S(1)}) custom-call(s32[3]{0:T(128)S(1)} %pad_add_fusion.place_ref, s32[1,1024]{1,0:T(1,128)S(1)} %get-tuple-element.56.slots_ref, f32[2,120,128]{2,1,0:T(8,128)S(1)} %get-tuple-element.57.refs_0_, f32[2,120,128]{2,1,0:T(8,128)S(1)} %collective-permute-done.4.refs_1_), custom_call_target="tpu_custom_call" | custom-call | tf_op jit(solution)/shard_map/place_early/pallas_call | solution.py:576
  24.9 2.3 %collective-permute-done.9.refs_1_ = f32[2,120,128]{2,1,0:T(8,128)S(1)} collective-permute-done((f32[2,120,128]{2,1,0:T(8,128)S(1)}, f32[2,120,128]{2,1,0:T(8,128)S(1)}, u32[]{:S(2)}, u32[]{:S(2)}) %collective-permute-start.9) | collective-permute-done | bytes 122912 | tf_op jit(solution)/shard_map/ppermute | solution.py:547
  27.2 1.8 %end_weights.1 = (f32[240,256]{1,0:T(8,128)}, f32[3,240,256]{2,1,0:T(8,128)}) custom-call(s32[3]{0:T(128)S(1)} %pad_add_fusion.place_ref, bf16[512,512]{1,0:T(8,128)(2,1)S(1)} %get-tuple-element.58.table_ref, f32[2,120,512]{2,1,0:T(8,128)S(1)} %get-tuple-element.62.sums_ref, f32[2,120,128]{2,1,0:T(8,128)S(1)} %collective-permute-done.8.refs_0_, ...), custom_call_target="tpu_custom_call" | custom-call | tf_op jit(solution)/shard_map/end_weights/pallas_call | solution.py:615
  29.0 0.4 %collective-permute-done.6.refs_2_ = f32[1,120,128]{2,1,0:T(8,128)S(1)} collective-permute-done((f32[1,120,128]{2,1,0:T(8,128)S(1)}, f32[1,120,128]{2,1,0:T(8,128)S(1)}, u32[]{:S(2)}, u32[]{:S(2)}) %collective-permute-start.6) | collective-permute-done | bytes 61472 | tf_op jit(solution)/shard_map/ppermute | solution.py:547
  29.4 1.0 %end_flux.1 = f32[240,256]{1,0:T(8,128)} custom-call(bf16[512,512]{1,0:T(8,128)(2,1)S(1)} %get-tuple-element.58.table_ref, f32[1,120,128]{2,1,0:T(8,128)S(1)} %get-tuple-element.54.refs_0_, f32[1,120,128]{2,1,0:T(8,128)S(1)} %collective-permute-done.5.refs_1_, f32[1,120,128]{2,1,0:T(8,128)S(1)} %collective-permute-done.6.refs_2_, ...), custom_call_target="tpu_custom_call" | custom-call | flops 125829120 | bytes 491520 | tf_op jit(solution)/shard_map/end_flux/pallas_call | solution.py:637
  (11 shorter events, 0.0 us)
Async XLA Ops:
  0.6 2.8 %copy-start = (f32[4,480,256]{2,1,0:T(8,128)S(1)}, f32[4,480,256]{2,1,0:T(8,128)}, u32[]{:S(2)}) copy-start(f32[4,480,256]{2,1,0:T(8,128)} %pixels_ref.3) | copy-start | bytes 5898244
  2.9 5.2 %collective-permute-start.3 = (f32[2,240,256]{2,1,0:T(8,128)S(1)}, f32[2,240,256]{2,1,0:T(8,128)S(1)}, u32[]{:S(2)}, u32[]{:S(2)}) collective-permute-start(f32[2,240,256]{2,1,0:T(8,128)S(1)} %get-tuple-element.50), channel_id=1, source_target_pairs={{0,1},{1,0},{2,3},{3,2},{4,5},{5,4},{6,7},{7,6},{8,9},{9,8},{10,11... | collective-permute-start | bytes 1474568 | tf_op jit(solution)/shard_map/ppermute | solution.py:671
  4.6 7.1 %collective-permute-start = (f32[2,8,128]{2,1,0:T(8,128)S(1)}, f32[2,8,128]{2,1,0:T(8,128)S(1)}, u32[]{:S(2)}, u32[]{:S(2)}) collective-permute-start(f32[2,8,128]{2,1,0:T(8,128)S(1)} %get-tuple-element.40), channel_id=1, source_target_pairs={{0,2},{2,4},{4,6},{6,0},{1,3},{3,5},{5,7},{7,1},{8,10},{10,12},{12... | collective-permute-start | bytes 24584 | tf_op jit(solution)/shard_map/ppermute | solution.py:676
  7.2 4.6 %collective-permute-start.1 = (f32[2,8,128]{2,1,0:T(8,128)S(1)}, f32[2,8,128]{2,1,0:T(8,128)S(1)}, u32[]{:S(2)}, u32[]{:S(2)}) collective-permute-start(f32[2,8,128]{2,1,0:T(8,128)S(1)} %get-tuple-element.41), channel_id=1, source_target_pairs={{2,0},{4,2},{6,4},{0,6},{3,1},{5,3},{7,5},{1,7},{10,8},{12,10},{14... | collective-permute-start | bytes 24584 | tf_op jit(solution)/shard_map/ppermute | solution.py:677
  8.7 10.4 %collective-permute-start.4 = (f32[2,120,128]{2,1,0:T(8,128)S(1)}, f32[2,120,128]{2,1,0:T(8,128)S(1)}, u32[]{:S(2)}, u32[]{:S(2)}) collective-permute-start(f32[2,120,128]{2,1,0:T(8,128)S(1)} %get-tuple-element.53), channel_id=1, source_target_pairs={{0,16},{8,24},{16,0},{24,8},{1,17},{9,25},{17,1},{25,9},{2,18},{10... | collective-permute-start | bytes 368648 | tf_op jit(solution)/shard_map/ppermute | solution.py:547
  14.4 4.7 %collective-permute-start.2 = (f32[1,240,256]{2,1,0:T(8,128)S(1)}, f32[1,240,256]{2,1,0:T(8,128)S(1)}, u32[]{:S(2)}, u32[]{:S(2)}) collective-permute-start(f32[1,240,256]{2,1,0:T(8,128)S(1)} %get-tuple-element.45), channel_id=1, source_target_pairs={{0,1},{1,0},{2,3},{3,2},{4,5},{5,4},{6,7},{7,6},{8,9},{9,8},{10,11... | collective-permute-start | bytes 737288 | tf_op jit(solution)/shard_map/ppermute | solution.py:686
  15.2 9.8 %collective-permute-start.8 = (f32[2,120,128]{2,1,0:T(8,128)S(1)}, f32[2,120,128]{2,1,0:T(8,128)S(1)}, u32[]{:S(2)}, u32[]{:S(2)}) collective-permute-start(f32[2,120,128]{2,1,0:T(8,128)S(1)} %get-tuple-element.63), channel_id=1, source_target_pairs={{0,8},{8,16},{16,24},{24,0},{1,9},{9,17},{17,25},{25,1},{2,10},{10... | collective-permute-start | bytes 368648 | tf_op jit(solution)/shard_map/ppermute | solution.py:547
  16.8 10.4 %collective-permute-start.9 = (f32[2,120,128]{2,1,0:T(8,128)S(1)}, f32[2,120,128]{2,1,0:T(8,128)S(1)}, u32[]{:S(2)}, u32[]{:S(2)}) collective-permute-start(f32[2,120,128]{2,1,0:T(8,128)S(1)} %get-tuple-element.64), channel_id=1, source_target_pairs={{0,24},{8,0},{16,8},{24,16},{1,25},{9,1},{17,9},{25,17},{2,26},{10... | collective-permute-start | bytes 368648 | tf_op jit(solution)/shard_map/ppermute | solution.py:547
  19.4 9.6 %collective-permute-start.5 = (f32[1,120,128]{2,1,0:T(8,128)S(1)}, f32[1,120,128]{2,1,0:T(8,128)S(1)}, u32[]{:S(2)}, u32[]{:S(2)}) collective-permute-start(f32[1,120,128]{2,1,0:T(8,128)S(1)} %get-tuple-element.59), channel_id=1, source_target_pairs={{0,8},{8,16},{16,24},{24,0},{1,9},{9,17},{17,25},{25,1},{2,10},{10... | collective-permute-start | bytes 184328 | tf_op jit(solution)/shard_map/ppermute | solution.py:547
  19.5 9.9 %collective-permute-start.6 = (f32[1,120,128]{2,1,0:T(8,128)S(1)}, f32[1,120,128]{2,1,0:T(8,128)S(1)}, u32[]{:S(2)}, u32[]{:S(2)}) collective-permute-start(f32[1,120,128]{2,1,0:T(8,128)S(1)} %get-tuple-element.60), channel_id=1, source_target_pairs={{0,16},{8,24},{16,0},{24,8},{1,17},{9,25},{17,1},{25,9},{2,18},{10... | collective-permute-start | bytes 184328 | tf_op jit(solution)/shard_map/ppermute | solution.py:547
  22.4 7.0 %collective-permute-start.7 = (f32[1,120,128]{2,1,0:T(8,128)S(1)}, f32[1,120,128]{2,1,0:T(8,128)S(1)}, u32[]{:S(2)}, u32[]{:S(2)}) collective-permute-start(f32[1,120,128]{2,1,0:T(8,128)S(1)} %get-tuple-element.61), channel_id=1, source_target_pairs={{0,24},{8,0},{16,8},{24,16},{1,25},{9,1},{17,9},{25,17},{2,26},{10... | collective-permute-start | bytes 184328 | tf_op jit(solution)/shard_map/ppermute | solution.py:547

commit v14 on v13

--- a/solution.py
+++ b/solution.py
@@ -623,9 +623,9 @@
     )(place, table, sums, *late_pieces)
 
 
-def flux_end_kernel(pack, table_ref, *refs):
+def flux_end_kernel(pack, order, table_ref, *refs):
     *piece_refs, flux_ref = refs
-    (flux,) = landed(piece_refs, table_ref[...])
+    (flux,) = landed([piece_refs[order.index(d)] for d in range(len(order))], table_ref[...])
     rows, fibres = flux_ref.shape
     part = rows // pack
     for h in range(pack):
@@ -634,15 +634,16 @@
 
 def end_flux(table, pieces, pack, fibres):
     rows = pieces[0].shape[1] * pack
-    return pl.pallas_call(
-        functools.partial(flux_end_kernel, pack),
+    order = sorted(range(len(pieces)), key=lambda d: (d > 0, abs(2 * d - len(pieces))))
+    return pl.pallas_call(
+        functools.partial(flux_end_kernel, pack, order),
         in_specs=[in_vmem] * (1 + len(pieces)),
         out_specs=in_vmem,
         out_shape=shaped((rows, fibres)),
         compiler_params=params(),
         cost_estimate=cost(2 * rows * table.size, 2 * rows * fibres * 4),
         name="end_flux",
-    )(table, *pieces)
+    )(table, *(pieces[d] for d in order))
 
 
 def after(value, done):

time: 30.6 us -> 30.6 us (level)
  no operation moved by 1% of the time
where the time goes in v14:
time: 30.6 us; the launch traced here: 30.4 us
  starting transfers between devices  15.1 us (49%)
  Pallas kernels  11.9 us (39%)
  waiting for transfers between devices  2.62 us (9%)
  between operations  0.73 us (2%)
    ppermute x6, starting transfers between devices, exchange(): lax.ppermute(pieces[d], 'fib', [(i, (i + d) % fib_count) for i in range(f...  10.9 us
    ppermute x6, waiting for transfers between devices, exchange(): lax.ppermute(pieces[d], 'fib', [(i, (i + d) % fib_count) for i in range(f...  2.61 us
    ppermute x1, starting transfers between devices, per_device(): left = lax.ppermute(up, 'wav', upward)  2.56 us
    pallas_call x1, Pallas kernels, flux_sums(): pl.pallas_call(functools.partial(solve_kernel, wav_count), in_specs=[in_s...  2.34 us
    pallas_call x1, Pallas kernels, sent_weights(): pl.pallas_call(functools.partial(sent_kernel, moves, wav_count), in_specs...  2.22 us
    pallas_call x1, Pallas kernels, end_weights(): pl.pallas_call(functools.partial(weights_end_kernel, pack, total, late, l...  1.78 us
    pallas_call x1, Pallas kernels, place_early(): pl.pallas_call(functools.partial(early_kernel, moves, which, len(weight_p...  1.62 us
    pallas_call x1, Pallas kernels, kept_weights(): pl.pallas_call(functools.partial(kept_kernel, wav_count), in_specs=[in_sm...  1.14 us
  transfers between devices with their start and end apart: 10, of which 2 were waited for; matrix products, arithmetic and copies ran while one was open for 0% of the time, Pallas kernels for 29%

profile of v14, /device:TPU:0, one launch (start us, length us, event | category | flops | bytes accessed | tf_op | source)
XLA Modules:
  0.0 30.4 jit_solution(15546587538857569064)
XLA Ops:
  0.6 0.1 pad_add_fusion.place_ref
  0.7 2.2 %sent_weights.1 = (f32[2,240,256]{2,1,0:T(8,128)S(1)}, f32[4,240,256]{2,1,0:T(8,128)S(1)}, bf16[512,512]{1,0:T(8,128)(2,1)S(1)}, s32[1,1024]{1,0:T(1,128)S(1)}, ...) custom-call(s32[3]{0:T(128)S(1)} %pad_add_fusion.place_ref, ...), custom_call_target="tpu_custom_call" | custom-call | flops 9830400 | bytes 2949120 | tf_op jit(solution)/shard_map/sent_weights/pallas_call | solution.py:263
  2.9 0.5 %collective-permute-start.3 = (f32[2,240,256]{2,1,0:T(8,128)S(1)}, f32[2,240,256]{2,1,0:T(8,128)S(1)}, u32[]{:S(2)}, u32[]{:S(2)}) collective-permute-start(f32[2,240,256]{2,1,0:T(8,128)S(1)} %get-tuple-element.50), channel_id=1, source_target_pairs={{0,1},{1,0},{2,3},{3,2},{4,5},{5,4},{6,7},{7,6},{8,9},{9,8},{10,11... | collective-permute-start | bytes 1474568 | tf_op jit(solution)/shard_map/ppermute | solution.py:672
  3.5 1.1 %kept_weights.1 = (f32[2,240,256]{2,1,0:T(8,128)S(1)}, f32[4,240,256]{2,1,0:T(8,128)S(1)}, f32[2,8,128]{2,1,0:T(8,128)S(1)}, f32[2,8,128]{2,1,0:T(8,128)S(1)}) custom-call(s32[3]{0:T(128)S(1)} %pad_add_fusion.place_ref, f32[1,256]{1,0:T(1,128)S(1)} %get-tuple-element.35.coupling_ref, s32[1,256]{1,0:T(1,128)S(1)} %get-tuple-element.36.counts_ref, ...), custom_call_target="tpu_custom_call" | custom-call | flops 9830400 | bytes 2949120 | tf_op jit(solution)/shard_map/kept_weights/pallas_call | solution.py:336
  4.6 2.6 %collective-permute-start = (f32[2,8,128]{2,1,0:T(8,128)S(1)}, f32[2,8,128]{2,1,0:T(8,128)S(1)}, u32[]{:S(2)}, u32[]{:S(2)}) collective-permute-start(f32[2,8,128]{2,1,0:T(8,128)S(1)} %get-tuple-element.40), channel_id=1, source_target_pairs={{0,2},{2,4},{4,6},{6,0},{1,3},{3,5},{5,7},{7,1},{8,10},{10,12},{12... | collective-permute-start | bytes 24584 | tf_op jit(solution)/shard_map/ppermute | solution.py:677
  7.2 1.0 %collective-permute-start.1 = (f32[2,8,128]{2,1,0:T(8,128)S(1)}, f32[2,8,128]{2,1,0:T(8,128)S(1)}, u32[]{:S(2)}, u32[]{:S(2)}) collective-permute-start(f32[2,8,128]{2,1,0:T(8,128)S(1)} %get-tuple-element.41), channel_id=1, source_target_pairs={{2,0},{4,2},{6,4},{0,6},{3,1},{5,3},{7,5},{1,7},{10,8},{12,10},{14... | collective-permute-start | bytes 24584 | tf_op jit(solution)/shard_map/ppermute | solution.py:678
  8.2 0.5 %sort_weights.1 = (f32[2,120,128]{2,1,0:T(8,128)S(1)}, f32[2,120,128]{2,1,0:T(8,128)S(1)}, f32[2,120,128]{2,1,0:T(8,128)S(1)}, f32[2,120,128]{2,1,0:T(8,128)S(1)}, f32[240,256]{1,0:T(8,128)S(1)}) custom-call(f32[2,240,256]{2,1,0:T(8,128)S(1)} %collective-permute-done.3.theirs_ref, f32[2,240,256]{2,1,0:T(8,128)S(1)} %get-tuple-element.51.mine_ref, ...), custom_call_target="tpu_custom_call" | custom-call | tf_op jit(solution)/shard_map/sort_weights/pallas_call | solution.py:531
  8.7 3.1 %collective-permute-start.4 = (f32[2,120,128]{2,1,0:T(8,128)S(1)}, f32[2,120,128]{2,1,0:T(8,128)S(1)}, u32[]{:S(2)}, u32[]{:S(2)}) collective-permute-start(f32[2,120,128]{2,1,0:T(8,128)S(1)} %get-tuple-element.53), channel_id=1, source_target_pairs={{0,16},{8,24},{16,0},{24,8},{1,17},{9,25},{17,1},{25,9},{2,18},{10... | collective-permute-start | bytes 368648 | tf_op jit(solution)/shard_map/ppermute | solution.py:547
  11.7 0.0 collective-permute-done.left_ref
  11.8 0.3 stream_layout.1
  12.0 2.3 %flux_sums.1 = (f32[1,240,256]{2,1,0:T(8,128)S(1)}, f32[3848,128]{1,0:T(8,128)S(1)}) custom-call(s32[3]{0:T(128)S(1)} %pad_add_fusion.place_ref, f32[1,256]{1,0:T(1,128)S(1)} %get-tuple-element.35.coupling_ref, f32[2,8,128]{2,1,0:T(8,128)S(1)} %collective-permute-done.left_ref, f32[2,8,128]{2,1,0:T(8,128)S(1)} %collective-permute-done.1.right_ref, ...), custom_call_target="tpu_custom_call" | custom-call | tf_op jit(solution)/shard_map/flux_sums/pallas_call | solution.py:467
  14.4 0.1 collective-permute-start.2
  14.4 0.7 %kept_flux.1.mine_ref = f32[1,240,256]{2,1,0:T(8,128)S(1)} custom-call(s32[3]{0:T(128)S(1)} %pad_add_fusion.place_ref, f32[1,256]{1,0:T(1,128)S(1)} %get-tuple-element.35.coupling_ref, f32[3848,128]{1,0:T(8,128)S(1)} %get-tuple-element.47.solved_ref, f32[4,240,256]{2,1,0:T(8,128)S(1)} %get-tuple-element.48.weight_ref), custom_call_target="tpu_custom_call" | custom-call | flops 491520 | bytes 1966080 | tf_op jit(solution)/shard_map/kept_flux/pallas_call | solution.py:485
  15.2 1.6 %collective-permute-start.8 = (f32[2,120,128]{2,1,0:T(8,128)S(1)}, f32[2,120,128]{2,1,0:T(8,128)S(1)}, u32[]{:S(2)}, u32[]{:S(2)}) collective-permute-start(f32[2,120,128]{2,1,0:T(8,128)S(1)} %get-tuple-element.63), channel_id=1, source_target_pairs={{0,8},{8,16},{16,24},{24,0},{1,9},{9,17},{17,25},{25,1},{2,10},{10... | collective-permute-start | bytes 368648 | tf_op jit(solution)/shard_map/ppermute | solution.py:547
  16.8 2.2 %collective-permute-start.9 = (f32[2,120,128]{2,1,0:T(8,128)S(1)}, f32[2,120,128]{2,1,0:T(8,128)S(1)}, u32[]{:S(2)}, u32[]{:S(2)}) collective-permute-start(f32[2,120,128]{2,1,0:T(8,128)S(1)} %get-tuple-element.64), channel_id=1, source_target_pairs={{0,24},{8,0},{16,8},{24,16},{1,25},{9,1},{17,9},{25,17},{2,26},{10... | collective-permute-start | bytes 368648 | tf_op jit(solution)/shard_map/ppermute | solution.py:547
  19.1 0.3 %sort_flux.1 = (f32[1,120,128]{2,1,0:T(8,128)S(1)}, f32[1,120,128]{2,1,0:T(8,128)S(1)}, f32[1,120,128]{2,1,0:T(8,128)S(1)}, f32[1,120,128]{2,1,0:T(8,128)S(1)}) custom-call(f32[1,240,256]{2,1,0:T(8,128)S(1)} %collective-permute-done.2.theirs_ref, f32[1,240,256]{2,1,0:T(8,128)S(1)} %kept_flux.1.mine_ref, bf16[512,512]{1,0:T(8,128)(2,1)S(1)} %get-tuple-element.49.table_ref, ...), custom_call_target="tpu_custom_call" | custom-call | tf_op jit(solution)/shard_map/sort_flux/pallas_call | solution.py:531
  19.4 0.1 collective-permute-start.5
  19.5 2.9 %collective-permute-start.6 = (f32[1,120,128]{2,1,0:T(8,128)S(1)}, f32[1,120,128]{2,1,0:T(8,128)S(1)}, u32[]{:S(2)}, u32[]{:S(2)}) collective-permute-start(f32[1,120,128]{2,1,0:T(8,128)S(1)} %get-tuple-element.60), channel_id=1, source_target_pairs={{0,8},{8,16},{16,24},{24,0},{1,9},{9,17},{17,25},{25,1},{2,10},{10... | collective-permute-start | bytes 184328 | tf_op jit(solution)/shard_map/ppermute | solution.py:547
  22.4 1.0 %collective-permute-start.7 = (f32[1,120,128]{2,1,0:T(8,128)S(1)}, f32[1,120,128]{2,1,0:T(8,128)S(1)}, u32[]{:S(2)}, u32[]{:S(2)}) collective-permute-start(f32[1,120,128]{2,1,0:T(8,128)S(1)} %get-tuple-element.61), channel_id=1, source_target_pairs={{0,24},{8,0},{16,8},{24,16},{1,25},{9,1},{17,9},{25,17},{2,26},{10... | collective-permute-start | bytes 184328 | tf_op jit(solution)/shard_map/ppermute | solution.py:547
  23.4 1.6 %place_early.1 = (bf16[512,512]{1,0:T(8,128)(2,1)S(1)}, f32[2,120,512]{2,1,0:T(8,128)S(1)}) custom-call(s32[3]{0:T(128)S(1)} %pad_add_fusion.place_ref, s32[1,1024]{1,0:T(1,128)S(1)} %get-tuple-element.56.slots_ref, f32[2,120,128]{2,1,0:T(8,128)S(1)} %get-tuple-element.57.refs_0_, f32[2,120,128]{2,1,0:T(8,128)S(1)} %collective-permute-done.4.refs_1_), custom_call_target="tpu_custom_call" | custom-call | tf_op jit(solution)/shard_map/place_early/pallas_call | solution.py:576
  25.0 0.8 %collective-permute-done.9.refs_1_ = f32[2,120,128]{2,1,0:T(8,128)S(1)} collective-permute-done((f32[2,120,128]{2,1,0:T(8,128)S(1)}, f32[2,120,128]{2,1,0:T(8,128)S(1)}, u32[]{:S(2)}, u32[]{:S(2)}) %collective-permute-start.9) | collective-permute-done | bytes 122912 | tf_op jit(solution)/shard_map/ppermute | solution.py:547
  25.8 1.8 %end_weights.1 = (f32[240,256]{1,0:T(8,128)}, f32[3,240,256]{2,1,0:T(8,128)}) custom-call(s32[3]{0:T(128)S(1)} %pad_add_fusion.place_ref, bf16[512,512]{1,0:T(8,128)(2,1)S(1)} %get-tuple-element.58.table_ref, f32[2,120,512]{2,1,0:T(8,128)S(1)} %get-tuple-element.62.sums_ref, f32[2,120,128]{2,1,0:T(8,128)S(1)} %collective-permute-done.8.refs_0_, ...), custom_call_target="tpu_custom_call" | custom-call | tf_op jit(solution)/shard_map/end_weights/pallas_call | solution.py:615
  27.6 1.8 %collective-permute-done.5.refs_1_ = f32[1,120,128]{2,1,0:T(8,128)S(1)} collective-permute-done((f32[1,120,128]{2,1,0:T(8,128)S(1)}, f32[1,120,128]{2,1,0:T(8,128)S(1)}, u32[]{:S(2)}, u32[]{:S(2)}) %collective-permute-start.5) | collective-permute-done | bytes 61472 | tf_op jit(solution)/shard_map/ppermute | solution.py:547
  29.4 1.0 %end_flux.1 = f32[240,256]{1,0:T(8,128)} custom-call(bf16[512,512]{1,0:T(8,128)(2,1)S(1)} %get-tuple-element.58.table_ref, f32[1,120,128]{2,1,0:T(8,128)S(1)} %get-tuple-element.54.refs_0_, f32[1,120,128]{2,1,0:T(8,128)S(1)} %collective-permute-done.5.refs_1_, f32[1,120,128]{2,1,0:T(8,128)S(1)} %collective-permute-done.6.refs_2_, ...), custom_call_target="tpu_custom_call" | custom-call | flops 125829120 | bytes 491520 | tf_op jit(solution)/shard_map/end_flux/pallas_call | solution.py:638
  (11 shorter events, 0.0 us)
Async XLA Ops:
  0.6 2.8 %copy-start = (f32[4,480,256]{2,1,0:T(8,128)S(1)}, f32[4,480,256]{2,1,0:T(8,128)}, u32[]{:S(2)}) copy-start(f32[4,480,256]{2,1,0:T(8,128)} %pixels_ref.3) | copy-start | bytes 5898244
  2.9 5.2 %collective-permute-start.3 = (f32[2,240,256]{2,1,0:T(8,128)S(1)}, f32[2,240,256]{2,1,0:T(8,128)S(1)}, u32[]{:S(2)}, u32[]{:S(2)}) collective-permute-start(f32[2,240,256]{2,1,0:T(8,128)S(1)} %get-tuple-element.50), channel_id=1, source_target_pairs={{0,1},{1,0},{2,3},{3,2},{4,5},{5,4},{6,7},{7,6},{8,9},{9,8},{10,11... | collective-permute-start | bytes 1474568 | tf_op jit(solution)/shard_map/ppermute | solution.py:672
  4.6 7.1 %collective-permute-start = (f32[2,8,128]{2,1,0:T(8,128)S(1)}, f32[2,8,128]{2,1,0:T(8,128)S(1)}, u32[]{:S(2)}, u32[]{:S(2)}) collective-permute-start(f32[2,8,128]{2,1,0:T(8,128)S(1)} %get-tuple-element.40), channel_id=1, source_target_pairs={{0,2},{2,4},{4,6},{6,0},{1,3},{3,5},{5,7},{7,1},{8,10},{10,12},{12... | collective-permute-start | bytes 24584 | tf_op jit(solution)/shard_map/ppermute | solution.py:677
  7.2 4.6 %collective-permute-start.1 = (f32[2,8,128]{2,1,0:T(8,128)S(1)}, f32[2,8,128]{2,1,0:T(8,128)S(1)}, u32[]{:S(2)}, u32[]{:S(2)}) collective-permute-start(f32[2,8,128]{2,1,0:T(8,128)S(1)} %get-tuple-element.41), channel_id=1, source_target_pairs={{2,0},{4,2},{6,4},{0,6},{3,1},{5,3},{7,5},{1,7},{10,8},{12,10},{14... | collective-permute-start | bytes 24584 | tf_op jit(solution)/shard_map/ppermute | solution.py:678
  8.7 10.4 %collective-permute-start.4 = (f32[2,120,128]{2,1,0:T(8,128)S(1)}, f32[2,120,128]{2,1,0:T(8,128)S(1)}, u32[]{:S(2)}, u32[]{:S(2)}) collective-permute-start(f32[2,120,128]{2,1,0:T(8,128)S(1)} %get-tuple-element.53), channel_id=1, source_target_pairs={{0,16},{8,24},{16,0},{24,8},{1,17},{9,25},{17,1},{25,9},{2,18},{10... | collective-permute-start | bytes 368648 | tf_op jit(solution)/shard_map/ppermute | solution.py:547
  14.4 4.7 %collective-permute-start.2 = (f32[1,240,256]{2,1,0:T(8,128)S(1)}, f32[1,240,256]{2,1,0:T(8,128)S(1)}, u32[]{:S(2)}, u32[]{:S(2)}) collective-permute-start(f32[1,240,256]{2,1,0:T(8,128)S(1)} %get-tuple-element.45), channel_id=1, source_target_pairs={{0,1},{1,0},{2,3},{3,2},{4,5},{5,4},{6,7},{7,6},{8,9},{9,8},{10,11... | collective-permute-start | bytes 737288 | tf_op jit(solution)/shard_map/ppermute | solution.py:687
  15.2 9.8 %collective-permute-start.8 = (f32[2,120,128]{2,1,0:T(8,128)S(1)}, f32[2,120,128]{2,1,0:T(8,128)S(1)}, u32[]{:S(2)}, u32[]{:S(2)}) collective-permute-start(f32[2,120,128]{2,1,0:T(8,128)S(1)} %get-tuple-element.63), channel_id=1, source_target_pairs={{0,8},{8,16},{16,24},{24,0},{1,9},{9,17},{17,25},{25,1},{2,10},{10... | collective-permute-start | bytes 368648 | tf_op jit(solution)/shard_map/ppermute | solution.py:547
  16.8 9.0 %collective-permute-start.9 = (f32[2,120,128]{2,1,0:T(8,128)S(1)}, f32[2,120,128]{2,1,0:T(8,128)S(1)}, u32[]{:S(2)}, u32[]{:S(2)}) collective-permute-start(f32[2,120,128]{2,1,0:T(8,128)S(1)} %get-tuple-element.64), channel_id=1, source_target_pairs={{0,24},{8,0},{16,8},{24,16},{1,25},{9,1},{17,9},{25,17},{2,26},{10... | collective-permute-start | bytes 368648 | tf_op jit(solution)/shard_map/ppermute | solution.py:547
  19.4 10.0 %collective-permute-start.5 = (f32[1,120,128]{2,1,0:T(8,128)S(1)}, f32[1,120,128]{2,1,0:T(8,128)S(1)}, u32[]{:S(2)}, u32[]{:S(2)}) collective-permute-start(f32[1,120,128]{2,1,0:T(8,128)S(1)} %get-tuple-element.59), channel_id=1, source_target_pairs={{0,16},{8,24},{16,0},{24,8},{1,17},{9,25},{17,1},{25,9},{2,18},{10... | collective-permute-start | bytes 184328 | tf_op jit(solution)/shard_map/ppermute | solution.py:547
  19.5 9.9 %collective-permute-start.6 = (f32[1,120,128]{2,1,0:T(8,128)S(1)}, f32[1,120,128]{2,1,0:T(8,128)S(1)}, u32[]{:S(2)}, u32[]{:S(2)}) collective-permute-start(f32[1,120,128]{2,1,0:T(8,128)S(1)} %get-tuple-element.60), channel_id=1, source_target_pairs={{0,8},{8,16},{16,24},{24,0},{1,9},{9,17},{17,25},{25,1},{2,10},{10... | collective-permute-start | bytes 184328 | tf_op jit(solution)/shard_map/ppermute | solution.py:547
  22.4 7.0 %collective-permute-start.7 = (f32[1,120,128]{2,1,0:T(8,128)S(1)}, f32[1,120,128]{2,1,0:T(8,128)S(1)}, u32[]{:S(2)}, u32[]{:S(2)}) collective-permute-start(f32[1,120,128]{2,1,0:T(8,128)S(1)} %get-tuple-element.61), channel_id=1, source_target_pairs={{0,24},{8,0},{16,8},{24,16},{1,25},{9,1},{17,9},{25,17},{2,26},{10... | collective-permute-start | bytes 184328 | tf_op jit(solution)/shard_map/ppermute | solution.py:547

commit v15 on v14

--- a/solution.py
+++ b/solution.py
@@ -121,9 +121,7 @@
     to_owner = (source == my_owner).astype(F32)
     counted = jnp.dot(to_owner.astype(BF16), earlier_fibres(fibres), preferred_element_type=F32)
     rank = jnp.sum(to_owner * counted, axis=0, keepdims=True).astype(jnp.int32)
-    target = my_owner
-    if rel:
-        target = jnp.where(my_owner >= me, my_owner - me, my_owner - me + fib_count)
+    target = my_owner ^ me if rel else my_owner
     base = target * lanes + rank
     place_of = jnp.concatenate([base + h * per for h in range(pack)], 1)
     row = lax.broadcasted_iota(jnp.int32, table_ref.shape, 0)
@@ -138,9 +136,7 @@
     source = lax.broadcasted_iota(jnp.int32, owner.shape, 0)
     mine = (owner == me.astype(F32)).astype(F32)
     rank_in = jnp.dot(mine.astype(BF16), earlier_fibres(fibres), preferred_element_type=F32).astype(jnp.int32)
-    order = source
-    if rel:
-        order = jnp.where(me >= source, me - source, me - source + fib_count)
+    order = source ^ me if rel else source
     arrival = jnp.where(mine > 0.0, order * lanes + rank_in, -total_lanes)
     tall = lax.broadcasted_iota(jnp.int32, (total_lanes, fibres), 0)
     landing = jnp.zeros((ROWS, total_lanes), F32)
@@ -542,10 +538,8 @@
 def exchange(pieces, fib_count):
     if len(pieces) == 1:
         return [lax.all_to_all(pieces[0], "fib", split_axis=2, concat_axis=2, tiled=True)]
-    arrived = [pieces[0]]
-    for d in range(1, fib_count):
-        arrived.append(lax.ppermute(pieces[d], "fib", [(i, (i + d) % fib_count) for i in range(fib_count)]))
-    return arrived
+    swapped = [lax.ppermute(pieces[d], "fib", [(i, i ^ d) for i in range(fib_count)]) for d in range(1, fib_count)]
+    return [pieces[0]] + swapped
 
 
 def landed(refs, table):
@@ -659,7 +653,7 @@
     pack = max(1, LANES // per)
     while pack > 1 and rows % (pack * ROWS):
         pack //= 2
-    rel = pack * per == LANES
+    rel = pack * per == LANES and fib_count & (fib_count - 1) == 0
     pieces = fib_count if rel else 1
     place = jnp.stack([lax.axis_index(axis) for axis in ("fib", "wav", "exp")]).astype(jnp.int32)
     coupling, counts, slots = coupling[None], counts[None], owner_slot[None]

time: 30.6 us -> 30.1 us (0.984)
  no operation moved by 1% of the time
where the time goes in v15:
time: 30.1 us; the launch traced here: 30 us
  starting transfers between devices  14.9 us (50%)
  Pallas kernels  12 us (40%)
  waiting for transfers between devices  2.35 us (8%)
  between operations  0.73 us (2%)
    ppermute x6, starting transfers between devices, exchange(): lax.ppermute(pieces[d], 'fib', [(i, i ^ d) for i in range(fib_count)])  10.7 us
    ppermute x1, starting transfers between devices, per_device(): left = lax.ppermute(up, 'wav', upward)  2.56 us
    pallas_call x1, Pallas kernels, flux_sums(): pl.pallas_call(functools.partial(solve_kernel, wav_count), in_specs=[in_s...  2.34 us
    ppermute x6, waiting for transfers between devices, exchange(): lax.ppermute(pieces[d], 'fib', [(i, i ^ d) for i in range(fib_count)])  2.34 us
    pallas_call x1, Pallas kernels, sent_weights(): pl.pallas_call(functools.partial(sent_kernel, moves, wav_count), in_specs...  2.22 us
    pallas_call x1, Pallas kernels, end_weights(): pl.pallas_call(functools.partial(weights_end_kernel, pack, total, late, l...  1.79 us
    pallas_call x1, Pallas kernels, place_early(): pl.pallas_call(functools.partial(early_kernel, moves, which, len(weight_p...  1.62 us
    pallas_call x1, Pallas kernels, kept_weights(): pl.pallas_call(functools.partial(kept_kernel, wav_count), in_specs=[in_sm...  1.14 us
  transfers between devices with their start and end apart: 10, of which 2 were waited for; matrix products, arithmetic and copies ran while one was open for 0% of the time, Pallas kernels for 29%

profile of v15, /device:TPU:0, one launch (start us, length us, event | category | flops | bytes accessed | tf_op | source)
XLA Modules:
  0.0 30.0 jit_solution(8704039500532945989)
XLA Ops:
  0.6 0.1 pad_add_fusion.place_ref
  0.7 2.2 %sent_weights.1 = (f32[2,240,256]{2,1,0:T(8,128)S(1)}, f32[4,240,256]{2,1,0:T(8,128)S(1)}, bf16[512,512]{1,0:T(8,128)(2,1)S(1)}, s32[1,1024]{1,0:T(1,128)S(1)}, ...) custom-call(s32[3]{0:T(128)S(1)} %pad_add_fusion.place_ref, ...), custom_call_target="tpu_custom_call" | custom-call | flops 9830400 | bytes 2949120 | tf_op jit(solution)/shard_map/sent_weights/pallas_call | solution.py:259
  2.9 0.5 %collective-permute-start.3 = (f32[2,240,256]{2,1,0:T(8,128)S(1)}, f32[2,240,256]{2,1,0:T(8,128)S(1)}, u32[]{:S(2)}, u32[]{:S(2)}) collective-permute-start(f32[2,240,256]{2,1,0:T(8,128)S(1)} %get-tuple-element.50), channel_id=1, source_target_pairs={{0,1},{1,0},{2,3},{3,2},{4,5},{5,4},{6,7},{7,6},{8,9},{9,8},{10,11... | collective-permute-start | bytes 1474568 | tf_op jit(solution)/shard_map/ppermute | solution.py:666
  3.5 1.1 %kept_weights.1 = (f32[2,240,256]{2,1,0:T(8,128)S(1)}, f32[4,240,256]{2,1,0:T(8,128)S(1)}, f32[2,8,128]{2,1,0:T(8,128)S(1)}, f32[2,8,128]{2,1,0:T(8,128)S(1)}) custom-call(s32[3]{0:T(128)S(1)} %pad_add_fusion.place_ref, f32[1,256]{1,0:T(1,128)S(1)} %get-tuple-element.35.coupling_ref, s32[1,256]{1,0:T(1,128)S(1)} %get-tuple-element.36.counts_ref, ...), custom_call_target="tpu_custom_call" | custom-call | flops 9830400 | bytes 2949120 | tf_op jit(solution)/shard_map/kept_weights/pallas_call | solution.py:332
  4.6 2.6 %collective-permute-start = (f32[2,8,128]{2,1,0:T(8,128)S(1)}, f32[2,8,128]{2,1,0:T(8,128)S(1)}, u32[]{:S(2)}, u32[]{:S(2)}) collective-permute-start(f32[2,8,128]{2,1,0:T(8,128)S(1)} %get-tuple-element.40), channel_id=1, source_target_pairs={{0,2},{2,4},{4,6},{6,0},{1,3},{3,5},{5,7},{7,1},{8,10},{10,12},{12... | collective-permute-start | bytes 24584 | tf_op jit(solution)/shard_map/ppermute | solution.py:671
  7.2 1.0 %collective-permute-start.1 = (f32[2,8,128]{2,1,0:T(8,128)S(1)}, f32[2,8,128]{2,1,0:T(8,128)S(1)}, u32[]{:S(2)}, u32[]{:S(2)}) collective-permute-start(f32[2,8,128]{2,1,0:T(8,128)S(1)} %get-tuple-element.41), channel_id=1, source_target_pairs={{2,0},{4,2},{6,4},{0,6},{3,1},{5,3},{7,5},{1,7},{10,8},{12,10},{14... | collective-permute-start | bytes 24584 | tf_op jit(solution)/shard_map/ppermute | solution.py:672
  8.2 0.0 collective-permute-done.3.theirs_ref
  8.2 0.5 %sort_weights.1 = (f32[2,120,128]{2,1,0:T(8,128)S(1)}, f32[2,120,128]{2,1,0:T(8,128)S(1)}, f32[2,120,128]{2,1,0:T(8,128)S(1)}, f32[2,120,128]{2,1,0:T(8,128)S(1)}, f32[240,256]{1,0:T(8,128)S(1)}) custom-call(f32[2,240,256]{2,1,0:T(8,128)S(1)} %collective-permute-done.3.theirs_ref, f32[2,240,256]{2,1,0:T(8,128)S(1)} %get-tuple-element.51.mine_ref, ...), custom_call_target="tpu_custom_call" | custom-call | tf_op jit(solution)/shard_map/sort_weights/pallas_call | solution.py:527
  8.7 3.1 %collective-permute-start.4 = (f32[2,120,128]{2,1,0:T(8,128)S(1)}, f32[2,120,128]{2,1,0:T(8,128)S(1)}, u32[]{:S(2)}, u32[]{:S(2)}) collective-permute-start(f32[2,120,128]{2,1,0:T(8,128)S(1)} %get-tuple-element.53), channel_id=1, source_target_pairs={{0,16},{8,24},{16,0},{24,8},{1,17},{9,25},{17,1},{25,9},{2,18},{10... | collective-permute-start | bytes 368648 | tf_op jit(solution)/shard_map/ppermute | solution.py:541
  11.8 0.3 stream_layout.1
  12.0 2.3 %flux_sums.1 = (f32[1,240,256]{2,1,0:T(8,128)S(1)}, f32[3848,128]{1,0:T(8,128)S(1)}) custom-call(s32[3]{0:T(128)S(1)} %pad_add_fusion.place_ref, f32[1,256]{1,0:T(1,128)S(1)} %get-tuple-element.35.coupling_ref, f32[2,8,128]{2,1,0:T(8,128)S(1)} %collective-permute-done.left_ref, f32[2,8,128]{2,1,0:T(8,128)S(1)} %collective-permute-done.1.right_ref, ...), custom_call_target="tpu_custom_call" | custom-call | tf_op jit(solution)/shard_map/flux_sums/pallas_call | solution.py:463
  14.4 0.1 collective-permute-start.2
  14.4 0.7 %kept_flux.1.mine_ref = f32[1,240,256]{2,1,0:T(8,128)S(1)} custom-call(s32[3]{0:T(128)S(1)} %pad_add_fusion.place_ref, f32[1,256]{1,0:T(1,128)S(1)} %get-tuple-element.35.coupling_ref, f32[3848,128]{1,0:T(8,128)S(1)} %get-tuple-element.47.solved_ref, f32[4,240,256]{2,1,0:T(8,128)S(1)} %get-tuple-element.48.weight_ref), custom_call_target="tpu_custom_call" | custom-call | flops 491520 | bytes 1966080 | tf_op jit(solution)/shard_map/kept_flux/pallas_call | solution.py:481
  15.2 1.6 %collective-permute-start.8 = (f32[2,120,128]{2,1,0:T(8,128)S(1)}, f32[2,120,128]{2,1,0:T(8,128)S(1)}, u32[]{:S(2)}, u32[]{:S(2)}) collective-permute-start(f32[2,120,128]{2,1,0:T(8,128)S(1)} %get-tuple-element.63), channel_id=1, source_target_pairs={{0,8},{8,0},{16,24},{24,16},{1,9},{9,1},{17,25},{25,17},{2,10},{10... | collective-permute-start | bytes 368648 | tf_op jit(solution)/shard_map/ppermute | solution.py:541
  16.8 1.5 %collective-permute-start.9 = (f32[2,120,128]{2,1,0:T(8,128)S(1)}, f32[2,120,128]{2,1,0:T(8,128)S(1)}, u32[]{:S(2)}, u32[]{:S(2)}) collective-permute-start(f32[2,120,128]{2,1,0:T(8,128)S(1)} %get-tuple-element.64), channel_id=1, source_target_pairs={{0,24},{8,16},{16,8},{24,0},{1,25},{9,17},{17,9},{25,1},{2,26},{10... | collective-permute-start | bytes 368648 | tf_op jit(solution)/shard_map/ppermute | solution.py:541
  18.4 0.3 %sort_flux.1 = (f32[1,120,128]{2,1,0:T(8,128)S(1)}, f32[1,120,128]{2,1,0:T(8,128)S(1)}, f32[1,120,128]{2,1,0:T(8,128)S(1)}, f32[1,120,128]{2,1,0:T(8,128)S(1)}) custom-call(f32[1,240,256]{2,1,0:T(8,128)S(1)} %collective-permute-done.2.theirs_ref, f32[1,240,256]{2,1,0:T(8,128)S(1)} %kept_flux.1.mine_ref, bf16[512,512]{1,0:T(8,128)(2,1)S(1)} %get-tuple-element.49.table_ref, ...), custom_call_target="tpu_custom_call" | custom-call | tf_op jit(solution)/shard_map/sort_flux/pallas_call | solution.py:527
  18.7 0.4 %collective-permute-start.5 = (f32[1,120,128]{2,1,0:T(8,128)S(1)}, f32[1,120,128]{2,1,0:T(8,128)S(1)}, u32[]{:S(2)}, u32[]{:S(2)}) collective-permute-start(f32[1,120,128]{2,1,0:T(8,128)S(1)} %get-tuple-element.59), channel_id=1, source_target_pairs={{0,16},{8,24},{16,0},{24,8},{1,17},{9,25},{17,1},{25,9},{2,18},{10... | collective-permute-start | bytes 184328 | tf_op jit(solution)/shard_map/ppermute | solution.py:541
  19.2 3.2 %collective-permute-start.6 = (f32[1,120,128]{2,1,0:T(8,128)S(1)}, f32[1,120,128]{2,1,0:T(8,128)S(1)}, u32[]{:S(2)}, u32[]{:S(2)}) collective-permute-start(f32[1,120,128]{2,1,0:T(8,128)S(1)} %get-tuple-element.60), channel_id=1, source_target_pairs={{0,8},{8,0},{16,24},{24,16},{1,9},{9,1},{17,25},{25,17},{2,10},{10... | collective-permute-start | bytes 184328 | tf_op jit(solution)/shard_map/ppermute | solution.py:541
  22.4 0.8 %collective-permute-start.7 = (f32[1,120,128]{2,1,0:T(8,128)S(1)}, f32[1,120,128]{2,1,0:T(8,128)S(1)}, u32[]{:S(2)}, u32[]{:S(2)}) collective-permute-start(f32[1,120,128]{2,1,0:T(8,128)S(1)} %get-tuple-element.61), channel_id=1, source_target_pairs={{0,24},{8,16},{16,8},{24,0},{1,25},{9,17},{17,9},{25,1},{2,26},{10... | collective-permute-start | bytes 184328 | tf_op jit(solution)/shard_map/ppermute | solution.py:541
  23.2 1.6 %place_early.1 = (bf16[512,512]{1,0:T(8,128)(2,1)S(1)}, f32[2,120,512]{2,1,0:T(8,128)S(1)}) custom-call(s32[3]{0:T(128)S(1)} %pad_add_fusion.place_ref, s32[1,1024]{1,0:T(1,128)S(1)} %get-tuple-element.56.slots_ref, f32[2,120,128]{2,1,0:T(8,128)S(1)} %get-tuple-element.57.refs_0_, f32[2,120,128]{2,1,0:T(8,128)S(1)} %collective-permute-done.4.refs_1_), custom_call_target="tpu_custom_call" | custom-call | tf_op jit(solution)/shard_map/place_early/pallas_call | solution.py:570
  24.8 0.4 %collective-permute-done.9.refs_1_ = f32[2,120,128]{2,1,0:T(8,128)S(1)} collective-permute-done((f32[2,120,128]{2,1,0:T(8,128)S(1)}, f32[2,120,128]{2,1,0:T(8,128)S(1)}, u32[]{:S(2)}, u32[]{:S(2)}) %collective-permute-start.9) | collective-permute-done | bytes 122912 | tf_op jit(solution)/shard_map/ppermute | solution.py:541
  25.2 1.8 %end_weights.1 = (f32[240,256]{1,0:T(8,128)}, f32[3,240,256]{2,1,0:T(8,128)}) custom-call(s32[3]{0:T(128)S(1)} %pad_add_fusion.place_ref, bf16[512,512]{1,0:T(8,128)(2,1)S(1)} %get-tuple-element.58.table_ref, f32[2,120,512]{2,1,0:T(8,128)S(1)} %get-tuple-element.62.sums_ref, f32[2,120,128]{2,1,0:T(8,128)S(1)} %collective-permute-done.8.refs_0_, ...), custom_call_target="tpu_custom_call" | custom-call | tf_op jit(solution)/shard_map/end_weights/pallas_call | solution.py:609
  27.0 2.0 %collective-permute-done.5.refs_1_ = f32[1,120,128]{2,1,0:T(8,128)S(1)} collective-permute-done((f32[1,120,128]{2,1,0:T(8,128)S(1)}, f32[1,120,128]{2,1,0:T(8,128)S(1)}, u32[]{:S(2)}, u32[]{:S(2)}) %collective-permute-start.5) | collective-permute-done | bytes 61472 | tf_op jit(solution)/shard_map/ppermute | solution.py:541
  28.9 1.0 %end_flux.1 = f32[240,256]{1,0:T(8,128)} custom-call(bf16[512,512]{1,0:T(8,128)(2,1)S(1)} %get-tuple-element.58.table_ref, f32[1,120,128]{2,1,0:T(8,128)S(1)} %get-tuple-element.54.refs_0_, f32[1,120,128]{2,1,0:T(8,128)S(1)} %collective-permute-done.5.refs_1_, f32[1,120,128]{2,1,0:T(8,128)S(1)} %collective-permute-done.6.refs_2_, ...), custom_call_target="tpu_custom_call" | custom-call | flops 125829120 | bytes 491520 | tf_op jit(solution)/shard_map/end_flux/pallas_call | solution.py:632
  (11 shorter events, 0.0 us)
Async XLA Ops:
  0.6 2.8 %copy-start = (f32[4,480,256]{2,1,0:T(8,128)S(1)}, f32[4,480,256]{2,1,0:T(8,128)}, u32[]{:S(2)}) copy-start(f32[4,480,256]{2,1,0:T(8,128)} %pixels_ref.3) | copy-start | bytes 5898244
  2.9 5.2 %collective-permute-start.3 = (f32[2,240,256]{2,1,0:T(8,128)S(1)}, f32[2,240,256]{2,1,0:T(8,128)S(1)}, u32[]{:S(2)}, u32[]{:S(2)}) collective-permute-start(f32[2,240,256]{2,1,0:T(8,128)S(1)} %get-tuple-element.50), channel_id=1, source_target_pairs={{0,1},{1,0},{2,3},{3,2},{4,5},{5,4},{6,7},{7,6},{8,9},{9,8},{10,11... | collective-permute-start | bytes 1474568 | tf_op jit(solution)/shard_map/ppermute | solution.py:666
  4.6 7.1 %collective-permute-start = (f32[2,8,128]{2,1,0:T(8,128)S(1)}, f32[2,8,128]{2,1,0:T(8,128)S(1)}, u32[]{:S(2)}, u32[]{:S(2)}) collective-permute-start(f32[2,8,128]{2,1,0:T(8,128)S(1)} %get-tuple-element.40), channel_id=1, source_target_pairs={{0,2},{2,4},{4,6},{6,0},{1,3},{3,5},{5,7},{7,1},{8,10},{10,12},{12... | collective-permute-start | bytes 24584 | tf_op jit(solution)/shard_map/ppermute | solution.py:671
  7.2 4.6 %collective-permute-start.1 = (f32[2,8,128]{2,1,0:T(8,128)S(1)}, f32[2,8,128]{2,1,0:T(8,128)S(1)}, u32[]{:S(2)}, u32[]{:S(2)}) collective-permute-start(f32[2,8,128]{2,1,0:T(8,128)S(1)} %get-tuple-element.41), channel_id=1, source_target_pairs={{2,0},{4,2},{6,4},{0,6},{3,1},{5,3},{7,5},{1,7},{10,8},{12,10},{14... | collective-permute-start | bytes 24584 | tf_op jit(solution)/shard_map/ppermute | solution.py:672
  8.7 9.7 %collective-permute-start.4 = (f32[2,120,128]{2,1,0:T(8,128)S(1)}, f32[2,120,128]{2,1,0:T(8,128)S(1)}, u32[]{:S(2)}, u32[]{:S(2)}) collective-permute-start(f32[2,120,128]{2,1,0:T(8,128)S(1)} %get-tuple-element.53), channel_id=1, source_target_pairs={{0,16},{8,24},{16,0},{24,8},{1,17},{9,25},{17,1},{25,9},{2,18},{10... | collective-permute-start | bytes 368648 | tf_op jit(solution)/shard_map/ppermute | solution.py:541
  14.4 4.0 %collective-permute-start.2 = (f32[1,240,256]{2,1,0:T(8,128)S(1)}, f32[1,240,256]{2,1,0:T(8,128)S(1)}, u32[]{:S(2)}, u32[]{:S(2)}) collective-permute-start(f32[1,240,256]{2,1,0:T(8,128)S(1)} %get-tuple-element.45), channel_id=1, source_target_pairs={{0,1},{1,0},{2,3},{3,2},{4,5},{5,4},{6,7},{7,6},{8,9},{9,8},{10,11... | collective-permute-start | bytes 737288 | tf_op jit(solution)/shard_map/ppermute | solution.py:681
  15.2 9.6 %collective-permute-start.8 = (f32[2,120,128]{2,1,0:T(8,128)S(1)}, f32[2,120,128]{2,1,0:T(8,128)S(1)}, u32[]{:S(2)}, u32[]{:S(2)}) collective-permute-start(f32[2,120,128]{2,1,0:T(8,128)S(1)} %get-tuple-element.63), channel_id=1, source_target_pairs={{0,8},{8,0},{16,24},{24,16},{1,9},{9,1},{17,25},{25,17},{2,10},{10... | collective-permute-start | bytes 368648 | tf_op jit(solution)/shard_map/ppermute | solution.py:541
  16.8 8.4 %collective-permute-start.9 = (f32[2,120,128]{2,1,0:T(8,128)S(1)}, f32[2,120,128]{2,1,0:T(8,128)S(1)}, u32[]{:S(2)}, u32[]{:S(2)}) collective-permute-start(f32[2,120,128]{2,1,0:T(8,128)S(1)} %get-tuple-element.64), channel_id=1, source_target_pairs={{0,24},{8,16},{16,8},{24,0},{1,25},{9,17},{17,9},{25,1},{2,26},{10... | collective-permute-start | bytes 368648 | tf_op jit(solution)/shard_map/ppermute | solution.py:541
  18.7 10.2 %collective-permute-start.5 = (f32[1,120,128]{2,1,0:T(8,128)S(1)}, f32[1,120,128]{2,1,0:T(8,128)S(1)}, u32[]{:S(2)}, u32[]{:S(2)}) collective-permute-start(f32[1,120,128]{2,1,0:T(8,128)S(1)} %get-tuple-element.59), channel_id=1, source_target_pairs={{0,16},{8,24},{16,0},{24,8},{1,17},{9,25},{17,1},{25,9},{2,18},{10... | collective-permute-start | bytes 184328 | tf_op jit(solution)/shard_map/ppermute | solution.py:541
  19.2 9.8 %collective-permute-start.6 = (f32[1,120,128]{2,1,0:T(8,128)S(1)}, f32[1,120,128]{2,1,0:T(8,128)S(1)}, u32[]{:S(2)}, u32[]{:S(2)}) collective-permute-start(f32[1,120,128]{2,1,0:T(8,128)S(1)} %get-tuple-element.60), channel_id=1, source_target_pairs={{0,8},{8,0},{16,24},{24,16},{1,9},{9,1},{17,25},{25,17},{2,10},{10... | collective-permute-start | bytes 184328 | tf_op jit(solution)/shard_map/ppermute | solution.py:541
  22.4 6.6 %collective-permute-start.7 = (f32[1,120,128]{2,1,0:T(8,128)S(1)}, f32[1,120,128]{2,1,0:T(8,128)S(1)}, u32[]{:S(2)}, u32[]{:S(2)}) collective-permute-start(f32[1,120,128]{2,1,0:T(8,128)S(1)} %get-tuple-element.61), channel_id=1, source_target_pairs={{0,24},{8,16},{16,8},{24,0},{1,25},{9,17},{17,9},{25,1},{2,26},{10... | collective-permute-start | bytes 184328 | tf_op jit(solution)/shard_map/ppermute | solution.py:541

commit v16 on v15

--- a/solution.py
+++ b/solution.py
@@ -628,7 +628,7 @@
 
 def end_flux(table, pieces, pack, fibres):
     rows = pieces[0].shape[1] * pack
-    order = sorted(range(len(pieces)), key=lambda d: (d > 0, abs(2 * d - len(pieces))))
+    order = [0] + sorted(range(1, len(pieces)), key=lambda d: (d < len(pieces) // 2, d))
     return pl.pallas_call(
         functools.partial(flux_end_kernel, pack, order),
         in_specs=[in_vmem] * (1 + len(pieces)),
@@ -676,7 +676,7 @@
     pixel_s, ivar_s = stream_layout(left[0] + right[0], pixels, ivar)
     theirs, solved = flux_sums(wav_count, place, coupling, left, right, pixel_s, ivar_s, weight_t)
     early = [0, fib_count // 2] if rel else [0]
-    late = [d for d in range(pieces) if d not in early]
+    late = [d for d in reversed(range(pieces)) if d not in early]
     ahead = weight_pieces[early[-1]][0, :ROWS, :] * 0.5
     arriving = lax.ppermute(theirs, "exp", swap)
     mine = kept_flux(after(place, theirs), coupling, solved, weight_m)

time: 30.1 us -> 30.6 us (1.017)
  waiting for transfers between devices: 2.35 us -> 3.3 us
  starting transfers between devices: 14.9 us -> 14.4 us
    ppermute x6, waiting for transfers between devices: 2.34 us -> 3.28 us  [exchange(): lax.ppermute(pieces[d], 'fib', [(i, i ^ d) for i in range(fib_count)])]
    ppermute x6, starting transfers between devices: 10.7 us -> 10.2 us  [exchange(): lax.ppermute(pieces[d], 'fib', [(i, i ^ d) for i in range(fib_count)])]
  transfers between devices with their start and end apart: 10 -> 10, of which waited for: 2 -> 3; matrix products, arithmetic and copies ran while one was open for 0% -> 0% of each run, Pallas kernels for 29% -> 28%
where the time goes in v16:
time: 30.6 us; the launch traced here: 30.5 us
  starting transfers between devices  14.4 us (47%)
  Pallas kernels  11.9 us (39%)
  waiting for transfers between devices  3.3 us (11%)
  between operations  0.73 us (2%)
    ppermute x6, starting transfers between devices, exchange(): lax.ppermute(pieces[d], 'fib', [(i, i ^ d) for i in range(fib_count)])  10.2 us
    ppermute x6, waiting for transfers between devices, exchange(): lax.ppermute(pieces[d], 'fib', [(i, i ^ d) for i in range(fib_count)])  3.28 us
    ppermute x1, starting transfers between devices, per_device(): left = lax.ppermute(up, 'wav', upward)  2.56 us
    pallas_call x1, Pallas kernels, flux_sums(): pl.pallas_call(functools.partial(solve_kernel, wav_count), in_specs=[in_s...  2.34 us
    pallas_call x1, Pallas kernels, sent_weights(): pl.pallas_call(functools.partial(sent_kernel, moves, wav_count), in_specs...  2.22 us
    pallas_call x1, Pallas kernels, end_weights(): pl.pallas_call(functools.partial(weights_end_kernel, pack, total, late, l...  1.78 us
    pallas_call x1, Pallas kernels, place_early(): pl.pallas_call(functools.partial(early_kernel, moves, which, len(weight_p...  1.62 us
    pallas_call x1, Pallas kernels, kept_weights(): pl.pallas_call(functools.partial(kept_kernel, wav_count), in_specs=[in_sm...  1.14 us
  transfers between devices with their start and end apart: 10, of which 3 were waited for; matrix products, arithmetic and copies ran while one was open for 0% of the time, Pallas kernels for 28%

profile of v16, /device:TPU:0, one launch (start us, length us, event | category | flops | bytes accessed | tf_op | source)
XLA Modules:
  0.0 30.5 jit_solution(5330100640302169748)
XLA Ops:
  0.6 0.1 pad_add_fusion.place_ref
  0.7 2.2 %sent_weights.1 = (f32[2,240,256]{2,1,0:T(8,128)S(1)}, f32[4,240,256]{2,1,0:T(8,128)S(1)}, bf16[512,512]{1,0:T(8,128)(2,1)S(1)}, s32[1,1024]{1,0:T(1,128)S(1)}, ...) custom-call(s32[3]{0:T(128)S(1)} %pad_add_fusion.place_ref, ...), custom_call_target="tpu_custom_call" | custom-call | flops 9830400 | bytes 2949120 | tf_op jit(solution)/shard_map/sent_weights/pallas_call | solution.py:259
  2.9 0.5 %collective-permute-start.3 = (f32[2,240,256]{2,1,0:T(8,128)S(1)}, f32[2,240,256]{2,1,0:T(8,128)S(1)}, u32[]{:S(2)}, u32[]{:S(2)}) collective-permute-start(f32[2,240,256]{2,1,0:T(8,128)S(1)} %get-tuple-element.50), channel_id=1, source_target_pairs={{0,1},{1,0},{2,3},{3,2},{4,5},{5,4},{6,7},{7,6},{8,9},{9,8},{10,11... | collective-permute-start | bytes 1474568 | tf_op jit(solution)/shard_map/ppermute | solution.py:666
  3.5 1.1 %kept_weights.1 = (f32[2,240,256]{2,1,0:T(8,128)S(1)}, f32[4,240,256]{2,1,0:T(8,128)S(1)}, f32[2,8,128]{2,1,0:T(8,128)S(1)}, f32[2,8,128]{2,1,0:T(8,128)S(1)}) custom-call(s32[3]{0:T(128)S(1)} %pad_add_fusion.place_ref, f32[1,256]{1,0:T(1,128)S(1)} %get-tuple-element.35.coupling_ref, s32[1,256]{1,0:T(1,128)S(1)} %get-tuple-element.36.counts_ref, ...), custom_call_target="tpu_custom_call" | custom-call | flops 9830400 | bytes 2949120 | tf_op jit(solution)/shard_map/kept_weights/pallas_call | solution.py:332
  4.6 2.6 %collective-permute-start = (f32[2,8,128]{2,1,0:T(8,128)S(1)}, f32[2,8,128]{2,1,0:T(8,128)S(1)}, u32[]{:S(2)}, u32[]{:S(2)}) collective-permute-start(f32[2,8,128]{2,1,0:T(8,128)S(1)} %get-tuple-element.40), channel_id=1, source_target_pairs={{0,2},{2,4},{4,6},{6,0},{1,3},{3,5},{5,7},{7,1},{8,10},{10,12},{12... | collective-permute-start | bytes 24584 | tf_op jit(solution)/shard_map/ppermute | solution.py:671
  7.2 1.0 %collective-permute-start.1 = (f32[2,8,128]{2,1,0:T(8,128)S(1)}, f32[2,8,128]{2,1,0:T(8,128)S(1)}, u32[]{:S(2)}, u32[]{:S(2)}) collective-permute-start(f32[2,8,128]{2,1,0:T(8,128)S(1)} %get-tuple-element.41), channel_id=1, source_target_pairs={{2,0},{4,2},{6,4},{0,6},{3,1},{5,3},{7,5},{1,7},{10,8},{12,10},{14... | collective-permute-start | bytes 24584 | tf_op jit(solution)/shard_map/ppermute | solution.py:672
  8.2 0.5 %sort_weights.1 = (f32[2,120,128]{2,1,0:T(8,128)S(1)}, f32[2,120,128]{2,1,0:T(8,128)S(1)}, f32[2,120,128]{2,1,0:T(8,128)S(1)}, f32[2,120,128]{2,1,0:T(8,128)S(1)}, f32[240,256]{1,0:T(8,128)S(1)}) custom-call(f32[2,240,256]{2,1,0:T(8,128)S(1)} %collective-permute-done.3.theirs_ref, f32[2,240,256]{2,1,0:T(8,128)S(1)} %get-tuple-element.51.mine_ref, ...), custom_call_target="tpu_custom_call" | custom-call | tf_op jit(solution)/shard_map/sort_weights/pallas_call | solution.py:527
  8.7 3.1 %collective-permute-start.4 = (f32[2,120,128]{2,1,0:T(8,128)S(1)}, f32[2,120,128]{2,1,0:T(8,128)S(1)}, u32[]{:S(2)}, u32[]{:S(2)}) collective-permute-start(f32[2,120,128]{2,1,0:T(8,128)S(1)} %get-tuple-element.53), channel_id=1, source_target_pairs={{0,16},{8,24},{16,0},{24,8},{1,17},{9,25},{17,1},{25,9},{2,18},{10... | collective-permute-start | bytes 368648 | tf_op jit(solution)/shard_map/ppermute | solution.py:541
  11.7 0.0 collective-permute-done.left_ref
  11.7 0.0 collective-permute-done.1.right_ref
  11.8 0.3 stream_layout.1
  12.0 2.3 %flux_sums.1 = (f32[1,240,256]{2,1,0:T(8,128)S(1)}, f32[3848,128]{1,0:T(8,128)S(1)}) custom-call(s32[3]{0:T(128)S(1)} %pad_add_fusion.place_ref, f32[1,256]{1,0:T(1,128)S(1)} %get-tuple-element.35.coupling_ref, f32[2,8,128]{2,1,0:T(8,128)S(1)} %collective-permute-done.left_ref, f32[2,8,128]{2,1,0:T(8,128)S(1)} %collective-permute-done.1.right_ref, ...), custom_call_target="tpu_custom_call" | custom-call | tf_op jit(solution)/shard_map/flux_sums/pallas_call | solution.py:463
  14.4 0.1 collective-permute-start.2
  14.4 0.7 %kept_flux.1.mine_ref = f32[1,240,256]{2,1,0:T(8,128)S(1)} custom-call(s32[3]{0:T(128)S(1)} %pad_add_fusion.place_ref, f32[1,256]{1,0:T(1,128)S(1)} %get-tuple-element.35.coupling_ref, f32[3848,128]{1,0:T(8,128)S(1)} %get-tuple-element.47.solved_ref, f32[4,240,256]{2,1,0:T(8,128)S(1)} %get-tuple-element.48.weight_ref), custom_call_target="tpu_custom_call" | custom-call | flops 491520 | bytes 1966080 | tf_op jit(solution)/shard_map/kept_flux/pallas_call | solution.py:481
  15.2 2.7 %collective-permute-start.8 = (f32[2,120,128]{2,1,0:T(8,128)S(1)}, f32[2,120,128]{2,1,0:T(8,128)S(1)}, u32[]{:S(2)}, u32[]{:S(2)}) collective-permute-start(f32[2,120,128]{2,1,0:T(8,128)S(1)} %get-tuple-element.63), channel_id=1, source_target_pairs={{0,24},{8,16},{16,8},{24,0},{1,25},{9,17},{17,9},{25,1},{2,26},{10... | collective-permute-start | bytes 368648 | tf_op jit(solution)/shard_map/ppermute | solution.py:541
  17.9 0.3 %sort_flux.1 = (f32[1,120,128]{2,1,0:T(8,128)S(1)}, f32[1,120,128]{2,1,0:T(8,128)S(1)}, f32[1,120,128]{2,1,0:T(8,128)S(1)}, f32[1,120,128]{2,1,0:T(8,128)S(1)}) custom-call(f32[1,240,256]{2,1,0:T(8,128)S(1)} %collective-permute-done.2.theirs_ref, f32[1,240,256]{2,1,0:T(8,128)S(1)} %kept_flux.1.mine_ref, bf16[512,512]{1,0:T(8,128)(2,1)S(1)} %get-tuple-element.49.table_ref, ...), custom_call_target="tpu_custom_call" | custom-call | tf_op jit(solution)/shard_map/sort_flux/pallas_call | solution.py:527
  18.3 1.8 %collective-permute-start.5 = (f32[1,120,128]{2,1,0:T(8,128)S(1)}, f32[1,120,128]{2,1,0:T(8,128)S(1)}, u32[]{:S(2)}, u32[]{:S(2)}) collective-permute-start(f32[1,120,128]{2,1,0:T(8,128)S(1)} %get-tuple-element.59), channel_id=1, source_target_pairs={{0,16},{8,24},{16,0},{24,8},{1,17},{9,25},{17,1},{25,9},{2,18},{10... | collective-permute-start | bytes 184328 | tf_op jit(solution)/shard_map/ppermute | solution.py:541
  20.1 2.7 %collective-permute-start.6 = (f32[1,120,128]{2,1,0:T(8,128)S(1)}, f32[1,120,128]{2,1,0:T(8,128)S(1)}, u32[]{:S(2)}, u32[]{:S(2)}) collective-permute-start(f32[1,120,128]{2,1,0:T(8,128)S(1)} %get-tuple-element.60), channel_id=1, source_target_pairs={{0,24},{8,16},{16,8},{24,0},{1,25},{9,17},{17,9},{25,1},{2,26},{10... | collective-permute-start | bytes 184328 | tf_op jit(solution)/shard_map/ppermute | solution.py:541
  22.7 1.6 %place_early.1 = (bf16[512,512]{1,0:T(8,128)(2,1)S(1)}, f32[2,120,512]{2,1,0:T(8,128)S(1)}) custom-call(s32[3]{0:T(128)S(1)} %pad_add_fusion.place_ref, s32[1,1024]{1,0:T(1,128)S(1)} %get-tuple-element.56.slots_ref, f32[2,120,128]{2,1,0:T(8,128)S(1)} %get-tuple-element.57.refs_0_, f32[2,120,128]{2,1,0:T(8,128)S(1)} %collective-permute-done.4.refs_1_), custom_call_target="tpu_custom_call" | custom-call | tf_op jit(solution)/shard_map/place_early/pallas_call | solution.py:570
  24.4 2.1 %collective-permute-done.9.refs_1_ = f32[2,120,128]{2,1,0:T(8,128)S(1)} collective-permute-done((f32[2,120,128]{2,1,0:T(8,128)S(1)}, f32[2,120,128]{2,1,0:T(8,128)S(1)}, u32[]{:S(2)}, u32[]{:S(2)}) %collective-permute-start.9) | collective-permute-done | bytes 122912 | tf_op jit(solution)/shard_map/ppermute | solution.py:541
  26.5 1.8 %end_weights.1 = (f32[240,256]{1,0:T(8,128)}, f32[3,240,256]{2,1,0:T(8,128)}) custom-call(s32[3]{0:T(128)S(1)} %pad_add_fusion.place_ref, bf16[512,512]{1,0:T(8,128)(2,1)S(1)} %get-tuple-element.58.table_ref, f32[2,120,512]{2,1,0:T(8,128)S(1)} %get-tuple-element.62.sums_ref, f32[2,120,128]{2,1,0:T(8,128)S(1)} %collective-permute-done.8.refs_0_, ...), custom_call_target="tpu_custom_call" | custom-call | tf_op jit(solution)/shard_map/end_weights/pallas_call | solution.py:609
  28.3 0.7 %collective-permute-done.5.refs_1_ = f32[1,120,128]{2,1,0:T(8,128)S(1)} collective-permute-done((f32[1,120,128]{2,1,0:T(8,128)S(1)}, f32[1,120,128]{2,1,0:T(8,128)S(1)}, u32[]{:S(2)}, u32[]{:S(2)}) %collective-permute-start.5) | collective-permute-done | bytes 61472 | tf_op jit(solution)/shard_map/ppermute | solution.py:541
  29.0 0.5 %collective-permute-done.7.refs_3_ = f32[1,120,128]{2,1,0:T(8,128)S(1)} collective-permute-done((f32[1,120,128]{2,1,0:T(8,128)S(1)}, f32[1,120,128]{2,1,0:T(8,128)S(1)}, u32[]{:S(2)}, u32[]{:S(2)}) %collective-permute-start.7) | collective-permute-done | bytes 61472 | tf_op jit(solution)/shard_map/ppermute | solution.py:541
  29.4 1.0 %end_flux.1 = f32[240,256]{1,0:T(8,128)} custom-call(bf16[512,512]{1,0:T(8,128)(2,1)S(1)} %get-tuple-element.58.table_ref, f32[1,120,128]{2,1,0:T(8,128)S(1)} %get-tuple-element.54.refs_0_, f32[1,120,128]{2,1,0:T(8,128)S(1)} %collective-permute-done.5.refs_1_, f32[1,120,128]{2,1,0:T(8,128)S(1)} %collective-permute-done.6.refs_2_, ...), custom_call_target="tpu_custom_call" | custom-call | flops 125829120 | bytes 491520 | tf_op jit(solution)/shard_map/end_flux/pallas_call | solution.py:632
  (11 shorter events, 0.0 us)
Async XLA Ops:
  0.6 2.8 %copy-start = (f32[4,480,256]{2,1,0:T(8,128)S(1)}, f32[4,480,256]{2,1,0:T(8,128)}, u32[]{:S(2)}) copy-start(f32[4,480,256]{2,1,0:T(8,128)} %pixels_ref.3) | copy-start | bytes 5898244
  2.9 5.2 %collective-permute-start.3 = (f32[2,240,256]{2,1,0:T(8,128)S(1)}, f32[2,240,256]{2,1,0:T(8,128)S(1)}, u32[]{:S(2)}, u32[]{:S(2)}) collective-permute-start(f32[2,240,256]{2,1,0:T(8,128)S(1)} %get-tuple-element.50), channel_id=1, source_target_pairs={{0,1},{1,0},{2,3},{3,2},{4,5},{5,4},{6,7},{7,6},{8,9},{9,8},{10,11... | collective-permute-start | bytes 1474568 | tf_op jit(solution)/shard_map/ppermute | solution.py:666
  4.6 7.1 %collective-permute-start = (f32[2,8,128]{2,1,0:T(8,128)S(1)}, f32[2,8,128]{2,1,0:T(8,128)S(1)}, u32[]{:S(2)}, u32[]{:S(2)}) collective-permute-start(f32[2,8,128]{2,1,0:T(8,128)S(1)} %get-tuple-element.40), channel_id=1, source_target_pairs={{0,2},{2,4},{4,6},{6,0},{1,3},{3,5},{5,7},{7,1},{8,10},{10,12},{12... | collective-permute-start | bytes 24584 | tf_op jit(solution)/shard_map/ppermute | solution.py:671
  7.2 4.6 %collective-permute-start.1 = (f32[2,8,128]{2,1,0:T(8,128)S(1)}, f32[2,8,128]{2,1,0:T(8,128)S(1)}, u32[]{:S(2)}, u32[]{:S(2)}) collective-permute-start(f32[2,8,128]{2,1,0:T(8,128)S(1)} %get-tuple-element.41), channel_id=1, source_target_pairs={{2,0},{4,2},{6,4},{0,6},{3,1},{5,3},{7,5},{1,7},{10,8},{12,10},{14... | collective-permute-start | bytes 24584 | tf_op jit(solution)/shard_map/ppermute | solution.py:672
  8.7 9.2 %collective-permute-start.4 = (f32[2,120,128]{2,1,0:T(8,128)S(1)}, f32[2,120,128]{2,1,0:T(8,128)S(1)}, u32[]{:S(2)}, u32[]{:S(2)}) collective-permute-start(f32[2,120,128]{2,1,0:T(8,128)S(1)} %get-tuple-element.53), channel_id=1, source_target_pairs={{0,16},{8,24},{16,0},{24,8},{1,17},{9,25},{17,1},{25,9},{2,18},{10... | collective-permute-start | bytes 368648 | tf_op jit(solution)/shard_map/ppermute | solution.py:541
  14.4 3.6 %collective-permute-start.2 = (f32[1,240,256]{2,1,0:T(8,128)S(1)}, f32[1,240,256]{2,1,0:T(8,128)S(1)}, u32[]{:S(2)}, u32[]{:S(2)}) collective-permute-start(f32[1,240,256]{2,1,0:T(8,128)S(1)} %get-tuple-element.45), channel_id=1, source_target_pairs={{0,1},{1,0},{2,3},{3,2},{4,5},{5,4},{6,7},{7,6},{8,9},{9,8},{10,11... | collective-permute-start | bytes 737288 | tf_op jit(solution)/shard_map/ppermute | solution.py:681
  15.2 9.2 %collective-permute-start.8 = (f32[2,120,128]{2,1,0:T(8,128)S(1)}, f32[2,120,128]{2,1,0:T(8,128)S(1)}, u32[]{:S(2)}, u32[]{:S(2)}) collective-permute-start(f32[2,120,128]{2,1,0:T(8,128)S(1)} %get-tuple-element.63), channel_id=1, source_target_pairs={{0,24},{8,16},{16,8},{24,0},{1,25},{9,17},{17,9},{25,1},{2,26},{10... | collective-permute-start | bytes 368648 | tf_op jit(solution)/shard_map/ppermute | solution.py:541
  17.9 8.6 %collective-permute-start.9 = (f32[2,120,128]{2,1,0:T(8,128)S(1)}, f32[2,120,128]{2,1,0:T(8,128)S(1)}, u32[]{:S(2)}, u32[]{:S(2)}) collective-permute-start(f32[2,120,128]{2,1,0:T(8,128)S(1)} %get-tuple-element.64), channel_id=1, source_target_pairs={{0,8},{8,0},{16,24},{24,16},{1,9},{9,1},{17,25},{25,17},{2,10},{10... | collective-permute-start | bytes 368648 | tf_op jit(solution)/shard_map/ppermute | solution.py:541
  18.3 10.7 %collective-permute-start.5 = (f32[1,120,128]{2,1,0:T(8,128)S(1)}, f32[1,120,128]{2,1,0:T(8,128)S(1)}, u32[]{:S(2)}, u32[]{:S(2)}) collective-permute-start(f32[1,120,128]{2,1,0:T(8,128)S(1)} %get-tuple-element.59), channel_id=1, source_target_pairs={{0,16},{8,24},{16,0},{24,8},{1,17},{9,25},{17,1},{25,9},{2,18},{10... | collective-permute-start | bytes 184328 | tf_op jit(solution)/shard_map/ppermute | solution.py:541
  20.1 8.9 %collective-permute-start.6 = (f32[1,120,128]{2,1,0:T(8,128)S(1)}, f32[1,120,128]{2,1,0:T(8,128)S(1)}, u32[]{:S(2)}, u32[]{:S(2)}) collective-permute-start(f32[1,120,128]{2,1,0:T(8,128)S(1)} %get-tuple-element.60), channel_id=1, source_target_pairs={{0,24},{8,16},{16,8},{24,0},{1,25},{9,17},{17,9},{25,1},{2,26},{10... | collective-permute-start | bytes 184328 | tf_op jit(solution)/shard_map/ppermute | solution.py:541
  22.7 6.7 %collective-permute-start.7 = (f32[1,120,128]{2,1,0:T(8,128)S(1)}, f32[1,120,128]{2,1,0:T(8,128)S(1)}, u32[]{:S(2)}, u32[]{:S(2)}) collective-permute-start(f32[1,120,128]{2,1,0:T(8,128)S(1)} %get-tuple-element.61), channel_id=1, source_target_pairs={{0,8},{8,0},{16,24},{24,16},{1,9},{9,1},{17,25},{25,17},{2,10},{10... | collective-permute-start | bytes 184328 | tf_op jit(solution)/shard_map/ppermute | solution.py:541

commit v17 on v8

--- a/solution.py
+++ b/solution.py
@@ -112,53 +112,38 @@
     return (row < col).astype(F32).astype(BF16)
 
 
-def write_send_table(fib_count, pack, per, rel, me, slots_ref, table_ref):
-    fibres = table_ref.shape[1] // pack
-    lanes = pack * per
+def write_send_table(fib_count, per, rel, me, slots_ref, table_ref):
+    fibres = table_ref.shape[1]
     owner, _ = owners(slots_ref, fib_count, fibres)
     source = lax.broadcasted_iota(jnp.int32, owner.shape, 0)
     my_owner = jnp.sum(jnp.where(source == me, owner, 0.0), axis=0, keepdims=True).astype(jnp.int32)
     to_owner = (source == my_owner).astype(F32)
     counted = jnp.dot(to_owner.astype(BF16), earlier_fibres(fibres), preferred_element_type=F32)
     rank = jnp.sum(to_owner * counted, axis=0, keepdims=True).astype(jnp.int32)
-    target = my_owner
-    if rel:
-        target = jnp.where(my_owner >= me, my_owner - me, my_owner - me + fib_count)
-    base = target * lanes + rank
-    place_of = jnp.concatenate([base + h * per for h in range(pack)], 1)
+    target = my_owner ^ me if rel else my_owner
     row = lax.broadcasted_iota(jnp.int32, table_ref.shape, 0)
-    table_ref[...] = (row == place_of).astype(F32).astype(BF16)
-
-
-def write_recv_table(fib_count, pack, per, rel, me, slots_ref, table_ref):
-    fibres = table_ref.shape[0] // pack
-    lanes = pack * per
-    total_lanes = fib_count * lanes
+    table_ref[...] = (row == target * per + rank).astype(F32).astype(BF16)
+
+
+def write_recv_table(fib_count, per, rel, me, slots_ref, table_ref):
+    fibres = table_ref.shape[0]
+    total_lanes = fib_count * per
     owner, column = owners(slots_ref, fib_count, fibres)
     source = lax.broadcasted_iota(jnp.int32, owner.shape, 0)
     mine = (owner == me.astype(F32)).astype(F32)
     rank_in = jnp.dot(mine.astype(BF16), earlier_fibres(fibres), preferred_element_type=F32).astype(jnp.int32)
-    order = source
-    if rel:
-        order = jnp.where(me >= source, me - source, me - source + fib_count)
-    arrival = jnp.where(mine > 0.0, order * lanes + rank_in, -total_lanes)
+    order = source ^ me if rel else source
+    arrival = jnp.where(mine > 0.0, order * per + rank_in, -1)
     tall = lax.broadcasted_iota(jnp.int32, (total_lanes, fibres), 0)
     landing = jnp.zeros((ROWS, total_lanes), F32)
     for s in range(fib_count):
         hit = tall == arrival[s : s + 1, :]
-        for h in range(1, pack):
-            hit = hit | (tall == arrival[s : s + 1, :] + h * per)
         values = jnp.broadcast_to(column[s : s + 1, :], (ROWS, fibres)).astype(BF16)
         landing = landing + lax.dot_general(
             values, hit.astype(F32).astype(BF16), NT, preferred_element_type=F32
         )
-    lane = lax.broadcasted_iota(jnp.int32, (1, total_lanes), 1)
-    landing = landing[0:1, :].astype(jnp.int32)
-    for h in range(1, pack):
-        inside = (lane % lanes >= h * per) & (lane % lanes < (h + 1) * per)
-        landing = jnp.where(inside, landing + h * fibres, landing)
     row = lax.broadcasted_iota(jnp.int32, table_ref.shape, 0)
-    table_ref[...] = (row == landing).astype(F32).astype(BF16)
+    table_ref[...] = (row == landing[0:1, :].astype(jnp.int32)).astype(F32).astype(BF16)
 
 
 def stream_coupling(coupling_ref, expos):
@@ -258,7 +243,7 @@
 def sent_weights(moves, wav_count, place, slots, coupling, counts, good, bits, ivar):
     expos, width, fibres = ivar.shape
     half = width // 2
-    fib_count, pack, per, _ = moves
+    fib_count, per, _ = moves
     inputs = (slots, coupling, counts, good, bits, ivar)
     return pl.pallas_call(
         functools.partial(sent_kernel, moves, wav_count),
@@ -267,7 +252,7 @@
         out_shape=[
             shaped((2, half, fibres)),
             shaped((expos, half, fibres)),
-            shaped((fib_count * pack * per, pack * fibres), BF16),
+            shaped((fib_count * per, fibres), BF16),
         ]
         + [shaped(x.shape, x.dtype) for x in inputs],
         scratch_shapes=[pltpu.SemaphoreType.DMA((5 + width // GROUP,))],
@@ -366,23 +351,6 @@
     )(arrived, pixels, ivar)
 
 
-def recv_kernel(moves, place_ref, slots_ref, table_ref):
-    write_recv_table(*moves, place_ref[0], slots_ref, table_ref)
-
-
-def recv_moves(moves, place, slots, fibres):
-    fib_count, pack, per, _ = moves
-    return pl.pallas_call(
-        functools.partial(recv_kernel, moves),
-        in_specs=[in_smem, in_vmem],
-        out_specs=in_vmem,
-        out_shape=shaped((pack * fibres, fib_count * pack * per), BF16),
-        compiler_params=params(),
-        cost_estimate=cost(1e6, 1e6),
-        name="recv_moves",
-    )(place, slots)
-
-
 def solve_kernel(
     wav_count, place_ref, coupling_ref, left_ref, right_ref, pixel_ref, ivar_ref, weight_ref,
     theirs_ref, solved_s, lead_s, rest_s,
@@ -529,19 +497,30 @@
         scale = 1.0 / jnp.maximum(totals[0], 1.0)
         scale_ref[...] = scale
         totals[1] = totals[1] * scale
-    x = jnp.concatenate(
-        [jnp.concatenate([t[h * part : (h + 1) * part] for h in range(pack)], 1) for t in totals], 0
-    )
-    moved = split_dot(x, table_ref[...], NT)
-    lanes = moved.shape[1] // len(out_refs)
-    for d, out_ref in enumerate(out_refs):
-        for v in range(values):
-            out_ref[v] = moved[v * part : (v + 1) * part, d * lanes : (d + 1) * lanes]
+    moved = split_dot(jnp.concatenate(totals, 0), table_ref[...], NT)
+    lanes = out_refs[0].shape[2]
+    for v in range(values):
+        halves = [moved[v * rows + h * part : v * rows + (h + 1) * part] for h in range(pack)]
+        for d, out_ref in enumerate(out_refs):
+            out_ref[v] = side_by_side(halves, d, lanes)
+
+
+def side_by_side(halves, d, lanes):
+    if len(halves) == 1:
+        return halves[0][:, d * lanes : (d + 1) * lanes]
+    at = slice(d // 2 * lanes, (d // 2 + 1) * lanes)
+    first, second = halves[0][:, at], halves[1][:, at]
+    if d % 2:
+        first = pltpu.roll(first, lanes // 2, 1)
+    else:
+        second = pltpu.roll(second, lanes // 2, 1)
+    lane = lax.broadcasted_iota(jnp.int32, first.shape, 1)
+    return jnp.where(lane < lanes // 2, first, second)
 
 
 def sort_fibres(theirs, mine, table, pack, pieces, scale=None, ahead=None):
     values, rows, fibres = mine.shape
-    lanes = table.shape[0] // pieces
+    lanes = table.shape[0] * pack // pieces
     scaled = scale is not None
     outs = [shaped((values, rows // pack, lanes))] * pieces + ([] if scaled else [shaped((rows, fibres))])
     args = (theirs, mine, table) + ((scale, ahead) if scaled else ())
@@ -559,38 +538,55 @@
 def exchange(pieces, fib_count):
     if len(pieces) == 1:
         return [lax.all_to_all(pieces[0], "fib", split_axis=2, concat_axis=2, tiled=True)]
-    arrived = [pieces[0]]
-    for d in range(1, fib_count):
-        arrived.append(lax.ppermute(pieces[d], "fib", [(i, (i + d) % fib_count) for i in range(fib_count)]))
-    return arrived
-
-
-def landed(refs, table):
-    values, part, _ = refs[0].shape
-    x = jnp.concatenate(
-        [jnp.concatenate([ref[v] for ref in refs], 1) if len(refs) > 1 else refs[0][v] for v in range(values)], 0
-    )
-    moved = split_dot(x, table, NT)
-    return [moved[v * part : (v + 1) * part] for v in range(values)]
+    swapped = [lax.ppermute(pieces[d], "fib", [(i, i ^ d) for i in range(fib_count)]) for d in range(1, fib_count)]
+    return [pieces[0]] + swapped
+
+
+def landed(pieces, table, pack):
+    values, part, lanes = pieces[0].shape
+    parts = []
+    for v in range(values):
+        blocks = [piece[v] for piece in pieces]
+        if pack == 1:
+            parts.append(jnp.concatenate(blocks, 1) if len(blocks) > 1 else blocks[0])
+        else:
+            for h in range(2):
+                pairs = range(0, len(blocks), 2)
+                parts.append(jnp.concatenate([side_by_side(blocks[d : d + 2], h, lanes) for d in pairs], 1))
+    moved = split_dot(jnp.concatenate(parts, 0), table, NT)
+    rows = part * pack
+    return [moved[v * rows : (v + 1) * rows] for v in range(values)]
+
+
+def recv_kernel(moves, place_ref, slots_ref, table_ref):
+    write_recv_table(*moves, place_ref[0], slots_ref, table_ref)
+
+
+def recv_moves(moves, place, slots, fibres):
+    fib_count, per, _ = moves
+    return pl.pallas_call(
+        functools.partial(recv_kernel, moves),
+        in_specs=[in_smem, in_vmem],
+        out_specs=in_vmem,
+        out_shape=shaped((fibres, fib_count * per), BF16),
+        compiler_params=params(),
+        cost_estimate=cost(1e6, 1e6),
+        name="recv_moves",
+    )(place, slots)
 
 
 def weights_end_kernel(pack, total, place_ref, table_ref, *refs):
     *piece_refs, ivar_ref, res_ref = refs
-    weight, band = landed(piece_refs, table_ref[...])
-    rows, fibres = ivar_ref.shape
-    part = rows // pack
+    weight, band = landed(piece_refs, table_ref[...], pack)
+    rows = weight.shape[0]
     start = (place_ref[1] * 2 + place_ref[2]) * rows
-    for h in range(pack):
-        at = slice(h * part, (h + 1) * part)
-        cut = slice(h * fibres, (h + 1) * fibres)
-        row = start + h * part + lax.broadcasted_iota(jnp.int32, (part, 1), 0)
-        w, b = weight[:, cut], band[:, cut]
-        before = jnp.where(row == 0, 0.0, b)
-        after = jnp.where(row == total - 1, 0.0, b)
-        ivar_ref[at, :] = w
-        res_ref[0, at, :] = before
-        res_ref[1, at, :] = jnp.minimum(w, 1.0) - before - after
-        res_ref[2, at, :] = after
+    row = start + lax.broadcasted_iota(jnp.int32, (rows, 1), 0)
+    before = jnp.where(row == 0, 0.0, band)
+    after = jnp.where(row == total - 1, 0.0, band)
+    ivar_ref[...] = weight
+    res_ref[0] = before
+    res_ref[1] = jnp.minimum(weight, 1.0) - before - after
+    res_ref[2] = after
 
 
 def end_weights(place, table, pieces, pack, fibres, total):
@@ -601,31 +597,28 @@
         out_specs=[in_vmem] * 2,
         out_shape=[shaped((rows, fibres)), shaped((3, rows, fibres))],
         compiler_params=params(),
-        cost_estimate=cost(4 * rows * table.size, 6 * rows * fibres * 4),
+        cost_estimate=cost(0, 0),
         name="end_weights",
     )(place, table, *pieces)
 
 
-def flux_end_kernel(pack, table_ref, *refs):
+def flux_end_kernel(pack, order, table_ref, *refs):
     *piece_refs, flux_ref = refs
-    (flux,) = landed(piece_refs, table_ref[...])
-    rows, fibres = flux_ref.shape
-    part = rows // pack
-    for h in range(pack):
-        flux_ref[h * part : (h + 1) * part, :] = flux[:, h * fibres : (h + 1) * fibres]
+    (flux_ref[...],) = landed([piece_refs[order.index(d)] for d in range(len(order))], table_ref[...], pack)
 
 
 def end_flux(table, pieces, pack, fibres):
     rows = pieces[0].shape[1] * pack
-    return pl.pallas_call(
-        functools.partial(flux_end_kernel, pack),
+    order = sorted(range(len(pieces)), key=lambda d: (d > 0, abs(2 * d - len(pieces))))
+    return pl.pallas_call(
+        functools.partial(flux_end_kernel, pack, order),
         in_specs=[in_vmem] * (1 + len(pieces)),
         out_specs=in_vmem,
         out_shape=shaped((rows, fibres)),
         compiler_params=params(),
         cost_estimate=cost(2 * rows * table.size, 2 * rows * fibres * 4),
         name="end_flux",
-    )(table, *pieces)
+    )(table, *(pieces[d] for d in order))
 
 
 def after(value, done):
@@ -638,15 +631,15 @@
     total = width * wav_count
     per = fibres // fib_count
     rows = width // 2
-    pack = max(1, LANES // per)
-    while pack > 1 and rows % (pack * ROWS):
-        pack //= 2
-    rel = pack * per == LANES
+    pack = 2 if 2 * per == LANES and rows % (2 * ROWS) == 0 else 1
+    rel = pack * per == LANES and fib_count & (fib_count - 1) == 0
+    if not rel:
+        pack = 1
     pieces = fib_count if rel else 1
     place = jnp.stack([lax.axis_index(axis) for axis in ("fib", "wav", "exp")]).astype(jnp.int32)
     coupling, counts, slots = coupling[None], counts[None], owner_slot[None]
     swap = [(0, 1), (1, 0)]
-    moves = (fib_count, pack, per, rel)
+    moves = (fib_count, per, rel)
 
     theirs, weight_t, send_table, slots, coupling, counts, good, bits, ivar = sent_weights(
         moves, wav_count, place, slots, coupling, counts, good_flags, clip_bits, pixel_ivar
@@ -663,13 +656,12 @@
 
     pixel_s, ivar_s = stream_layout(left[0] + right[0], pixels, ivar)
     theirs, solved = flux_sums(wav_count, place, coupling, left, right, pixel_s, ivar_s, weight_t)
-    ahead = sum(piece[0, :ROWS, :] for piece in weight_pieces[1:-1] or weight_pieces)
+    ahead = weight_pieces[fib_count // 2 if rel else 0][0, :ROWS, :LANES] * 0.5
     arriving = lax.ppermute(theirs, "exp", swap)
     mine = kept_flux(after(place, theirs), coupling, solved, weight_m)
     sorted_pieces = sort_fibres(arriving, mine, send_table, pack, pieces, scale, ahead)
     flux_pieces = exchange(sorted_pieces, fib_count)
     recv_table = recv_moves(moves, after(place, sorted_pieces[0]), slots, fibres)
-
     ivar, res = end_weights(place, recv_table, weight_pieces, pack, fibres, total)
     flux = end_flux(recv_table, flux_pieces, pack, fibres)
     return (flux, ivar, res)

time: 31.3 us -> 30.1 us (0.962)
  waiting for transfers between devices: 4.39 us -> 3.03 us
  starting transfers between devices: 14.1 us -> 14.9 us
  Pallas kernels: 11.8 us -> 11.2 us
    ppermute x6, waiting for transfers between devices: 4.38 us -> 3.02 us  [exchange(): lax.ppermute(pieces[d], 'fib', [(i, i ^ d) for i in range(fib_count)])]
    ppermute x6, starting transfers between devices: 9.9 us -> 10.8 us  [exchange(): lax.ppermute(pieces[d], 'fib', [(i, i ^ d) for i in range(fib_count)])]
    pallas_call x1, Pallas kernels: 1.4 us -> 0.98 us  [recv_moves(): pl.pallas_call(functools.partial(recv_kernel, moves), in_specs=[in_smem,...]
  transfers between devices with their start and end apart: 10 -> 10, of which waited for: 2 -> 2; matrix products, arithmetic and copies ran while one was open for 0% -> 0% of each run, Pallas kernels for 28% -> 27%
where the time goes in v17:
time: 30.1 us; the launch traced here: 29.9 us
  starting transfers between devices  14.9 us (50%)
  Pallas kernels  11.2 us (37%)
  waiting for transfers between devices  3.03 us (10%)
  between operations  0.73 us (2%)
    ppermute x6, starting transfers between devices, exchange(): lax.ppermute(pieces[d], 'fib', [(i, i ^ d) for i in range(fib_count)])  10.8 us
    ppermute x6, waiting for transfers between devices, exchange(): lax.ppermute(pieces[d], 'fib', [(i, i ^ d) for i in range(fib_count)])  3.02 us
    ppermute x1, starting transfers between devices, per_device(): left = lax.ppermute(up, 'wav', upward)  2.56 us
    pallas_call x1, Pallas kernels, flux_sums(): pl.pallas_call(functools.partial(solve_kernel, wav_count), in_specs=[in_s...  2.34 us
    pallas_call x1, Pallas kernels, sent_weights(): pl.pallas_call(functools.partial(sent_kernel, moves, wav_count), in_specs...  2.22 us
    pallas_call x1, Pallas kernels, end_weights(): pl.pallas_call(functools.partial(weights_end_kernel, pack, total), in_spe...  1.77 us
    pallas_call x1, Pallas kernels, kept_weights(): pl.pallas_call(functools.partial(kept_kernel, wav_count), in_specs=[in_sm...  1.14 us
    ppermute x1, starting transfers between devices, per_device(): right = lax.ppermute(down, 'wav', [(j, i) for i, j in upward])  1.02 us
  transfers between devices with their start and end apart: 10, of which 2 were waited for; matrix products, arithmetic and copies ran while one was open for 0% of the time, Pallas kernels for 27%

profile of v17, /device:TPU:0, one launch (start us, length us, event | category | flops | bytes accessed | tf_op | source)
XLA Modules:
  0.0 29.9 jit_solution(13655885091865214568)
XLA Ops:
  0.6 0.1 pad_add_fusion.place_ref
  0.7 2.2 %sent_weights.1 = (f32[2,240,256]{2,1,0:T(8,128)S(1)}, f32[4,240,256]{2,1,0:T(8,128)S(1)}, bf16[256,256]{1,0:T(8,128)(2,1)S(1)}, s32[1,1024]{1,0:T(1,128)S(1)}, ...) custom-call(s32[3]{0:T(128)S(1)} %pad_add_fusion.place_ref, ...), custom_call_target="tpu_custom_call" | custom-call | flops 9830400 | bytes 2949120 | tf_op jit(solution)/shard_map/sent_weights/pallas_call | solution.py:248
  2.9 0.5 %collective-permute-start.3 = (f32[2,240,256]{2,1,0:T(8,128)S(1)}, f32[2,240,256]{2,1,0:T(8,128)S(1)}, u32[]{:S(2)}, u32[]{:S(2)}) collective-permute-start(f32[2,240,256]{2,1,0:T(8,128)S(1)} %get-tuple-element.48), channel_id=1, source_target_pairs={{0,1},{1,0},{2,3},{3,2},{4,5},{5,4},{6,7},{7,6},{8,9},{9,8},{10,11... | collective-permute-start | bytes 1474568 | tf_op jit(solution)/shard_map/ppermute | solution.py:647
  3.5 1.1 %kept_weights.1 = (f32[2,240,256]{2,1,0:T(8,128)S(1)}, f32[4,240,256]{2,1,0:T(8,128)S(1)}, f32[2,8,128]{2,1,0:T(8,128)S(1)}, f32[2,8,128]{2,1,0:T(8,128)S(1)}) custom-call(s32[3]{0:T(128)S(1)} %pad_add_fusion.place_ref, f32[1,256]{1,0:T(1,128)S(1)} %get-tuple-element.33.coupling_ref, s32[1,256]{1,0:T(1,128)S(1)} %get-tuple-element.34.counts_ref, ...), custom_call_target="tpu_custom_call" | custom-call | flops 9830400 | bytes 2949120 | tf_op jit(solution)/shard_map/kept_weights/pallas_call | solution.py:321
  4.6 2.6 %collective-permute-start = (f32[2,8,128]{2,1,0:T(8,128)S(1)}, f32[2,8,128]{2,1,0:T(8,128)S(1)}, u32[]{:S(2)}, u32[]{:S(2)}) collective-permute-start(f32[2,8,128]{2,1,0:T(8,128)S(1)} %get-tuple-element.38), channel_id=1, source_target_pairs={{0,2},{2,4},{4,6},{6,0},{1,3},{3,5},{5,7},{7,1},{8,10},{10,12},{12... | collective-permute-start | bytes 24584 | tf_op jit(solution)/shard_map/ppermute | solution.py:652
  7.2 1.0 %collective-permute-start.1 = (f32[2,8,128]{2,1,0:T(8,128)S(1)}, f32[2,8,128]{2,1,0:T(8,128)S(1)}, u32[]{:S(2)}, u32[]{:S(2)}) collective-permute-start(f32[2,8,128]{2,1,0:T(8,128)S(1)} %get-tuple-element.39), channel_id=1, source_target_pairs={{2,0},{4,2},{6,4},{0,6},{3,1},{5,3},{7,5},{1,7},{10,8},{12,10},{14... | collective-permute-start | bytes 24584 | tf_op jit(solution)/shard_map/ppermute | solution.py:653
  8.2 0.0 collective-permute-done.3.theirs_ref
  8.2 0.4 %sort_weights.1 = (f32[2,120,128]{2,1,0:T(8,128)S(1)}, f32[2,120,128]{2,1,0:T(8,128)S(1)}, f32[2,120,128]{2,1,0:T(8,128)S(1)}, f32[2,120,128]{2,1,0:T(8,128)S(1)}, f32[240,256]{1,0:T(8,128)S(1)}) custom-call(f32[2,240,256]{2,1,0:T(8,128)S(1)} %collective-permute-done.3.theirs_ref, f32[2,240,256]{2,1,0:T(8,128)S(1)} %get-tuple-element.49.mine_ref, ...), custom_call_target="tpu_custom_call" | custom-call | tf_op jit(solution)/shard_map/sort_weights/pallas_call | solution.py:527
  8.6 3.1 %collective-permute-start.4 = (f32[2,120,128]{2,1,0:T(8,128)S(1)}, f32[2,120,128]{2,1,0:T(8,128)S(1)}, u32[]{:S(2)}, u32[]{:S(2)}) collective-permute-start(f32[2,120,128]{2,1,0:T(8,128)S(1)} %get-tuple-element.51), channel_id=1, source_target_pairs={{0,16},{8,24},{16,0},{24,8},{1,17},{9,25},{17,1},{25,9},{2,18},{10... | collective-permute-start | bytes 368648 | tf_op jit(solution)/shard_map/ppermute | solution.py:541
  11.7 0.3 stream_layout.1
  12.0 2.3 %flux_sums.1 = (f32[1,240,256]{2,1,0:T(8,128)S(1)}, f32[3848,128]{1,0:T(8,128)S(1)}) custom-call(s32[3]{0:T(128)S(1)} %pad_add_fusion.place_ref, f32[1,256]{1,0:T(1,128)S(1)} %get-tuple-element.33.coupling_ref, f32[2,8,128]{2,1,0:T(8,128)S(1)} %collective-permute-done.left_ref, f32[2,8,128]{2,1,0:T(8,128)S(1)} %collective-permute-done.1.right_ref, ...), custom_call_target="tpu_custom_call" | custom-call | tf_op jit(solution)/shard_map/flux_sums/pallas_call | solution.py:452
  14.3 0.1 collective-permute-start.2
  14.4 0.7 %kept_flux.1.mine_ref = f32[1,240,256]{2,1,0:T(8,128)S(1)} custom-call(s32[3]{0:T(128)S(1)} %pad_add_fusion.place_ref, f32[1,256]{1,0:T(1,128)S(1)} %get-tuple-element.33.coupling_ref, f32[3848,128]{1,0:T(8,128)S(1)} %get-tuple-element.45.solved_ref, f32[4,240,256]{2,1,0:T(8,128)S(1)} %get-tuple-element.46.weight_ref), custom_call_target="tpu_custom_call" | custom-call | flops 491520 | bytes 1966080 | tf_op jit(solution)/shard_map/kept_flux/pallas_call | solution.py:470
  15.1 1.6 %collective-permute-start.8 = (f32[2,120,128]{2,1,0:T(8,128)S(1)}, f32[2,120,128]{2,1,0:T(8,128)S(1)}, u32[]{:S(2)}, u32[]{:S(2)}) collective-permute-start(f32[2,120,128]{2,1,0:T(8,128)S(1)} %get-tuple-element.59), channel_id=1, source_target_pairs={{0,8},{8,0},{16,24},{24,16},{1,9},{9,1},{17,25},{25,17},{2,10},{10... | collective-permute-start | bytes 368648 | tf_op jit(solution)/shard_map/ppermute | solution.py:541
  16.7 1.6 %collective-permute-start.9 = (f32[2,120,128]{2,1,0:T(8,128)S(1)}, f32[2,120,128]{2,1,0:T(8,128)S(1)}, u32[]{:S(2)}, u32[]{:S(2)}) collective-permute-start(f32[2,120,128]{2,1,0:T(8,128)S(1)} %get-tuple-element.60), channel_id=1, source_target_pairs={{0,24},{8,16},{16,8},{24,0},{1,25},{9,17},{17,9},{25,1},{2,26},{10... | collective-permute-start | bytes 368648 | tf_op jit(solution)/shard_map/ppermute | solution.py:541
  18.4 0.3 %sort_flux.1 = (f32[1,120,128]{2,1,0:T(8,128)S(1)}, f32[1,120,128]{2,1,0:T(8,128)S(1)}, f32[1,120,128]{2,1,0:T(8,128)S(1)}, f32[1,120,128]{2,1,0:T(8,128)S(1)}) custom-call(f32[1,240,256]{2,1,0:T(8,128)S(1)} %collective-permute-done.2.theirs_ref, f32[1,240,256]{2,1,0:T(8,128)S(1)} %kept_flux.1.mine_ref, bf16[256,256]{1,0:T(8,128)(2,1)S(1)} %get-tuple-element.47.table_ref, ...), custom_call_target="tpu_custom_call" | custom-call | tf_op jit(solution)/shard_map/sort_flux/pallas_call | solution.py:527
  18.7 0.4 %collective-permute-start.5 = (f32[1,120,128]{2,1,0:T(8,128)S(1)}, f32[1,120,128]{2,1,0:T(8,128)S(1)}, u32[]{:S(2)}, u32[]{:S(2)}) collective-permute-start(f32[1,120,128]{2,1,0:T(8,128)S(1)} %get-tuple-element.55), channel_id=1, source_target_pairs={{0,16},{8,24},{16,0},{24,8},{1,17},{9,25},{17,1},{25,9},{2,18},{10... | collective-permute-start | bytes 184328 | tf_op jit(solution)/shard_map/ppermute | solution.py:541
  19.1 3.2 %collective-permute-start.6 = (f32[1,120,128]{2,1,0:T(8,128)S(1)}, f32[1,120,128]{2,1,0:T(8,128)S(1)}, u32[]{:S(2)}, u32[]{:S(2)}) collective-permute-start(f32[1,120,128]{2,1,0:T(8,128)S(1)} %get-tuple-element.56), channel_id=1, source_target_pairs={{0,8},{8,0},{16,24},{24,16},{1,9},{9,1},{17,25},{25,17},{2,10},{10... | collective-permute-start | bytes 184328 | tf_op jit(solution)/shard_map/ppermute | solution.py:541
  22.3 0.9 %collective-permute-start.7 = (f32[1,120,128]{2,1,0:T(8,128)S(1)}, f32[1,120,128]{2,1,0:T(8,128)S(1)}, u32[]{:S(2)}, u32[]{:S(2)}) collective-permute-start(f32[1,120,128]{2,1,0:T(8,128)S(1)} %get-tuple-element.57), channel_id=1, source_target_pairs={{0,24},{8,16},{16,8},{24,0},{1,25},{9,17},{17,9},{25,1},{2,26},{10... | collective-permute-start | bytes 184328 | tf_op jit(solution)/shard_map/ppermute | solution.py:541
  23.2 1.0 %recv_moves.1.table_ref = bf16[256,256]{1,0:T(8,128)(2,1)S(1)} custom-call(s32[3]{0:T(128)S(1)} %pad_add_fusion.place_ref, s32[1,1024]{1,0:T(1,128)S(1)} %get-tuple-element.54.slots_ref), custom_call_target="tpu_custom_call" | custom-call | flops 1000000 | bytes 1000000 | tf_op jit(solution)/shard_map/recv_moves/pallas_call | solution.py:567
  24.2 1.0 %collective-permute-done.9.refs_3_ = f32[2,120,128]{2,1,0:T(8,128)S(1)} collective-permute-done((f32[2,120,128]{2,1,0:T(8,128)S(1)}, f32[2,120,128]{2,1,0:T(8,128)S(1)}, u32[]{:S(2)}, u32[]{:S(2)}) %collective-permute-start.9) | collective-permute-done | bytes 122912 | tf_op jit(solution)/shard_map/ppermute | solution.py:541
  25.2 1.8 %end_weights.1 = (f32[240,256]{1,0:T(8,128)}, f32[3,240,256]{2,1,0:T(8,128)}) custom-call(s32[3]{0:T(128)S(1)} %pad_add_fusion.place_ref, bf16[256,256]{1,0:T(8,128)(2,1)S(1)} %recv_moves.1.table_ref, f32[2,120,128]{2,1,0:T(8,128)S(1)} %get-tuple-element.58.refs_0_, f32[2,120,128]{2,1,0:T(8,128)S(1)} %collective-permute-done.8.refs_1_, ...), custom_call_target="tpu_custom_call" | custom-call | tf_op jit(solution)/shard_map/end_weights/pallas_call | solution.py:594
  27.0 2.0 %collective-permute-done.5.refs_1_ = f32[1,120,128]{2,1,0:T(8,128)S(1)} collective-permute-done((f32[1,120,128]{2,1,0:T(8,128)S(1)}, f32[1,120,128]{2,1,0:T(8,128)S(1)}, u32[]{:S(2)}, u32[]{:S(2)}) %collective-permute-start.5) | collective-permute-done | bytes 61472 | tf_op jit(solution)/shard_map/ppermute | solution.py:541
  29.0 1.0 %end_flux.1 = f32[240,256]{1,0:T(8,128)} custom-call(bf16[256,256]{1,0:T(8,128)(2,1)S(1)} %recv_moves.1.table_ref, f32[1,120,128]{2,1,0:T(8,128)S(1)} %get-tuple-element.52.refs_0_, f32[1,120,128]{2,1,0:T(8,128)S(1)} %collective-permute-done.5.refs_1_, f32[1,120,128]{2,1,0:T(8,128)S(1)} %collective-permute-done.6.refs_2_, ...), custom_call_target="tpu_custom_call" | custom-call | flops 31457280 | bytes 491520 | tf_op jit(solution)/shard_map/end_flux/pallas_call | solution.py:613
  (11 shorter events, 0.0 us)
Async XLA Ops:
  0.6 2.8 %copy-start = (f32[4,480,256]{2,1,0:T(8,128)S(1)}, f32[4,480,256]{2,1,0:T(8,128)}, u32[]{:S(2)}) copy-start(f32[4,480,256]{2,1,0:T(8,128)} %pixels_ref.3) | copy-start | bytes 5898244
  2.9 5.3 %collective-permute-start.3 = (f32[2,240,256]{2,1,0:T(8,128)S(1)}, f32[2,240,256]{2,1,0:T(8,128)S(1)}, u32[]{:S(2)}, u32[]{:S(2)}) collective-permute-start(f32[2,240,256]{2,1,0:T(8,128)S(1)} %get-tuple-element.48), channel_id=1, source_target_pairs={{0,1},{1,0},{2,3},{3,2},{4,5},{5,4},{6,7},{7,6},{8,9},{9,8},{10,11... | collective-permute-start | bytes 1474568 | tf_op jit(solution)/shard_map/ppermute | solution.py:647
  4.6 7.1 %collective-permute-start = (f32[2,8,128]{2,1,0:T(8,128)S(1)}, f32[2,8,128]{2,1,0:T(8,128)S(1)}, u32[]{:S(2)}, u32[]{:S(2)}) collective-permute-start(f32[2,8,128]{2,1,0:T(8,128)S(1)} %get-tuple-element.38), channel_id=1, source_target_pairs={{0,2},{2,4},{4,6},{6,0},{1,3},{3,5},{5,7},{7,1},{8,10},{10,12},{12... | collective-permute-start | bytes 24584 | tf_op jit(solution)/shard_map/ppermute | solution.py:652
  7.2 4.5 %collective-permute-start.1 = (f32[2,8,128]{2,1,0:T(8,128)S(1)}, f32[2,8,128]{2,1,0:T(8,128)S(1)}, u32[]{:S(2)}, u32[]{:S(2)}) collective-permute-start(f32[2,8,128]{2,1,0:T(8,128)S(1)} %get-tuple-element.39), channel_id=1, source_target_pairs={{2,0},{4,2},{6,4},{0,6},{3,1},{5,3},{7,5},{1,7},{10,8},{12,10},{14... | collective-permute-start | bytes 24584 | tf_op jit(solution)/shard_map/ppermute | solution.py:653
  8.6 9.8 %collective-permute-start.4 = (f32[2,120,128]{2,1,0:T(8,128)S(1)}, f32[2,120,128]{2,1,0:T(8,128)S(1)}, u32[]{:S(2)}, u32[]{:S(2)}) collective-permute-start(f32[2,120,128]{2,1,0:T(8,128)S(1)} %get-tuple-element.51), channel_id=1, source_target_pairs={{0,16},{8,24},{16,0},{24,8},{1,17},{9,25},{17,1},{25,9},{2,18},{10... | collective-permute-start | bytes 368648 | tf_op jit(solution)/shard_map/ppermute | solution.py:541
  14.3 4.1 %collective-permute-start.2 = (f32[1,240,256]{2,1,0:T(8,128)S(1)}, f32[1,240,256]{2,1,0:T(8,128)S(1)}, u32[]{:S(2)}, u32[]{:S(2)}) collective-permute-start(f32[1,240,256]{2,1,0:T(8,128)S(1)} %get-tuple-element.43), channel_id=1, source_target_pairs={{0,1},{1,0},{2,3},{3,2},{4,5},{5,4},{6,7},{7,6},{8,9},{9,8},{10,11... | collective-permute-start | bytes 737288 | tf_op jit(solution)/shard_map/ppermute | solution.py:660
  15.1 9.0 %collective-permute-start.8 = (f32[2,120,128]{2,1,0:T(8,128)S(1)}, f32[2,120,128]{2,1,0:T(8,128)S(1)}, u32[]{:S(2)}, u32[]{:S(2)}) collective-permute-start(f32[2,120,128]{2,1,0:T(8,128)S(1)} %get-tuple-element.59), channel_id=1, source_target_pairs={{0,8},{8,0},{16,24},{24,16},{1,9},{9,1},{17,25},{25,17},{2,10},{10... | collective-permute-start | bytes 368648 | tf_op jit(solution)/shard_map/ppermute | solution.py:541
  16.7 8.5 %collective-permute-start.9 = (f32[2,120,128]{2,1,0:T(8,128)S(1)}, f32[2,120,128]{2,1,0:T(8,128)S(1)}, u32[]{:S(2)}, u32[]{:S(2)}) collective-permute-start(f32[2,120,128]{2,1,0:T(8,128)S(1)} %get-tuple-element.60), channel_id=1, source_target_pairs={{0,24},{8,16},{16,8},{24,0},{1,25},{9,17},{17,9},{25,1},{2,26},{10... | collective-permute-start | bytes 368648 | tf_op jit(solution)/shard_map/ppermute | solution.py:541
  18.7 10.2 %collective-permute-start.5 = (f32[1,120,128]{2,1,0:T(8,128)S(1)}, f32[1,120,128]{2,1,0:T(8,128)S(1)}, u32[]{:S(2)}, u32[]{:S(2)}) collective-permute-start(f32[1,120,128]{2,1,0:T(8,128)S(1)} %get-tuple-element.55), channel_id=1, source_target_pairs={{0,16},{8,24},{16,0},{24,8},{1,17},{9,25},{17,1},{25,9},{2,18},{10... | collective-permute-start | bytes 184328 | tf_op jit(solution)/shard_map/ppermute | solution.py:541
  19.1 9.9 %collective-permute-start.6 = (f32[1,120,128]{2,1,0:T(8,128)S(1)}, f32[1,120,128]{2,1,0:T(8,128)S(1)}, u32[]{:S(2)}, u32[]{:S(2)}) collective-permute-start(f32[1,120,128]{2,1,0:T(8,128)S(1)} %get-tuple-element.56), channel_id=1, source_target_pairs={{0,8},{8,0},{16,24},{24,16},{1,9},{9,1},{17,25},{25,17},{2,10},{10... | collective-permute-start | bytes 184328 | tf_op jit(solution)/shard_map/ppermute | solution.py:541
  22.3 6.7 %collective-permute-start.7 = (f32[1,120,128]{2,1,0:T(8,128)S(1)}, f32[1,120,128]{2,1,0:T(8,128)S(1)}, u32[]{:S(2)}, u32[]{:S(2)}) collective-permute-start(f32[1,120,128]{2,1,0:T(8,128)S(1)} %get-tuple-element.57), channel_id=1, source_target_pairs={{0,24},{8,16},{16,8},{24,0},{1,25},{9,17},{17,9},{25,1},{2,26},{10... | collective-permute-start | bytes 184328 | tf_op jit(solution)/shard_map/ppermute | solution.py:541

commit v18 on v17

--- a/solution.py
+++ b/solution.py
@@ -196,9 +196,24 @@
         sums_ref[1, at, :] = band_sum
 
 
+def edge_copies(source_ref, target_ref):
+    expos, width, fibres = source_ref.shape
+    count = -(-HALO // ROWS) * ROWS
+    pitch = odd(2 * count)
+    return [
+        (
+            source_ref.at[e, pl.ds(first, count), pl.ds(h * LANES, LANES)],
+            target_ref.at[pl.ds((h * expos + e) * pitch + at, count), :],
+        )
+        for h in range(fibres // LANES)
+        for e in range(expos)
+        for first, at in ((0, 0), (width - count, count))
+    ]
+
+
 def sent_kernel(
-    moves, wav_count, place_ref, slots_ref, coupling_ref, counts_ref, good_ref, bits_ref, ivar_ref,
-    sums_ref, weight_ref, table_ref, slots_v, coupling_v, counts_v, good_v, bits_v, ivar_v, sems,
+    moves, wav_count, place_ref, slots_ref, coupling_ref, counts_ref, good_ref, bits_ref, ivar_ref, pixels_ref,
+    sums_ref, weight_ref, table_ref, slots_v, coupling_v, counts_v, good_v, bits_v, ivar_v, edges_v, sems,
 ):
     expos, width, _ = ivar_ref.shape
     half = width // 2
@@ -218,7 +233,8 @@
             (bits_ref, bits_v),
         ]
         + [part(ivar_ref, ivar_v, which * half + g) for g in range(0, half, GROUP)]
-        + [part(ivar_ref, ivar_v, (1 - which) * half + g) for g in range(0, half, GROUP)],
+        + [part(ivar_ref, ivar_v, (1 - which) * half + g) for g in range(0, half, GROUP)]
+        + edge_copies(pixels_ref, edges_v),
         sems,
     )
     waits[0].wait()
@@ -240,26 +256,29 @@
         wait.wait()
 
 
-def sent_weights(moves, wav_count, place, slots, coupling, counts, good, bits, ivar):
+def sent_weights(moves, wav_count, place, slots, coupling, counts, good, bits, ivar, pixels):
     expos, width, fibres = ivar.shape
     half = width // 2
     fib_count, per, _ = moves
     inputs = (slots, coupling, counts, good, bits, ivar)
+    streams = expos * fibres // LANES
+    count = -(-HALO // ROWS) * ROWS
     return pl.pallas_call(
         functools.partial(sent_kernel, moves, wav_count),
-        in_specs=[in_smem] + [in_hbm] * 6,
-        out_specs=[in_vmem] * 9,
+        in_specs=[in_smem] + [in_hbm] * 7,
+        out_specs=[in_vmem] * 10,
         out_shape=[
             shaped((2, half, fibres)),
             shaped((expos, half, fibres)),
             shaped((fib_count * per, fibres), BF16),
         ]
-        + [shaped(x.shape, x.dtype) for x in inputs],
-        scratch_shapes=[pltpu.SemaphoreType.DMA((5 + width // GROUP,))],
+        + [shaped(x.shape, x.dtype) for x in inputs]
+        + [shaped((streams * odd(2 * count), LANES))],
+        scratch_shapes=[pltpu.SemaphoreType.DMA((5 + width // GROUP + 2 * streams,))],
         compiler_params=params(),
         cost_estimate=cost(20 * ivar.size, 6 * ivar.size),
         name="sent_weights",
-    )(place, *held_in_hbm(*inputs))
+    )(place, *held_in_hbm(*inputs, pixels))
 
 
 def lay_out(source_ref, target_ref, pieces, pitch):
@@ -273,8 +292,8 @@
 
 
 def kept_kernel(
-    wav_count, place_ref, coupling_ref, counts_ref, good_ref, pixels_ref, ivar_ref, bits_ref,
-    sums_ref, weight_ref, up_ref, down_ref, ivar_s, pixel_s,
+    wav_count, place_ref, coupling_ref, counts_ref, good_ref, pixel_s, ivar_ref, bits_ref,
+    sums_ref, weight_ref, up_ref, down_ref, ivar_s,
 ):
     expos, width, fibres = ivar_ref.shape
     half = width // 2
@@ -285,7 +304,6 @@
     words = GROUP // BITS
     edges = [(0, count, 0), (width - count, count, count)]
     lay_out(ivar_ref, ivar_s, edges, pitch)
-    lay_out(pixels_ref, pixel_s, edges, pitch)
     coupling = stream_coupling(coupling_ref, expos)
     back = 1.0 / coupling
     zero = jnp.zeros((streams, LANES), F32)
@@ -323,7 +341,7 @@
         in_specs=[in_smem] + [in_vmem] * 6,
         out_specs=[in_vmem] * 4,
         out_shape=[shaped((2, half, fibres)), shaped((expos, half, fibres)), edge, edge],
-        scratch_shapes=[edge_scratch, edge_scratch],
+        scratch_shapes=[edge_scratch],
         compiler_params=params(),
         cost_estimate=cost(20 * ivar.size, 6 * ivar.size),
         name="kept_weights",
@@ -641,12 +659,12 @@
     swap = [(0, 1), (1, 0)]
     moves = (fib_count, per, rel)
 
-    theirs, weight_t, send_table, slots, coupling, counts, good, bits, ivar = sent_weights(
-        moves, wav_count, place, slots, coupling, counts, good_flags, clip_bits, pixel_ivar
+    theirs, weight_t, send_table, slots, coupling, counts, good, bits, ivar, pixel_edges = sent_weights(
+        moves, wav_count, place, slots, coupling, counts, good_flags, clip_bits, pixel_ivar, pixels
     )
     arriving = lax.ppermute(theirs, "exp", swap)
     mine, weight_m, up, down = kept_weights(
-        wav_count, place, coupling, counts, good, pixels, ivar, bits
+        wav_count, place, coupling, counts, good, pixel_edges, ivar, bits
     )
     upward = [(i, (i + 1) % wav_count) for i in range(wav_count)]
     left = lax.ppermute(up, "wav", upward)
@@ -654,7 +672,7 @@
     *sorted_pieces, scale = sort_fibres(arriving, mine, send_table, pack, pieces)
     weight_pieces = exchange(sorted_pieces, fib_count)
 
-    pixel_s, ivar_s = stream_layout(left[0] + right[0], pixels, ivar)
+    pixel_s, ivar_s = stream_layout(left[0] + right[0], after(pixels, theirs), ivar)
     theirs, solved = flux_sums(wav_count, place, coupling, left, right, pixel_s, ivar_s, weight_t)
     ahead = weight_pieces[fib_count // 2 if rel else 0][0, :ROWS, :LANES] * 0.5
     arriving = lax.ppermute(theirs, "exp", swap)

time: 30.1 us -> 30.3 us (level)
  transfers between devices with their start and end apart: 10 -> 10, of which waited for: 2 -> 2; matrix products, arithmetic and copies ran while one was open for 0% -> 0% of each run, Pallas kernels for 27% -> 26%
where the time goes in v18:
time: 30.3 us; the launch traced here: 30.1 us
  starting transfers between devices  14.9 us (49%)
  Pallas kernels  11.3 us (37%)
  waiting for transfers between devices  3.03 us (10%)
  between operations  0.73 us (2%)
    ppermute x6, starting transfers between devices, exchange(): lax.ppermute(pieces[d], 'fib', [(i, i ^ d) for i in range(fib_count)])  10.8 us
    ppermute x6, waiting for transfers between devices, exchange(): lax.ppermute(pieces[d], 'fib', [(i, i ^ d) for i in range(fib_count)])  3.02 us
    ppermute x1, starting transfers between devices, per_device(): left = lax.ppermute(up, 'wav', upward)  2.56 us
    pallas_call x1, Pallas kernels, sent_weights(): pl.pallas_call(functools.partial(sent_kernel, moves, wav_count), in_specs...  2.39 us
    pallas_call x1, Pallas kernels, flux_sums(): pl.pallas_call(functools.partial(solve_kernel, wav_count), in_specs=[in_s...  2.34 us
    pallas_call x1, Pallas kernels, end_weights(): pl.pallas_call(functools.partial(weights_end_kernel, pack, total), in_spe...  1.77 us
    pallas_call x1, Pallas kernels, kept_weights(): pl.pallas_call(functools.partial(kept_kernel, wav_count), in_specs=[in_sm...  1.1 us
    ppermute x1, starting transfers between devices, per_device(): right = lax.ppermute(down, 'wav', [(j, i) for i, j in upward])  1.02 us
  transfers between devices with their start and end apart: 10, of which 2 were waited for; matrix products, arithmetic and copies ran while one was open for 0% of the time, Pallas kernels for 26%

profile of v18, /device:TPU:0, one launch (start us, length us, event | category | flops | bytes accessed | tf_op | source)
XLA Modules:
  0.0 30.1 jit_solution(14491595755414032425)
XLA Ops:
  0.6 0.1 pad_add_fusion.place_ref
  0.7 2.4 %sent_weights.1 = (f32[2,240,256]{2,1,0:T(8,128)S(1)}, f32[4,240,256]{2,1,0:T(8,128)S(1)}, bf16[256,256]{1,0:T(8,128)(2,1)S(1)}, s32[1,1024]{1,0:T(1,128)S(1)}, ...) custom-call(s32[3]{0:T(128)S(1)} %pad_add_fusion.place_ref, ...), custom_call_target="tpu_custom_call" | custom-call | flops 9830400 | bytes 2949120 | tf_op jit(solution)/shard_map/sent_weights/pallas_call | solution.py:266
  3.1 0.0 copy-start
  3.1 0.5 %collective-permute-start.3 = (f32[2,240,256]{2,1,0:T(8,128)S(1)}, f32[2,240,256]{2,1,0:T(8,128)S(1)}, u32[]{:S(2)}, u32[]{:S(2)}) collective-permute-start(f32[2,240,256]{2,1,0:T(8,128)S(1)} %get-tuple-element.43), channel_id=1, source_target_pairs={{0,1},{1,0},{2,3},{3,2},{4,5},{5,4},{6,7},{7,6},{8,9},{9,8},{10,11... | collective-permute-start | bytes 1474568 | tf_op jit(solution)/shard_map/ppermute | solution.py:665
  3.6 1.1 %kept_weights.1 = (f32[2,240,256]{2,1,0:T(8,128)S(1)}, f32[4,240,256]{2,1,0:T(8,128)S(1)}, f32[2,8,128]{2,1,0:T(8,128)S(1)}, f32[2,8,128]{2,1,0:T(8,128)S(1)}) custom-call(s32[3]{0:T(128)S(1)} %pad_add_fusion.place_ref, f32[1,256]{1,0:T(1,128)S(1)} %get-tuple-element.35.coupling_ref, s32[1,256]{1,0:T(1,128)S(1)} %get-tuple-element.36.counts_ref, ...), custom_call_target="tpu_custom_call" | custom-call | flops 9830400 | bytes 2949120 | tf_op jit(solution)/shard_map/kept_weights/pallas_call | solution.py:339
  4.7 2.6 %collective-permute-start = (f32[2,8,128]{2,1,0:T(8,128)S(1)}, f32[2,8,128]{2,1,0:T(8,128)S(1)}, u32[]{:S(2)}, u32[]{:S(2)}) collective-permute-start(f32[2,8,128]{2,1,0:T(8,128)S(1)} %get-tuple-element.41), channel_id=1, source_target_pairs={{0,2},{2,4},{4,6},{6,0},{1,3},{3,5},{5,7},{7,1},{8,10},{10,12},{12... | collective-permute-start | bytes 24584 | tf_op jit(solution)/shard_map/ppermute | solution.py:670
  7.3 1.0 %collective-permute-start.1 = (f32[2,8,128]{2,1,0:T(8,128)S(1)}, f32[2,8,128]{2,1,0:T(8,128)S(1)}, u32[]{:S(2)}, u32[]{:S(2)}) collective-permute-start(f32[2,8,128]{2,1,0:T(8,128)S(1)} %get-tuple-element.42), channel_id=1, source_target_pairs={{2,0},{4,2},{6,4},{0,6},{3,1},{5,3},{7,5},{1,7},{10,8},{12,10},{14... | collective-permute-start | bytes 24584 | tf_op jit(solution)/shard_map/ppermute | solution.py:671
  8.3 0.4 %sort_weights.1 = (f32[2,120,128]{2,1,0:T(8,128)S(1)}, f32[2,120,128]{2,1,0:T(8,128)S(1)}, f32[2,120,128]{2,1,0:T(8,128)S(1)}, f32[2,120,128]{2,1,0:T(8,128)S(1)}, f32[240,256]{1,0:T(8,128)S(1)}) custom-call(f32[2,240,256]{2,1,0:T(8,128)S(1)} %collective-permute-done.3.theirs_ref, f32[2,240,256]{2,1,0:T(8,128)S(1)} %get-tuple-element.53.mine_ref, ...), custom_call_target="tpu_custom_call" | custom-call | tf_op jit(solution)/shard_map/sort_weights/pallas_call | solution.py:545
  8.8 3.0 %collective-permute-start.4 = (f32[2,120,128]{2,1,0:T(8,128)S(1)}, f32[2,120,128]{2,1,0:T(8,128)S(1)}, u32[]{:S(2)}, u32[]{:S(2)}) collective-permute-start(f32[2,120,128]{2,1,0:T(8,128)S(1)} %get-tuple-element.55), channel_id=1, source_target_pairs={{0,16},{8,24},{16,0},{24,8},{1,17},{9,25},{17,1},{25,9},{2,18},{10... | collective-permute-start | bytes 368648 | tf_op jit(solution)/shard_map/ppermute | solution.py:559
  11.8 0.3 stream_layout.1
  12.1 2.3 %flux_sums.1 = (f32[1,240,256]{2,1,0:T(8,128)S(1)}, f32[3848,128]{1,0:T(8,128)S(1)}) custom-call(s32[3]{0:T(128)S(1)} %pad_add_fusion.place_ref, f32[1,256]{1,0:T(1,128)S(1)} %get-tuple-element.35.coupling_ref, f32[2,8,128]{2,1,0:T(8,128)S(1)} %collective-permute-done.left_ref, f32[2,8,128]{2,1,0:T(8,128)S(1)} %collective-permute-done.1.right_ref, ...), custom_call_target="tpu_custom_call" | custom-call | tf_op jit(solution)/shard_map/flux_sums/pallas_call | solution.py:470
  14.4 0.1 collective-permute-start.2
  14.5 0.7 %kept_flux.1.mine_ref = f32[1,240,256]{2,1,0:T(8,128)S(1)} custom-call(s32[3]{0:T(128)S(1)} %pad_add_fusion.place_ref, f32[1,256]{1,0:T(1,128)S(1)} %get-tuple-element.35.coupling_ref, f32[3848,128]{1,0:T(8,128)S(1)} %get-tuple-element.50.solved_ref, f32[4,240,256]{2,1,0:T(8,128)S(1)} %get-tuple-element.51.weight_ref), custom_call_target="tpu_custom_call" | custom-call | flops 491520 | bytes 1966080 | tf_op jit(solution)/shard_map/kept_flux/pallas_call | solution.py:488
  15.2 1.6 %collective-permute-start.8 = (f32[2,120,128]{2,1,0:T(8,128)S(1)}, f32[2,120,128]{2,1,0:T(8,128)S(1)}, u32[]{:S(2)}, u32[]{:S(2)}) collective-permute-start(f32[2,120,128]{2,1,0:T(8,128)S(1)} %get-tuple-element.63), channel_id=1, source_target_pairs={{0,8},{8,0},{16,24},{24,16},{1,9},{9,1},{17,25},{25,17},{2,10},{10... | collective-permute-start | bytes 368648 | tf_op jit(solution)/shard_map/ppermute | solution.py:559
  16.9 1.6 %collective-permute-start.9 = (f32[2,120,128]{2,1,0:T(8,128)S(1)}, f32[2,120,128]{2,1,0:T(8,128)S(1)}, u32[]{:S(2)}, u32[]{:S(2)}) collective-permute-start(f32[2,120,128]{2,1,0:T(8,128)S(1)} %get-tuple-element.64), channel_id=1, source_target_pairs={{0,24},{8,16},{16,8},{24,0},{1,25},{9,17},{17,9},{25,1},{2,26},{10... | collective-permute-start | bytes 368648 | tf_op jit(solution)/shard_map/ppermute | solution.py:559
  18.5 0.3 %sort_flux.1 = (f32[1,120,128]{2,1,0:T(8,128)S(1)}, f32[1,120,128]{2,1,0:T(8,128)S(1)}, f32[1,120,128]{2,1,0:T(8,128)S(1)}, f32[1,120,128]{2,1,0:T(8,128)S(1)}) custom-call(f32[1,240,256]{2,1,0:T(8,128)S(1)} %collective-permute-done.2.theirs_ref, f32[1,240,256]{2,1,0:T(8,128)S(1)} %kept_flux.1.mine_ref, bf16[256,256]{1,0:T(8,128)(2,1)S(1)} %get-tuple-element.52.table_ref, ...), custom_call_target="tpu_custom_call" | custom-call | tf_op jit(solution)/shard_map/sort_flux/pallas_call | solution.py:545
  18.9 0.4 %collective-permute-start.5 = (f32[1,120,128]{2,1,0:T(8,128)S(1)}, f32[1,120,128]{2,1,0:T(8,128)S(1)}, u32[]{:S(2)}, u32[]{:S(2)}) collective-permute-start(f32[1,120,128]{2,1,0:T(8,128)S(1)} %get-tuple-element.59), channel_id=1, source_target_pairs={{0,16},{8,24},{16,0},{24,8},{1,17},{9,25},{17,1},{25,9},{2,18},{10... | collective-permute-start | bytes 184328 | tf_op jit(solution)/shard_map/ppermute | solution.py:559
  19.2 3.2 %collective-permute-start.6 = (f32[1,120,128]{2,1,0:T(8,128)S(1)}, f32[1,120,128]{2,1,0:T(8,128)S(1)}, u32[]{:S(2)}, u32[]{:S(2)}) collective-permute-start(f32[1,120,128]{2,1,0:T(8,128)S(1)} %get-tuple-element.60), channel_id=1, source_target_pairs={{0,8},{8,0},{16,24},{24,16},{1,9},{9,1},{17,25},{25,17},{2,10},{10... | collective-permute-start | bytes 184328 | tf_op jit(solution)/shard_map/ppermute | solution.py:559
  22.4 0.9 %collective-permute-start.7 = (f32[1,120,128]{2,1,0:T(8,128)S(1)}, f32[1,120,128]{2,1,0:T(8,128)S(1)}, u32[]{:S(2)}, u32[]{:S(2)}) collective-permute-start(f32[1,120,128]{2,1,0:T(8,128)S(1)} %get-tuple-element.61), channel_id=1, source_target_pairs={{0,24},{8,16},{16,8},{24,0},{1,25},{9,17},{17,9},{25,1},{2,26},{10... | collective-permute-start | bytes 184328 | tf_op jit(solution)/shard_map/ppermute | solution.py:559
  23.3 1.0 %recv_moves.1.table_ref = bf16[256,256]{1,0:T(8,128)(2,1)S(1)} custom-call(s32[3]{0:T(128)S(1)} %pad_add_fusion.place_ref, s32[1,1024]{1,0:T(1,128)S(1)} %get-tuple-element.58.slots_ref), custom_call_target="tpu_custom_call" | custom-call | flops 1000000 | bytes 1000000 | tf_op jit(solution)/shard_map/recv_moves/pallas_call | solution.py:585
  24.3 1.0 %collective-permute-done.9.refs_3_ = f32[2,120,128]{2,1,0:T(8,128)S(1)} collective-permute-done((f32[2,120,128]{2,1,0:T(8,128)S(1)}, f32[2,120,128]{2,1,0:T(8,128)S(1)}, u32[]{:S(2)}, u32[]{:S(2)}) %collective-permute-start.9) | collective-permute-done | bytes 122912 | tf_op jit(solution)/shard_map/ppermute | solution.py:559
  25.3 1.8 %end_weights.1 = (f32[240,256]{1,0:T(8,128)}, f32[3,240,256]{2,1,0:T(8,128)}) custom-call(s32[3]{0:T(128)S(1)} %pad_add_fusion.place_ref, bf16[256,256]{1,0:T(8,128)(2,1)S(1)} %recv_moves.1.table_ref, f32[2,120,128]{2,1,0:T(8,128)S(1)} %get-tuple-element.62.refs_0_, f32[2,120,128]{2,1,0:T(8,128)S(1)} %collective-permute-done.8.refs_1_, ...), custom_call_target="tpu_custom_call" | custom-call | tf_op jit(solution)/shard_map/end_weights/pallas_call | solution.py:612
  27.1 2.0 %collective-permute-done.5.refs_1_ = f32[1,120,128]{2,1,0:T(8,128)S(1)} collective-permute-done((f32[1,120,128]{2,1,0:T(8,128)S(1)}, f32[1,120,128]{2,1,0:T(8,128)S(1)}, u32[]{:S(2)}, u32[]{:S(2)}) %collective-permute-start.5) | collective-permute-done | bytes 61472 | tf_op jit(solution)/shard_map/ppermute | solution.py:559
  29.1 1.0 %end_flux.1 = f32[240,256]{1,0:T(8,128)} custom-call(bf16[256,256]{1,0:T(8,128)(2,1)S(1)} %recv_moves.1.table_ref, f32[1,120,128]{2,1,0:T(8,128)S(1)} %get-tuple-element.56.refs_0_, f32[1,120,128]{2,1,0:T(8,128)S(1)} %collective-permute-done.5.refs_1_, f32[1,120,128]{2,1,0:T(8,128)S(1)} %collective-permute-done.6.refs_2_, ...), custom_call_target="tpu_custom_call" | custom-call | flops 31457280 | bytes 491520 | tf_op jit(solution)/shard_map/end_flux/pallas_call | solution.py:631
  (11 shorter events, 0.0 us)
Async XLA Ops:
  3.1 8.7 %copy-start = (f32[4,480,256]{2,1,0:T(8,128)S(1)}, f32[4,480,256]{2,1,0:T(8,128)}, u32[]{:S(2)}) copy-start(f32[4,480,256]{2,1,0:T(8,128)} %pixels_ref.2) | copy-start | bytes 5898244
  3.1 5.2 %collective-permute-start.3 = (f32[2,240,256]{2,1,0:T(8,128)S(1)}, f32[2,240,256]{2,1,0:T(8,128)S(1)}, u32[]{:S(2)}, u32[]{:S(2)}) collective-permute-start(f32[2,240,256]{2,1,0:T(8,128)S(1)} %get-tuple-element.43), channel_id=1, source_target_pairs={{0,1},{1,0},{2,3},{3,2},{4,5},{5,4},{6,7},{7,6},{8,9},{9,8},{10,11... | collective-permute-start | bytes 1474568 | tf_op jit(solution)/shard_map/ppermute | solution.py:665
  4.7 7.0 %collective-permute-start = (f32[2,8,128]{2,1,0:T(8,128)S(1)}, f32[2,8,128]{2,1,0:T(8,128)S(1)}, u32[]{:S(2)}, u32[]{:S(2)}) collective-permute-start(f32[2,8,128]{2,1,0:T(8,128)S(1)} %get-tuple-element.41), channel_id=1, source_target_pairs={{0,2},{2,4},{4,6},{6,0},{1,3},{3,5},{5,7},{7,1},{8,10},{10,12},{12... | collective-permute-start | bytes 24584 | tf_op jit(solution)/shard_map/ppermute | solution.py:670
  7.3 4.5 %collective-permute-start.1 = (f32[2,8,128]{2,1,0:T(8,128)S(1)}, f32[2,8,128]{2,1,0:T(8,128)S(1)}, u32[]{:S(2)}, u32[]{:S(2)}) collective-permute-start(f32[2,8,128]{2,1,0:T(8,128)S(1)} %get-tuple-element.42), channel_id=1, source_target_pairs={{2,0},{4,2},{6,4},{0,6},{3,1},{5,3},{7,5},{1,7},{10,8},{12,10},{14... | collective-permute-start | bytes 24584 | tf_op jit(solution)/shard_map/ppermute | solution.py:671
  8.8 9.7 %collective-permute-start.4 = (f32[2,120,128]{2,1,0:T(8,128)S(1)}, f32[2,120,128]{2,1,0:T(8,128)S(1)}, u32[]{:S(2)}, u32[]{:S(2)}) collective-permute-start(f32[2,120,128]{2,1,0:T(8,128)S(1)} %get-tuple-element.55), channel_id=1, source_target_pairs={{0,16},{8,24},{16,0},{24,8},{1,17},{9,25},{17,1},{25,9},{2,18},{10... | collective-permute-start | bytes 368648 | tf_op jit(solution)/shard_map/ppermute | solution.py:559
  14.4 4.1 %collective-permute-start.2 = (f32[1,240,256]{2,1,0:T(8,128)S(1)}, f32[1,240,256]{2,1,0:T(8,128)S(1)}, u32[]{:S(2)}, u32[]{:S(2)}) collective-permute-start(f32[1,240,256]{2,1,0:T(8,128)S(1)} %get-tuple-element.48), channel_id=1, source_target_pairs={{0,1},{1,0},{2,3},{3,2},{4,5},{5,4},{6,7},{7,6},{8,9},{9,8},{10,11... | collective-permute-start | bytes 737288 | tf_op jit(solution)/shard_map/ppermute | solution.py:678
  15.2 9.1 %collective-permute-start.8 = (f32[2,120,128]{2,1,0:T(8,128)S(1)}, f32[2,120,128]{2,1,0:T(8,128)S(1)}, u32[]{:S(2)}, u32[]{:S(2)}) collective-permute-start(f32[2,120,128]{2,1,0:T(8,128)S(1)} %get-tuple-element.63), channel_id=1, source_target_pairs={{0,8},{8,0},{16,24},{24,16},{1,9},{9,1},{17,25},{25,17},{2,10},{10... | collective-permute-start | bytes 368648 | tf_op jit(solution)/shard_map/ppermute | solution.py:559
  16.9 8.5 %collective-permute-start.9 = (f32[2,120,128]{2,1,0:T(8,128)S(1)}, f32[2,120,128]{2,1,0:T(8,128)S(1)}, u32[]{:S(2)}, u32[]{:S(2)}) collective-permute-start(f32[2,120,128]{2,1,0:T(8,128)S(1)} %get-tuple-element.64), channel_id=1, source_target_pairs={{0,24},{8,16},{16,8},{24,0},{1,25},{9,17},{17,9},{25,1},{2,26},{10... | collective-permute-start | bytes 368648 | tf_op jit(solution)/shard_map/ppermute | solution.py:559
  18.9 10.2 %collective-permute-start.5 = (f32[1,120,128]{2,1,0:T(8,128)S(1)}, f32[1,120,128]{2,1,0:T(8,128)S(1)}, u32[]{:S(2)}, u32[]{:S(2)}) collective-permute-start(f32[1,120,128]{2,1,0:T(8,128)S(1)} %get-tuple-element.59), channel_id=1, source_target_pairs={{0,16},{8,24},{16,0},{24,8},{1,17},{9,25},{17,1},{25,9},{2,18},{10... | collective-permute-start | bytes 184328 | tf_op jit(solution)/shard_map/ppermute | solution.py:559
  19.2 9.9 %collective-permute-start.6 = (f32[1,120,128]{2,1,0:T(8,128)S(1)}, f32[1,120,128]{2,1,0:T(8,128)S(1)}, u32[]{:S(2)}, u32[]{:S(2)}) collective-permute-start(f32[1,120,128]{2,1,0:T(8,128)S(1)} %get-tuple-element.60), channel_id=1, source_target_pairs={{0,8},{8,0},{16,24},{24,16},{1,9},{9,1},{17,25},{25,17},{2,10},{10... | collective-permute-start | bytes 184328 | tf_op jit(solution)/shard_map/ppermute | solution.py:559
  22.4 6.7 %collective-permute-start.7 = (f32[1,120,128]{2,1,0:T(8,128)S(1)}, f32[1,120,128]{2,1,0:T(8,128)S(1)}, u32[]{:S(2)}, u32[]{:S(2)}) collective-permute-start(f32[1,120,128]{2,1,0:T(8,128)S(1)} %get-tuple-element.61), channel_id=1, source_target_pairs={{0,24},{8,16},{16,8},{24,0},{1,25},{9,17},{17,9},{25,1},{2,26},{10... | collective-permute-start | bytes 184328 | tf_op jit(solution)/shard_map/ppermute | solution.py:559

commit v19 on v16

--- a/solution.py
+++ b/solution.py
@@ -628,7 +628,7 @@
 
 def end_flux(table, pieces, pack, fibres):
     rows = pieces[0].shape[1] * pack
-    order = [0] + sorted(range(1, len(pieces)), key=lambda d: (d < len(pieces) // 2, d))
+    order = sorted(range(len(pieces)), key=lambda d: (d > 0, abs(2 * d - len(pieces))))
     return pl.pallas_call(
         functools.partial(flux_end_kernel, pack, order),
         in_specs=[in_vmem] * (1 + len(pieces)),

time: 30.6 us -> 30.7 us (level)
  no operation moved by 1% of the time
where the time goes in v19:
time: 30.7 us; the launch traced here: 30.5 us
  starting transfers between devices  14.4 us (47%)
  Pallas kernels  11.9 us (39%)
  waiting for transfers between devices  3.34 us (11%)
  between operations  0.73 us (2%)
    ppermute x6, starting transfers between devices, exchange(): lax.ppermute(pieces[d], 'fib', [(i, i ^ d) for i in range(fib_count)])  10.3 us
    ppermute x6, waiting for transfers between devices, exchange(): lax.ppermute(pieces[d], 'fib', [(i, i ^ d) for i in range(fib_count)])  3.33 us
    ppermute x1, starting transfers between devices, per_device(): left = lax.ppermute(up, 'wav', upward)  2.56 us
    pallas_call x1, Pallas kernels, flux_sums(): pl.pallas_call(functools.partial(solve_kernel, wav_count), in_specs=[in_s...  2.34 us
    pallas_call x1, Pallas kernels, sent_weights(): pl.pallas_call(functools.partial(sent_kernel, moves, wav_count), in_specs...  2.22 us
    pallas_call x1, Pallas kernels, end_weights(): pl.pallas_call(functools.partial(weights_end_kernel, pack, total, late, l...  1.78 us
    pallas_call x1, Pallas kernels, place_early(): pl.pallas_call(functools.partial(early_kernel, moves, which, len(weight_p...  1.62 us
    pallas_call x1, Pallas kernels, kept_weights(): pl.pallas_call(functools.partial(kept_kernel, wav_count), in_specs=[in_sm...  1.14 us
  transfers between devices with their start and end apart: 10, of which 3 were waited for; matrix products, arithmetic and copies ran while one was open for 0% of the time, Pallas kernels for 28%

profile of v19, /device:TPU:0, one launch (start us, length us, event | category | flops | bytes accessed | tf_op | source)
XLA Modules:
  0.0 30.5 jit_solution(4899655852256011428)
XLA Ops:
  0.6 0.1 pad_add_fusion.place_ref
  0.7 2.2 %sent_weights.1 = (f32[2,240,256]{2,1,0:T(8,128)S(1)}, f32[4,240,256]{2,1,0:T(8,128)S(1)}, bf16[512,512]{1,0:T(8,128)(2,1)S(1)}, s32[1,1024]{1,0:T(1,128)S(1)}, ...) custom-call(s32[3]{0:T(128)S(1)} %pad_add_fusion.place_ref, ...), custom_call_target="tpu_custom_call" | custom-call | flops 9830400 | bytes 2949120 | tf_op jit(solution)/shard_map/sent_weights/pallas_call | solution.py:259
  2.9 0.5 %collective-permute-start.3 = (f32[2,240,256]{2,1,0:T(8,128)S(1)}, f32[2,240,256]{2,1,0:T(8,128)S(1)}, u32[]{:S(2)}, u32[]{:S(2)}) collective-permute-start(f32[2,240,256]{2,1,0:T(8,128)S(1)} %get-tuple-element.50), channel_id=1, source_target_pairs={{0,1},{1,0},{2,3},{3,2},{4,5},{5,4},{6,7},{7,6},{8,9},{9,8},{10,11... | collective-permute-start | bytes 1474568 | tf_op jit(solution)/shard_map/ppermute | solution.py:666
  3.5 1.1 %kept_weights.1 = (f32[2,240,256]{2,1,0:T(8,128)S(1)}, f32[4,240,256]{2,1,0:T(8,128)S(1)}, f32[2,8,128]{2,1,0:T(8,128)S(1)}, f32[2,8,128]{2,1,0:T(8,128)S(1)}) custom-call(s32[3]{0:T(128)S(1)} %pad_add_fusion.place_ref, f32[1,256]{1,0:T(1,128)S(1)} %get-tuple-element.35.coupling_ref, s32[1,256]{1,0:T(1,128)S(1)} %get-tuple-element.36.counts_ref, ...), custom_call_target="tpu_custom_call" | custom-call | flops 9830400 | bytes 2949120 | tf_op jit(solution)/shard_map/kept_weights/pallas_call | solution.py:332
  4.6 2.6 %collective-permute-start = (f32[2,8,128]{2,1,0:T(8,128)S(1)}, f32[2,8,128]{2,1,0:T(8,128)S(1)}, u32[]{:S(2)}, u32[]{:S(2)}) collective-permute-start(f32[2,8,128]{2,1,0:T(8,128)S(1)} %get-tuple-element.40), channel_id=1, source_target_pairs={{0,2},{2,4},{4,6},{6,0},{1,3},{3,5},{5,7},{7,1},{8,10},{10,12},{12... | collective-permute-start | bytes 24584 | tf_op jit(solution)/shard_map/ppermute | solution.py:671
  7.2 1.0 %collective-permute-start.1 = (f32[2,8,128]{2,1,0:T(8,128)S(1)}, f32[2,8,128]{2,1,0:T(8,128)S(1)}, u32[]{:S(2)}, u32[]{:S(2)}) collective-permute-start(f32[2,8,128]{2,1,0:T(8,128)S(1)} %get-tuple-element.41), channel_id=1, source_target_pairs={{2,0},{4,2},{6,4},{0,6},{3,1},{5,3},{7,5},{1,7},{10,8},{12,10},{14... | collective-permute-start | bytes 24584 | tf_op jit(solution)/shard_map/ppermute | solution.py:672
  8.2 0.5 %sort_weights.1 = (f32[2,120,128]{2,1,0:T(8,128)S(1)}, f32[2,120,128]{2,1,0:T(8,128)S(1)}, f32[2,120,128]{2,1,0:T(8,128)S(1)}, f32[2,120,128]{2,1,0:T(8,128)S(1)}, f32[240,256]{1,0:T(8,128)S(1)}) custom-call(f32[2,240,256]{2,1,0:T(8,128)S(1)} %collective-permute-done.3.theirs_ref, f32[2,240,256]{2,1,0:T(8,128)S(1)} %get-tuple-element.51.mine_ref, ...), custom_call_target="tpu_custom_call" | custom-call | tf_op jit(solution)/shard_map/sort_weights/pallas_call | solution.py:527
  8.7 3.1 %collective-permute-start.4 = (f32[2,120,128]{2,1,0:T(8,128)S(1)}, f32[2,120,128]{2,1,0:T(8,128)S(1)}, u32[]{:S(2)}, u32[]{:S(2)}) collective-permute-start(f32[2,120,128]{2,1,0:T(8,128)S(1)} %get-tuple-element.53), channel_id=1, source_target_pairs={{0,16},{8,24},{16,0},{24,8},{1,17},{9,25},{17,1},{25,9},{2,18},{10... | collective-permute-start | bytes 368648 | tf_op jit(solution)/shard_map/ppermute | solution.py:541
  11.7 0.0 collective-permute-done.left_ref
  11.8 0.3 stream_layout.1
  12.0 2.3 %flux_sums.1 = (f32[1,240,256]{2,1,0:T(8,128)S(1)}, f32[3848,128]{1,0:T(8,128)S(1)}) custom-call(s32[3]{0:T(128)S(1)} %pad_add_fusion.place_ref, f32[1,256]{1,0:T(1,128)S(1)} %get-tuple-element.35.coupling_ref, f32[2,8,128]{2,1,0:T(8,128)S(1)} %collective-permute-done.left_ref, f32[2,8,128]{2,1,0:T(8,128)S(1)} %collective-permute-done.1.right_ref, ...), custom_call_target="tpu_custom_call" | custom-call | tf_op jit(solution)/shard_map/flux_sums/pallas_call | solution.py:463
  14.4 0.1 collective-permute-start.2
  14.4 0.7 %kept_flux.1.mine_ref = f32[1,240,256]{2,1,0:T(8,128)S(1)} custom-call(s32[3]{0:T(128)S(1)} %pad_add_fusion.place_ref, f32[1,256]{1,0:T(1,128)S(1)} %get-tuple-element.35.coupling_ref, f32[3848,128]{1,0:T(8,128)S(1)} %get-tuple-element.47.solved_ref, f32[4,240,256]{2,1,0:T(8,128)S(1)} %get-tuple-element.48.weight_ref), custom_call_target="tpu_custom_call" | custom-call | flops 491520 | bytes 1966080 | tf_op jit(solution)/shard_map/kept_flux/pallas_call | solution.py:481
  15.2 2.7 %collective-permute-start.8 = (f32[2,120,128]{2,1,0:T(8,128)S(1)}, f32[2,120,128]{2,1,0:T(8,128)S(1)}, u32[]{:S(2)}, u32[]{:S(2)}) collective-permute-start(f32[2,120,128]{2,1,0:T(8,128)S(1)} %get-tuple-element.63), channel_id=1, source_target_pairs={{0,24},{8,16},{16,8},{24,0},{1,25},{9,17},{17,9},{25,1},{2,26},{10... | collective-permute-start | bytes 368648 | tf_op jit(solution)/shard_map/ppermute | solution.py:541
  17.9 0.3 %sort_flux.1 = (f32[1,120,128]{2,1,0:T(8,128)S(1)}, f32[1,120,128]{2,1,0:T(8,128)S(1)}, f32[1,120,128]{2,1,0:T(8,128)S(1)}, f32[1,120,128]{2,1,0:T(8,128)S(1)}) custom-call(f32[1,240,256]{2,1,0:T(8,128)S(1)} %collective-permute-done.2.theirs_ref, f32[1,240,256]{2,1,0:T(8,128)S(1)} %kept_flux.1.mine_ref, bf16[512,512]{1,0:T(8,128)(2,1)S(1)} %get-tuple-element.49.table_ref, ...), custom_call_target="tpu_custom_call" | custom-call | tf_op jit(solution)/shard_map/sort_flux/pallas_call | solution.py:527
  18.3 1.8 %collective-permute-start.5 = (f32[1,120,128]{2,1,0:T(8,128)S(1)}, f32[1,120,128]{2,1,0:T(8,128)S(1)}, u32[]{:S(2)}, u32[]{:S(2)}) collective-permute-start(f32[1,120,128]{2,1,0:T(8,128)S(1)} %get-tuple-element.59), channel_id=1, source_target_pairs={{0,16},{8,24},{16,0},{24,8},{1,17},{9,25},{17,1},{25,9},{2,18},{10... | collective-permute-start | bytes 184328 | tf_op jit(solution)/shard_map/ppermute | solution.py:541
  20.1 2.4 %collective-permute-start.6 = (f32[1,120,128]{2,1,0:T(8,128)S(1)}, f32[1,120,128]{2,1,0:T(8,128)S(1)}, u32[]{:S(2)}, u32[]{:S(2)}) collective-permute-start(f32[1,120,128]{2,1,0:T(8,128)S(1)} %get-tuple-element.60), channel_id=1, source_target_pairs={{0,8},{8,0},{16,24},{24,16},{1,9},{9,1},{17,25},{25,17},{2,10},{10... | collective-permute-start | bytes 184328 | tf_op jit(solution)/shard_map/ppermute | solution.py:541
  22.4 0.3 %collective-permute-start.7 = (f32[1,120,128]{2,1,0:T(8,128)S(1)}, f32[1,120,128]{2,1,0:T(8,128)S(1)}, u32[]{:S(2)}, u32[]{:S(2)}) collective-permute-start(f32[1,120,128]{2,1,0:T(8,128)S(1)} %get-tuple-element.61), channel_id=1, source_target_pairs={{0,24},{8,16},{16,8},{24,0},{1,25},{9,17},{17,9},{25,1},{2,26},{10... | collective-permute-start | bytes 184328 | tf_op jit(solution)/shard_map/ppermute | solution.py:541
  22.7 1.6 %place_early.1 = (bf16[512,512]{1,0:T(8,128)(2,1)S(1)}, f32[2,120,512]{2,1,0:T(8,128)S(1)}) custom-call(s32[3]{0:T(128)S(1)} %pad_add_fusion.place_ref, s32[1,1024]{1,0:T(1,128)S(1)} %get-tuple-element.56.slots_ref, f32[2,120,128]{2,1,0:T(8,128)S(1)} %get-tuple-element.57.refs_0_, f32[2,120,128]{2,1,0:T(8,128)S(1)} %collective-permute-done.4.refs_1_), custom_call_target="tpu_custom_call" | custom-call | tf_op jit(solution)/shard_map/place_early/pallas_call | solution.py:570
  24.4 2.1 %collective-permute-done.9.refs_1_ = f32[2,120,128]{2,1,0:T(8,128)S(1)} collective-permute-done((f32[2,120,128]{2,1,0:T(8,128)S(1)}, f32[2,120,128]{2,1,0:T(8,128)S(1)}, u32[]{:S(2)}, u32[]{:S(2)}) %collective-permute-start.9) | collective-permute-done | bytes 122912 | tf_op jit(solution)/shard_map/ppermute | solution.py:541
  26.5 1.8 %end_weights.1 = (f32[240,256]{1,0:T(8,128)}, f32[3,240,256]{2,1,0:T(8,128)}) custom-call(s32[3]{0:T(128)S(1)} %pad_add_fusion.place_ref, bf16[512,512]{1,0:T(8,128)(2,1)S(1)} %get-tuple-element.58.table_ref, f32[2,120,512]{2,1,0:T(8,128)S(1)} %get-tuple-element.62.sums_ref, f32[2,120,128]{2,1,0:T(8,128)S(1)} %collective-permute-done.8.refs_0_, ...), custom_call_target="tpu_custom_call" | custom-call | tf_op jit(solution)/shard_map/end_weights/pallas_call | solution.py:609
  28.3 0.3 collective-permute-done.6.refs_2_
  28.5 1.0 %collective-permute-done.7.refs_3_ = f32[1,120,128]{2,1,0:T(8,128)S(1)} collective-permute-done((f32[1,120,128]{2,1,0:T(8,128)S(1)}, f32[1,120,128]{2,1,0:T(8,128)S(1)}, u32[]{:S(2)}, u32[]{:S(2)}) %collective-permute-start.7) | collective-permute-done | bytes 61472 | tf_op jit(solution)/shard_map/ppermute | solution.py:541
  29.5 1.0 %end_flux.1 = f32[240,256]{1,0:T(8,128)} custom-call(bf16[512,512]{1,0:T(8,128)(2,1)S(1)} %get-tuple-element.58.table_ref, f32[1,120,128]{2,1,0:T(8,128)S(1)} %get-tuple-element.54.refs_0_, f32[1,120,128]{2,1,0:T(8,128)S(1)} %collective-permute-done.5.refs_1_, f32[1,120,128]{2,1,0:T(8,128)S(1)} %collective-permute-done.6.refs_2_, ...), custom_call_target="tpu_custom_call" | custom-call | flops 125829120 | bytes 491520 | tf_op jit(solution)/shard_map/end_flux/pallas_call | solution.py:632
  (11 shorter events, 0.0 us)
Async XLA Ops:
  0.6 2.8 %copy-start = (f32[4,480,256]{2,1,0:T(8,128)S(1)}, f32[4,480,256]{2,1,0:T(8,128)}, u32[]{:S(2)}) copy-start(f32[4,480,256]{2,1,0:T(8,128)} %pixels_ref.3) | copy-start | bytes 5898244
  2.9 5.2 %collective-permute-start.3 = (f32[2,240,256]{2,1,0:T(8,128)S(1)}, f32[2,240,256]{2,1,0:T(8,128)S(1)}, u32[]{:S(2)}, u32[]{:S(2)}) collective-permute-start(f32[2,240,256]{2,1,0:T(8,128)S(1)} %get-tuple-element.50), channel_id=1, source_target_pairs={{0,1},{1,0},{2,3},{3,2},{4,5},{5,4},{6,7},{7,6},{8,9},{9,8},{10,11... | collective-permute-start | bytes 1474568 | tf_op jit(solution)/shard_map/ppermute | solution.py:666
  4.6 7.1 %collective-permute-start = (f32[2,8,128]{2,1,0:T(8,128)S(1)}, f32[2,8,128]{2,1,0:T(8,128)S(1)}, u32[]{:S(2)}, u32[]{:S(2)}) collective-permute-start(f32[2,8,128]{2,1,0:T(8,128)S(1)} %get-tuple-element.40), channel_id=1, source_target_pairs={{0,2},{2,4},{4,6},{6,0},{1,3},{3,5},{5,7},{7,1},{8,10},{10,12},{12... | collective-permute-start | bytes 24584 | tf_op jit(solution)/shard_map/ppermute | solution.py:671
  7.2 4.6 %collective-permute-start.1 = (f32[2,8,128]{2,1,0:T(8,128)S(1)}, f32[2,8,128]{2,1,0:T(8,128)S(1)}, u32[]{:S(2)}, u32[]{:S(2)}) collective-permute-start(f32[2,8,128]{2,1,0:T(8,128)S(1)} %get-tuple-element.41), channel_id=1, source_target_pairs={{2,0},{4,2},{6,4},{0,6},{3,1},{5,3},{7,5},{1,7},{10,8},{12,10},{14... | collective-permute-start | bytes 24584 | tf_op jit(solution)/shard_map/ppermute | solution.py:672
  8.7 9.2 %collective-permute-start.4 = (f32[2,120,128]{2,1,0:T(8,128)S(1)}, f32[2,120,128]{2,1,0:T(8,128)S(1)}, u32[]{:S(2)}, u32[]{:S(2)}) collective-permute-start(f32[2,120,128]{2,1,0:T(8,128)S(1)} %get-tuple-element.53), channel_id=1, source_target_pairs={{0,16},{8,24},{16,0},{24,8},{1,17},{9,25},{17,1},{25,9},{2,18},{10... | collective-permute-start | bytes 368648 | tf_op jit(solution)/shard_map/ppermute | solution.py:541
  14.4 3.6 %collective-permute-start.2 = (f32[1,240,256]{2,1,0:T(8,128)S(1)}, f32[1,240,256]{2,1,0:T(8,128)S(1)}, u32[]{:S(2)}, u32[]{:S(2)}) collective-permute-start(f32[1,240,256]{2,1,0:T(8,128)S(1)} %get-tuple-element.45), channel_id=1, source_target_pairs={{0,1},{1,0},{2,3},{3,2},{4,5},{5,4},{6,7},{7,6},{8,9},{9,8},{10,11... | collective-permute-start | bytes 737288 | tf_op jit(solution)/shard_map/ppermute | solution.py:681
  15.2 9.2 %collective-permute-start.8 = (f32[2,120,128]{2,1,0:T(8,128)S(1)}, f32[2,120,128]{2,1,0:T(8,128)S(1)}, u32[]{:S(2)}, u32[]{:S(2)}) collective-permute-start(f32[2,120,128]{2,1,0:T(8,128)S(1)} %get-tuple-element.63), channel_id=1, source_target_pairs={{0,24},{8,16},{16,8},{24,0},{1,25},{9,17},{17,9},{25,1},{2,26},{10... | collective-permute-start | bytes 368648 | tf_op jit(solution)/shard_map/ppermute | solution.py:541
  17.9 8.6 %collective-permute-start.9 = (f32[2,120,128]{2,1,0:T(8,128)S(1)}, f32[2,120,128]{2,1,0:T(8,128)S(1)}, u32[]{:S(2)}, u32[]{:S(2)}) collective-permute-start(f32[2,120,128]{2,1,0:T(8,128)S(1)} %get-tuple-element.64), channel_id=1, source_target_pairs={{0,8},{8,0},{16,24},{24,16},{1,9},{9,1},{17,25},{25,17},{2,10},{10... | collective-permute-start | bytes 368648 | tf_op jit(solution)/shard_map/ppermute | solution.py:541
  18.3 10.0 %collective-permute-start.5 = (f32[1,120,128]{2,1,0:T(8,128)S(1)}, f32[1,120,128]{2,1,0:T(8,128)S(1)}, u32[]{:S(2)}, u32[]{:S(2)}) collective-permute-start(f32[1,120,128]{2,1,0:T(8,128)S(1)} %get-tuple-element.59), channel_id=1, source_target_pairs={{0,16},{8,24},{16,0},{24,8},{1,17},{9,25},{17,1},{25,9},{2,18},{10... | collective-permute-start | bytes 184328 | tf_op jit(solution)/shard_map/ppermute | solution.py:541
  20.1 8.5 %collective-permute-start.6 = (f32[1,120,128]{2,1,0:T(8,128)S(1)}, f32[1,120,128]{2,1,0:T(8,128)S(1)}, u32[]{:S(2)}, u32[]{:S(2)}) collective-permute-start(f32[1,120,128]{2,1,0:T(8,128)S(1)} %get-tuple-element.60), channel_id=1, source_target_pairs={{0,8},{8,0},{16,24},{24,16},{1,9},{9,1},{17,25},{25,17},{2,10},{10... | collective-permute-start | bytes 184328 | tf_op jit(solution)/shard_map/ppermute | solution.py:541
  22.4 7.1 %collective-permute-start.7 = (f32[1,120,128]{2,1,0:T(8,128)S(1)}, f32[1,120,128]{2,1,0:T(8,128)S(1)}, u32[]{:S(2)}, u32[]{:S(2)}) collective-permute-start(f32[1,120,128]{2,1,0:T(8,128)S(1)} %get-tuple-element.61), channel_id=1, source_target_pairs={{0,24},{8,16},{16,8},{24,0},{1,25},{9,17},{17,9},{25,1},{2,26},{10... | collective-permute-start | bytes 184328 | tf_op jit(solution)/shard_map/ppermute | solution.py:541

commit v20 on v16

--- a/solution.py
+++ b/solution.py
@@ -676,7 +676,7 @@
     pixel_s, ivar_s = stream_layout(left[0] + right[0], pixels, ivar)
     theirs, solved = flux_sums(wav_count, place, coupling, left, right, pixel_s, ivar_s, weight_t)
     early = [0, fib_count // 2] if rel else [0]
-    late = [d for d in reversed(range(pieces)) if d not in early]
+    late = [d for d in range(pieces) if d not in early]
     ahead = weight_pieces[early[-1]][0, :ROWS, :] * 0.5
     arriving = lax.ppermute(theirs, "exp", swap)
     mine = kept_flux(after(place, theirs), coupling, solved, weight_m)

time: 30.6 us -> 30.1 us (0.984)
  starting transfers between devices: 14.4 us -> 14 us
    ppermute x6, starting transfers between devices: 10.2 us -> 9.87 us  [exchange(): lax.ppermute(pieces[d], 'fib', [(i, i ^ d) for i in range(fib_count)])]
  transfers between devices with their start and end apart: 10 -> 10, of which waited for: 3 -> 2; matrix products, arithmetic and copies ran while one was open for 0% -> 0% of each run, Pallas kernels for 28% -> 29%
where the time goes in v20:
time: 30.1 us; the launch traced here: 30 us
  starting transfers between devices  14 us (47%)
  Pallas kernels  11.9 us (40%)
  waiting for transfers between devices  3.17 us (11%)
  between operations  0.73 us (2%)
    ppermute x6, starting transfers between devices, exchange(): lax.ppermute(pieces[d], 'fib', [(i, i ^ d) for i in range(fib_count)])  9.87 us
    ppermute x6, waiting for transfers between devices, exchange(): lax.ppermute(pieces[d], 'fib', [(i, i ^ d) for i in range(fib_count)])  3.16 us
    ppermute x1, starting transfers between devices, per_device(): left = lax.ppermute(up, 'wav', upward)  2.56 us
    pallas_call x1, Pallas kernels, flux_sums(): pl.pallas_call(functools.partial(solve_kernel, wav_count), in_specs=[in_s...  2.34 us
    pallas_call x1, Pallas kernels, sent_weights(): pl.pallas_call(functools.partial(sent_kernel, moves, wav_count), in_specs...  2.22 us
    pallas_call x1, Pallas kernels, end_weights(): pl.pallas_call(functools.partial(weights_end_kernel, pack, total, late, l...  1.79 us
    pallas_call x1, Pallas kernels, place_early(): pl.pallas_call(functools.partial(early_kernel, moves, which, len(weight_p...  1.62 us
    pallas_call x1, Pallas kernels, kept_weights(): pl.pallas_call(functools.partial(kept_kernel, wav_count), in_specs=[in_sm...  1.14 us
  transfers between devices with their start and end apart: 10, of which 2 were waited for; matrix products, arithmetic and copies ran while one was open for 0% of the time, Pallas kernels for 29%

profile of v20, /device:TPU:0, one launch (start us, length us, event | category | flops | bytes accessed | tf_op | source)
XLA Modules:
  0.0 30.0 jit_solution(2354887452770237687)
XLA Ops:
  0.6 0.1 pad_add_fusion.place_ref
  0.7 2.2 %sent_weights.1 = (f32[2,240,256]{2,1,0:T(8,128)S(1)}, f32[4,240,256]{2,1,0:T(8,128)S(1)}, bf16[512,512]{1,0:T(8,128)(2,1)S(1)}, s32[1,1024]{1,0:T(1,128)S(1)}, ...) custom-call(s32[3]{0:T(128)S(1)} %pad_add_fusion.place_ref, ...), custom_call_target="tpu_custom_call" | custom-call | flops 9830400 | bytes 2949120 | tf_op jit(solution)/shard_map/sent_weights/pallas_call | solution.py:259
  2.9 0.5 %collective-permute-start.3 = (f32[2,240,256]{2,1,0:T(8,128)S(1)}, f32[2,240,256]{2,1,0:T(8,128)S(1)}, u32[]{:S(2)}, u32[]{:S(2)}) collective-permute-start(f32[2,240,256]{2,1,0:T(8,128)S(1)} %get-tuple-element.50), channel_id=1, source_target_pairs={{0,1},{1,0},{2,3},{3,2},{4,5},{5,4},{6,7},{7,6},{8,9},{9,8},{10,11... | collective-permute-start | bytes 1474568 | tf_op jit(solution)/shard_map/ppermute | solution.py:666
  3.5 1.1 %kept_weights.1 = (f32[2,240,256]{2,1,0:T(8,128)S(1)}, f32[4,240,256]{2,1,0:T(8,128)S(1)}, f32[2,8,128]{2,1,0:T(8,128)S(1)}, f32[2,8,128]{2,1,0:T(8,128)S(1)}) custom-call(s32[3]{0:T(128)S(1)} %pad_add_fusion.place_ref, f32[1,256]{1,0:T(1,128)S(1)} %get-tuple-element.35.coupling_ref, s32[1,256]{1,0:T(1,128)S(1)} %get-tuple-element.36.counts_ref, ...), custom_call_target="tpu_custom_call" | custom-call | flops 9830400 | bytes 2949120 | tf_op jit(solution)/shard_map/kept_weights/pallas_call | solution.py:332
  4.6 2.6 %collective-permute-start = (f32[2,8,128]{2,1,0:T(8,128)S(1)}, f32[2,8,128]{2,1,0:T(8,128)S(1)}, u32[]{:S(2)}, u32[]{:S(2)}) collective-permute-start(f32[2,8,128]{2,1,0:T(8,128)S(1)} %get-tuple-element.40), channel_id=1, source_target_pairs={{0,2},{2,4},{4,6},{6,0},{1,3},{3,5},{5,7},{7,1},{8,10},{10,12},{12... | collective-permute-start | bytes 24584 | tf_op jit(solution)/shard_map/ppermute | solution.py:671
  7.2 1.0 %collective-permute-start.1 = (f32[2,8,128]{2,1,0:T(8,128)S(1)}, f32[2,8,128]{2,1,0:T(8,128)S(1)}, u32[]{:S(2)}, u32[]{:S(2)}) collective-permute-start(f32[2,8,128]{2,1,0:T(8,128)S(1)} %get-tuple-element.41), channel_id=1, source_target_pairs={{2,0},{4,2},{6,4},{0,6},{3,1},{5,3},{7,5},{1,7},{10,8},{12,10},{14... | collective-permute-start | bytes 24584 | tf_op jit(solution)/shard_map/ppermute | solution.py:672
  8.2 0.0 collective-permute-done.3.theirs_ref
  8.2 0.5 %sort_weights.1 = (f32[2,120,128]{2,1,0:T(8,128)S(1)}, f32[2,120,128]{2,1,0:T(8,128)S(1)}, f32[2,120,128]{2,1,0:T(8,128)S(1)}, f32[2,120,128]{2,1,0:T(8,128)S(1)}, f32[240,256]{1,0:T(8,128)S(1)}) custom-call(f32[2,240,256]{2,1,0:T(8,128)S(1)} %collective-permute-done.3.theirs_ref, f32[2,240,256]{2,1,0:T(8,128)S(1)} %get-tuple-element.51.mine_ref, ...), custom_call_target="tpu_custom_call" | custom-call | tf_op jit(solution)/shard_map/sort_weights/pallas_call | solution.py:527
  8.7 3.1 %collective-permute-start.4 = (f32[2,120,128]{2,1,0:T(8,128)S(1)}, f32[2,120,128]{2,1,0:T(8,128)S(1)}, u32[]{:S(2)}, u32[]{:S(2)}) collective-permute-start(f32[2,120,128]{2,1,0:T(8,128)S(1)} %get-tuple-element.53), channel_id=1, source_target_pairs={{0,16},{8,24},{16,0},{24,8},{1,17},{9,25},{17,1},{25,9},{2,18},{10... | collective-permute-start | bytes 368648 | tf_op jit(solution)/shard_map/ppermute | solution.py:541
  11.8 0.3 stream_layout.1
  12.0 2.3 %flux_sums.1 = (f32[1,240,256]{2,1,0:T(8,128)S(1)}, f32[3848,128]{1,0:T(8,128)S(1)}) custom-call(s32[3]{0:T(128)S(1)} %pad_add_fusion.place_ref, f32[1,256]{1,0:T(1,128)S(1)} %get-tuple-element.35.coupling_ref, f32[2,8,128]{2,1,0:T(8,128)S(1)} %collective-permute-done.left_ref, f32[2,8,128]{2,1,0:T(8,128)S(1)} %collective-permute-done.1.right_ref, ...), custom_call_target="tpu_custom_call" | custom-call | tf_op jit(solution)/shard_map/flux_sums/pallas_call | solution.py:463
  14.4 0.1 collective-permute-start.2
  14.4 0.7 %kept_flux.1.mine_ref = f32[1,240,256]{2,1,0:T(8,128)S(1)} custom-call(s32[3]{0:T(128)S(1)} %pad_add_fusion.place_ref, f32[1,256]{1,0:T(1,128)S(1)} %get-tuple-element.35.coupling_ref, f32[3848,128]{1,0:T(8,128)S(1)} %get-tuple-element.47.solved_ref, f32[4,240,256]{2,1,0:T(8,128)S(1)} %get-tuple-element.48.weight_ref), custom_call_target="tpu_custom_call" | custom-call | flops 491520 | bytes 1966080 | tf_op jit(solution)/shard_map/kept_flux/pallas_call | solution.py:481
  15.2 1.6 %collective-permute-start.8 = (f32[2,120,128]{2,1,0:T(8,128)S(1)}, f32[2,120,128]{2,1,0:T(8,128)S(1)}, u32[]{:S(2)}, u32[]{:S(2)}) collective-permute-start(f32[2,120,128]{2,1,0:T(8,128)S(1)} %get-tuple-element.63), channel_id=1, source_target_pairs={{0,8},{8,0},{16,24},{24,16},{1,9},{9,1},{17,25},{25,17},{2,10},{10... | collective-permute-start | bytes 368648 | tf_op jit(solution)/shard_map/ppermute | solution.py:541
  16.8 1.5 %collective-permute-start.9 = (f32[2,120,128]{2,1,0:T(8,128)S(1)}, f32[2,120,128]{2,1,0:T(8,128)S(1)}, u32[]{:S(2)}, u32[]{:S(2)}) collective-permute-start(f32[2,120,128]{2,1,0:T(8,128)S(1)} %get-tuple-element.64), channel_id=1, source_target_pairs={{0,24},{8,16},{16,8},{24,0},{1,25},{9,17},{17,9},{25,1},{2,26},{10... | collective-permute-start | bytes 368648 | tf_op jit(solution)/shard_map/ppermute | solution.py:541
  18.4 0.3 %sort_flux.1 = (f32[1,120,128]{2,1,0:T(8,128)S(1)}, f32[1,120,128]{2,1,0:T(8,128)S(1)}, f32[1,120,128]{2,1,0:T(8,128)S(1)}, f32[1,120,128]{2,1,0:T(8,128)S(1)}) custom-call(f32[1,240,256]{2,1,0:T(8,128)S(1)} %collective-permute-done.2.theirs_ref, f32[1,240,256]{2,1,0:T(8,128)S(1)} %kept_flux.1.mine_ref, bf16[512,512]{1,0:T(8,128)(2,1)S(1)} %get-tuple-element.49.table_ref, ...), custom_call_target="tpu_custom_call" | custom-call | tf_op jit(solution)/shard_map/sort_flux/pallas_call | solution.py:527
  18.7 0.4 %collective-permute-start.5 = (f32[1,120,128]{2,1,0:T(8,128)S(1)}, f32[1,120,128]{2,1,0:T(8,128)S(1)}, u32[]{:S(2)}, u32[]{:S(2)}) collective-permute-start(f32[1,120,128]{2,1,0:T(8,128)S(1)} %get-tuple-element.59), channel_id=1, source_target_pairs={{0,16},{8,24},{16,0},{24,8},{1,17},{9,25},{17,1},{25,9},{2,18},{10... | collective-permute-start | bytes 184328 | tf_op jit(solution)/shard_map/ppermute | solution.py:541
  19.2 2.7 %collective-permute-start.6 = (f32[1,120,128]{2,1,0:T(8,128)S(1)}, f32[1,120,128]{2,1,0:T(8,128)S(1)}, u32[]{:S(2)}, u32[]{:S(2)}) collective-permute-start(f32[1,120,128]{2,1,0:T(8,128)S(1)} %get-tuple-element.60), channel_id=1, source_target_pairs={{0,24},{8,16},{16,8},{24,0},{1,25},{9,17},{17,9},{25,1},{2,26},{10... | collective-permute-start | bytes 184328 | tf_op jit(solution)/shard_map/ppermute | solution.py:541
  21.9 0.5 %collective-permute-start.7 = (f32[1,120,128]{2,1,0:T(8,128)S(1)}, f32[1,120,128]{2,1,0:T(8,128)S(1)}, u32[]{:S(2)}, u32[]{:S(2)}) collective-permute-start(f32[1,120,128]{2,1,0:T(8,128)S(1)} %get-tuple-element.61), channel_id=1, source_target_pairs={{0,8},{8,0},{16,24},{24,16},{1,9},{9,1},{17,25},{25,17},{2,10},{10... | collective-permute-start | bytes 184328 | tf_op jit(solution)/shard_map/ppermute | solution.py:541
  22.4 1.6 %place_early.1 = (bf16[512,512]{1,0:T(8,128)(2,1)S(1)}, f32[2,120,512]{2,1,0:T(8,128)S(1)}) custom-call(s32[3]{0:T(128)S(1)} %pad_add_fusion.place_ref, s32[1,1024]{1,0:T(1,128)S(1)} %get-tuple-element.56.slots_ref, f32[2,120,128]{2,1,0:T(8,128)S(1)} %get-tuple-element.57.refs_0_, f32[2,120,128]{2,1,0:T(8,128)S(1)} %collective-permute-done.4.refs_1_), custom_call_target="tpu_custom_call" | custom-call | tf_op jit(solution)/shard_map/place_early/pallas_call | solution.py:570
  24.0 1.2 %collective-permute-done.9.refs_1_ = f32[2,120,128]{2,1,0:T(8,128)S(1)} collective-permute-done((f32[2,120,128]{2,1,0:T(8,128)S(1)}, f32[2,120,128]{2,1,0:T(8,128)S(1)}, u32[]{:S(2)}, u32[]{:S(2)}) %collective-permute-start.9) | collective-permute-done | bytes 122912 | tf_op jit(solution)/shard_map/ppermute | solution.py:541
  25.2 1.8 %end_weights.1 = (f32[240,256]{1,0:T(8,128)}, f32[3,240,256]{2,1,0:T(8,128)}) custom-call(s32[3]{0:T(128)S(1)} %pad_add_fusion.place_ref, bf16[512,512]{1,0:T(8,128)(2,1)S(1)} %get-tuple-element.58.table_ref, f32[2,120,512]{2,1,0:T(8,128)S(1)} %get-tuple-element.62.sums_ref, f32[2,120,128]{2,1,0:T(8,128)S(1)} %collective-permute-done.8.refs_0_, ...), custom_call_target="tpu_custom_call" | custom-call | tf_op jit(solution)/shard_map/end_weights/pallas_call | solution.py:609
  27.0 2.0 %collective-permute-done.5.refs_1_ = f32[1,120,128]{2,1,0:T(8,128)S(1)} collective-permute-done((f32[1,120,128]{2,1,0:T(8,128)S(1)}, f32[1,120,128]{2,1,0:T(8,128)S(1)}, u32[]{:S(2)}, u32[]{:S(2)}) %collective-permute-start.5) | collective-permute-done | bytes 61472 | tf_op jit(solution)/shard_map/ppermute | solution.py:541
  28.9 1.0 %end_flux.1 = f32[240,256]{1,0:T(8,128)} custom-call(bf16[512,512]{1,0:T(8,128)(2,1)S(1)} %get-tuple-element.58.table_ref, f32[1,120,128]{2,1,0:T(8,128)S(1)} %get-tuple-element.54.refs_0_, f32[1,120,128]{2,1,0:T(8,128)S(1)} %collective-permute-done.5.refs_1_, f32[1,120,128]{2,1,0:T(8,128)S(1)} %collective-permute-done.6.refs_2_, ...), custom_call_target="tpu_custom_call" | custom-call | flops 125829120 | bytes 491520 | tf_op jit(solution)/shard_map/end_flux/pallas_call | solution.py:632
  (11 shorter events, 0.0 us)
Async XLA Ops:
  0.6 2.8 %copy-start = (f32[4,480,256]{2,1,0:T(8,128)S(1)}, f32[4,480,256]{2,1,0:T(8,128)}, u32[]{:S(2)}) copy-start(f32[4,480,256]{2,1,0:T(8,128)} %pixels_ref.3) | copy-start | bytes 5898244
  2.9 5.2 %collective-permute-start.3 = (f32[2,240,256]{2,1,0:T(8,128)S(1)}, f32[2,240,256]{2,1,0:T(8,128)S(1)}, u32[]{:S(2)}, u32[]{:S(2)}) collective-permute-start(f32[2,240,256]{2,1,0:T(8,128)S(1)} %get-tuple-element.50), channel_id=1, source_target_pairs={{0,1},{1,0},{2,3},{3,2},{4,5},{5,4},{6,7},{7,6},{8,9},{9,8},{10,11... | collective-permute-start | bytes 1474568 | tf_op jit(solution)/shard_map/ppermute | solution.py:666
  4.6 7.1 %collective-permute-start = (f32[2,8,128]{2,1,0:T(8,128)S(1)}, f32[2,8,128]{2,1,0:T(8,128)S(1)}, u32[]{:S(2)}, u32[]{:S(2)}) collective-permute-start(f32[2,8,128]{2,1,0:T(8,128)S(1)} %get-tuple-element.40), channel_id=1, source_target_pairs={{0,2},{2,4},{4,6},{6,0},{1,3},{3,5},{5,7},{7,1},{8,10},{10,12},{12... | collective-permute-start | bytes 24584 | tf_op jit(solution)/shard_map/ppermute | solution.py:671
  7.2 4.6 %collective-permute-start.1 = (f32[2,8,128]{2,1,0:T(8,128)S(1)}, f32[2,8,128]{2,1,0:T(8,128)S(1)}, u32[]{:S(2)}, u32[]{:S(2)}) collective-permute-start(f32[2,8,128]{2,1,0:T(8,128)S(1)} %get-tuple-element.41), channel_id=1, source_target_pairs={{2,0},{4,2},{6,4},{0,6},{3,1},{5,3},{7,5},{1,7},{10,8},{12,10},{14... | collective-permute-start | bytes 24584 | tf_op jit(solution)/shard_map/ppermute | solution.py:672
  8.7 9.7 %collective-permute-start.4 = (f32[2,120,128]{2,1,0:T(8,128)S(1)}, f32[2,120,128]{2,1,0:T(8,128)S(1)}, u32[]{:S(2)}, u32[]{:S(2)}) collective-permute-start(f32[2,120,128]{2,1,0:T(8,128)S(1)} %get-tuple-element.53), channel_id=1, source_target_pairs={{0,16},{8,24},{16,0},{24,8},{1,17},{9,25},{17,1},{25,9},{2,18},{10... | collective-permute-start | bytes 368648 | tf_op jit(solution)/shard_map/ppermute | solution.py:541
  14.4 4.0 %collective-permute-start.2 = (f32[1,240,256]{2,1,0:T(8,128)S(1)}, f32[1,240,256]{2,1,0:T(8,128)S(1)}, u32[]{:S(2)}, u32[]{:S(2)}) collective-permute-start(f32[1,240,256]{2,1,0:T(8,128)S(1)} %get-tuple-element.45), channel_id=1, source_target_pairs={{0,1},{1,0},{2,3},{3,2},{4,5},{5,4},{6,7},{7,6},{8,9},{9,8},{10,11... | collective-permute-start | bytes 737288 | tf_op jit(solution)/shard_map/ppermute | solution.py:681
  15.2 8.8 %collective-permute-start.8 = (f32[2,120,128]{2,1,0:T(8,128)S(1)}, f32[2,120,128]{2,1,0:T(8,128)S(1)}, u32[]{:S(2)}, u32[]{:S(2)}) collective-permute-start(f32[2,120,128]{2,1,0:T(8,128)S(1)} %get-tuple-element.63), channel_id=1, source_target_pairs={{0,8},{8,0},{16,24},{24,16},{1,9},{9,1},{17,25},{25,17},{2,10},{10... | collective-permute-start | bytes 368648 | tf_op jit(solution)/shard_map/ppermute | solution.py:541
  16.8 8.4 %collective-permute-start.9 = (f32[2,120,128]{2,1,0:T(8,128)S(1)}, f32[2,120,128]{2,1,0:T(8,128)S(1)}, u32[]{:S(2)}, u32[]{:S(2)}) collective-permute-start(f32[2,120,128]{2,1,0:T(8,128)S(1)} %get-tuple-element.64), channel_id=1, source_target_pairs={{0,24},{8,16},{16,8},{24,0},{1,25},{9,17},{17,9},{25,1},{2,26},{10... | collective-permute-start | bytes 368648 | tf_op jit(solution)/shard_map/ppermute | solution.py:541
  18.7 10.2 %collective-permute-start.5 = (f32[1,120,128]{2,1,0:T(8,128)S(1)}, f32[1,120,128]{2,1,0:T(8,128)S(1)}, u32[]{:S(2)}, u32[]{:S(2)}) collective-permute-start(f32[1,120,128]{2,1,0:T(8,128)S(1)} %get-tuple-element.59), channel_id=1, source_target_pairs={{0,16},{8,24},{16,0},{24,8},{1,17},{9,25},{17,1},{25,9},{2,18},{10... | collective-permute-start | bytes 184328 | tf_op jit(solution)/shard_map/ppermute | solution.py:541
  19.2 9.8 %collective-permute-start.6 = (f32[1,120,128]{2,1,0:T(8,128)S(1)}, f32[1,120,128]{2,1,0:T(8,128)S(1)}, u32[]{:S(2)}, u32[]{:S(2)}) collective-permute-start(f32[1,120,128]{2,1,0:T(8,128)S(1)} %get-tuple-element.60), channel_id=1, source_target_pairs={{0,24},{8,16},{16,8},{24,0},{1,25},{9,17},{17,9},{25,1},{2,26},{10... | collective-permute-start | bytes 184328 | tf_op jit(solution)/shard_map/ppermute | solution.py:541
  21.9 7.1 %collective-permute-start.7 = (f32[1,120,128]{2,1,0:T(8,128)S(1)}, f32[1,120,128]{2,1,0:T(8,128)S(1)}, u32[]{:S(2)}, u32[]{:S(2)}) collective-permute-start(f32[1,120,128]{2,1,0:T(8,128)S(1)} %get-tuple-element.61), channel_id=1, source_target_pairs={{0,8},{8,0},{16,24},{24,16},{1,9},{9,1},{17,25},{25,17},{2,10},{10... | collective-permute-start | bytes 184328 | tf_op jit(solution)/shard_map/ppermute | solution.py:541
